TPU v7x, 32 devices: a whole 2x2x4 slice. The times are simulated.
32 devices in a mesh: section: 2 (over core), shard: 4 (over z), rep: 4 (over y, x).
Axes of the slice: x: 2, y: 2, z: 4, core: 2. Of those that a mesh axis runs over, the one named last changes fastest.
Arguments:
- boundary_in: bfloat16 [2, 2, 4, 1024, 1536], P('section', None, 'rep', 'shard'), may hold values from -6 to 6
- lengths: int32 [2, 4, 4], P(None, 'rep'), may hold values from 0 to 1024, as said below
- seq_order: int32 [2, 4, 4], P(None, 'rep'), may hold values from 0 to 3, each once within a row
- norm_gain: bfloat16 [2, 1536], P('section', 'shard'), may hold values from 0.5 to 1.5
- in_weight: bfloat16 [2, 1536, 6448], P('section', 'shard'), may hold values from -0.15625 to 0.15625
- conv_weight: bfloat16 [2, 4, 3328], P('section', None, 'shard'), may hold values from -3 to 3
- conv_bias: bfloat16 [2, 3328], P('section', 'shard'), may hold values from -1.5 to 1.5
- dt_bias: bfloat16 [2, 48], P('section', 'shard'), may hold values from -12 to -3
- a_log: bfloat16 [2, 48], P('section', 'shard'), may hold values from -0.5 to 0.5
- d_skip: bfloat16 [2, 48], P('section', 'shard'), may hold values from 0.5 to 1.5
- out_gain: bfloat16 [2, 3072], P('section', 'shard'), may hold values from 0.5 to 1.5
- out_weight: bfloat16 [2, 3072, 1536], P('section', 'shard'), may hold values from -0.109375 to 0.109375
Outputs:
- boundary: float32 [2, 2, 4, 1024, 1536], P('section', None, 'rep', 'shard')
- norm_gain_grad: float32 [2, 1536], P('section', 'shard')
- in_weight_grad: float32 [2, 1536, 6448], P('section', 'shard')
- conv_weight_grad: float32 [2, 4, 3328], P('section', None, 'shard')
- conv_bias_grad: float32 [2, 3328], P('section', 'shard')
- dt_bias_grad: float32 [2, 48], P('section', 'shard')
- a_log_grad: float32 [2, 48], P('section', 'shard')
- d_skip_grad: float32 [2, 48], P('section', 'shard')
- out_gain_grad: float32 [2, 3072], P('section', 'shard')
- out_weight_grad: float32 [2, 3072, 1536], P('section', 'shard')
Inputs may be any that keep to these rules, and one draw needn't show every extreme that they name: Each row of 4 lengths sums to 1024; in each replica one micro-batch, chosen by the seed, is one sequence of all 1024 tokens with zeros in its other slots; other rows may hold zeros. `seq_order`: each row is a permutation of the 4 slots.
All inputs are finite; a program needn't handle non-finite values.
Results may differ from a plain program's by a relative error of at most 0.025.
Values may be sent and summed in bfloat16 or wider, within the bound.
A program may use at most 384 MiB of HBM per device.

v0:
```python
import jax
import jax.numpy as jnp
from jax import lax
from jax.sharding import PartitionSpec as P

D = 1536
P_SIZE = 64
N = 128
KW = 4
BLOCK = 256
MICRO = 2
NSEQ = 4
DI = 3072
H = 48
CONV = 3328


EPSILON = 1e-05
PRECISE = lax.Precision.HIGHEST


def from_behind(shard, axis, by):
    devices = lax.axis_size(axis)
    pairs = [(i, i + by) for i in range(devices) if 0 <= i + by < devices]
    return lax.ppermute(shard, axis, pairs)


def entering(value, axis, join, neutral):
    count, mine = (lax.axis_size(axis), lax.axis_index(axis))
    pieces = jax.tree.map(lambda part: lax.all_gather(part, axis), value)
    subtotal = jax.tree.map(
        lambda part, zero: jnp.full_like(part, 0) + jnp.asarray(zero, part.dtype), value, neutral
    )

    def turn(position, subtotal):
        longer = join(subtotal, jax.tree.map(lambda part: part[position], pieces))
        return jax.tree.map(lambda new, old: jnp.where(position < mine, new, old), longer, subtotal)

    return lax.fori_loop(0, count - 1, turn, subtotal)


def entering_2(shard, axis, join, neutral):
    count = lax.axis_size(axis)
    place = lax.axis_index(axis)
    ahead = count - 1 - place
    gathered = jax.tree.map(
        lambda a, kind: lax.all_gather(a.astype(kind), axis),
        shard,
        jax.tree.map(lambda a: jnp.bfloat16 if a.dtype == jnp.float32 else a.dtype, shard),
    )
    state = jax.tree.map(lambda a, e: jnp.zeros_like(a) + jnp.asarray(e, a.dtype), shard, neutral)

    def one(turn, state):
        source = count - 1 - turn
        return join(
            state,
            jax.tree.map(
                lambda a, own: lax.dynamic_index_in_dim(a, source, 0, False).astype(own.dtype),
                gathered,
                shard,
            ),
        )

    return lax.fori_loop(0, ahead, one, state)


def contract(left, right, left_dim, right_dim):
    return lax.dot_general(
        left, right, (((left_dim,), (right_dim,)), ((), ())), preferred_element_type=jnp.float32
    )


def input_norm(source, gain):
    inv_rms = lax.rsqrt(jnp.mean(source * source, axis=-1, keepdims=True) + EPSILON)
    return source * inv_rms * gain


def block_step(carry_state, pieces):
    x_heads, b_rows, c_rows, log_decay, step_size, segment, before = pieces
    running = jnp.cumsum(log_decay, axis=0)
    places = jnp.arange(x_heads.shape[0])
    linked = (places[:, None] >= places[None, :]) & (segment[:, None] == segment[None, :])
    linked3 = linked[:, :, None]
    gap_sums = jnp.where(linked3, running[:, None, :] - running[None, :, :], 0.0)
    decays = jnp.where(linked3, jnp.exp(gap_sums), 0.0)
    scores = jnp.dot(c_rows, b_rows.T, precision=PRECISE)
    mixing = scores[:, :, None] * decays * step_size[None, :, :]
    inside_part = jnp.einsum("tsh,shp->thp", mixing, x_heads, precision=PRECISE)
    carried = (segment == before).astype(jnp.float32)
    reach = jnp.exp(running) * carried[:, None]
    carried_part = (
        jnp.einsum("tn,hpn->thp", c_rows, carry_state, precision=PRECISE) * reach[:, :, None]
    )
    closing = segment[-1]
    tail_weight = (
        jnp.exp(running[-1][None, :] - running)
        * step_size
        * (segment == closing).astype(jnp.float32)[:, None]
    )
    fresh_state = jnp.einsum("sh,shp,sn->hpn", tail_weight, x_heads, b_rows, precision=PRECISE)
    retained = jnp.exp(running[-1]) * (closing == before).astype(jnp.float32)
    return (retained[:, None, None] * carry_state + fresh_state, inside_part + carried_part)


def conv_inputs(wide_rows, raw_step, conv_weight, conv_bias, dt_bias, a_log, lag_masks):
    rows_here = raw_step.shape[0]
    conv_sum = conv_bias + conv_weight[KW - 1] * wide_rows[KW - 1 :]
    for lag in range(1, KW):
        conv_sum = (
            conv_sum
            + conv_weight[KW - 1 - lag]
            * wide_rows[KW - 1 - lag : KW - 1 - lag + rows_here]
            * lag_masks[lag - 1][:, None]
        )
    active = jax.nn.silu(conv_sum)
    x_heads = active[:, :DI].reshape(rows_here, H, P_SIZE)
    b_rows = active[:, DI : DI + N]
    c_rows = active[:, DI + N :]
    step_size = jax.nn.softplus(raw_step + dt_bias)
    log_decay = -step_size * jnp.exp(a_log)
    return (x_heads, b_rows, c_rows, log_decay, step_size)


def local_scan(x_heads, b_rows, c_rows, log_decay, step_size, segment, befores, seg_before):
    rows_here = x_heads.shape[0]

    def blocks(member):
        return member.reshape((rows_here // BLOCK, BLOCK) + member.shape[1:])

    start_state = jnp.zeros((H, P_SIZE, N), jnp.float32)
    pieces = (
        blocks(x_heads),
        blocks(b_rows),
        blocks(c_rows),
        blocks(log_decay),
        blocks(step_size),
        blocks(segment),
        befores,
    )
    end_state, mixer_out = lax.scan(jax.checkpoint(block_step), start_state, pieces)
    retained = jnp.exp(jnp.sum(log_decay, axis=0)) * (segment[-1] == seg_before).astype(jnp.float32)
    return (mixer_out.reshape(rows_here, H, P_SIZE), end_state, retained)


def state_entry(c_rows, log_decay, state_in, carried):
    reach = jnp.exp(jnp.cumsum(log_decay, axis=0)) * carried[:, None]
    return jnp.einsum("tn,hpn->thp", c_rows, state_in, precision=PRECISE) * reach[:, :, None]


def gate_norm(mixer_out, x_heads, d_skip, gate_part, out_gain):
    rows_here = x_heads.shape[0]
    total_out = mixer_out + d_skip[:, None] * x_heads
    gated = total_out.reshape(rows_here, DI) * jax.nn.silu(gate_part)
    inv_gated = lax.rsqrt(jnp.mean(gated * gated, axis=-1, keepdims=True) + EPSILON)
    return gated * inv_gated * out_gain


def carry_forward(earlier, later):
    return (earlier[0] * later[0], later[0][:, None, None] * earlier[1] + later[1])


def carry_backward(earlier, later):
    return (later[0] * earlier[0], later[1] + later[0][:, None, None] * earlier[1])


def segment_marks(lengths, seq_order, micro_slot, row_start, rows_here):
    micro_slot = jnp.clip(micro_slot, 0, MICRO - 1)
    seq_lengths = lax.dynamic_index_in_dim(lengths[:, 0], micro_slot, 0, keepdims=False)
    row_order = lax.dynamic_index_in_dim(seq_order[:, 0], micro_slot, 0, keepdims=False)
    picks = (row_order[:, None] == jnp.arange(NSEQ, dtype=jnp.int32)[None, :]).astype(jnp.int32)
    placed = jnp.sum(picks * seq_lengths[None, :], axis=1)
    finish = jnp.cumsum(placed, dtype=jnp.int32)
    positions = row_start + jnp.arange(-(KW - 1), rows_here, dtype=jnp.int32)
    extended = jnp.sum((positions[:, None] >= finish[None, :]).astype(jnp.int32), axis=1)
    extended = jnp.where(positions < 0, -1, extended)
    segment = extended[KW - 1 :]
    seg_before = extended[KW - 2]
    lag_masks = jnp.stack(
        [
            (extended[KW - 1 - lag : KW - 1 - lag + rows_here] == segment).astype(jnp.float32)
            for lag in range(1, KW)
        ]
    )
    befores = jnp.concatenate([seg_before[None], segment[:-1]])[::BLOCK]
    carried = (segment == seg_before).astype(jnp.float32)
    return (segment, lag_masks, befores, seg_before, carried)


def mixer_pass(projected, weights, marks):
    norm_gain, in_weight, conv_weight, conv_bias, dt_bias, a_log, d_skip, out_gain, out_weight = (
        weights
    )
    segment, lag_masks, befores, seg_before, carried = marks
    rows_here = projected.shape[0]
    gate_part = projected[:, :DI].astype(jnp.float32)
    mixed_part = projected[:, DI : DI + CONV]
    raw_step = projected[:, DI + CONV :].astype(jnp.float32)
    rim_rows = from_behind(mixed_part[rows_here - (KW - 1) :], "shard", 1)
    wide_rows = jnp.concatenate([rim_rows, mixed_part], axis=0).astype(jnp.float32)

    def conv_section(wide_rows, raw_step, conv_weight, conv_bias, dt_bias, a_log):
        return conv_inputs(wide_rows, raw_step, conv_weight, conv_bias, dt_bias, a_log, lag_masks)

    conv_outs, conv_pull = jax.vjp(
        conv_section, wide_rows, raw_step, conv_weight, conv_bias, dt_bias, a_log
    )
    x_heads, b_rows, c_rows, log_decay, step_size = conv_outs

    def scan_section(x_heads, b_rows, c_rows, log_decay, step_size):
        return local_scan(
            x_heads, b_rows, c_rows, log_decay, step_size, segment, befores, seg_before
        )

    scan_outs, scan_pull = jax.vjp(scan_section, x_heads, b_rows, c_rows, log_decay, step_size)
    local_out, end_state, retained = scan_outs
    identity = (jnp.ones((H,), jnp.float32), jnp.zeros((H, P_SIZE, N), jnp.float32))
    prefix = entering((retained, end_state), "shard", carry_forward, identity)
    state_in = prefix[1]

    def entry_section(c_rows, log_decay, state_in):
        return state_entry(c_rows, log_decay, state_in, carried)

    entered, entry_pull = jax.vjp(entry_section, c_rows, log_decay, state_in)
    mixer_out = local_out + entered
    outgoing, norm_pull = jax.vjp(gate_norm, mixer_out, x_heads, d_skip, gate_part, out_gain)
    return (
        outgoing.astype(jnp.bfloat16),
        (conv_pull, scan_pull, entry_pull, norm_pull, retained, state_in),
    )


def mamba_forward(source, weights, marks):
    normed = input_norm(source, weights[0]).astype(jnp.bfloat16)
    projected = jnp.dot(normed, weights[1], preferred_element_type=jnp.float32).astype(jnp.bfloat16)
    outgoing, unused_pulls = mixer_pass(projected, weights, marks)
    return source + jnp.dot(outgoing, weights[8], preferred_element_type=jnp.float32)


def mamba_backward(source, incoming, weights, marks):
    norm_gain, in_weight, conv_weight, conv_bias, dt_bias, a_log, d_skip, out_gain, out_weight = (
        weights
    )
    rows_here = source.shape[0]
    normed, front_pull = jax.vjp(input_norm, source, norm_gain)
    normed_low = normed.astype(jnp.bfloat16)
    projected = jnp.dot(normed_low, in_weight, preferred_element_type=jnp.float32).astype(
        jnp.bfloat16
    )
    outgoing, pulls = mixer_pass(projected, weights, marks)
    conv_pull, scan_pull, entry_pull, norm_pull, retained, state_in = pulls
    incoming_low = incoming.astype(jnp.bfloat16)
    out_weight_grad = contract(outgoing, incoming_low, 0, 0)
    outgoing_grad = contract(incoming_low, out_weight, 1, 1)
    mixer_grad, x_grad_a, d_skip_grad, gate_grad, out_gain_grad = norm_pull(outgoing_grad)
    c_grad_a, decay_grad_a, direct = entry_pull(mixer_grad)
    identity = (jnp.ones((H,), jnp.float32), jnp.zeros((H, P_SIZE, N), jnp.float32))
    suffix = entering_2((retained, direct), "shard", carry_backward, identity)
    later_grad = suffix[1]
    retained_grad = jnp.sum(later_grad * state_in, axis=(1, 2))
    x_grad_b, b_grad, c_grad_b, decay_grad_b, step_grad = scan_pull(
        (mixer_grad, later_grad, retained_grad)
    )
    conv_grads = conv_pull(
        (x_grad_a + x_grad_b, b_grad, c_grad_a + c_grad_b, decay_grad_a + decay_grad_b, step_grad)
    )
    wide_grad, raw_grad, conv_weight_grad, conv_bias_grad, dt_bias_grad, a_log_grad = conv_grads
    back_rows = from_behind(wide_grad[: KW - 1].astype(jnp.bfloat16), "shard", -1).astype(
        jnp.float32
    )
    filler = jnp.zeros((rows_here - (KW - 1), CONV), jnp.float32)
    mixed_grad = wide_grad[KW - 1 :] + jnp.concatenate([filler, back_rows], axis=0)
    projected_grad = jnp.concatenate([gate_grad, mixed_grad, raw_grad], axis=1).astype(jnp.bfloat16)
    in_weight_grad = contract(normed_low, projected_grad, 0, 0)
    normed_grad = contract(projected_grad, in_weight, 1, 1)
    source_grad, norm_gain_grad = front_pull(normed_grad)
    weight_grads = (
        norm_gain_grad,
        in_weight_grad,
        conv_weight_grad,
        conv_bias_grad,
        dt_bias_grad,
        a_log_grad,
        d_skip_grad,
        out_gain_grad,
        out_weight_grad,
    )
    return (incoming + source_grad, weight_grads)


def per_device(
    boundary_in,
    lengths,
    seq_order,
    norm_gain,
    in_weight,
    conv_weight,
    conv_bias,
    dt_bias,
    a_log,
    d_skip,
    out_gain,
    out_weight,
):
    section_index = lax.axis_index("section")
    is_first = section_index == 0
    rows_here = boundary_in.shape[3]
    row_start = lax.axis_index("shard") * rows_here

    def current():
        whole = (
            lax.all_gather(norm_gain, "shard", axis=1, tiled=True),
            lax.all_gather(in_weight, "shard", axis=1, tiled=True),
            lax.all_gather(conv_weight, "shard", axis=2, tiled=True),
            lax.all_gather(conv_bias, "shard", axis=1, tiled=True),
            lax.all_gather(dt_bias, "shard", axis=1, tiled=True),
            lax.all_gather(a_log, "shard", axis=1, tiled=True),
            lax.all_gather(d_skip, "shard", axis=1, tiled=True),
            lax.all_gather(out_gain, "shard", axis=1, tiled=True),
            lax.all_gather(out_weight, "shard", axis=1, tiled=True),
        )
        return tuple(
            (
                member[0] if slot_index in (1, 8) else member[0].astype(jnp.float32)
                for slot_index, member in enumerate(whole)
            )
        )

    source_rows = boundary_in[0, :, 0]
    arrived = jnp.zeros((rows_here, D), jnp.bfloat16)
    inputs = []
    results = []
    for step_index in range(MICRO + 1):
        own_rows = source_rows[min(step_index, MICRO - 1)]
        layer_in = jnp.where(is_first, own_rows, arrived)
        inputs.append(layer_in)
        marks = segment_marks(lengths, seq_order, step_index - section_index, row_start, rows_here)
        layer_out = mamba_forward(layer_in.astype(jnp.float32), current(), marks)
        results.append(layer_out)
        if step_index < MICRO:
            arrived = from_behind(layer_out.astype(jnp.bfloat16), "section", 1)
    returned = jnp.zeros((rows_here, D), jnp.bfloat16)
    totals = None
    source_grads = []
    for step_index in range(MICRO + 1):
        micro_slot = step_index - 1 + section_index
        is_valid = (micro_slot >= 0) & (micro_slot < MICRO)
        own_rows = source_rows[min(step_index, MICRO - 1)]
        incoming = jnp.where(is_first, returned, own_rows).astype(jnp.float32)
        incoming = jnp.where(is_valid, incoming, 0.0)
        layer_in = jnp.where(
            is_first, inputs[max(step_index - 1, 0)], inputs[min(step_index + 1, MICRO)]
        )
        marks = segment_marks(lengths, seq_order, micro_slot, row_start, rows_here)
        source_grad, weight_grads = mamba_backward(
            layer_in.astype(jnp.float32), incoming, current(), marks
        )
        if totals is None:
            totals = tuple(weight_grads)
        else:
            totals = tuple((earlier + added for earlier, added in zip(totals, weight_grads)))
        source_grads.append(source_grad)
        if step_index < MICRO:
            returned = from_behind(source_grad.astype(jnp.bfloat16), "section", -1)
    boundary = jnp.stack(
        [
            jnp.where(is_first, source_grads[micro_pos + 1], results[micro_pos + 1])
            for micro_pos in range(MICRO)
        ]
    )[None, :, None]
    shares = (
        lax.psum_scatter(
            totals[0][None].astype(jnp.bfloat16), "shard", scatter_dimension=1, tiled=True
        ).astype(jnp.float32),
        lax.psum_scatter(
            totals[1][None].astype(jnp.bfloat16), "shard", scatter_dimension=1, tiled=True
        ).astype(jnp.float32),
        lax.psum_scatter(
            totals[2][None].astype(jnp.bfloat16), "shard", scatter_dimension=2, tiled=True
        ).astype(jnp.float32),
        lax.psum_scatter(
            totals[3][None].astype(jnp.bfloat16), "shard", scatter_dimension=1, tiled=True
        ).astype(jnp.float32),
        lax.psum_scatter(
            totals[4][None].astype(jnp.bfloat16), "shard", scatter_dimension=1, tiled=True
        ).astype(jnp.float32),
        lax.psum_scatter(
            totals[5][None].astype(jnp.bfloat16), "shard", scatter_dimension=1, tiled=True
        ).astype(jnp.float32),
        lax.psum_scatter(
            totals[6][None].astype(jnp.bfloat16), "shard", scatter_dimension=1, tiled=True
        ).astype(jnp.float32),
        lax.psum_scatter(
            totals[7][None].astype(jnp.bfloat16), "shard", scatter_dimension=1, tiled=True
        ).astype(jnp.float32),
        lax.psum_scatter(
            totals[8][None].astype(jnp.bfloat16), "shard", scatter_dimension=1, tiled=True
        ).astype(jnp.float32),
    )
    reduced = (
        lax.psum(shares[0].astype(jnp.bfloat16), "rep").astype(jnp.float32),
        lax.psum(shares[1].astype(jnp.bfloat16), "rep").astype(jnp.float32),
        lax.psum(shares[2].astype(jnp.bfloat16), "rep").astype(jnp.float32),
        lax.psum(shares[3].astype(jnp.bfloat16), "rep").astype(jnp.float32),
        lax.psum(shares[4].astype(jnp.bfloat16), "rep").astype(jnp.float32),
        lax.psum(shares[5].astype(jnp.bfloat16), "rep").astype(jnp.float32),
        lax.psum(shares[6].astype(jnp.bfloat16), "rep").astype(jnp.float32),
        lax.psum(shares[7].astype(jnp.bfloat16), "rep").astype(jnp.float32),
        lax.psum(shares[8].astype(jnp.bfloat16), "rep").astype(jnp.float32),
    )
    return (boundary,) + tuple(reduced)


def solution(mesh):
    return jax.shard_map(
        per_device,
        mesh=mesh,
        in_specs=(
            P("section", None, "rep", "shard", None),
            P(None, "rep", None),
            P(None, "rep", None),
            P("section", "shard"),
            P("section", "shard", None),
            P("section", None, "shard"),
            P("section", "shard"),
            P("section", "shard"),
            P("section", "shard"),
            P("section", "shard"),
            P("section", "shard"),
            P("section", "shard", None),
        ),
        out_specs=(
            P("section", None, "rep", "shard", None),
            P("section", "shard"),
            P("section", "shard", None),
            P("section", None, "shard"),
            P("section", "shard"),
            P("section", "shard"),
            P("section", "shard"),
            P("section", "shard"),
            P("section", "shard"),
            P("section", "shard", None),
        ),
        check_vma=False,
    )
```

profile of v0, /device:TPU:16, one launch (start us, length us, event | category | flops | bytes accessed | tf_op | source)
XLA Modules:
  0.0 3058.9 jit_solution(5378442103072952849)
XLA Ops:
  25.1 67.3 %all_gather.73 = bf16[1,4,3328]{1,0,2:T(2,128)(2,1)S(1)} all-gather(bf16[1,4,832]{1,0,2:T(2,128)(2,1)S(1)} %copy.739), channel_id=1, replica_groups=mesh['section'=2,'shard'=4,'rep'=4] {'shard'}, dimensions={2}, use_global_device_ids=true | all-gather | bytes 33280 | tf_op jit(solution)/shard_map/all_gather | solution.py:313
  114.6 69.9 %slice_reduce_fusion.3 = (f32[3328]{0:T(1024)S(1)}, f32[3328]{0:T(1024)S(1)}, f32[3328]{0:T(1024)S(1)}, f32[3328]{0:T(1024)S(1)}) fusion(f32[1,4,3328]{1,0,2:T(1,128)S(1)} %convert_element_type.802), kind=kLoop, calls=%fused_computation.475 | loop fusion | bytes 106496 | tf_op jit(solution)/shard_map/jvp()/slice | solution.py:107
  184.6 190.3 %all-gather.30.cloned.1.call-done = bf16[1,1536,6448]{1,2,0:T(8,128)(2,1)} async-done(((bf16[1,384,6448]{1,2,0:T(8,128)(2,1)}), bf16[1,1536,6448]{1,2,0:T(8,128)(2,1)}) %all-gather.30.cloned.1.call-update) | async-done | bytes 19808272 | tf_op jit(solution)/shard_map/all_gather | solution.py:312
  448.2 77.8 %all-gather.34.cloned.1.call-done = f32[192,64,128]{2,1,0:T(8,128)} async-done(((f32[48,64,128]{2,1,0:T(8,128)}), f32[192,64,128]{2,1,0:T(8,128)}) %all-gather.34.cloned.1.call-update) | async-done | bytes 6291472 | tf_op jit(solution)/shard_map/all_gather | solution.py:30
  535.2 18.7 fusion.259
  561.2 131.4 %all-gather.32.cloned.1.call-done = bf16[1,3072,1536]{2,1,0:T(8,128)(2,1)} async-done(((bf16[1,768,1536]{2,1,0:T(8,128)(2,1)}), bf16[1,3072,1536]{2,1,0:T(8,128)(2,1)}) %all-gather.32.cloned.1.call-update) | async-done | bytes 9437200 | tf_op jit(solution)/shard_map/all_gather | solution.py:319
  777.4 86.2 %all-gather.40.cloned.1.call-done = f32[192,64,128]{2,1,0:T(8,128)} async-done(((f32[48,64,128]{2,1,0:T(8,128)}), f32[192,64,128]{2,1,0:T(8,128)}) %all-gather.40.cloned.1.call-update) | async-done | bytes 6291472 | tf_op jit(solution)/shard_map/all_gather | solution.py:30
  872.7 18.6 fusion.252
  1083.1 40.2 %all-gather.36.cloned.1.call-done = f32[192,64,128]{2,1,0:T(8,128)} async-done(((f32[48,64,128]{2,1,0:T(8,128)}), f32[192,64,128]{2,1,0:T(8,128)}) %all-gather.36.cloned.1.call-update) | async-done | bytes 6291472 | tf_op jit(solution)/shard_map/all_gather | solution.py:30
  1140.9 19.0 fusion.257
  1297.0 20.4 fusion.117
  1438.4 37.5 %all-gather.42.cloned.1.call-done = f32[192,64,128]{2,1,0:T(8,128)} async-done(((f32[48,64,128]{2,1,0:T(8,128)}), f32[192,64,128]{2,1,0:T(8,128)}) %all-gather.42.cloned.1.call-update) | async-done | bytes 6291472 | tf_op jit(solution)/shard_map/all_gather | solution.py:30
  1485.9 18.9 fusion.250
  1568.8 23.6 all-gather.44.cloned.1.call-done
  1616.5 20.4 fusion.119
  1747.7 31.9 %all-gather.46.cloned.1.call-done = f32[192,64,128]{2,1,0:T(8,128)} async-done(((f32[48,64,128]{2,1,0:T(8,128)}), f32[192,64,128]{2,1,0:T(8,128)}) %all-gather.46.cloned.1.call-update) | async-done | bytes 6291472 | tf_op jit(solution)/shard_map/all_gather | solution.py:30
  1793.1 19.0 fusion.245
  1841.6 18.4 fusion.431
  1860.0 17.9 fusion.430
  1929.5 20.4 fusion.121
  2023.4 33.2 %fusion.6 = bf16[1,1536,6448]{1,2,0:T(8,128)(2,1)} fusion(f32[1536,6448]{0,1:T(8,128)} %fusion.431, f32[1536,6448]{0,1:T(8,128)} %fusion.430, bf16[256,48]{1,0:T(8,128)(2,1)S(1)} %get-tuple-element.2022, bf16[256,3328]{1,0:T(8,128)(2,1)S(1)} %fusion.189, bf16[256,3072]{1,0:T(8,128)(2,1)S(1)} %copy-done.69, bf16[256,1536]{1,0:T(8,128)(2,1)S(1)} %copy-done.75, ...), kind=kOutput, calls=%fused_computation.25 | convolution fusion | flops 5112102912 | bytes 103136256 | tf_op jit(solution)/shard_map/dot_general | solution.py:68
  2056.5 84.9 %copy.881 = bf16[1,1536,6448]{2,0,1:T(2,128)(2,1)} copy(bf16[1,1536,6448]{1,2,0:T(8,128)(2,1)} %fusion.6) | data formatting | bytes 39616512
  2141.4 27.3 copy.899
  2188.9 17.6 fusion.85
  2276.4 229.0 %reduce-scatter.24.cloned.1.call-done = bf16[384,6448]{1,0:T(8,128)(2,1)} async-done(((bf16[1536,6448]{1,0:T(8,128)(2,1)}), bf16[384,6448]{1,0:T(8,128)(2,1)}) %reduce-scatter.24.cloned.1.call-update) | async-done | bytes 4952080
  2513.2 21.5 copy.882
  2534.7 135.7 %reduce-scatter.20.cloned.1.call-done = bf16[1,768,1536]{2,1,0:T(8,128)(2,1)} async-done(((bf16[1,3072,1536]{2,1,0:T(8,128)(2,1)}), bf16[1,768,1536]{2,1,0:T(8,128)(2,1)}) %reduce-scatter.20.cloned.1.call-update) | async-done | bytes 2359312 | tf_op jit(solution)/shard_map/reduce_scatter | solution.py:395
  2721.1 20.7 reduce-scatter.22.cloned.1.call-done
  2742.8 23.8 reduce-scatter.26.cloned.1.call-done
  2788.7 93.8 %all-gather.50.cloned.1.call-done = f32[192,64,128]{2,1,0:T(8,128)} async-done(((f32[48,64,128]{2,1,0:T(8,128)}), f32[192,64,128]{2,1,0:T(8,128)}) %all-gather.50.cloned.1.call-update) | async-done | bytes 6291472 | tf_op jit(solution)/shard_map/all_gather | solution.py:30
  2891.6 18.7 fusion.240
  2925.4 116.5 %all-reduce.66.cloned.1.call-done = (bf16[1,384,6448]{1,2,0:T(8,128)(2,1)}, bf16[1,768,1536]{2,1,0:T(8,128)(2,1)}) async-done(((bf16[1,384,6448]{1,2,0:T(8,128)(2,1)}, bf16[1,768,1536]{2,1,0:T(8,128)(2,1)}), (bf16[1,384,6448]{1,2,0:T(8,128)(2,1)}, bf16[1,768,1536]{2,1,0:T(8,128)(2,1)})) %all-reduce.66.cloned.1.call-update) | async-done | bytes 7311376 | tf_op jit(solution)/shard_map/psum | solution.py:401
  (1284 shorter events, 1297.3 us)
Async XLA Ops:
  7.3 367.6 %all-gather.30.cloned.1.call-start = ((), (), s32[]{:S(2)}) async-start(), calls=%async_computation.6 | async-start | bytes 24760320 | tf_op jit(solution)/shard_map/all_gather | solution.py:312
  8.0 518.0 %all-gather.34.cloned.1.call-start = ((), (), s32[]{:S(2)}) async-start(), calls=%async_computation.9 | async-start | bytes 7864320 | tf_op jit(solution)/shard_map/all_gather | solution.py:30
  94.1 634.5 %copy-start.172 = (f32[48]{0:T(128)}, f32[48]{0:T(128)S(1)}, u32[]{:S(2)}) copy-start(f32[48]{0:T(128)S(1)} %add.1238) | copy-start | bytes 580
  385.6 8.3 collective-permute-start
  411.6 281.0 %all-gather.32.cloned.1.call-start = ((), (), s32[]{:S(2)}) async-start(), calls=%async_computation.7 | async-start | bytes 11796480 | tf_op jit(solution)/shard_map/all_gather | solution.py:319
  412.4 451.2 %all-gather.40.cloned.1.call-start = ((), (), s32[]{:S(2)}) async-start(), calls=%async_computation.12 | async-start | bytes 7864320 | tf_op jit(solution)/shard_map/all_gather | solution.py:30
  700.7 6.8 collective-permute-start.1
  722.1 10.8 collective-permute-start.5
  749.3 374.0 %all-gather.36.cloned.1.call-start = ((), (), s32[]{:S(2)}) async-start(), calls=%async_computation.10 | async-start | bytes 7864320 | tf_op jit(solution)/shard_map/all_gather | solution.py:30
  904.8 19.7 collective-permute-start.6
  917.5 5.8 collective-permute-start.2
  939.6 46.7 %collective-permute-start.10 = (bf16[3,3328]{1,0:T(4,128)(2,1)}, bf16[3,3328]{1,0:T(4,128)(2,1)}, u32[]{:S(2)}, u32[]{:S(2)}) collective-permute-start(bf16[3,3328]{1,0:T(4,128)(2,1)} %slice.918), channel_id=1, source_target_pairs={{0,4},{4,8},{8,12},{1,5},{5,9},{9,13},{2,6},{6,10},{10,14},{3,7},{... | collective-permute-start | bytes 59912 | tf_op jit(solution)/shard_map/ppermute | solution.py:25
  1008.6 247.7 %all-gather.38.cloned.1.call-start = ((), (), s32[]{:S(2)}) async-start(), calls=%async_computation.11 | async-start | bytes 3932160 | tf_op jit(solution)/shard_map/all_gather | solution.py:47
  1035.5 174.4 %collective-permute-start.7 = (bf16[3,3328]{1,0:T(4,128)(2,1)}, bf16[3,3328]{1,0:T(4,128)(2,1)}, u32[]{:S(2)}, u32[]{:S(2)}) collective-permute-start(bf16[3,3328]{1,0:T(4,128)(2,1)} %slice.898), channel_id=1, source_target_pairs={{0,4},{4,8},{8,12},{1,5},{5,9},{9,13},{2,6},{6,10},{10,14},{3,7},{... | collective-permute-start | bytes 59912 | tf_op jit(solution)/shard_map/ppermute | solution.py:25
  1037.4 174.5 %collective-permute-start.12 = (bf16[3,3328]{1,0:T(4,128)(2,1)}, bf16[3,3328]{1,0:T(4,128)(2,1)}, u32[]{:S(2)}, u32[]{:S(2)}) collective-permute-start(bf16[3,3328]{1,0:T(4,128)(2,1)} %slice.938), channel_id=1, source_target_pairs={{0,4},{4,8},{8,12},{1,5},{5,9},{9,13},{2,6},{6,10},{10,14},{3,7},{... | collective-permute-start | bytes 59912 | tf_op jit(solution)/shard_map/ppermute | solution.py:25
  1189.3 286.6 %all-gather.42.cloned.1.call-start = ((), (), s32[]{:S(2)}) async-start(), calls=%async_computation.13 | async-start | bytes 7864320 | tf_op jit(solution)/shard_map/all_gather | solution.py:30
  1353.3 239.1 %all-gather.44.cloned.1.call-start = ((), (), s32[]{:S(2)}) async-start(), calls=%async_computation.14 | async-start | bytes 3932160 | tf_op jit(solution)/shard_map/all_gather | solution.py:47
  1400.9 10.8 collective-permute-start.3
  1424.5 11.7 collective-permute-start.4
  1530.1 249.6 %all-gather.46.cloned.1.call-start = ((), (), s32[]{:S(2)}) async-start(), calls=%async_computation.15 | async-start | bytes 7864320 | tf_op jit(solution)/shard_map/all_gather | solution.py:30
  1662.8 241.1 %all-gather.48.cloned.1.call-start = ((), (), s32[]{:S(2)}) async-start(), calls=%async_computation.16 | async-start | bytes 3932160 | tf_op jit(solution)/shard_map/all_gather | solution.py:47
  1710.8 6.4 collective-permute-start.8
  1730.7 14.7 collective-permute-start.9
  1841.6 663.8 %reduce-scatter.24.cloned.1.call-start = ((), (), s32[]{:S(2)}) async-start(), calls=%async_computation.19 | async-start | bytes 25067520
  2015.9 5.9 collective-permute-start.11
  2168.8 501.5 %reduce-scatter.20.cloned.1.call-start = ((), (), s32[]{:S(2)}) async-start(), calls=%async_computation.8 | async-start | bytes 11796480 | tf_op jit(solution)/shard_map/reduce_scatter | solution.py:395
  2206.6 487.8 %reduce-scatter.30.cloned.1.call-start = ((), (), s32[]{:S(2)}) async-start(), calls=%async_computation.22 | async-start | bytes 983040
  2234.5 485.5 %reduce-scatter.28.cloned.1.call-start = ((), (), s32[]{:S(2)}) async-start(), calls=%async_computation.21 | async-start | bytes 1064960
  2240.8 501.0 %reduce-scatter.22.cloned.1.call-start = ((), (), s32[]{:S(2)}) async-start(), calls=%async_computation.18 | async-start | bytes 491520
  2258.2 508.4 %reduce-scatter.26.cloned.1.call-start = ((), (), s32[]{:S(2)}) async-start(), calls=%async_computation.20 | async-start | bytes 1064960
  2267.7 614.7 %all-gather.50.cloned.1.call-start = ((), (), s32[]{:S(2)}) async-start(), calls=%async_computation.17 | async-start | bytes 7864320 | tf_op jit(solution)/shard_map/all_gather | solution.py:30
  2273.5 768.4 %all-reduce.66.cloned.1.call-start = ((), (), s32[]{:S(2)}) async-start(), calls=%async_computation.23 | async-start | bytes 14622720 | tf_op jit(solution)/shard_map/psum | solution.py:401
  (307 other events, 5199.9 us)
Sparse Core Ops, SparseCore 0:
  9.7 365.1 all-gather.29
  411.7 114.2 all-gather.33
  527.6 164.9 all-gather.31
  749.5 114.0 all-gather.39
  1008.7 114.5 all-gather.35
  1189.4 63.3 all-gather.37
  1353.4 122.4 all-gather.41
  1530.2 62.1 all-gather.43
  1662.9 116.7 all-gather.45
  1841.7 62.1 all-gather.47
  2168.9 336.4 reduce-scatter.23
  2508.2 162.0 reduce-scatter.19
  2672.6 21.6 reduce-scatter.29
  2696.5 23.4 reduce-scatter.27
  2722.2 19.5 reduce-scatter.21
  2744.0 22.5 reduce-scatter.25
  2768.1 114.2 all-gather.49
  2886.2 155.6 all-reduce.65
where the time goes:
time: 3080 us; the launch traced here: 3060 us
  waiting for transfers between devices  1290 us (42%)
  matrix products  691 us (22%)
  local copies, waits for them, and re-layouts  495 us (16%)
  other arithmetic  333 us (11%)
  blocking collectives  177 us (6%)
  between operations  41.1 us (1%)
  starting transfers between devices  35.6 us (1%)
    all_gather x6, waiting for transfers between devices, entering(): pieces = jax.tree.map(lambda part: lax.all_gather(part, axis), value)  367 us
    unnamed x23, waiting for transfers between devices  307 us
    dot_general x12, matrix products, block_step(): inside_part = jnp.einsum('tsh,shp->thp', mixing, x_heads, precision=PRECISE)  216 us
    all_gather x1, waiting for transfers between devices, current(): lax.all_gather(in_weight, 'shard', axis=1, tiled=True)  190 us
    unnamed x651, local copies, waits for them, and re-layouts  177 us
    dot_general x12, matrix products, contract(): lax.dot_general(left, right, (((left_dim,), (right_dim,)), ((), ())), pre...  165 us
    reduce_scatter x1, waiting for transfers between devices, per_device(): lax.psum_scatter(totals[8][None].astype(jnp.bfloat16), 'shard', scatter_d...  136 us
    all_gather x1, waiting for transfers between devices, current(): lax.all_gather(out_weight, 'shard', axis=1, tiled=True)  131 us
  transfers between devices with their start and end apart: 31, of which 21 were waited for; matrix products, arithmetic and copies ran while one was open for 27% of the time, Pallas kernels for 0%

commit v1 on v0

--- a/solution.py
+++ b/solution.py
@@ -1,6 +1,10 @@
+import functools
+
 import jax
 import jax.numpy as jnp
 from jax import lax
+from jax.experimental import pallas as pl
+from jax.experimental.pallas import tpu as pltpu
 from jax.sharding import PartitionSpec as P
 
 D = 1536
@@ -410,9 +414,1244 @@
     return (boundary,) + tuple(reduced)
 
 
+Q = 128
+LANES = 128
+VMEM_BYTES = 56 * 1024 * 1024
+EXACT = lax.Precision.HIGHEST
+
+
+def mm(a, b, da=1, db=0):
+    return lax.dot_general(
+        a, b, (((da,), (db,)), ((), ())), preferred_element_type=jnp.float32
+    )
+
+
+def exact(a, b):
+    return jnp.dot(a, b, precision=EXACT, preferred_element_type=jnp.float32)
+
+
+def low(v):
+    return v.astype(jnp.bfloat16)
+
+
+def iota(shape, dim):
+    return lax.broadcasted_iota(jnp.int32, shape, dim)
+
+
+def pair_cols(v, p):
+    rows = v.shape[0]
+    left = jnp.broadcast_to(v[:, 2 * p : 2 * p + 1], (rows, LANES))
+    right = jnp.broadcast_to(v[:, 2 * p + 1 : 2 * p + 2], (rows, LANES))
+    return jnp.where(iota((rows, LANES), 1) < LANES // 2, left, right)
+
+
+def widen(v, pairs):
+    return jnp.concatenate([pair_cols(v, p) for p in range(pairs)], axis=1)
+
+
+def stack_pair(v, p):
+    block = v[:, p * LANES : (p + 1) * LANES]
+    left = iota(block.shape, 1) < LANES // 2
+    zero = jnp.zeros_like(block)
+    return jnp.concatenate([jnp.where(left, block, zero), jnp.where(left, zero, block)], axis=0)
+
+
+def softplus(v):
+    small = jnp.exp(-jnp.abs(v))
+    series = small * (1 + small * (-1 / 2 + small * (1 / 3 + small * (-1 / 4 + small / 5))))
+    return jnp.maximum(v, 0.0) + jnp.where(small < 0.01, series, jnp.log(1 + small))
+
+
+def sigmoid(v):
+    return 1.0 / (1.0 + jnp.exp(-v))
+
+
+def chunk_parts(width, proj, before8, marks, seg_row, conv_w, conv_b, dt_bias, rate, pick):
+    span = width + 2 * LANES
+    gate = proj[:, :width].astype(jnp.float32)
+    mixed = proj[:, width : width + span].astype(jnp.float32)
+    raw = mm(proj[:, width + span :], pick)
+    shifts = [mixed]
+    top = iota((8, span), 0)
+    for lag in range(1, KW):
+        rolled = pltpu.roll(mixed, lag, 0)
+        head = jnp.where(top < lag, pltpu.roll(before8, lag, 0), rolled[:8])
+        moved = jnp.concatenate([head, rolled[8:]], axis=0)
+        shifts.append(moved * marks[:, lag - 1 : lag])
+    conv = conv_b
+    for lag in range(KW):
+        conv = conv + conv_w[KW - 1 - lag : KW - lag] * shifts[lag]
+    sig = sigmoid(conv)
+    active = conv * sig
+    stepped = raw + dt_bias
+    step = softplus(stepped)
+    decay = -step * rate
+    lower = iota((Q, Q), 0) >= iota((Q, Q), 1)
+    total = exact(lower.astype(jnp.float32), decay)
+    linked = lower & (marks[:, 5:6] == seg_row)
+    shut = jnp.where(linked, 0.0, -1e30)
+    reach = jnp.exp(total) * marks[:, 3:4]
+    tail = jnp.exp(total[Q - 1 : Q] - total) * marks[:, 4:5]
+    return gate, mixed, shifts, conv, sig, active, stepped, step, decay, total, shut, reach, tail
+
+
+def forward_kernel(
+    width, proj_ref, marks_ref, seg_ref, conv_w_ref, conv_b_ref, dt_bias_ref, rate_ref, pick_ref,
+    skip_ref, gain_ref, gg_ref, squares_ref, mixer_ref, starts_ref, state, before,
+):
+    pairs = width // LANES
+
+    @pl.when(pl.program_id(0) == 0)
+    def _():
+        state[...] = jnp.zeros_like(state)
+        before[...] = jnp.zeros_like(before)
+
+    gate, mixed, _, _, _, active, _, step, _, total, shut, reach, tail = chunk_parts(
+        width, proj_ref[...], before[...], marks_ref[...], seg_ref[...], conv_w_ref[...],
+        conv_b_ref[...], dt_bias_ref[...], rate_ref[...], pick_ref[...],
+    )
+    before[...] = mixed[Q - 8 :]
+    heads = active[:, :width]
+    b_low = low(active[:, width : width + LANES])
+    c_low = low(active[:, width + LANES :])
+    entry = state[...]
+    starts_ref[0] = entry
+    scores = mm(c_low, b_low, 1, 1)
+    total_t = total.T
+    scaled = heads * widen(step, pairs)
+    scaled_low = low(scaled)
+    inside = []
+    for p in range(pairs):
+        both = []
+        for h in (2 * p, 2 * p + 1):
+            both.append(low(jnp.exp(total[:, h : h + 1] - total_t[h : h + 1] + shut) * scores))
+        inside.append(mm(jnp.concatenate(both, axis=1), stack_pair(scaled_low, p)))
+    mixer = jnp.concatenate(inside, axis=1) + widen(reach, pairs) * mm(c_low, low(entry))
+    b_turned = low(active[:, width : width + LANES].T)
+    state[...] = entry * widen(reach[Q - 1 : Q], pairs) + mm(
+        b_turned, low(scaled * widen(tail, pairs))
+    )
+    mixer_ref[...] = mixer
+    gated = (mixer + skip_ref[...] * heads) * (gate * sigmoid(gate))
+    squares_ref[...] = jnp.sum(gated * gated, axis=1, keepdims=True)
+    gg_ref[...] = low(gated * gain_ref[...])
+
+
+def backward_kernel(
+    width, whole_width, proj_ref, rim_ref, marks_ref, seg_ref, conv_w_ref, conv_b_ref, dt_bias_ref,
+    rate_ref, pick_ref, skip_ref, gain_ref, mixer_ref, starts_ref, og_ref, rows_ref,
+    pg_ref, outgoing_ref, wide_ref, conv_ref, head_ref, later, after,
+):
+    pairs = width // LANES
+    turn = pl.program_id(0)
+    chunk = pl.num_programs(0) - 1 - turn
+
+    @pl.when(turn == 0)
+    def _():
+        later[...] = jnp.zeros_like(later)
+        after[...] = jnp.zeros_like(after)
+        wide_ref[...] = jnp.zeros_like(wide_ref)
+        conv_ref[...] = jnp.zeros_like(conv_ref)
+        head_ref[...] = jnp.zeros_like(head_ref)
+
+    span = width + 2 * LANES
+    marks = marks_ref[...]
+    rim = rim_ref[...][8:, width : width + span].astype(jnp.float32)
+    rim = jnp.where(chunk > 0, rim, 0.0)
+    gate, mixed, shifts, conv, sig, active, stepped, step, decay, total, shut, reach, tail = (
+        chunk_parts(
+            width, proj_ref[...], rim, marks, seg_ref[...], conv_w_ref[...], conv_b_ref[...],
+            dt_bias_ref[...], rate_ref[...], pick_ref[...],
+        )
+    )
+    heads = active[:, :width]
+    b_low = low(active[:, width : width + LANES])
+    c_low = low(active[:, width + LANES :])
+
+    inv = rows_ref[:, 0:1]
+    dots = rows_ref[:, 1:2]
+    og = og_ref[...]
+    mixer = mixer_ref[...]
+    out = mixer + skip_ref[...] * heads
+    gate_sig = sigmoid(gate)
+    gate_on = gate * gate_sig
+    hat = out * gate_on * inv
+    outgoing_ref[...] = low(hat * gain_ref[...])
+    gated_grad = inv * (gain_ref[...] * og - hat * (dots * (1.0 / whole_width)))
+    out_grad = gated_grad * gate_on
+    gate_grad = gated_grad * out * (gate_sig * (1.0 + gate * (1.0 - gate_sig)))
+
+    entry = starts_ref[0]
+    entry_low = low(entry)
+    late = later[...]
+    late_low = low(late)
+    scores = mm(c_low, b_low, 1, 1)
+    total_t = total.T
+    step_wide = widen(step, pairs)
+    scaled = heads * step_wide
+    scaled_low = low(scaled)
+    grad_low = low(out_grad)
+    from_late = widen(tail, pairs) * mm(b_low, late_low)
+    inside = []
+    score_grad = jnp.zeros((Q, Q), jnp.float32)
+    for p in range(pairs):
+        gains = []
+        both = []
+        for h in (2 * p, 2 * p + 1):
+            gain = jnp.exp(total[:, h : h + 1] - total_t[h : h + 1] + shut)
+            gains.append(gain)
+            both.append(low(gain * scores))
+        stacked = stack_pair(grad_low, p)
+        inside.append(mm(jnp.concatenate(both, axis=0), stacked, 0, 0))
+        mix_grad = mm(stacked, scaled_low[:, p * LANES : (p + 1) * LANES], 1, 1)
+        score_grad = score_grad + gains[0] * mix_grad[:Q] + gains[1] * mix_grad[Q:]
+    scaled_grad = jnp.concatenate(inside, axis=1) + from_late
+    reached = low(widen(reach, pairs) * out_grad)
+    score_low = low(score_grad)
+    c_grad = mm(score_low, b_low) + mm(reached, entry_low, 1, 1)
+    b_grad = mm(score_low, c_low, 0, 0) + mm(low(scaled * widen(tail, pairs)), late_low, 1, 1)
+    kept = widen(reach[Q - 1 : Q], pairs)
+    later[...] = late * kept + mm(c_low, reached, 0, 0)
+
+    scaled_seen = scaled_low.astype(jnp.float32)
+    balance = grad_low.astype(jnp.float32) * mixer - scaled_seen * scaled_grad
+    closing = jnp.sum(scaled_seen * from_late, axis=0, keepdims=True) + kept * jnp.sum(
+        late * entry, axis=0, keepdims=True
+    )
+    picks = (iota((width, LANES), 0) // (LANES // 2) == iota((width, LANES), 1)).astype(jnp.float32)
+    sums = exact(
+        jnp.concatenate([balance, heads * scaled_grad, jnp.broadcast_to(closing, (8, width))], 0),
+        picks,
+    )
+    upper = (iota((Q, Q), 0) <= iota((Q, Q), 1)).astype(jnp.float32)
+    decay_grad = exact(upper, sums[:Q]) + sums[2 * Q : 2 * Q + 1]
+    step_grad = sums[Q : 2 * Q] - decay_grad * rate_ref[...]
+    raw_grad = step_grad * sigmoid(stepped)
+
+    head_grad = step_wide * scaled_grad + skip_ref[...] * out_grad
+    conv_grad = jnp.concatenate([head_grad, b_grad, c_grad], axis=1) * (
+        sig * (1.0 + conv * (1.0 - sig))
+    )
+    mixed_grad = conv_w_ref[KW - 1 : KW] * conv_grad
+    bottom = iota((8, span), 0)
+    for lag in range(1, KW):
+        sent = conv_grad * marks[:, lag - 1 : lag]
+        rolled = pltpu.roll(sent, Q - lag, 0)
+        ending = jnp.where(
+            bottom >= 8 - lag, pltpu.roll(after[lag - 1], 8 - lag, 0), rolled[Q - 8 :]
+        )
+        mixed_grad = mixed_grad + conv_w_ref[KW - 1 - lag : KW - lag] * jnp.concatenate(
+            [rolled[: Q - 8], ending], axis=0
+        )
+        after[lag - 1] = sent[:8]
+    pg_ref[...] = low(
+        jnp.concatenate([gate_grad, mixed_grad, mm(low(raw_grad), pick_ref[...], 1, 1)], axis=1)
+    )
+
+    wide_ref[0:1] += jnp.sum(hat * og, axis=0, keepdims=True)
+    wide_ref[1:2] += jnp.sum(out_grad * heads, axis=0, keepdims=True)
+    for lag in range(KW):
+        conv_ref[KW - 1 - lag : KW - lag] += jnp.sum(
+            conv_grad * shifts[lag], axis=0, keepdims=True
+        )
+    conv_ref[KW : KW + 1] += jnp.sum(conv_grad, axis=0, keepdims=True)
+    head_ref[0:1] += jnp.sum(raw_grad, axis=0, keepdims=True)
+    head_ref[1:2] += jnp.sum(decay_grad * decay, axis=0, keepdims=True)
+
+
+def full_spec(shape):
+    return pl.BlockSpec(shape, lambda i: (0,) * len(shape))
+
+
+def mixer_forward(projected, marks, seg_row, small):
+    rows, columns = projected.shape
+    width = small["gain"].shape[1]
+    chunks = rows // Q
+    span = width + 2 * LANES
+
+    def by_row(count):
+        return pl.BlockSpec((Q, count), lambda i: (i, 0))
+
+    weights = [small[k] for k in ("conv_w", "conv_b", "dt_bias", "rate", "pick", "skip", "gain")]
+    return pl.pallas_call(
+        functools.partial(forward_kernel, width),
+        grid=(chunks,),
+        in_specs=[by_row(columns), by_row(8), pl.BlockSpec((1, Q), lambda i: (0, i))]
+        + [full_spec(w.shape) for w in weights],
+        out_specs=[
+            by_row(width),
+            by_row(1),
+            by_row(width),
+            pl.BlockSpec((1, LANES, width), lambda i: (i, 0, 0)),
+        ],
+        out_shape=[
+            jax.ShapeDtypeStruct((rows, width), jnp.bfloat16),
+            jax.ShapeDtypeStruct((rows, 1), jnp.float32),
+            jax.ShapeDtypeStruct((rows, width), jnp.float32),
+            jax.ShapeDtypeStruct((chunks, LANES, width), jnp.float32),
+        ],
+        scratch_shapes=[
+            pltpu.VMEM((LANES, width), jnp.float32),
+            pltpu.VMEM((8, span), jnp.float32),
+        ],
+        compiler_params=pltpu.CompilerParams(vmem_limit_bytes=VMEM_BYTES),
+        name="mixer_forward",
+    )(projected, marks, seg_row, *weights)
+
+
+def mixer_backward(projected, marks, seg_row, small, mixer, starts, og, per_row, whole_width):
+    rows, columns = projected.shape
+    width = small["gain"].shape[1]
+    chunks = rows // Q
+    span = width + 2 * LANES
+
+    def by_row(count):
+        return pl.BlockSpec((Q, count), lambda i: (chunks - 1 - i, 0))
+
+    weights = [small[k] for k in ("conv_w", "conv_b", "dt_bias", "rate", "pick", "skip", "gain")]
+    rim = pl.BlockSpec(
+        (16, columns), lambda i: (jnp.maximum((chunks - 1 - i) * (Q // 16) - 1, 0), 0)
+    )
+    return pl.pallas_call(
+        functools.partial(backward_kernel, width, whole_width),
+        grid=(chunks,),
+        in_specs=[by_row(columns), rim, by_row(8), pl.BlockSpec((1, Q), lambda i: (0, chunks - 1 - i))]
+        + [full_spec(w.shape) for w in weights]
+        + [
+            by_row(width),
+            pl.BlockSpec((1, LANES, width), lambda i: (chunks - 1 - i, 0, 0)),
+            by_row(width),
+            by_row(2),
+        ],
+        out_specs=[
+            by_row(columns),
+            by_row(width),
+            full_spec((8, width)),
+            full_spec((8, span)),
+            full_spec((8, LANES)),
+        ],
+        out_shape=[
+            jax.ShapeDtypeStruct((rows, columns), jnp.bfloat16),
+            jax.ShapeDtypeStruct((rows, width), jnp.bfloat16),
+            jax.ShapeDtypeStruct((8, width), jnp.float32),
+            jax.ShapeDtypeStruct((8, span), jnp.float32),
+            jax.ShapeDtypeStruct((8, LANES), jnp.float32),
+        ],
+        scratch_shapes=[
+            pltpu.VMEM((LANES, width), jnp.float32),
+            pltpu.VMEM((KW - 1, 8, span), jnp.float32),
+        ],
+        compiler_params=pltpu.CompilerParams(vmem_limit_bytes=VMEM_BYTES),
+        name="mixer_backward",
+    )(projected, projected, marks, seg_row, *weights, mixer, starts, og, per_row)
+
+
+CORES = 2
+GROUP = 4
+SHARED = CONV - DI + H
+LOCAL = 2 * DI // GROUP + SHARED + 16
+HALF = LOCAL // 2
+CHUNKS = 2
+LANE_PART = D // 4
+OUT_PART = DI // 16
+UNITS = CHUNKS + 1
+
+
+def place():
+    c, z, r = (lax.axis_index(name) for name in ("section", "shard", "rep"))
+    return c, z, lax.div(r, 2), lax.rem(r, 2)
+
+
+def weight_pieces(quarter):
+    part = DI // 16
+    found = []
+    for side in range(2):
+        for zz in range(4):
+            found.append(
+                (side * 4 * part + zz * part, side * DI + zz * 4 * part + quarter * part, part)
+            )
+    found.append((8 * part, 2 * DI, SHARED))
+    return found
+
+
+def gather_kernel(
+    layer, in_ref, out_ref, w_ref, wo_ref,
+    local_sem, core_send, core_recv, right_send, left_send, z_recv, y_send, y_recv,
+):
+    c, z, y, x = place()
+    core, y_other = {"section": 1 - c}, {"rep": (1 - y) * 2 + x}
+    barrier = pltpu.get_barrier_semaphore()
+    pl.semaphore_signal(barrier, inc=1, device_id=core, device_id_type=pl.DeviceIdType.MESH)
+    pl.semaphore_signal(barrier, inc=1, device_id=y_other, device_id_type=pl.DeviceIdType.MESH)
+
+    @pl.when(z < 3)
+    def _():
+        pl.semaphore_signal(
+            barrier, inc=1, device_id={"shard": z + 1}, device_id_type=pl.DeviceIdType.MESH
+        )
+
+    @pl.when(z > 0)
+    def _():
+        pl.semaphore_signal(
+            barrier, inc=1, device_id={"shard": z - 1}, device_id_type=pl.DeviceIdType.MESH
+        )
+
+    ends = jnp.where(z == 0, 1, 0) + jnp.where(z == 3, 1, 0)
+    pl.semaphore_wait(barrier, 4 - ends)
+
+    lanes = pl.ds(pl.multiple_of(z * LANE_PART, LANES), LANE_PART)
+    out_rows = pl.ds(pl.multiple_of(z * OUT_PART, 16), OUT_PART)
+
+    def own_pieces(quarter):
+        found = []
+        for at, start, count in weight_pieces(quarter):
+            source = in_ref.at[pl.ds(pl.multiple_of(start, 16), count)]
+            found.append((source, w_ref.at[pl.ds(at, count), lanes]))
+        start = pl.multiple_of(quarter * OUT_PART, 16)
+        found.append((out_ref.at[pl.ds(start, OUT_PART)], wo_ref.at[out_rows]))
+        return found
+
+    def local_copies():
+        return [
+            pltpu.make_async_copy(source, target, local_sem.at[i])
+            for i, (source, target) in enumerate(own_pieces(2 * x + c))
+        ]
+
+    def core_copies():
+        return [
+            pltpu.make_async_remote_copy(
+                src_ref=source, dst_ref=target, send_sem=core_send.at[i],
+                recv_sem=core_recv.at[i], device_id=core, device_id_type=pl.DeviceIdType.MESH,
+            )
+            for i, (source, target) in enumerate(own_pieces(2 * x + 1 - c))
+        ]
+
+    w_ref[LOCAL - 16 :, lanes] = jnp.zeros((16, LANE_PART), w_ref.dtype)
+
+    @pl.when(c == layer)
+    def _():
+        for copy in core_copies():
+            copy.start()
+        for copy in local_copies():
+            copy.start()
+        for copy in local_copies():
+            copy.wait()
+
+    @pl.when(c != layer)
+    def _():
+        for copy in core_copies():
+            copy.wait_recv()
+
+    def slab(unit, shard, side):
+        if unit == CHUNKS:
+            start = shard * OUT_PART + side * (OUT_PART // 2)
+            return wo_ref.at[pl.ds(pl.multiple_of(start, 16), OUT_PART // 2)]
+        start = pl.multiple_of(side * HALF + unit * (HALF // CHUNKS), 16)
+        return w_ref.at[
+            pl.ds(start, HALF // CHUNKS),
+            pl.ds(pl.multiple_of(shard * LANE_PART, LANES), LANE_PART),
+        ]
+
+    def z_copy(unit, shard, step, k):
+        there = z + 1 if step > 0 else z - 1
+        return pltpu.make_async_remote_copy(
+            src_ref=slab(unit, shard, y), dst_ref=slab(unit, shard, y),
+            send_sem=(right_send if step > 0 else left_send).at[unit, k],
+            recv_sem=z_recv.at[unit, shard],
+            device_id={"shard": there}, device_id_type=pl.DeviceIdType.MESH,
+        )
+
+    def y_copy(unit, shard, side):
+        return pltpu.make_async_remote_copy(
+            src_ref=slab(unit, shard, side), dst_ref=slab(unit, shard, side),
+            send_sem=y_send.at[unit, shard], recv_sem=y_recv.at[unit, shard],
+            device_id=y_other, device_id_type=pl.DeviceIdType.MESH,
+        )
+
+    def first(unit):
+        @pl.when(z < 3)
+        def _():
+            z_copy(unit, z, 1, 0).start()
+
+        @pl.when(z > 0)
+        def _():
+            z_copy(unit, z, -1, 0).start()
+
+    def arrive(unit, k):
+        for step in (1, -1):
+            shard = z - k * step
+            there = (shard >= 0) if step > 0 else (shard <= 3)
+            more = (z < 3) if step > 0 else (z > 0)
+
+            @pl.when(there)
+            def _():
+                z_copy(unit, shard, step, 0).wait_recv()
+
+                @pl.when(more)
+                def _():
+                    z_copy(unit, shard, step, k).start()
+
+                y_copy(unit, shard, y).start()
+
+    for unit in range(CHUNKS):
+        first(unit)
+    for k in (1, 2):
+        for unit in range(CHUNKS):
+            arrive(unit, k)
+    first(CHUNKS)
+    for unit in range(CHUNKS):
+        arrive(unit, 3)
+    for k in (1, 2, 3):
+        arrive(CHUNKS, k)
+
+    for unit in range(UNITS):
+        for away in (1, 2, 3):
+            shard = lax.rem(z + away, 4)
+            y_copy(unit, shard, 1 - y).wait_recv()
+            y_copy(unit, shard, y).wait_send()
+        for step in (1, -1):
+            for k in range(3):
+                shard = z - k * step
+                there = (shard >= 0) if step > 0 else (shard <= 3)
+                more = (z < 3) if step > 0 else (z > 0)
+
+                @pl.when(there & more)
+                def _():
+                    z_copy(unit, shard, step, k).wait_send()
+
+    @pl.when(c == layer)
+    def _():
+        for copy in core_copies():
+            copy.wait_send()
+
+
+def gather_weights(layer, in_rows, out_rows):
+    dma = pltpu.SemaphoreType.DMA
+    return pl.pallas_call(
+        functools.partial(gather_kernel, layer),
+        in_specs=[pl.BlockSpec(memory_space=pl.ANY)] * 2,
+        out_specs=[pl.BlockSpec(memory_space=pltpu.VMEM)] * 2,
+        out_shape=[
+            jax.ShapeDtypeStruct((LOCAL, D), jnp.bfloat16),
+            jax.ShapeDtypeStruct((DI // GROUP, D), jnp.bfloat16),
+        ],
+        scratch_shapes=[
+            dma((10,)), dma((10,)), dma((10,)),
+            dma((UNITS, 3)), dma((UNITS, 3)), dma((UNITS, 4)), dma((UNITS, 4)), dma((UNITS, 4)),
+        ],
+        compiler_params=pltpu.CompilerParams(
+            collective_id=layer, has_side_effects=True, vmem_limit_bytes=VMEM_BYTES
+        ),
+        name="gather_weights",
+    )(in_rows, out_rows)
+
+
+def swap_core(v):
+    return lax.ppermute(v, "section", [(0, 1), (1, 0)])
+
+
+def swap_x(v):
+    return lax.ppermute(v, "rep", [(i, i ^ 1) for i in range(4)])
+
+
+def swap_y(v):
+    return lax.ppermute(v, "rep", [(i, i ^ 2) for i in range(4)])
+
+
+def swap_z(v, bit):
+    return lax.ppermute(v, "shard", [(i, i ^ bit) for i in range(4)])
+
+
+def ordered(first, mine, other, axis=0):
+    return jnp.where(first, jnp.stack([mine, other], axis), jnp.stack([other, mine], axis))
+
+
+def joined(first, mine, other, axis=0):
+    return jnp.where(
+        first, jnp.concatenate([mine, other], axis), jnp.concatenate([other, mine], axis)
+    )
+
+
+def after(value, *earlier):
+    return lax.optimization_barrier((value,) + earlier)[0]
+
+
+def pick_last(v, quarter):
+    parts = v.reshape(v.shape[:-1] + (4, GROUP, v.shape[-1] // (4 * GROUP)))
+    return lax.dynamic_index_in_dim(parts, quarter, v.ndim, False).reshape(v.shape[:-1] + (-1,))
+
+
+def place_last(v, quarter):
+    parts = v.reshape(v.shape[:-1] + (4, 1, v.shape[-1] // 4))
+    empty = jnp.zeros(v.shape[:-1] + (4, GROUP, v.shape[-1] // 4), v.dtype)
+    return lax.dynamic_update_slice_in_dim(empty, parts, quarter, v.ndim).reshape(
+        v.shape[:-1] + (-1,)
+    )
+
+
+def rows_at(start, count):
+    return pl.ds(pl.multiple_of(start, 16), count)
+
+
+def finish_kernel(
+    grad_ref, out_grad_ref, late_ref, late_out_ref, tiny_ref,
+    all_ref, out_all_ref, tiny_out_ref,
+    y_buf, z_buf, s_buf, zo_buf, so_buf, yo_buf, yo_mine, t1_buf, t1_sum, t2_buf, t2_sum, t3_buf,
+    y_send, y_recv, z_send, z_recv, zo_send, zo_recv, yo_sem,
+    core_send, core_recv, x_send, x_recv, ya_send, ya_recv, relay_send, relay_recv,
+    xo_send, xo_recv, t_send, t_recv, local_sem,
+):
+    c, z, y, x = place()
+    quarter = 2 * x + c
+    core, x_other, y_other = {"section": 1 - c}, {"rep": 2 * y + 1 - x}, {"rep": 2 * (1 - y) + x}
+    diagonal = {"rep": 2 * (1 - y) + 1 - x}
+    part = HALF // CHUNKS
+
+    def copy(source, target, send, recv, device):
+        return pltpu.make_async_remote_copy(
+            src_ref=source, dst_ref=target, send_sem=send, recv_sem=recv,
+            device_id=device, device_id_type=pl.DeviceIdType.MESH,
+        )
+
+    barrier = pltpu.get_barrier_semaphore()
+    reps = (x_other, y_other, diagonal)
+    shards = tuple({"shard": lax.rem(z + away, 4)} for away in (1, 2, 3))
+    for device in (core,) + reps + shards:
+        pl.semaphore_signal(barrier, inc=1, device_id=device, device_id_type=pl.DeviceIdType.MESH)
+    pl.semaphore_wait(barrier, 7)
+
+    orders = ((3, 2, 1, 0), (3, 0, 2, 1), (0, 3, 1, 2), (0, 1, 2, 3))
+
+    def shard_at(i):
+        found = jnp.int32(orders[3][i])
+        for zz in range(3):
+            found = jnp.where(z == zz, orders[zz][i], found)
+        return found
+
+    def grad_part(shard, side, ch):
+        return grad_ref.at[
+            rows_at(side * HALF + ch * part, part),
+            pl.ds(pl.multiple_of(shard * LANE_PART, LANES), LANE_PART),
+        ]
+
+    def y_copy(shard, ch):
+        return copy(
+            grad_part(shard, 1 - y, ch), y_buf.at[shard, pl.ds(ch * part, part)],
+            y_send.at[shard, ch], y_recv.at[shard, ch], y_other,
+        )
+
+    def z_target(shard):
+        right = shard > z
+        there = {"shard": jnp.clip(z + jnp.where(right, 1, -1), 0, 3)}
+        slot = jnp.where(right, shard, jnp.where(shard == z - 1, 4, shard))
+        return there, slot
+
+    def z_copy(shard, ch):
+        there, slot = z_target(shard)
+        return copy(
+            s_buf.at[shard, pl.ds(ch * part, part)], z_buf.at[slot, pl.ds(ch * part, part)],
+            z_send.at[shard, ch], z_recv.at[slot, ch], there,
+        )
+
+    def z_wait(slot, ch):
+        there, _ = z_target(shard_at(0))
+        copy(
+            s_buf.at[0, pl.ds(ch * part, part)], z_buf.at[slot, pl.ds(ch * part, part)],
+            z_send.at[0, ch], z_recv.at[slot, ch], there,
+        ).wait_recv()
+
+    def zo_copy(shard):
+        there, slot = z_target(shard)
+        return copy(
+            so_buf.at[shard], zo_buf.at[slot], zo_send.at[shard], zo_recv.at[slot], there
+        )
+
+    def zo_wait(slot):
+        there, _ = z_target(shard_at(0))
+        copy(so_buf.at[0], zo_buf.at[slot], zo_send.at[0], zo_recv.at[slot], there).wait_recv()
+
+    def all_part(which, side, ch):
+        return all_ref.at[which, rows_at(side * HALF + ch * part, part)]
+
+    def out_part(which):
+        return out_all_ref.at[rows_at(which * OUT_PART, OUT_PART)]
+
+    def x_copy(who, ch):
+        piece = all_part(2 * x + who, y, ch)
+        return copy(piece, piece, x_send.at[who, ch], x_recv.at[who, ch], x_other)
+
+    def ya_copy(who, ch):
+        piece = all_part(2 * x + who, y, ch)
+        return copy(piece, piece, ya_send.at[who, ch], ya_recv.at[who, ch], y_other)
+
+    def relay_copy(who, ch):
+        piece = all_part(2 * x + who, 1 - y, ch)
+        return copy(piece, piece, relay_send.at[who, ch], relay_recv.at[who, ch], x_other)
+
+    def xo_copy(who):
+        piece = out_part(2 * x + who)
+        return copy(piece, piece, xo_send.at[who], xo_recv.at[who], x_other)
+
+    def spread(who, ch):
+        x_copy(who, ch).start()
+        ya_copy(who, ch).start()
+
+    def late_copy(ch):
+        return copy(
+            late_ref.at[pl.ds(ch * part, part)], all_part(quarter, y, ch),
+            core_send.at[ch], core_recv.at[ch], core,
+        )
+
+    def late_out_copy():
+        return copy(
+            late_out_ref, out_part(quarter), core_send.at[CHUNKS], core_recv.at[CHUNKS], core
+        )
+
+    def first_copy(ch):
+        piece = all_part(quarter, y, ch)
+        return copy(z_buf.at[4, pl.ds(ch * part, part)], piece, core_send.at[ch], core_recv.at[ch], core)
+
+    def first_out_copy():
+        return copy(
+            yo_mine, out_part(quarter), core_send.at[CHUNKS], core_recv.at[CHUNKS], core
+        )
+
+    def t1_copy():
+        return copy(tiny_ref.at[1 - c], t1_buf, t_send.at[0], t_recv.at[0], core)
+
+    def t2_copy(away):
+        return copy(
+            t1_sum.at[lax.rem(z + away, 4)], t2_buf.at[away - 1],
+            t_send.at[away], t_recv.at[away], shards[away - 1],
+        )
+
+    def t3_copy(i):
+        return copy(t2_sum, t3_buf.at[i], t_send.at[4 + i], t_recv.at[4 + i], reps[i])
+
+    def yo_copy():
+        return copy(yo_mine, yo_buf, yo_sem.at[0], yo_sem.at[1], y_other)
+
+    t1_copy().start()
+    for i in range(4):
+        shard = shard_at(i)
+        for ch in range(CHUNKS):
+            y_copy(shard, ch).start()
+
+    @pl.when(c == 0)
+    def _():
+        for ch in range(CHUNKS):
+            late_copy(ch).start()
+        late_out_copy().start()
+
+    @pl.when(c == 1)
+    def _():
+        for ch in range(CHUNKS):
+            all_part(quarter, y, ch)[...] = late_ref[pl.ds(ch * part, part)]
+        out_part(quarter)[...] = late_out_ref[...]
+
+    def own_out(shard):
+        return out_grad_ref[rows_at(shard * OUT_PART, OUT_PART)].astype(jnp.float32)
+
+    def more(shard):
+        return ((shard > z) & (z > 0)) | ((shard < z) & (z < 3))
+
+    def send_out(i):
+        shard = shard_at(i)
+
+        @pl.when(more(shard))
+        def _():
+            zo_wait(shard)
+            so_buf[shard] = low(own_out(shard) + zo_buf[shard].astype(jnp.float32))
+
+        @pl.when(jnp.logical_not(more(shard)))
+        def _():
+            so_buf[shard] = out_grad_ref[rows_at(shard * OUT_PART, OUT_PART)]
+
+        zo_copy(shard).start()
+
+    def send_in(i, ch):
+        shard = shard_at(i)
+        span = pl.ds(ch * part, part)
+        y_copy(shard, ch).wait_recv()
+        both = grad_part(shard, y, ch)[...].astype(jnp.float32) + y_buf[shard, span].astype(
+            jnp.float32
+        )
+
+        @pl.when(more(shard))
+        def _():
+            z_wait(shard, ch)
+            s_buf[shard, span] = low(both + z_buf[shard, span].astype(jnp.float32))
+
+        @pl.when(jnp.logical_not(more(shard)))
+        def _():
+            s_buf[shard, span] = low(both)
+
+        z_copy(shard, ch).start()
+
+    send_out(0)
+    send_out(1)
+
+    t1_copy().wait_recv()
+    t1_sum[...] = tiny_ref[c] + t1_buf[...]
+    for away in (1, 2, 3):
+        t2_copy(away).start()
+
+    @pl.when(c == 1)
+    def _():
+        for ch in range(CHUNKS):
+            late_copy(ch).wait_recv()
+            for who in range(CORES):
+                spread(who, ch)
+        late_out_copy().wait_recv()
+        for who in range(CORES):
+            xo_copy(who).start()
+
+    for ch in range(CHUNKS):
+        send_in(0, ch)
+    send_out(2)
+    for away in (1, 2, 3):
+        t2_copy(away).wait_recv()
+    t2_sum[...] = (t1_sum[z] + t2_buf[0]) + (t2_buf[1] + t2_buf[2])
+    for i in range(3):
+        t3_copy(i).start()
+    for ch in range(CHUNKS):
+        send_in(1, ch)
+
+    yo_mine[...] = low(own_out(z))
+
+    @pl.when(z > 0)
+    def _():
+        zo_wait(z)
+        yo_mine[...] = low(own_out(z) + zo_buf[z].astype(jnp.float32))
+
+    @pl.when(z < 3)
+    def _():
+        zo_wait(4)
+        yo_mine[...] = low(yo_mine[...].astype(jnp.float32) + zo_buf[4].astype(jnp.float32))
+
+    yo_copy().start()
+    for ch in range(CHUNKS):
+        send_in(2, ch)
+    for i in range(3):
+        t3_copy(i).wait_recv()
+    tiny_out_ref[...] = (t2_sum[...] + t3_buf[0]) + (t3_buf[1] + t3_buf[2])
+
+    yo_copy().wait()
+    total = low(yo_mine[...].astype(jnp.float32) + yo_buf[...].astype(jnp.float32))
+
+    @pl.when(c == 0)
+    def _():
+        out_part(quarter)[...] = total
+
+    @pl.when(c == 1)
+    def _():
+        yo_mine[...] = total
+        first_out_copy().start()
+
+    @pl.when(c == 0)
+    def _():
+        first_out_copy().wait_recv()
+        for who in range(CORES):
+            xo_copy(who).start()
+
+    for ch in range(CHUNKS):
+        span = pl.ds(ch * part, part)
+        y_copy(z, ch).wait_recv()
+        s_buf[z, span] = low(
+            grad_part(z, y, ch)[...].astype(jnp.float32) + y_buf[z, span].astype(jnp.float32)
+        )
+
+        @pl.when(z > 0)
+        def _():
+            z_wait(z, ch)
+            s_buf[z, span] = low(
+                s_buf[z, span].astype(jnp.float32) + z_buf[z, span].astype(jnp.float32)
+            )
+
+        @pl.when(z < 3)
+        def _():
+            z_wait(4, ch)
+            s_buf[z, span] = low(
+                s_buf[z, span].astype(jnp.float32) + z_buf[4, span].astype(jnp.float32)
+            )
+
+        @pl.when(c == 1)
+        def _():
+            z_buf[4, span] = s_buf[z, span]
+            first_copy(ch).start()
+
+        @pl.when(c == 0)
+        def _():
+            all_part(quarter, y, ch)[...] = s_buf[z, span]
+            spread(0, ch)
+            first_copy(ch).wait_recv()
+            spread(1, ch)
+
+    for ch in range(CHUNKS):
+        for who in range(CORES):
+            ya_copy(who, ch).wait_recv()
+            relay_copy(who, ch).start()
+    for ch in range(CHUNKS):
+        for who in range(CORES):
+            x_copy(who, ch).wait()
+            ya_copy(who, ch).wait_send()
+            relay_copy(who, ch).wait()
+    for who in range(CORES):
+        xo_copy(who).wait()
+    t1_copy().wait_send()
+    for away in (1, 2, 3):
+        t2_copy(away).wait_send()
+    for i in range(3):
+        t3_copy(i).wait_send()
+        zo_copy(shard_at(i)).wait_send()
+        for ch in range(CHUNKS):
+            z_copy(shard_at(i), ch).wait_send()
+    for i in range(4):
+        for ch in range(CHUNKS):
+            y_copy(shard_at(i), ch).wait_send()
+
+    @pl.when(c == 0)
+    def _():
+        for ch in range(CHUNKS):
+            late_copy(ch).wait_send()
+        late_out_copy().wait_send()
+
+    @pl.when(c == 1)
+    def _():
+        for ch in range(CHUNKS):
+            first_copy(ch).wait_send()
+        first_out_copy().wait_send()
+
+
+def finish_sums(grad, out_grad, late, late_out, tiny):
+    dma = pltpu.SemaphoreType.DMA
+    span = (HALF, LANE_PART)
+    out = (OUT_PART, D)
+    small = tiny.shape[2:]
+    two = (CORES, CHUNKS)
+    return pl.pallas_call(
+        finish_kernel,
+        in_specs=[pl.BlockSpec(memory_space=pltpu.VMEM)] * 5,
+        out_specs=[pl.BlockSpec(memory_space=pltpu.VMEM)] * 3,
+        out_shape=[
+            jax.ShapeDtypeStruct((GROUP, LOCAL, LANE_PART), jnp.bfloat16),
+            jax.ShapeDtypeStruct((DI // GROUP, D), jnp.bfloat16),
+            jax.ShapeDtypeStruct(small, jnp.float32),
+        ],
+        scratch_shapes=[
+            pltpu.VMEM((4,) + span, jnp.bfloat16),
+            pltpu.VMEM((5,) + span, jnp.bfloat16),
+            pltpu.VMEM((4,) + span, jnp.bfloat16),
+            pltpu.VMEM((5,) + out, jnp.bfloat16),
+            pltpu.VMEM((4,) + out, jnp.bfloat16),
+            pltpu.VMEM(out, jnp.bfloat16),
+            pltpu.VMEM(out, jnp.bfloat16),
+            pltpu.VMEM((4,) + small, jnp.float32),
+            pltpu.VMEM((4,) + small, jnp.float32),
+            pltpu.VMEM((3,) + small, jnp.float32),
+            pltpu.VMEM(small, jnp.float32),
+            pltpu.VMEM((3,) + small, jnp.float32),
+            dma((4, CHUNKS)), dma((4, CHUNKS)), dma((4, CHUNKS)), dma((5, CHUNKS)),
+            dma((4,)), dma((5,)), dma((2,)),
+            dma((CHUNKS + 1,)), dma((CHUNKS + 1,)),
+            dma(two), dma(two), dma(two), dma(two), dma(two), dma(two),
+            dma((CORES,)), dma((CORES,)), dma((7,)), dma((7,)), dma((1,)),
+        ],
+        compiler_params=pltpu.CompilerParams(
+            collective_id=2, has_side_effects=True, vmem_limit_bytes=VMEM_BYTES
+        ),
+        name="finish_sums",
+    )(grad, out_grad, late, late_out, tiny)
+
+
+def assemble_kernel(part_ref, shared_ref, total_ref):
+    last = pl.program_id(0) == 8
+    step = DI // 16
+
+    @pl.when(last)
+    def _():
+        shared = [shared_ref[i, :SHARED].astype(jnp.float32) for i in range(GROUP)]
+        total_ref[:SHARED] = (shared[0] + shared[1]) + (shared[2] + shared[3])
+
+    @pl.when(jnp.logical_not(last))
+    def _():
+        for i in range(GROUP):
+            total_ref[i * step : (i + 1) * step] = part_ref[i].astype(jnp.float32)
+
+
+def assemble_rows(parts):
+    lanes = parts.shape[-1]
+    step = DI // 16
+    return pl.pallas_call(
+        assemble_kernel,
+        grid=(9,),
+        in_specs=[
+            pl.BlockSpec((GROUP, step, lanes), lambda i: (0, jnp.minimum(i, 7), 0)),
+            pl.BlockSpec((GROUP, 2 * step, lanes), lambda i: (0, 4, 0)),
+        ],
+        out_specs=pl.BlockSpec((GROUP * step, lanes), lambda i: (i, 0)),
+        out_shape=jax.ShapeDtypeStruct((DI + CONV + H, lanes), jnp.float32),
+        compiler_params=pltpu.CompilerParams(vmem_limit_bytes=VMEM_BYTES),
+        name="assemble_rows",
+    )(parts, parts)
+
+
+def per_device_split(
+    boundary_in,
+    lengths,
+    seq_order,
+    norm_gain,
+    in_weight,
+    conv_weight,
+    conv_bias,
+    dt_bias,
+    a_log,
+    d_skip,
+    out_gain,
+    out_weight,
+):
+    c = lax.axis_index("section")
+    z = lax.axis_index("shard")
+    r = lax.axis_index("rep")
+    y, x = r // 2, r % 2
+    block = boundary_in.shape[3]
+    rows = GROUP * block
+    width = DI // GROUP
+    heads = H // GROUP
+    span = width + 2 * N
+    quarter = 2 * x + c
+
+    def spot(cc, zz, rr):
+        return (cc * 4 + zz) * 4 + rr
+
+    def home(m, zz, rr):
+        return spot(zz % 2, 2 * m + rr % 2, (rr // 2) * 2 + zz // 2)
+
+    places = [(cc, zz, rr) for cc in range(2) for zz in range(4) for rr in range(4)]
+    axes = ("section", "shard", "rep")
+    straight = [(spot(*p), home(p[0], p[1], p[2])) for p in places]
+    crossed = [(spot(*p), home(1 - p[0], p[1], p[2])) for p in places]
+
+    def go_back(value, cc):
+        ways = []
+        for m in range(MICRO):
+            pairs = [(home(m, zz, rr), spot(cc, zz, rr)) for zz in range(4) for rr in range(4)]
+            ways.append(lax.ppermute(value, axes, pairs))
+        return ways
+
+    in_rows = jnp.swapaxes(in_weight[0], 0, 1)
+    w_in0, w_out0 = gather_weights(0, in_rows, out_weight[0])
+
+    arrive_a = lax.ppermute(
+        lax.dynamic_index_in_dim(boundary_in[0, :, 0], c, 0, False), axes, straight
+    )
+    arrive_b = lax.ppermute(
+        lax.dynamic_index_in_dim(boundary_in[0, :, 0], 1 - c, 0, False), axes, crossed
+    )
+    source = jnp.where(z < 2, arrive_a, arrive_b)
+    cotangent = jnp.where(z < 2, arrive_b, arrive_a)
+
+    order = jnp.stack([lengths[:, 0], seq_order[:, 0]])
+    order = jnp.where(x == z % 2, order, swap_x(order))
+    order = lax.dynamic_index_in_dim(order, z // 2, 1, False)
+    chosen = (order[1][:, None] == jnp.arange(NSEQ, dtype=jnp.int32)[None, :]).astype(jnp.int32)
+    finish = jnp.cumsum(jnp.sum(chosen * order[0][None, :], axis=1), dtype=jnp.int32)
+
+    def segment_of(positions):
+        found = jnp.sum((positions[:, None] >= finish[None, :]).astype(jnp.int32), axis=1)
+        return jnp.where(positions < 0, -1, found)
+
+    token = jnp.arange(rows, dtype=jnp.int32)
+    segment = segment_of(token)
+    opening = token // Q * Q
+    columns = [segment_of(token - lag) == segment for lag in range(1, KW)]
+    columns.append(segment_of(opening - 1) == segment)
+    columns.append(segment_of(opening + (Q - 1)) == segment)
+    columns = [column.astype(jnp.float32) for column in columns] + [segment.astype(jnp.float32)]
+    marks = jnp.stack(columns + [jnp.zeros((rows,), jnp.float32)] * 2, axis=1)
+    seg_row = segment.astype(jnp.float32)[None]
+
+    params = (norm_gain, conv_weight, conv_bias, dt_bias, a_log, d_skip, out_gain)
+    count = sum(p.size for p in params)
+    filler = -count % LANES
+    flat = jnp.concatenate([p.reshape(-1) for p in params] + [jnp.zeros((filler,), jnp.bfloat16)])
+    flat = ordered(c == 0, flat, swap_core(flat))
+    flat = ordered(z % 2 == 0, flat, swap_z(flat, 1))
+    flat = ordered(z // 2 == 0, flat, swap_z(flat, 2))
+    flat = flat.reshape((4, CORES, count + filler)).astype(jnp.float32)
+
+    given = jnp.arange(SHARED - 2 * N + 16)[:, None]
+    local = jnp.arange(LANES)[None, :]
+    picked = (given % 12 // 3 == quarter) & (local == given // 12 * 3 + given % 3) & (given < H)
+    picked = low(picked.astype(jnp.float32))
+
+    def layer_params(layer):
+        found = []
+        at = 0
+        for p in params:
+            part = flat[:, layer, at : at + p.size].reshape((4,) + p.shape[1:])
+            at += p.size
+            found.append(jnp.moveaxis(part, 0, -2).reshape(p.shape[1:-1] + (-1,)))
+        gain, conv_w, conv_b, dt_b, log_a, skip, gain_out = found
+
+        def spread(v):
+            return jnp.pad(pick_last(v, quarter), (0, LANES - heads))[None]
+
+        def taps(v):
+            return jnp.concatenate([pick_last(v[:, :DI], quarter), v[:, DI:]], axis=1)
+
+        return {
+            "norm": gain,
+            "conv_w": taps(conv_w),
+            "conv_b": taps(conv_b[None]),
+            "dt_bias": spread(dt_b),
+            "rate": spread(jnp.exp(log_a)),
+            "pick": picked,
+            "skip": jnp.repeat(pick_last(skip, quarter), P_SIZE)[None],
+            "gain": pick_last(gain_out, quarter)[None],
+        }
+
+    small = [layer_params(0), layer_params(1)]
+
+    def group_rows(v):
+        count = v.shape[0]
+        near = swap_x(v)
+        other = swap_core(v)
+        far = swap_core(near)
+        whole = jnp.zeros((GROUP * count,) + v.shape[1:], v.dtype)
+        for part, at in (
+            (v, 2 * x + c),
+            (other, 2 * x + 1 - c),
+            (near, 2 * (1 - x) + c),
+            (far, 2 * (1 - x) + 1 - c),
+        ):
+            whole = lax.dynamic_update_slice_in_dim(whole, part, at * count, 0)
+        return whole
+
+    def group_product(left, product):
+        blocks = left.reshape((2, 2, block) + left.shape[1:])
+        theirs = lax.dynamic_index_in_dim(blocks, 1 - c, 1, False)
+        theirs = product(theirs.reshape((2 * block,) + left.shape[1:]))
+        received = swap_core(low(theirs)).reshape((2, block, -1))
+        mine = lax.dynamic_index_in_dim(blocks, c, 1, False)
+
+        def summed(at):
+            part = product(lax.dynamic_index_in_dim(mine, at, 0, False))
+            return part + lax.dynamic_index_in_dim(received, at, 0, False).astype(jnp.float32)
+
+        across = swap_x(low(summed(1 - x)))
+        return summed(x) + across.astype(jnp.float32)
+
+    def own(v):
+        return lax.dynamic_slice_in_dim(v, (2 * x + c) * block, block, 0)
+
+    def forward(layer, entering, w_in, w_out):
+        gain = small[layer]["norm"]
+        inv = lax.rsqrt(jnp.mean(entering * entering, axis=-1, keepdims=True) + EPSILON)
+        normed = group_rows(low(entering * inv * gain))
+        projected = low(mm(normed, w_in, 1, 1))
+        gg, squares, mixer, starts = mixer_forward(projected, marks, seg_row, small[layer])
+        half = squares.reshape((rows // LANES, LANES))
+        half = half + swap_core(half)
+        half = half + swap_x(half)
+        out_inv = lax.rsqrt(half / DI + EPSILON).reshape((rows, 1))
+        product = group_product(gg, lambda v: mm(v, w_out))
+        added = own(out_inv) * product
+        return entering + added, (entering, inv, normed, projected, mixer, starts, out_inv, added)
+
+    def backward(layer, kept, incoming, w_in, w_out):
+        entering, inv, normed, projected, mixer, starts, out_inv, added = kept
+        gain = small[layer]["norm"]
+        incoming32 = incoming.astype(jnp.float32)
+        dots = jnp.sum(incoming32 * added, axis=1).reshape((-1, LANES))
+        dots = group_rows(dots).reshape((rows, 1))
+        g = group_rows(incoming)
+        og = mm(g, w_out, 1, 1)
+        per_row = jnp.concatenate([out_inv, dots], axis=1)
+        pg, outgoing, wide, conv, head = mixer_backward(
+            projected, marks, seg_row, small[layer], mixer, starts, og, per_row, DI
+        )
+        out_grad = low(mm(outgoing, g, 0, 0))
+        normed_grad = group_product(pg, lambda v: mm(v, w_in))
+        in_grad = low(mm(pg, normed, 0, 0))
+        hat = entering * inv
+        hat_grad = normed_grad * gain
+        mean = jnp.mean(hat_grad * hat, axis=-1, keepdims=True)
+        source_grad = incoming32 + inv * (hat_grad - hat * mean)
+        norm_grad = jnp.sum(normed_grad * hat, axis=0)
+        taps = jnp.concatenate([place_last(conv[:5, :width], quarter), conv[:5, width:]], axis=1)
+        tiny = [
+            norm_grad[None],
+            taps[:KW],
+            taps[KW:],
+            place_last(head[0:1, :heads], quarter),
+            place_last(head[1:2, :heads], quarter),
+            place_last(wide[1].reshape((1, heads, P_SIZE)).sum(axis=2), quarter),
+            place_last(wide[0:1], quarter),
+        ]
+        tiny = [jnp.moveaxis(t.reshape((t.shape[0], 4, -1)), 1, 0).reshape((4, -1)) for t in tiny]
+        tiny = jnp.concatenate(tiny + [jnp.zeros((4, filler), jnp.float32)], axis=1)
+        return source_grad, in_grad, out_grad, tiny
+
+    def scatter_in(grad):
+        parts = grad.reshape((2, HALF, D))
+        sent = swap_y(lax.dynamic_index_in_dim(parts, 1 - y, 0, False))
+        kept = lax.dynamic_index_in_dim(parts, y, 0, False)
+        both = low(kept.astype(jnp.float32) + sent.astype(jnp.float32))
+        both = jnp.stack([both[:, zz * LANE_PART : (zz + 1) * LANE_PART] for zz in range(4)])
+        return lax.psum_scatter(both, "shard", scatter_dimension=0, tiled=False)
+
+    def scatter_out(grad):
+        part = lax.psum_scatter(
+            grad.reshape((4, OUT_PART, D)), "shard", scatter_dimension=0, tiled=False
+        )
+        return low(part.astype(jnp.float32) + swap_y(part).astype(jnp.float32))
+
+    middle, kept0 = forward(0, source.astype(jnp.float32), w_in0, w_out0)
+    in_rows_late = after(in_rows, kept0[4])
+    w_in1, w_out1 = gather_weights(1, in_rows_late, out_weight[0])
+    result, kept1 = forward(1, low(middle).astype(jnp.float32), w_in1, w_out1)
+    result_ways = go_back(low(result), 1)
+    middle_grad, in_grad1, out_grad1, tiny1 = backward(1, kept1, cotangent, w_in1, w_out1)
+    out_part1 = scatter_out(out_grad1)
+    in_part1 = scatter_in(in_grad1)
+    entry_grad, in_grad0, out_grad0, tiny0 = backward(0, kept0, low(middle_grad), w_in0, w_out0)
+    grad_ways = go_back(low(entry_grad), 0)
+
+    boundary = jnp.stack(
+        [jnp.where(c == 0, grad_ways[m], result_ways[m]) for m in range(MICRO)]
+    ).astype(jnp.float32)[None, :, None]
+
+    tiny = jnp.stack([tiny0, tiny1]).reshape((CORES, 4, -1, LANES))
+    in_grad0 = after(in_grad0, entry_grad)
+    in_all, out_all, tiny = finish_sums(in_grad0, out_grad0, in_part1, out_part1, tiny)
+    in_total = jnp.swapaxes(assemble_rows(in_all), 0, 1)[None]
+    out_total = out_all.astype(jnp.float32)[None]
+    tiny = tiny.reshape(-1)
+    totals = []
+    at = 0
+    for p in params:
+        totals.append(tiny[at : at + p.size].reshape(p.shape))
+        at += p.size
+    norm_total, conv_total, bias_total, dt_total, log_total, skip_total, gain_total = totals
+    return (
+        boundary,
+        norm_total,
+        in_total,
+        conv_total,
+        bias_total,
+        dt_total,
+        log_total,
+        skip_total,
+        gain_total,
+        out_total,
+    )
+
+
 def solution(mesh):
+    fits = mesh.shape["shard"] == GROUP and mesh.shape["rep"] == 4
     return jax.shard_map(
-        per_device,
+        per_device_split if fits else per_device,
         mesh=mesh,
         in_specs=(
             P("section", None, "rep", "shard", None),

time: 3080 us -> 930 us (0.30)
  waiting for transfers between devices: 1290 us -> 150 us
  matrix products: 691 us -> 115 us
  Pallas kernels: 0 us -> 471 us
  local copies, waits for them, and re-layouts: 495 us -> 65.3 us
  other arithmetic: 333 us -> 35.5 us
  blocking collectives: 177 us -> 0 us
  starting transfers between devices: 35.6 us -> 69.4 us
    all_gather x11 -> x0, waiting for transfers between devices: 719 us -> none  [the longest x6 367 us: entering(): pieces = jax.tree.map(lambda part: lax.all_gather(part, axis), value)]
    dot_general x84 -> x20, matrix products: 691 us -> 115 us  [mm(): lax.dot_general(a, b, (((da,), (db,)), ((), ())), preferred_element_type=...]
    pallas_call x0 -> x8, Pallas kernels: none -> 471 us  [the longest x2 192 us: gather_weights(): pl.pallas_call(functools.partial(gather_kernel, layer), in_specs=[pl.Bloc...]
    unnamed x23 -> x2, waiting for transfers between devices: 307 us -> 0.03 us
    unnamed x651 -> x64, local copies, waits for them, and re-layouts: 177 us -> 5.05 us
    ppermute x13 -> x42, waiting for transfers between devices: 7.01 us -> 150 us  [the longest x13 95.3 us: swap_x(): return lax.ppermute(v, 'rep', [(i, i ^ 1) for i in range(4)])]
    reduce_scatter x1 -> x2, waiting for transfers between devices: 136 us -> 0.01 us  [the longest x1 0.01 us: scatter_out(): lax.psum_scatter(grad.reshape((4, OUT_PART, D)), 'shard', scatter_dimensi...]
    slice x54 -> x24, local copies, waits for them, and re-layouts: 137 us -> 6.13 us  [the longest x3 2.2 us: per_device_split(): totals.append(tiny[at:at + p.size].reshape(p.shape))]
  transfers between devices with their start and end apart: 31 -> 44, of which waited for: 21 -> 17; matrix products, arithmetic and copies ran while one was open for 27% -> 16% of each run, Pallas kernels for 0% -> 28%
where the time goes in v1:
time: 930 us; the launch traced here: 920 us
  Pallas kernels  471 us (51%)
  waiting for transfers between devices  150 us (16%)
  matrix products  115 us (12%)
  starting transfers between devices  69.4 us (7%)
  local copies, waits for them, and re-layouts  65.3 us (7%)
  other arithmetic  35.5 us (4%)
  between operations  15.4 us (2%)
    pallas_call x2, Pallas kernels, gather_weights(): pl.pallas_call(functools.partial(gather_kernel, layer), in_specs=[pl.Bloc...  192 us
    pallas_call x1, Pallas kernels, finish_sums(): pl.pallas_call(finish_kernel, in_specs=[pl.BlockSpec(memory_space=pltpu.V...  168 us
    dot_general x20, matrix products, mm(): lax.dot_general(a, b, (((da,), (db,)), ((), ())), preferred_element_type=...  115 us
    ppermute x13, waiting for transfers between devices, swap_x(): return lax.ppermute(v, 'rep', [(i, i ^ 1) for i in range(4)])  95.3 us
    pallas_call x2, Pallas kernels, mixer_backward(): pl.pallas_call(functools.partial(backward_kernel, width, whole_width), gr...  70.4 us
    pallas_call x2, Pallas kernels, mixer_forward(): pl.pallas_call(functools.partial(forward_kernel, width), grid=(chunks,),...  32 us
    ppermute x4, starting transfers between devices, go_back(): ways.append(lax.ppermute(value, axes, pairs))  22.4 us
    ppermute x2, waiting for transfers between devices, swap_y(): return lax.ppermute(v, 'rep', [(i, i ^ 2) for i in range(4)])  20.9 us
  transfers between devices with their start and end apart: 44, of which 17 were waited for; matrix products, arithmetic and copies ran while one was open for 16% of the time, Pallas kernels for 28%

profile of v1, /device:TPU:16, one launch (start us, length us, event | category | flops | bytes accessed | tf_op | source)
XLA Modules:
  0.0 920.3 jit_solution(5879231608344736675)
XLA Ops:
  19.5 110.8 %gather_weights.2 = (bf16[1856,1536]{1,0:T(8,128)(2,1)}, bf16[768,1536]{1,0:T(8,128)(2,1)}) custom-call(bf16[6448,384]{1,0:T(8,128)(2,1)} %bitcast.250, bf16[768,1536]{1,0:T(8,128)(2,1)} %bitcast.253), custom_call_target="tpu_custom_call" | custom-call | tf_op jit(solution)/shard_map/gather_weights/pallas_call | solution.py:930
  137.3 16.5 %collective-permute-start.4 = (bf16[2,2,5376]{2,1,0:T(2,128)(2,1)S(1)}, bf16[2,2,5376]{2,1,0:T(2,128)(2,1)S(1)}, u32[]{:S(2)}, u32[]{:S(2)}) collective-permute-start(bf16[2,2,5376]{2,1,0:T(2,128)(2,1)S(1)} %broadcast_select_fusion.3), channel_id=1, source_target_pairs={{0,8},{4,12},{8,0},{12,4},{1,9},{5,13},{9,1},{13,5},{2,10},{6,14},... | collective-permute-start | bytes 129032 | tf_op jit(solution)/shard_map/ppermute | solution.py:962
  170.3 11.3 %collective-permute-done.6 = bf16[256,1536]{1,0:T(8,128)(2,1)S(1)} collective-permute-done((bf16[256,1536]{1,0:T(8,128)(2,1)}, bf16[256,1536]{1,0:T(8,128)(2,1)S(1)}, u32[]{:S(2)}, u32[]{:S(2)}) %collective-permute-start.6) | collective-permute-done | bytes 786464 | tf_op jit(solution)/shard_map/ppermute | solution.py:954
  186.1 11.5 %convolution_convert_fusion.3.proj_ref.rim_ref = bf16[1024,1856]{1,0:T(8,128)(2,1)} fusion(bf16[1024,1536]{1,0:T(8,128)(2,1)} %constant_dynamic-update-slice_fusion.20, bf16[1856,1536]{1,0:T(8,128)(2,1)} %get-tuple-element.37), kind=kOutput, calls=%fused_computation.5 | convolution fusion | flops 5840371712 | bytes 12648448 | tf_op jit(solution)/shard_map/dot_general | solution.py:424
  197.7 16.0 %mixer_forward.2 = (bf16[1024,768]{1,0:T(8,128)(2,1)}, f32[1024,1]{1,0:T(8,128)}, f32[1024,768]{1,0:T(8,128)}, f32[8,128,768]{2,1,0:T(8,128)}) custom-call(bf16[1024,1856]{1,0:T(8,128)(2,1)} %convolution_convert_fusion.3.proj_ref.rim_ref, f32[1024,8]{1,0:T(8,128)} %copy.164.marks_ref, f32[1,1024]{1,0:T(1,128)} %bitcast.283, ...), custom_call_target="tpu_custom_call" | custom-call | tf_op jit(solution)/shard_map/mixer_forward/pallas_call | solution.py:676
  230.4 15.6 %collective-permute-done.10 = f32[8,128]{1,0:T(8,128)S(1)} collective-permute-done((f32[8,128]{1,0:T(8,128)S(1)}, f32[8,128]{1,0:T(8,128)S(1)}, u32[]{:S(2)}, u32[]{:S(2)}) %collective-permute-start.10) | collective-permute-done | bytes 4128 | tf_op jit(solution)/shard_map/ppermute | solution.py:954
  258.1 14.8 %collective-permute-done.14 = bf16[256,1536]{1,0:T(8,128)(2,1)S(1)} collective-permute-done((bf16[256,1536]{1,0:T(8,128)(2,1)}, bf16[256,1536]{1,0:T(8,128)(2,1)S(1)}, u32[]{:S(2)}, u32[]{:S(2)}) %collective-permute-start.14) | collective-permute-done | bytes 786464 | tf_op jit(solution)/shard_map/ppermute | solution.py:954
  274.6 80.9 %gather_weights.3 = (bf16[1856,1536]{1,0:T(8,128)(2,1)}, bf16[768,1536]{1,0:T(8,128)(2,1)}) custom-call(bf16[6448,384]{1,0:T(8,128)(2,1)} %bitcast.251, bf16[768,1536]{1,0:T(8,128)(2,1)} %bitcast.254), custom_call_target="tpu_custom_call" | custom-call | tf_op jit(solution)/shard_map/gather_weights/pallas_call | solution.py:930
  359.6 11.8 %convolution_convert_fusion.2.proj_ref.rim_ref = bf16[1024,1856]{1,0:T(8,128)(2,1)} fusion(bf16[1024,1536]{1,0:T(8,128)(2,1)} %constant_dynamic-update-slice_fusion.16, bf16[1856,1536]{1,0:T(8,128)(2,1)} %get-tuple-element.43), kind=kOutput, calls=%fused_computation.4 | convolution fusion | flops 5840371712 | bytes 12648448 | tf_op jit(solution)/shard_map/dot_general | solution.py:424
  371.3 16.0 %mixer_forward.3 = (bf16[1024,768]{1,0:T(8,128)(2,1)}, f32[1024,1]{1,0:T(8,128)}, f32[1024,768]{1,0:T(8,128)}, f32[8,128,768]{2,1,0:T(8,128)}) custom-call(bf16[1024,1856]{1,0:T(8,128)(2,1)} %convolution_convert_fusion.2.proj_ref.rim_ref, f32[1024,8]{1,0:T(8,128)} %copy.164.marks_ref, f32[1,1024]{1,0:T(1,128)} %bitcast.284, ...), custom_call_target="tpu_custom_call" | custom-call | tf_op jit(solution)/shard_map/mixer_forward/pallas_call | solution.py:676
  401.5 15.9 %collective-permute-done.20 = f32[8,128]{1,0:T(8,128)S(1)} collective-permute-done((f32[8,128]{1,0:T(8,128)S(1)}, f32[8,128]{1,0:T(8,128)S(1)}, u32[]{:S(2)}, u32[]{:S(2)}) %collective-permute-start.20) | collective-permute-done | bytes 4128 | tf_op jit(solution)/shard_map/ppermute | solution.py:954
  422.9 6.1 collective-permute-start.39
  430.6 13.7 %collective-permute-done.24 = f32[2,128]{1,0:T(2,128)S(1)} collective-permute-done((f32[2,128]{1,0:T(2,128)S(1)}, f32[2,128]{1,0:T(2,128)S(1)}, u32[]{:S(2)}, u32[]{:S(2)}) %collective-permute-start.24) | collective-permute-done | bytes 1056 | tf_op jit(solution)/shard_map/ppermute | solution.py:954
  451.8 6.1 fusion.113.og_ref
  457.9 35.2 %mixer_backward.2 = (bf16[1024,1856]{1,0:T(8,128)(2,1)}, bf16[1024,768]{1,0:T(8,128)(2,1)}, f32[8,768]{1,0:T(8,128)}, f32[8,1024]{1,0:T(8,128)}, f32[8,128]{1,0:T(8,128)}) custom-call(bf16[1024,1856]{1,0:T(8,128)(2,1)} %convolution_convert_fusion.2.proj_ref.rim_ref, bf16[1024,1856]{1,0:T(8,128)(2,1)} %convolution_convert_fusion.2.proj_ref.rim_ref, ...), custom_call_target="tpu_custom_call" | custom-call | tf_op jit(solution)/shard_map/mixer_backward/pallas_call | solution.py:715
  494.8 7.4 convolution_convert_fusion.7
  502.4 8.7 convolution_convert_fusion
  515.3 5.0 collective-permute-start.40
  524.8 5.8 fusion.28
  533.6 4.7 fusion.42
  538.3 12.0 %collective-permute-done.27 = bf16[256,1536]{1,0:T(8,128)(2,1)} collective-permute-done((bf16[256,1536]{1,0:T(8,128)(2,1)}, bf16[256,1536]{1,0:T(8,128)(2,1)}, u32[]{:S(2)}, u32[]{:S(2)}) %collective-permute-start.27) | collective-permute-done | bytes 786464 | tf_op jit(solution)/shard_map/ppermute | solution.py:954
  562.0 20.9 %collective-permute-done.40 = bf16[928,1536]{1,0:T(8,128)(2,1)} collective-permute-done((bf16[928,1536]{1,0:T(8,128)(2,1)}, bf16[928,1536]{1,0:T(8,128)(2,1)}, u32[]{:S(2)}, u32[]{:S(2)}) %collective-permute-start.40) | collective-permute-done | bytes 2850848 | tf_op jit(solution)/shard_map/ppermute | solution.py:958
  593.0 6.2 fusion.114.og_ref
  599.2 35.2 %mixer_backward.3 = (bf16[1024,1856]{1,0:T(8,128)(2,1)}, bf16[1024,768]{1,0:T(8,128)(2,1)}, f32[8,768]{1,0:T(8,128)}, f32[8,1024]{1,0:T(8,128)}, f32[8,128]{1,0:T(8,128)}) custom-call(bf16[1024,1856]{1,0:T(8,128)(2,1)} %convolution_convert_fusion.3.proj_ref.rim_ref, bf16[1024,1856]{1,0:T(8,128)(2,1)} %convolution_convert_fusion.3.proj_ref.rim_ref, ...), custom_call_target="tpu_custom_call" | custom-call | tf_op jit(solution)/shard_map/mixer_backward/pallas_call | solution.py:715
  641.2 9.9 %convolution_convert_fusion.1.grad_ref = bf16[1856,1536]{1,0:T(8,128)(2,1)} fusion(bf16[1024,1856]{1,0:T(8,128)(2,1)S(1)} %copy-done.16, bf16[1024,1536]{1,0:T(8,128)(2,1)} %constant_dynamic-update-slice_fusion.20), kind=kOutput, calls=%fused_computation.1 | convolution fusion | flops 5841321984 | bytes 12648448 | tf_op jit(solution)/shard_map/dot_general | solution.py:424
  656.1 5.9 fusion.26
  662.1 5.9 convolution_convert_fusion.5.out_grad_ref
  669.8 12.0 %collective-permute-done.35 = bf16[256,1536]{1,0:T(8,128)(2,1)} collective-permute-done((bf16[256,1536]{1,0:T(8,128)(2,1)}, bf16[256,1536]{1,0:T(8,128)(2,1)}, u32[]{:S(2)}, u32[]{:S(2)}) %collective-permute-start.35) | collective-permute-done | bytes 786464 | tf_op jit(solution)/shard_map/ppermute | solution.py:954
  684.5 13.5 %collective-permute-start.38 = (bf16[256,1536]{1,0:T(8,128)(2,1)S(1)}, bf16[256,1536]{1,0:T(8,128)(2,1)S(1)}, u32[]{:S(2)}, u32[]{:S(2)}) collective-permute-start(bf16[256,1536]{1,0:T(8,128)(2,1)S(1)} %convert_add_fusion.3), channel_id=1, source_target_pairs={{8,0},{12,1},{10,2},{14,3},{24,4},{28,5},{26,6},{30,7},{9,8},{13,9... | collective-permute-start | bytes 2359304 | tf_op jit(solution)/shard_map/ppermute | solution.py:1439
  705.4 17.4 %collective-permute-done.38 = bf16[256,1536]{1,0:T(8,128)(2,1)S(1)} collective-permute-done((bf16[256,1536]{1,0:T(8,128)(2,1)S(1)}, bf16[256,1536]{1,0:T(8,128)(2,1)S(1)}, u32[]{:S(2)}, u32[]{:S(2)}) %collective-permute-start.38) | collective-permute-done | bytes 786464 | tf_op jit(solution)/shard_map/ppermute | solution.py:1439
  725.7 168.2 %finish_sums.1 = (bf16[4,1856,384]{2,1,0:T(8,128)(2,1)}, bf16[768,1536]{1,0:T(8,128)(2,1)}, f32[42,128]{1,0:T(8,128)}) custom-call(bf16[1856,1536]{1,0:T(8,128)(2,1)} %convolution_convert_fusion.1.grad_ref, bf16[768,1536]{1,0:T(8,128)(2,1)} %convolution_convert_fusion.5.out_grad_ref, bf16[928,384]{1,0:T(8,128)(2,1)} %bitcast.277, ...), custom_call_target="tpu_custom_call" | custom-call | tf_op jit(solution)/shard_map/finish_sums/pallas_call | solution.py:1332
  898.7 8.3 assemble_rows.1
  (400 shorter events, 175.8 us)
Async XLA Ops:
  7.2 660.8 %reduce-scatter.5.cloned.1.call-start = ((), (), s32[]{:S(2)}) async-start(), calls=%async_computation.3 | async-start | bytes 2949120 | tf_op jit(solution)/shard_map/reduce_scatter | solution.py:1605
  12.2 121.0 %collective-permute-start.2 = (bf16[5376]{0:T(1024)(128)(2,1)S(1)}, bf16[5376]{0:T(1024)(128)(2,1)S(1)}, u32[]{:S(2)}, u32[]{:S(2)}) collective-permute-start(bf16[5376]{0:T(1024)(128)(2,1)S(1)} %concatenate.87), channel_id=1, source_target_pairs={{0,16},{16,0},{1,17},{17,1},{2,18},{18,2},{3,19},{19,3},{4,20},{20... | collective-permute-start | bytes 32264 | tf_op jit(solution)/shard_map/ppermute | solution.py:950
  13.7 145.2 %collective-permute-start.1 = (bf16[256,1536]{1,0:T(8,128)(2,1)S(1)}, bf16[256,1536]{1,0:T(8,128)(2,1)S(1)}, u32[]{:S(2)}, u32[]{:S(2)}) collective-permute-start(bf16[256,1536]{1,0:T(8,128)(2,1)S(1)} %get-tuple-element.108), channel_id=1, source_target_pairs={{0,0},{1,4},{2,2},{3,6},{4,16},{5,20},{6,18},{7,22},{8,1},{9,5},{1... | collective-permute-start | bytes 2359304 | tf_op jit(solution)/shard_map/ppermute | solution.py:1445
  16.9 142.0 %collective-permute-start = (bf16[256,1536]{1,0:T(8,128)(2,1)S(1)}, bf16[256,1536]{1,0:T(8,128)(2,1)S(1)}, u32[]{:S(2)}, u32[]{:S(2)}) collective-permute-start(bf16[256,1536]{1,0:T(8,128)(2,1)S(1)} %get-tuple-element.107), channel_id=1, source_target_pairs={{0,8},{1,12},{2,10},{3,14},{4,24},{5,28},{6,26},{7,30},{8,9},{9,13... | collective-permute-start | bytes 2359304 | tf_op jit(solution)/shard_map/ppermute | solution.py:1448
  17.7 113.3 %collective-permute-start.8 = (s32[2,2,4]{2,1,0:T(2,128)S(1)}, s32[2,2,4]{2,1,0:T(2,128)S(1)}, u32[]{:S(2)}, u32[]{:S(2)}) collective-permute-start(s32[2,2,4]{2,1,0:T(2,128)S(1)} %pad_add_fusion), channel_id=1, source_target_pairs={{0,1},{1,0},{2,3},{3,2},{4,5},{5,4},{6,7},{7,6},{8,9},{9,8},{10,11... | collective-permute-start | bytes 200 | tf_op jit(solution)/shard_map/ppermute | solution.py:954
  137.3 18.5 %collective-permute-start.4 = (bf16[2,2,5376]{2,1,0:T(2,128)(2,1)S(1)}, bf16[2,2,5376]{2,1,0:T(2,128)(2,1)S(1)}, u32[]{:S(2)}, u32[]{:S(2)}) collective-permute-start(bf16[2,2,5376]{2,1,0:T(2,128)(2,1)S(1)} %broadcast_select_fusion.3), channel_id=1, source_target_pairs={{0,8},{4,12},{8,0},{12,4},{1,9},{5,13},{9,1},{13,5},{2,10},{6,14},... | collective-permute-start | bytes 129032 | tf_op jit(solution)/shard_map/ppermute | solution.py:962
  162.6 19.0 %collective-permute-start.6 = (bf16[256,1536]{1,0:T(8,128)(2,1)}, bf16[256,1536]{1,0:T(8,128)(2,1)S(1)}, u32[]{:S(2)}, u32[]{:S(2)}) collective-permute-start(bf16[256,1536]{1,0:T(8,128)(2,1)} %get-tuple-element.99), channel_id=1, source_target_pairs={{0,1},{1,0},{2,3},{3,2},{4,5},{5,4},{6,7},{7,6},{8,9},{9,8},{10,11... | collective-permute-start | bytes 2359304 | tf_op jit(solution)/shard_map/ppermute | solution.py:954
  167.2 16.2 %collective-permute-start.5 = (bf16[256,1536]{1,0:T(8,128)(2,1)}, bf16[256,1536]{1,0:T(8,128)(2,1)S(1)}, u32[]{:S(2)}, u32[]{:S(2)}) collective-permute-start(bf16[256,1536]{1,0:T(8,128)(2,1)} %get-tuple-element.99), channel_id=1, source_target_pairs={{0,16},{16,0},{1,17},{17,1},{2,18},{18,2},{3,19},{19,3},{4,20},{20... | collective-permute-start | bytes 2359304 | tf_op jit(solution)/shard_map/ppermute | solution.py:950
  225.8 20.1 %collective-permute-start.12 = (bf16[256,1536]{1,0:T(8,128)(2,1)}, bf16[256,1536]{1,0:T(8,128)(2,1)S(1)}, u32[]{:S(2)}, u32[]{:S(2)}) collective-permute-start(bf16[256,1536]{1,0:T(8,128)(2,1)} %fusion.33), channel_id=1, source_target_pairs={{0,1},{1,0},{2,3},{3,2},{4,5},{5,4},{6,7},{7,6},{8,9},{9,8},{10,11... | collective-permute-start | bytes 2359304 | tf_op jit(solution)/shard_map/ppermute | solution.py:954
  230.1 15.9 %collective-permute-start.10 = (f32[8,128]{1,0:T(8,128)S(1)}, f32[8,128]{1,0:T(8,128)S(1)}, u32[]{:S(2)}, u32[]{:S(2)}) collective-permute-start(f32[8,128]{1,0:T(8,128)S(1)} %bitcast_add_fusion.1), channel_id=1, source_target_pairs={{0,1},{1,0},{2,3},{3,2},{4,5},{5,4},{6,7},{7,6},{8,9},{9,8},{10,11... | collective-permute-start | bytes 12296 | tf_op jit(solution)/shard_map/ppermute | solution.py:954
  253.7 19.2 %collective-permute-start.14 = (bf16[256,1536]{1,0:T(8,128)(2,1)}, bf16[256,1536]{1,0:T(8,128)(2,1)S(1)}, u32[]{:S(2)}, u32[]{:S(2)}) collective-permute-start(bf16[256,1536]{1,0:T(8,128)(2,1)} %get-tuple-element.95), channel_id=1, source_target_pairs={{0,1},{1,0},{2,3},{3,2},{4,5},{5,4},{6,7},{7,6},{8,9},{9,8},{10,11... | collective-permute-start | bytes 2359304 | tf_op jit(solution)/shard_map/ppermute | solution.py:954
  255.4 100.1 %collective-permute-start.13 = (bf16[256,1536]{1,0:T(8,128)(2,1)}, bf16[256,1536]{1,0:T(8,128)(2,1)}, u32[]{:S(2)}, u32[]{:S(2)}) collective-permute-start(bf16[256,1536]{1,0:T(8,128)(2,1)} %get-tuple-element.95), channel_id=1, source_target_pairs={{0,16},{16,0},{1,17},{17,1},{2,18},{18,2},{3,19},{19,3},{4,20},{20... | collective-permute-start | bytes 2359304 | tf_op jit(solution)/shard_map/ppermute | solution.py:950
  272.9 85.7 %collective-permute-start.15 = (bf16[256,1536]{1,0:T(8,128)(2,1)S(1)}, bf16[256,1536]{1,0:T(8,128)(2,1)S(1)}, u32[]{:S(2)}, u32[]{:S(2)}) collective-permute-start(bf16[256,1536]{1,0:T(8,128)(2,1)S(1)} %collective-permute-done.14), channel_id=1, source_target_pairs={{0,16},{16,0},{1,17},{17,1},{2,18},{18,2},{3,19},{19,3},{4,20},{20... | collective-permute-start | bytes 2359304 | tf_op jit(solution)/shard_map/ppermute | solution.py:950
  397.6 19.8 %collective-permute-start.22 = (bf16[256,1536]{1,0:T(8,128)(2,1)S(1)}, bf16[256,1536]{1,0:T(8,128)(2,1)S(1)}, u32[]{:S(2)}, u32[]{:S(2)}) collective-permute-start(bf16[256,1536]{1,0:T(8,128)(2,1)S(1)} %fusion.30), channel_id=1, source_target_pairs={{0,1},{1,0},{2,3},{3,2},{4,5},{5,4},{6,7},{7,6},{8,9},{9,8},{10,11... | collective-permute-start | bytes 2359304 | tf_op jit(solution)/shard_map/ppermute | solution.py:954
  398.2 19.2 %collective-permute-start.20 = (f32[8,128]{1,0:T(8,128)S(1)}, f32[8,128]{1,0:T(8,128)S(1)}, u32[]{:S(2)}, u32[]{:S(2)}) collective-permute-start(f32[8,128]{1,0:T(8,128)S(1)} %bitcast_add_fusion), channel_id=1, source_target_pairs={{0,1},{1,0},{2,3},{3,2},{4,5},{5,4},{6,7},{7,6},{8,9},{9,8},{10,11... | collective-permute-start | bytes 12296 | tf_op jit(solution)/shard_map/ppermute | solution.py:954
  420.1 24.2 %collective-permute-start.17 = (bf16[256,1536]{1,0:T(8,128)(2,1)S(1)}, bf16[256,1536]{1,0:T(8,128)(2,1)S(1)}, u32[]{:S(2)}, u32[]{:S(2)}) collective-permute-start(bf16[256,1536]{1,0:T(8,128)(2,1)S(1)} %get-tuple-element.93), channel_id=1, source_target_pairs={{0,1},{1,0},{2,3},{3,2},{4,5},{5,4},{6,7},{7,6},{8,9},{9,8},{10,11... | collective-permute-start | bytes 2359304 | tf_op jit(solution)/shard_map/ppermute | solution.py:954
  420.6 26.0 %collective-permute-start.16 = (bf16[256,1536]{1,0:T(8,128)(2,1)S(1)}, bf16[256,1536]{1,0:T(8,128)(2,1)}, u32[]{:S(2)}, u32[]{:S(2)}) collective-permute-start(bf16[256,1536]{1,0:T(8,128)(2,1)S(1)} %get-tuple-element.93), channel_id=1, source_target_pairs={{0,16},{16,0},{1,17},{17,1},{2,18},{18,2},{3,19},{19,3},{4,20},{20... | collective-permute-start | bytes 2359304 | tf_op jit(solution)/shard_map/ppermute | solution.py:950
  420.6 8.5 collective-permute-start.23
  421.1 23.2 %collective-permute-start.24 = (f32[2,128]{1,0:T(2,128)S(1)}, f32[2,128]{1,0:T(2,128)S(1)}, u32[]{:S(2)}, u32[]{:S(2)}) collective-permute-start(f32[2,128]{1,0:T(2,128)S(1)} %bitcast.323), channel_id=1, source_target_pairs={{0,1},{1,0},{2,3},{3,2},{4,5},{5,4},{6,7},{7,6},{8,9},{9,8},{10,11... | collective-permute-start | bytes 3080 | tf_op jit(solution)/shard_map/ppermute | solution.py:954
  422.9 282.5 %collective-permute-start.39 = (bf16[256,1536]{1,0:T(8,128)(2,1)}, bf16[256,1536]{1,0:T(8,128)(2,1)}, u32[]{:S(2)}, u32[]{:S(2)}) collective-permute-start(bf16[256,1536]{1,0:T(8,128)(2,1)} %get-tuple-element.102), channel_id=1, source_target_pairs={{8,16},{12,17},{10,18},{14,19},{24,20},{28,21},{26,22},{30,23},{9,... | collective-permute-start | bytes 2359304 | tf_op jit(solution)/shard_map/ppermute | solution.py:1439
  429.0 293.8 %collective-permute-start.37 = (bf16[256,1536]{1,0:T(8,128)(2,1)}, bf16[256,1536]{1,0:T(8,128)(2,1)}, u32[]{:S(2)}, u32[]{:S(2)}) collective-permute-start(bf16[256,1536]{1,0:T(8,128)(2,1)} %get-tuple-element.102), channel_id=1, source_target_pairs={{0,16},{4,17},{2,18},{6,19},{16,20},{20,21},{18,22},{22,23},{1,24}... | collective-permute-start | bytes 2359304 | tf_op jit(solution)/shard_map/ppermute | solution.py:1439
  502.2 22.6 %collective-permute-start.26 = (bf16[512,1536]{1,0:T(8,128)(2,1)}, bf16[512,1536]{1,0:T(8,128)(2,1)}, u32[]{:S(2)}, u32[]{:S(2)}) collective-permute-start(bf16[512,1536]{1,0:T(8,128)(2,1)} %convolution_convert_fusion.7), channel_id=1, source_target_pairs={{0,16},{16,0},{1,17},{17,1},{2,18},{18,2},{3,19},{19,3},{4,20},{20... | collective-permute-start | bytes 4718600 | tf_op jit(solution)/shard_map/ppermute | solution.py:950
  515.3 67.6 %collective-permute-start.40 = (bf16[928,1536]{1,0:T(8,128)(2,1)}, bf16[928,1536]{1,0:T(8,128)(2,1)}, u32[]{:S(2)}, u32[]{:S(2)}) collective-permute-start(bf16[928,1536]{1,0:T(8,128)(2,1)} %dynamic-slice_bitcast_fusion), channel_id=1, source_target_pairs={{0,2},{1,3},{2,0},{3,1},{4,6},{5,7},{6,4},{7,5},{8,10},{9,11},{10,... | collective-permute-start | bytes 8552456 | tf_op jit(solution)/shard_map/ppermute | solution.py:958
  524.3 201.3 %reduce-scatter.3.cloned.1.call-start = ((), (), s32[]{:S(2)}) async-start(), calls=%async_computation.2 | async-start | bytes 3563520 | tf_op jit(solution)/shard_map/reduce_scatter | solution.py:1602
  530.5 19.8 %collective-permute-start.27 = (bf16[256,1536]{1,0:T(8,128)(2,1)}, bf16[256,1536]{1,0:T(8,128)(2,1)}, u32[]{:S(2)}, u32[]{:S(2)}) collective-permute-start(bf16[256,1536]{1,0:T(8,128)(2,1)} %fusion.28), channel_id=1, source_target_pairs={{0,1},{1,0},{2,3},{3,2},{4,5},{5,4},{6,7},{7,6},{8,9},{9,8},{10,11... | collective-permute-start | bytes 2359304 | tf_op jit(solution)/shard_map/ppermute | solution.py:954
  556.9 32.1 %collective-permute-start.28 = (bf16[256,1536]{1,0:T(8,128)(2,1)S(1)}, bf16[256,1536]{1,0:T(8,128)(2,1)S(1)}, u32[]{:S(2)}, u32[]{:S(2)}) collective-permute-start(bf16[256,1536]{1,0:T(8,128)(2,1)S(1)} %get-tuple-element.90), channel_id=1, source_target_pairs={{0,16},{16,0},{1,17},{17,1},{2,18},{18,2},{3,19},{19,3},{4,20},{20... | collective-permute-start | bytes 2359304 | tf_op jit(solution)/shard_map/ppermute | solution.py:950
  559.3 27.1 %collective-permute-start.29 = (bf16[256,1536]{1,0:T(8,128)(2,1)S(1)}, bf16[256,1536]{1,0:T(8,128)(2,1)S(1)}, u32[]{:S(2)}, u32[]{:S(2)}) collective-permute-start(bf16[256,1536]{1,0:T(8,128)(2,1)S(1)} %get-tuple-element.90), channel_id=1, source_target_pairs={{0,1},{1,0},{2,3},{3,2},{4,5},{5,4},{6,7},{7,6},{8,9},{9,8},{10,11... | collective-permute-start | bytes 2359304 | tf_op jit(solution)/shard_map/ppermute | solution.py:954
  640.7 15.4 %collective-permute-start.34 = (bf16[512,1536]{1,0:T(8,128)(2,1)}, bf16[512,1536]{1,0:T(8,128)(2,1)}, u32[]{:S(2)}, u32[]{:S(2)}) collective-permute-start(bf16[512,1536]{1,0:T(8,128)(2,1)} %convolution_convert_fusion.6), channel_id=1, source_target_pairs={{0,16},{16,0},{1,17},{17,1},{2,18},{18,2},{3,19},{19,3},{4,20},{20... | collective-permute-start | bytes 4718600 | tf_op jit(solution)/shard_map/ppermute | solution.py:950
  662.0 19.8 %collective-permute-start.35 = (bf16[256,1536]{1,0:T(8,128)(2,1)}, bf16[256,1536]{1,0:T(8,128)(2,1)}, u32[]{:S(2)}, u32[]{:S(2)}) collective-permute-start(bf16[256,1536]{1,0:T(8,128)(2,1)} %fusion.26), channel_id=1, source_target_pairs={{0,1},{1,0},{2,3},{3,2},{4,5},{5,4},{6,7},{7,6},{8,9},{9,8},{10,11... | collective-permute-start | bytes 2359304 | tf_op jit(solution)/shard_map/ppermute | solution.py:954
  668.0 34.3 %collective-permute-start.41 = (bf16[192,1536]{1,0:T(8,128)(2,1)}, bf16[192,1536]{1,0:T(8,128)(2,1)}, u32[]{:S(2)}, u32[]{:S(2)}) collective-permute-start(bf16[192,1536]{1,0:T(8,128)(2,1)} %bitcast.278), channel_id=1, source_target_pairs={{0,2},{1,3},{2,0},{3,1},{4,6},{5,7},{6,4},{7,5},{8,10},{9,11},{10,... | collective-permute-start | bytes 1769480 | tf_op jit(solution)/shard_map/ppermute | solution.py:958
  684.5 38.3 %collective-permute-start.38 = (bf16[256,1536]{1,0:T(8,128)(2,1)S(1)}, bf16[256,1536]{1,0:T(8,128)(2,1)S(1)}, u32[]{:S(2)}, u32[]{:S(2)}) collective-permute-start(bf16[256,1536]{1,0:T(8,128)(2,1)S(1)} %convert_add_fusion.3), channel_id=1, source_target_pairs={{8,0},{12,1},{10,2},{14,3},{24,4},{28,5},{26,6},{30,7},{9,8},{13,9... | collective-permute-start | bytes 2359304 | tf_op jit(solution)/shard_map/ppermute | solution.py:1439
  701.0 22.7 %collective-permute-start.36 = (bf16[256,1536]{1,0:T(8,128)(2,1)S(1)}, bf16[256,1536]{1,0:T(8,128)(2,1)S(1)}, u32[]{:S(2)}, u32[]{:S(2)}) collective-permute-start(bf16[256,1536]{1,0:T(8,128)(2,1)S(1)} %convert_add_fusion.3), channel_id=1, source_target_pairs={{0,0},{4,1},{2,2},{6,3},{16,4},{20,5},{18,6},{22,7},{1,8},{5,9},{3... | collective-permute-start | bytes 2359304 | tf_op jit(solution)/shard_map/ppermute | solution.py:1439
  (42 other events, 392.2 us)
Sparse Core Ops, SparseCore 0:
  524.5 56.7 reduce-scatter.4
  589.1 65.4 reduce-scatter.2

commit v2 on v1

--- a/solution.py
+++ b/solution.py
@@ -774,176 +774,446 @@
     return found
 
 
-def gather_kernel(
-    layer, in_ref, out_ref, w_ref, wo_ref,
-    local_sem, core_send, core_recv, right_send, left_send, z_recv, y_send, y_recv,
+def mesh_copy(source, target, send, recv, device):
+    return pltpu.make_async_remote_copy(
+        src_ref=source, dst_ref=target, send_sem=send, recv_sem=recv,
+        device_id=device, device_id_type=pl.DeviceIdType.MESH,
+    )
+
+
+def greet(barrier, device):
+    pl.semaphore_signal(barrier, inc=1, device_id=device, device_id_type=pl.DeviceIdType.MESH)
+
+
+def rows_at(start, count):
+    return pl.ds(pl.multiple_of(start, 16), count)
+
+
+class WeightGather:
+    def __init__(self, layer, in_ref, out_ref, w_ref, wo_ref, sems):
+        self.layer, self.in_ref, self.out_ref = layer, in_ref, out_ref
+        self.w_ref, self.wo_ref = w_ref, wo_ref
+        (
+            self.local_sem, self.core_send, self.core_recv, self.right_send, self.left_send,
+            self.z_recv, self.y_send, self.y_recv,
+        ) = sems
+        self.c, self.z, self.y, self.x = place()
+        self.core = {"section": 1 - self.c}
+        self.y_other = {"rep": (1 - self.y) * 2 + self.x}
+
+    def own_pieces(self, quarter):
+        lanes = pl.ds(pl.multiple_of(self.z * LANE_PART, LANES), LANE_PART)
+        found = []
+        for at, start, count in weight_pieces(quarter):
+            found.append((self.in_ref.at[rows_at(start, count)], self.w_ref.at[pl.ds(at, count), lanes]))
+        found.append(
+            (
+                self.out_ref.at[rows_at(quarter * OUT_PART, OUT_PART)],
+                self.wo_ref.at[rows_at(self.z * OUT_PART, OUT_PART)],
+            )
+        )
+        return found
+
+    def local_copies(self):
+        return [
+            pltpu.make_async_copy(source, target, self.local_sem.at[i])
+            for i, (source, target) in enumerate(self.own_pieces(2 * self.x + self.c))
+        ]
+
+    def core_copies(self):
+        return [
+            mesh_copy(source, target, self.core_send.at[i], self.core_recv.at[i], self.core)
+            for i, (source, target) in enumerate(self.own_pieces(2 * self.x + 1 - self.c))
+        ]
+
+    def begin(self):
+        lanes = pl.ds(pl.multiple_of(self.z * LANE_PART, LANES), LANE_PART)
+        self.w_ref[LOCAL - 16 :, lanes] = jnp.zeros((16, LANE_PART), self.w_ref.dtype)
+
+        @pl.when(self.c == self.layer)
+        def _():
+            for copy in self.core_copies():
+                copy.start()
+            for copy in self.local_copies():
+                copy.start()
+            for copy in self.local_copies():
+                copy.wait()
+
+        @pl.when(self.c != self.layer)
+        def _():
+            for copy in self.core_copies():
+                copy.wait_recv()
+
+    def slab(self, unit, shard, side):
+        if unit == CHUNKS:
+            return self.wo_ref.at[rows_at(shard * OUT_PART + side * (OUT_PART // 2), OUT_PART // 2)]
+        return self.w_ref.at[
+            rows_at(side * HALF + unit * (HALF // CHUNKS), HALF // CHUNKS),
+            pl.ds(pl.multiple_of(shard * LANE_PART, LANES), LANE_PART),
+        ]
+
+    def z_copy(self, unit, shard, step, k):
+        piece = self.slab(unit, shard, self.y)
+        send = (self.right_send if step > 0 else self.left_send).at[unit, k]
+        return mesh_copy(piece, piece, send, self.z_recv.at[unit, shard], {"shard": self.z + step})
+
+    def y_copy(self, unit, shard, side):
+        piece = self.slab(unit, shard, side)
+        return mesh_copy(
+            piece, piece, self.y_send.at[unit, shard], self.y_recv.at[unit, shard], self.y_other
+        )
+
+    def cases(self, step, k):
+        shard = self.z - k * step
+        there = (shard >= 0) if step > 0 else (shard <= 3)
+        more = (self.z < 3) if step > 0 else (self.z > 0)
+        return shard, there, more
+
+    def first(self, unit):
+        for step in (1, -1):
+            _, _, more = self.cases(step, 0)
+
+            @pl.when(more)
+            def _():
+                self.z_copy(unit, self.z, step, 0).start()
+
+    def arrive(self, unit, k):
+        for step in (1, -1):
+            shard, there, more = self.cases(step, k)
+
+            @pl.when(there)
+            def _():
+                self.z_copy(unit, shard, step, 0).wait_recv()
+
+                @pl.when(more)
+                def _():
+                    self.z_copy(unit, shard, step, k).start()
+
+                self.y_copy(unit, shard, self.y).start()
+
+    def end(self):
+        for unit in range(UNITS):
+            for away in (1, 2, 3):
+                shard = lax.rem(self.z + away, 4)
+                self.y_copy(unit, shard, 1 - self.y).wait_recv()
+                self.y_copy(unit, shard, self.y).wait_send()
+            for step in (1, -1):
+                for k in range(3):
+                    shard, there, more = self.cases(step, k)
+
+                    @pl.when(there & more)
+                    def _():
+                        self.z_copy(unit, shard, step, k).wait_send()
+
+        @pl.when(self.c == self.layer)
+        def _():
+            for copy in self.core_copies():
+                copy.wait_send()
+
+
+def weight_scratch():
+    dma = pltpu.SemaphoreType.DMA
+    return [
+        dma((10,)), dma((10,)), dma((10,)),
+        dma((UNITS, 3)), dma((UNITS, 3)), dma((UNITS, 4)), dma((UNITS, 4)), dma((UNITS, 4)),
+    ]
+
+
+class RowGather:
+    def __init__(self, whole, count, sems):
+        self.whole, self.count = whole, count
+        self.send, self.recv = sems
+        self.c, self.z, self.y, self.x = place()
+
+    def copy(self, i, xx, cc, device):
+        piece = self.whole.at[rows_at((2 * xx + cc) * self.count, self.count)]
+        return mesh_copy(piece, piece, self.send.at[i], self.recv.at[i], device)
+
+    def near(self):
+        return self.copy(0, self.x, self.c, {"rep": 2 * self.y + 1 - self.x})
+
+    def other(self):
+        return self.copy(1, self.x, self.c, {"section": 1 - self.c})
+
+    def far(self):
+        return self.copy(2, 1 - self.x, self.c, {"section": 1 - self.c})
+
+    def begin(self, value):
+        self.whole[rows_at((2 * self.x + self.c) * self.count, self.count)] = value
+        self.near().start()
+        self.other().start()
+
+    def middle(self):
+        self.near().wait_recv()
+        self.far().start()
+
+    def end(self):
+        self.near().wait_send()
+        self.other().wait()
+        self.far().wait()
+
+
+def normal_rows(rows, gain):
+    inv = lax.rsqrt(jnp.mean(rows * rows, axis=-1, keepdims=True) + EPSILON)
+    return low(rows * inv * gain)
+
+
+def enter_first_kernel(
+    in_ref, out_ref, blocks_ref, flat_ref, w_ref, wo_ref, rows_ref, normed_ref, params_ref,
+    row_send, row_recv, home_send, home_recv, p_send, p_recv, *sems,
 ):
     c, z, y, x = place()
-    core, y_other = {"section": 1 - c}, {"rep": (1 - y) * 2 + x}
+    weights = WeightGather(0, in_ref, out_ref, w_ref, wo_ref, sems)
+    gather = RowGather(normed_ref, rows_ref.shape[0], (row_send, row_recv))
+    source = {"section": 0, "shard": 2 * x + c, "rep": 2 * y + lax.rem(z, 2)}
+    from_self = (c == 0) & (z == 2 * x) & (x == lax.rem(z, 2))
+    targets = tuple(
+        {"section": lax.rem(z, 2), "shard": 2 * m + x, "rep": 2 * y + lax.div(z, 2)}
+        for m in range(MICRO)
+    )
+    to_self = tuple(
+        (lax.rem(z, 2) == 0) & (z == 2 * m + x) & (x == lax.div(z, 2)) for m in range(MICRO)
+    )
+    others = [{"section": 1 - c}]
+    for away in (1, 2, 3):
+        others.append({"shard": lax.rem(z + away, 4)})
+        others.append({"section": 1 - c, "shard": lax.rem(z + away, 4)})
+
     barrier = pltpu.get_barrier_semaphore()
-    pl.semaphore_signal(barrier, inc=1, device_id=core, device_id_type=pl.DeviceIdType.MESH)
-    pl.semaphore_signal(barrier, inc=1, device_id=y_other, device_id_type=pl.DeviceIdType.MESH)
+    for device in others + [{"rep": 2 * y + 1 - x}, {"rep": 2 * (1 - y) + x}]:
+        greet(barrier, device)
+
+    @pl.when(jnp.logical_not(from_self))
+    def _():
+        greet(barrier, source)
+
+    guests = sum(jnp.logical_not(own).astype(jnp.int32) for own in to_self)
+    pl.semaphore_wait(barrier, 9 + jnp.where(c == 0, guests, 0))
+
+    def home_copy(m):
+        return mesh_copy(
+            blocks_ref.at[0, m, 0], rows_ref, home_send.at[m], home_recv.at[0], targets[m]
+        )
+
+    def own_copy(m):
+        return pltpu.make_async_copy(blocks_ref.at[0, m, 0], rows_ref, home_send.at[m])
+
+    def param_copy(i):
+        return mesh_copy(
+            flat_ref, params_ref.at[4 * c + z], p_send.at[i], p_recv.at[i], others[i]
+        )
+
+    def param_from(i):
+        cc = c if i % 2 == 1 else 1 - c
+        zz = z if i == 0 else lax.rem(z + 4 - (i + 1) // 2, 4)
+        return mesh_copy(
+            flat_ref, params_ref.at[4 * cc + zz], p_send.at[i], p_recv.at[i], others[i]
+        )
+
+    for m in range(MICRO):
+
+        @pl.when((c == 0) & jnp.logical_not(to_self[m]))
+        def _():
+            home_copy(m).start()
+
+        @pl.when((c == 0) & to_self[m])
+        def _():
+            own_copy(m).start()
+
+    for i in range(7):
+        param_copy(i).start()
+    params_ref[4 * c + z] = flat_ref[...]
+    weights.begin()
+    for unit in range(CHUNKS):
+        weights.first(unit)
+    for unit in range(CHUNKS):
+        weights.arrive(unit, 1)
+
+    for i in range(7):
+        param_from(i).wait_recv()
+
+    @pl.when(jnp.logical_not(from_self))
+    def _():
+        home_copy(0).wait_recv()
+
+    for m in range(MICRO):
+
+        @pl.when((c == 0) & to_self[m])
+        def _():
+            own_copy(m).wait()
+
+    gains = [params_ref[zz].astype(jnp.float32) for zz in range(4)]
+    gain = jnp.concatenate([g[i : i + 1] for g in gains for i in range(3)], axis=1)
+    gather.begin(normal_rows(rows_ref[...].astype(jnp.float32), gain))
+    for unit in range(CHUNKS):
+        weights.arrive(unit, 2)
+    weights.first(CHUNKS)
+    gather.middle()
+    for unit in range(CHUNKS):
+        weights.arrive(unit, 3)
+    for k in (1, 2, 3):
+        weights.arrive(CHUNKS, k)
+    weights.end()
+    gather.end()
+    for i in range(7):
+        param_copy(i).wait_send()
+    for m in range(MICRO):
+
+        @pl.when((c == 0) & jnp.logical_not(to_self[m]))
+        def _():
+            home_copy(m).wait_send()
+
+
+def weight_shapes():
+    return [
+        jax.ShapeDtypeStruct((LOCAL, D), jnp.bfloat16),
+        jax.ShapeDtypeStruct((DI // GROUP, D), jnp.bfloat16),
+    ]
+
+
+def enter_first(in_rows, out_rows, blocks, flat):
+    dma = pltpu.SemaphoreType.DMA
+    block = blocks.shape[-2]
+    anywhere, inside = pl.BlockSpec(memory_space=pl.ANY), pl.BlockSpec(memory_space=pltpu.VMEM)
+    return pl.pallas_call(
+        enter_first_kernel,
+        in_specs=[anywhere] * 3 + [inside],
+        out_specs=[inside] * 5,
+        out_shape=weight_shapes()
+        + [
+            jax.ShapeDtypeStruct((block, D), jnp.bfloat16),
+            jax.ShapeDtypeStruct((GROUP * block, D), jnp.bfloat16),
+            jax.ShapeDtypeStruct((2 * 4,) + flat.shape, jnp.bfloat16),
+        ],
+        scratch_shapes=[dma((3,)), dma((3,)), dma((MICRO,)), dma((1,)), dma((7,)), dma((7,))]
+        + weight_scratch(),
+        compiler_params=pltpu.CompilerParams(
+            collective_id=0, has_side_effects=True, vmem_limit_bytes=VMEM_BYTES
+        ),
+        name="enter_first",
+    )(in_rows, out_rows, blocks, flat)
+
+
+def enter_second_kernel(
+    in_ref, out_ref, theirs_ref, mine_ref, squares_ref, entering_ref, gain_ref, g_ref,
+    w_ref, wo_ref, added_ref, middle_ref, normed_ref, g_all_ref, inv_ref,
+    n_core, n_send, n_across, s_core, s_mine, s_across,
+    row_send, row_recv, g_send, g_recv, n_sem, s_sem, *sems,
+):
+    c, z, y, x = place()
+    weights = WeightGather(1, in_ref, out_ref, w_ref, wo_ref, sems)
+    block = entering_ref.shape[0]
+    gather = RowGather(normed_ref, block, (row_send, row_recv))
+    g_gather = RowGather(g_all_ref, block, (g_send, g_recv))
+    core, x_other = {"section": 1 - c}, {"rep": 2 * y + 1 - x}
+    barrier = pltpu.get_barrier_semaphore()
+    for device in (core, x_other, {"rep": 2 * (1 - y) + x}):
+        greet(barrier, device)
 
     @pl.when(z < 3)
     def _():
-        pl.semaphore_signal(
-            barrier, inc=1, device_id={"shard": z + 1}, device_id_type=pl.DeviceIdType.MESH
-        )
+        greet(barrier, {"shard": z + 1})
 
     @pl.when(z > 0)
     def _():
-        pl.semaphore_signal(
-            barrier, inc=1, device_id={"shard": z - 1}, device_id_type=pl.DeviceIdType.MESH
-        )
+        greet(barrier, {"shard": z - 1})
 
     ends = jnp.where(z == 0, 1, 0) + jnp.where(z == 3, 1, 0)
-    pl.semaphore_wait(barrier, 4 - ends)
-
-    lanes = pl.ds(pl.multiple_of(z * LANE_PART, LANES), LANE_PART)
-    out_rows = pl.ds(pl.multiple_of(z * OUT_PART, 16), OUT_PART)
-
-    def own_pieces(quarter):
-        found = []
-        for at, start, count in weight_pieces(quarter):
-            source = in_ref.at[pl.ds(pl.multiple_of(start, 16), count)]
-            found.append((source, w_ref.at[pl.ds(at, count), lanes]))
-        start = pl.multiple_of(quarter * OUT_PART, 16)
-        found.append((out_ref.at[pl.ds(start, OUT_PART)], wo_ref.at[out_rows]))
-        return found
-
-    def local_copies():
-        return [
-            pltpu.make_async_copy(source, target, local_sem.at[i])
-            for i, (source, target) in enumerate(own_pieces(2 * x + c))
-        ]
-
-    def core_copies():
-        return [
-            pltpu.make_async_remote_copy(
-                src_ref=source, dst_ref=target, send_sem=core_send.at[i],
-                recv_sem=core_recv.at[i], device_id=core, device_id_type=pl.DeviceIdType.MESH,
-            )
-            for i, (source, target) in enumerate(own_pieces(2 * x + 1 - c))
-        ]
-
-    w_ref[LOCAL - 16 :, lanes] = jnp.zeros((16, LANE_PART), w_ref.dtype)
-
-    @pl.when(c == layer)
-    def _():
-        for copy in core_copies():
-            copy.start()
-        for copy in local_copies():
-            copy.start()
-        for copy in local_copies():
-            copy.wait()
-
-    @pl.when(c != layer)
-    def _():
-        for copy in core_copies():
-            copy.wait_recv()
-
-    def slab(unit, shard, side):
-        if unit == CHUNKS:
-            start = shard * OUT_PART + side * (OUT_PART // 2)
-            return wo_ref.at[pl.ds(pl.multiple_of(start, 16), OUT_PART // 2)]
-        start = pl.multiple_of(side * HALF + unit * (HALF // CHUNKS), 16)
-        return w_ref.at[
-            pl.ds(start, HALF // CHUNKS),
-            pl.ds(pl.multiple_of(shard * LANE_PART, LANES), LANE_PART),
-        ]
-
-    def z_copy(unit, shard, step, k):
-        there = z + 1 if step > 0 else z - 1
-        return pltpu.make_async_remote_copy(
-            src_ref=slab(unit, shard, y), dst_ref=slab(unit, shard, y),
-            send_sem=(right_send if step > 0 else left_send).at[unit, k],
-            recv_sem=z_recv.at[unit, shard],
-            device_id={"shard": there}, device_id_type=pl.DeviceIdType.MESH,
-        )
-
-    def y_copy(unit, shard, side):
-        return pltpu.make_async_remote_copy(
-            src_ref=slab(unit, shard, side), dst_ref=slab(unit, shard, side),
-            send_sem=y_send.at[unit, shard], recv_sem=y_recv.at[unit, shard],
-            device_id=y_other, device_id_type=pl.DeviceIdType.MESH,
-        )
-
-    def first(unit):
-        @pl.when(z < 3)
-        def _():
-            z_copy(unit, z, 1, 0).start()
-
-        @pl.when(z > 0)
-        def _():
-            z_copy(unit, z, -1, 0).start()
-
-    def arrive(unit, k):
-        for step in (1, -1):
-            shard = z - k * step
-            there = (shard >= 0) if step > 0 else (shard <= 3)
-            more = (z < 3) if step > 0 else (z > 0)
-
-            @pl.when(there)
-            def _():
-                z_copy(unit, shard, step, 0).wait_recv()
-
-                @pl.when(more)
-                def _():
-                    z_copy(unit, shard, step, k).start()
-
-                y_copy(unit, shard, y).start()
-
+    pl.semaphore_wait(barrier, 5 - ends)
+
+    n_core_copy = mesh_copy(theirs_ref, n_core, n_sem.at[0], n_sem.at[1], core)
+    n_x_copy = mesh_copy(n_send, n_across, n_sem.at[2], n_sem.at[3], x_other)
+    s_core_copy = mesh_copy(squares_ref, s_core, s_sem.at[0], s_sem.at[1], core)
+    s_x_copy = mesh_copy(s_mine, s_across, s_sem.at[2], s_sem.at[3], x_other)
+
+    n_core_copy.start()
+    s_core_copy.start()
+    weights.begin()
     for unit in range(CHUNKS):
-        first(unit)
-    for k in (1, 2):
-        for unit in range(CHUNKS):
-            arrive(unit, k)
-    first(CHUNKS)
+        weights.first(unit)
+
+    def summed(which):
+        rows = rows_at(which * block, block)
+        return mine_ref[rows] + n_core[rows].astype(jnp.float32)
+
+    s_core_copy.wait_recv()
+    s_mine[...] = squares_ref[...] + s_core[...]
+    s_x_copy.start()
+    n_core_copy.wait_recv()
+    n_send[...] = low(summed(1 - x))
+    n_x_copy.start()
     for unit in range(CHUNKS):
-        arrive(unit, 3)
+        weights.arrive(unit, 1)
+
+    s_x_copy.wait_recv()
+    inv_ref[...] = lax.rsqrt((s_mine[...] + s_across[...]) * (1.0 / DI) + EPSILON)
+    n_x_copy.wait_recv()
+    product = summed(x) + n_across[...].astype(jnp.float32)
+    per = block // LANES
+    here = (2 * x + c) * per
+    own_inv = jnp.concatenate(
+        [
+            jnp.broadcast_to(inv_ref[pl.ds(here + i, 1)], (LANES, LANES)).T[:, :1]
+            for i in range(per)
+        ],
+        axis=0,
+    )
+    added = own_inv * product
+    added_ref[...] = added
+    middle = low(entering_ref[...].astype(jnp.float32) + added)
+    middle_ref[...] = middle
+    gather.begin(normal_rows(middle.astype(jnp.float32), gain_ref[...]))
+    g_gather.begin(g_ref[...])
+    for unit in range(CHUNKS):
+        weights.arrive(unit, 2)
+    weights.first(CHUNKS)
+    for unit in range(CHUNKS):
+        weights.arrive(unit, 3)
+    gather.middle()
     for k in (1, 2, 3):
-        arrive(CHUNKS, k)
-
-    for unit in range(UNITS):
-        for away in (1, 2, 3):
-            shard = lax.rem(z + away, 4)
-            y_copy(unit, shard, 1 - y).wait_recv()
-            y_copy(unit, shard, y).wait_send()
-        for step in (1, -1):
-            for k in range(3):
-                shard = z - k * step
-                there = (shard >= 0) if step > 0 else (shard <= 3)
-                more = (z < 3) if step > 0 else (z > 0)
-
-                @pl.when(there & more)
-                def _():
-                    z_copy(unit, shard, step, k).wait_send()
-
-    @pl.when(c == layer)
-    def _():
-        for copy in core_copies():
-            copy.wait_send()
-
-
-def gather_weights(layer, in_rows, out_rows):
+        weights.arrive(CHUNKS, k)
+    g_gather.middle()
+    weights.end()
+    gather.end()
+    g_gather.end()
+    n_core_copy.wait_send()
+    n_x_copy.wait_send()
+    s_core_copy.wait_send()
+    s_x_copy.wait_send()
+
+
+def enter_second(in_rows, out_rows, theirs, mine, squares, entering, gain, g):
     dma = pltpu.SemaphoreType.DMA
+    block = entering.shape[0]
+    anywhere, inside = pl.BlockSpec(memory_space=pl.ANY), pl.BlockSpec(memory_space=pltpu.VMEM)
+    whole = jax.ShapeDtypeStruct((GROUP * block, D), jnp.bfloat16)
     return pl.pallas_call(
-        functools.partial(gather_kernel, layer),
-        in_specs=[pl.BlockSpec(memory_space=pl.ANY)] * 2,
-        out_specs=[pl.BlockSpec(memory_space=pltpu.VMEM)] * 2,
-        out_shape=[
-            jax.ShapeDtypeStruct((LOCAL, D), jnp.bfloat16),
-            jax.ShapeDtypeStruct((DI // GROUP, D), jnp.bfloat16),
+        enter_second_kernel,
+        in_specs=[anywhere] * 2 + [inside] * 6,
+        out_specs=[inside] * 7,
+        out_shape=weight_shapes()
+        + [
+            jax.ShapeDtypeStruct((block, D), jnp.float32),
+            jax.ShapeDtypeStruct((block, D), jnp.bfloat16),
+            whole,
+            whole,
+            jax.ShapeDtypeStruct(squares.shape, jnp.float32),
         ],
         scratch_shapes=[
-            dma((10,)), dma((10,)), dma((10,)),
-            dma((UNITS, 3)), dma((UNITS, 3)), dma((UNITS, 4)), dma((UNITS, 4)), dma((UNITS, 4)),
-        ],
+            pltpu.VMEM(theirs.shape, jnp.bfloat16),
+            pltpu.VMEM(entering.shape, jnp.bfloat16),
+            pltpu.VMEM(entering.shape, jnp.bfloat16),
+            pltpu.VMEM(squares.shape, jnp.float32),
+            pltpu.VMEM(squares.shape, jnp.float32),
+            pltpu.VMEM(squares.shape, jnp.float32),
+            dma((3,)), dma((3,)), dma((3,)), dma((3,)), dma((4,)), dma((4,)),
+        ]
+        + weight_scratch(),
         compiler_params=pltpu.CompilerParams(
-            collective_id=layer, has_side_effects=True, vmem_limit_bytes=VMEM_BYTES
+            collective_id=1, has_side_effects=True, vmem_limit_bytes=VMEM_BYTES
         ),
-        name="gather_weights",
-    )(in_rows, out_rows)
+        name="enter_second",
+    )(in_rows, out_rows, theirs, mine, squares, entering, gain, g)
 
 
 def swap_core(v):
@@ -989,17 +1259,14 @@
     )
 
 
-def rows_at(start, count):
-    return pl.ds(pl.multiple_of(start, 16), count)
-
-
 def finish_kernel(
     grad_ref, out_grad_ref, late_ref, late_out_ref, tiny_ref,
-    all_ref, out_all_ref, tiny_out_ref,
-    y_buf, z_buf, s_buf, zo_buf, so_buf, yo_buf, yo_mine, t1_buf, t1_sum, t2_buf, t2_sum, t3_buf,
+    theirs_ref, mine_ref, entering_ref, incoming_ref, gain_ref,
+    all_ref, out_all_ref, tiny_out_ref, bound_ref,
+    n_core, n_send, n_across, n_done, tiny_mine, y_buf, z_buf, s_buf, zo_buf, so_buf, yo_buf, yo_mine, t1_buf, t1_sum, t2_buf, t2_sum, t3_buf,
     y_send, y_recv, z_send, z_recv, zo_send, zo_recv, yo_sem,
     core_send, core_recv, x_send, x_recv, ya_send, ya_recv, relay_send, relay_recv,
-    xo_send, xo_recv, t_send, t_recv, local_sem,
+    xo_send, xo_recv, t_send, t_recv, n_sem, home_send, home_recv,
 ):
     c, z, y, x = place()
     quarter = 2 * x + c
@@ -1007,18 +1274,30 @@
     diagonal = {"rep": 2 * (1 - y) + 1 - x}
     part = HALF // CHUNKS
 
-    def copy(source, target, send, recv, device):
-        return pltpu.make_async_remote_copy(
-            src_ref=source, dst_ref=target, send_sem=send, recv_sem=recv,
-            device_id=device, device_id_type=pl.DeviceIdType.MESH,
-        )
+    copy = mesh_copy
+
+    block = n_done.shape[0]
+    home = {"section": 0, "shard": quarter, "rep": 2 * y + lax.rem(z, 2)}
+    at_home = (c == 0) & (z == quarter) & (x == lax.rem(z, 2))
+    guests = tuple(
+        {"section": lax.rem(z, 2), "shard": 2 * m + x, "rep": 2 * y + lax.div(z, 2)}
+        for m in range(MICRO)
+    )
 
     barrier = pltpu.get_barrier_semaphore()
     reps = (x_other, y_other, diagonal)
     shards = tuple({"shard": lax.rem(z + away, 4)} for away in (1, 2, 3))
+
     for device in (core,) + reps + shards:
-        pl.semaphore_signal(barrier, inc=1, device_id=device, device_id_type=pl.DeviceIdType.MESH)
-    pl.semaphore_wait(barrier, 7)
+        greet(barrier, device)
+    for m in range(MICRO):
+        own = (lax.rem(z, 2) == 0) & (z == 2 * m + x) & (x == lax.div(z, 2))
+
+        @pl.when((c == 0) & jnp.logical_not(own))
+        def _():
+            greet(barrier, guests[m])
+
+    pl.semaphore_wait(barrier, 8 - at_home.astype(jnp.int32))
 
     orders = ((3, 2, 1, 0), (3, 0, 2, 1), (0, 3, 1, 2), (0, 1, 2, 3))
 
@@ -1117,7 +1396,7 @@
         )
 
     def t1_copy():
-        return copy(tiny_ref.at[1 - c], t1_buf, t_send.at[0], t_recv.at[0], core)
+        return copy(tiny_mine.at[1 - c], t1_buf, t_send.at[0], t_recv.at[0], core)
 
     def t2_copy(away):
         return copy(
@@ -1131,7 +1410,16 @@
     def yo_copy():
         return copy(yo_mine, yo_buf, yo_sem.at[0], yo_sem.at[1], y_other)
 
-    t1_copy().start()
+    def n_core_copy():
+        return copy(theirs_ref, n_core, n_sem.at[0], n_sem.at[1], core)
+
+    def n_x_copy():
+        return copy(n_send, n_across, n_sem.at[2], n_sem.at[3], x_other)
+
+    def home_copy(m):
+        return copy(n_done, bound_ref.at[m], home_send.at[0], home_recv.at[m], home)
+
+    n_core_copy().start()
     for i in range(4):
         shard = shard_at(i)
         for ch in range(CHUNKS):
@@ -1189,70 +1477,90 @@
         z_copy(shard, ch).start()
 
     send_out(0)
+
+    def summed(which):
+        rows = rows_at(which * block, block)
+        return mine_ref[rows] + n_core[rows].astype(jnp.float32)
+
+    n_core_copy().wait_recv()
+    n_send[...] = low(summed(1 - x))
+    n_x_copy().start()
+    for ch in range(CHUNKS):
+        send_in(0, ch)
     send_out(1)
 
-    t1_copy().wait_recv()
-    t1_sum[...] = tiny_ref[c] + t1_buf[...]
-    for away in (1, 2, 3):
-        t2_copy(away).start()
+    n_x_copy().wait_recv()
+    normed_grad = summed(x) + n_across[...].astype(jnp.float32)
+    entering = entering_ref[...].astype(jnp.float32)
+    inv = lax.rsqrt(jnp.mean(entering * entering, axis=-1, keepdims=True) + EPSILON)
+    hat = entering * inv
+    hat_grad = normed_grad * gain_ref[...]
+    mean = jnp.mean(hat_grad * hat, axis=-1, keepdims=True)
+    n_done[...] = low(incoming_ref[...].astype(jnp.float32) + inv * (hat_grad - hat * mean))
+    for m in range(MICRO):
+        there = lax.div(z, 2) == m
+
+        @pl.when(there & jnp.logical_not(at_home))
+        def _():
+            home_copy(m).start()
+
+        @pl.when(there & at_home)
+        def _():
+            bound_ref[m] = n_done[...]
+
+    norm_grad = jnp.sum(normed_grad * hat, axis=0, keepdims=True)
+    tiny_mine[...] = tiny_ref[...]
+    for zz in range(4):
+        for row in range(3):
+            at = (3 * zz + row) * LANES
+            tiny_mine[0, zz, row : row + 1] += norm_grad[:, at : at + LANES]
+    t1_copy().start()
 
     @pl.when(c == 1)
     def _():
         for ch in range(CHUNKS):
             late_copy(ch).wait_recv()
             for who in range(CORES):
-                spread(who, ch)
+                x_copy(who, ch).start()
         late_out_copy().wait_recv()
         for who in range(CORES):
             xo_copy(who).start()
 
     for ch in range(CHUNKS):
-        send_in(0, ch)
+        send_in(1, ch)
     send_out(2)
+
+    t1_copy().wait_recv()
+    t1_sum[...] = tiny_mine[c] + t1_buf[...]
+    for away in (1, 2, 3):
+        t2_copy(away).start()
+    for ch in range(CHUNKS):
+        send_in(2, ch)
+
+    @pl.when(c == 1)
+    def _():
+        for ch in range(CHUNKS):
+            for who in range(CORES):
+                ya_copy(who, ch).start()
+
+    yo_mine[...] = low(own_out(z))
+
+    @pl.when(z > 0)
+    def _():
+        zo_wait(z)
+        yo_mine[...] = low(own_out(z) + zo_buf[z].astype(jnp.float32))
+
+    @pl.when(z < 3)
+    def _():
+        zo_wait(4)
+        yo_mine[...] = low(yo_mine[...].astype(jnp.float32) + zo_buf[4].astype(jnp.float32))
+
+    yo_copy().start()
     for away in (1, 2, 3):
         t2_copy(away).wait_recv()
     t2_sum[...] = (t1_sum[z] + t2_buf[0]) + (t2_buf[1] + t2_buf[2])
     for i in range(3):
         t3_copy(i).start()
-    for ch in range(CHUNKS):
-        send_in(1, ch)
-
-    yo_mine[...] = low(own_out(z))
-
-    @pl.when(z > 0)
-    def _():
-        zo_wait(z)
-        yo_mine[...] = low(own_out(z) + zo_buf[z].astype(jnp.float32))
-
-    @pl.when(z < 3)
-    def _():
-        zo_wait(4)
-        yo_mine[...] = low(yo_mine[...].astype(jnp.float32) + zo_buf[4].astype(jnp.float32))
-
-    yo_copy().start()
-    for ch in range(CHUNKS):
-        send_in(2, ch)
-    for i in range(3):
-        t3_copy(i).wait_recv()
-    tiny_out_ref[...] = (t2_sum[...] + t3_buf[0]) + (t3_buf[1] + t3_buf[2])
-
-    yo_copy().wait()
-    total = low(yo_mine[...].astype(jnp.float32) + yo_buf[...].astype(jnp.float32))
-
-    @pl.when(c == 0)
-    def _():
-        out_part(quarter)[...] = total
-
-    @pl.when(c == 1)
-    def _():
-        yo_mine[...] = total
-        first_out_copy().start()
-
-    @pl.when(c == 0)
-    def _():
-        first_out_copy().wait_recv()
-        for who in range(CORES):
-            xo_copy(who).start()
 
     for ch in range(CHUNKS):
         span = pl.ds(ch * part, part)
@@ -1286,6 +1594,28 @@
             spread(0, ch)
             first_copy(ch).wait_recv()
             spread(1, ch)
+
+    yo_copy().wait()
+    total = low(yo_mine[...].astype(jnp.float32) + yo_buf[...].astype(jnp.float32))
+
+    @pl.when(c == 0)
+    def _():
+        out_part(quarter)[...] = total
+
+    @pl.when(c == 1)
+    def _():
+        yo_mine[...] = total
+        first_out_copy().start()
+
+    @pl.when(c == 0)
+    def _():
+        first_out_copy().wait_recv()
+        for who in range(CORES):
+            xo_copy(who).start()
+
+    for i in range(3):
+        t3_copy(i).wait_recv()
+    tiny_out_ref[...] = (t2_sum[...] + t3_buf[0]) + (t3_buf[1] + t3_buf[2])
 
     for ch in range(CHUNKS):
         for who in range(CORES):
@@ -1298,6 +1628,20 @@
             relay_copy(who, ch).wait()
     for who in range(CORES):
         xo_copy(who).wait()
+    n_core_copy().wait_send()
+    n_x_copy().wait_send()
+
+    @pl.when(jnp.logical_not(at_home))
+    def _():
+        home_copy(0).wait_send()
+
+    for m in range(MICRO):
+        own = (lax.rem(z, 2) == 0) & (z == 2 * m + x) & (x == lax.div(z, 2))
+
+        @pl.when((c == 0) & jnp.logical_not(own))
+        def _():
+            home_copy(m).wait_recv()
+
     t1_copy().wait_send()
     for away in (1, 2, 3):
         t2_copy(away).wait_send()
@@ -1323,7 +1667,7 @@
         first_out_copy().wait_send()
 
 
-def finish_sums(grad, out_grad, late, late_out, tiny):
+def finish_sums(grad, out_grad, late, late_out, tiny, theirs, mine, entering, incoming, gain):
     dma = pltpu.SemaphoreType.DMA
     span = (HALF, LANE_PART)
     out = (OUT_PART, D)
@@ -1331,14 +1675,20 @@
     two = (CORES, CHUNKS)
     return pl.pallas_call(
         finish_kernel,
-        in_specs=[pl.BlockSpec(memory_space=pltpu.VMEM)] * 5,
-        out_specs=[pl.BlockSpec(memory_space=pltpu.VMEM)] * 3,
+        in_specs=[pl.BlockSpec(memory_space=pltpu.VMEM)] * 10,
+        out_specs=[pl.BlockSpec(memory_space=pltpu.VMEM)] * 4,
         out_shape=[
             jax.ShapeDtypeStruct((GROUP, LOCAL, LANE_PART), jnp.bfloat16),
             jax.ShapeDtypeStruct((DI // GROUP, D), jnp.bfloat16),
             jax.ShapeDtypeStruct(small, jnp.float32),
+            jax.ShapeDtypeStruct((MICRO,) + entering.shape, jnp.bfloat16),
         ],
         scratch_shapes=[
+            pltpu.VMEM(theirs.shape, jnp.bfloat16),
+            pltpu.VMEM(entering.shape, jnp.bfloat16),
+            pltpu.VMEM(entering.shape, jnp.bfloat16),
+            pltpu.VMEM(entering.shape, jnp.bfloat16),
+            pltpu.VMEM(tiny.shape, jnp.float32),
             pltpu.VMEM((4,) + span, jnp.bfloat16),
             pltpu.VMEM((5,) + span, jnp.bfloat16),
             pltpu.VMEM((4,) + span, jnp.bfloat16),
@@ -1355,13 +1705,13 @@
             dma((4,)), dma((5,)), dma((2,)),
             dma((CHUNKS + 1,)), dma((CHUNKS + 1,)),
             dma(two), dma(two), dma(two), dma(two), dma(two), dma(two),
-            dma((CORES,)), dma((CORES,)), dma((7,)), dma((7,)), dma((1,)),
+            dma((CORES,)), dma((CORES,)), dma((7,)), dma((7,)), dma((4,)), dma((1,)), dma((MICRO,)),
         ],
         compiler_params=pltpu.CompilerParams(
             collective_id=2, has_side_effects=True, vmem_limit_bytes=VMEM_BYTES
         ),
         name="finish_sums",
-    )(grad, out_grad, late, late_out, tiny)
+    )(grad, out_grad, late, late_out, tiny, theirs, mine, entering, incoming, gain)
 
 
 def assemble_kernel(part_ref, shared_ref, total_ref):
@@ -1439,16 +1789,19 @@
             ways.append(lax.ppermute(value, axes, pairs))
         return ways
 
+    params = (norm_gain, conv_weight, conv_bias, dt_bias, a_log, d_skip, out_gain)
+    count = sum(p.size for p in params)
+    filler = -count % LANES
+    flat = jnp.concatenate(
+        [p.reshape(-1) for p in params] + [jnp.zeros((-count % (16 * LANES),), jnp.bfloat16)]
+    )
     in_rows = jnp.swapaxes(in_weight[0], 0, 1)
-    w_in0, w_out0 = gather_weights(0, in_rows, out_weight[0])
-
-    arrive_a = lax.ppermute(
-        lax.dynamic_index_in_dim(boundary_in[0, :, 0], c, 0, False), axes, straight
-    )
-    arrive_b = lax.ppermute(
-        lax.dynamic_index_in_dim(boundary_in[0, :, 0], 1 - c, 0, False), axes, crossed
-    )
-    source = jnp.where(z < 2, arrive_a, arrive_b)
+    w_in0, w_out0, source, normed0, flat = enter_first(
+        in_rows, out_weight[0], boundary_in, flat.reshape((-1, LANES))
+    )
+    late_in = after(boundary_in, source)[0, :, 0]
+    arrive_a = lax.ppermute(lax.dynamic_index_in_dim(late_in, c, 0, False), axes, straight)
+    arrive_b = lax.ppermute(lax.dynamic_index_in_dim(late_in, 1 - c, 0, False), axes, crossed)
     cotangent = jnp.where(z < 2, arrive_b, arrive_a)
 
     order = jnp.stack([lengths[:, 0], seq_order[:, 0]])
@@ -1471,14 +1824,7 @@
     marks = jnp.stack(columns + [jnp.zeros((rows,), jnp.float32)] * 2, axis=1)
     seg_row = segment.astype(jnp.float32)[None]
 
-    params = (norm_gain, conv_weight, conv_bias, dt_bias, a_log, d_skip, out_gain)
-    count = sum(p.size for p in params)
-    filler = -count % LANES
-    flat = jnp.concatenate([p.reshape(-1) for p in params] + [jnp.zeros((filler,), jnp.bfloat16)])
-    flat = ordered(c == 0, flat, swap_core(flat))
-    flat = ordered(z % 2 == 0, flat, swap_z(flat, 1))
-    flat = ordered(z // 2 == 0, flat, swap_z(flat, 2))
-    flat = flat.reshape((4, CORES, count + filler)).astype(jnp.float32)
+    flat = flat.reshape((CORES, 4, -1)).astype(jnp.float32)
 
     given = jnp.arange(SHARED - 2 * N + 16)[:, None]
     local = jnp.arange(LANES)[None, :]
@@ -1489,7 +1835,7 @@
         found = []
         at = 0
         for p in params:
-            part = flat[:, layer, at : at + p.size].reshape((4,) + p.shape[1:])
+            part = flat[layer, :, at : at + p.size].reshape((4,) + p.shape[1:])
             at += p.size
             found.append(jnp.moveaxis(part, 0, -2).reshape(p.shape[1:-1] + (-1,)))
         gain, conv_w, conv_b, dt_b, log_a, skip, gain_out = found
@@ -1528,60 +1874,44 @@
             whole = lax.dynamic_update_slice_in_dim(whole, part, at * count, 0)
         return whole
 
-    def group_product(left, product):
+    def group_parts(left, product):
         blocks = left.reshape((2, 2, block) + left.shape[1:])
         theirs = lax.dynamic_index_in_dim(blocks, 1 - c, 1, False)
-        theirs = product(theirs.reshape((2 * block,) + left.shape[1:]))
-        received = swap_core(low(theirs)).reshape((2, block, -1))
+        theirs = low(product(theirs.reshape((2 * block,) + left.shape[1:])))
         mine = lax.dynamic_index_in_dim(blocks, c, 1, False)
-
-        def summed(at):
-            part = product(lax.dynamic_index_in_dim(mine, at, 0, False))
-            return part + lax.dynamic_index_in_dim(received, at, 0, False).astype(jnp.float32)
-
-        across = swap_x(low(summed(1 - x)))
-        return summed(x) + across.astype(jnp.float32)
+        return theirs, product(mine.reshape((2 * block,) + left.shape[1:]))
+
+    def group_sum(parts):
+        theirs, mine = parts
+        both = (mine + swap_core(theirs).astype(jnp.float32)).reshape((2, block, -1))
+        across = swap_x(low(lax.dynamic_index_in_dim(both, 1 - x, 0, False)))
+        return lax.dynamic_index_in_dim(both, x, 0, False) + across.astype(jnp.float32)
 
     def own(v):
         return lax.dynamic_slice_in_dim(v, (2 * x + c) * block, block, 0)
 
-    def forward(layer, entering, w_in, w_out):
-        gain = small[layer]["norm"]
-        inv = lax.rsqrt(jnp.mean(entering * entering, axis=-1, keepdims=True) + EPSILON)
-        normed = group_rows(low(entering * inv * gain))
+    def row_sums(v):
+        v = v + swap_core(v)
+        return v + swap_x(v)
+
+    def forward(layer, normed, w_in):
         projected = low(mm(normed, w_in, 1, 1))
         gg, squares, mixer, starts = mixer_forward(projected, marks, seg_row, small[layer])
-        half = squares.reshape((rows // LANES, LANES))
-        half = half + swap_core(half)
-        half = half + swap_x(half)
-        out_inv = lax.rsqrt(half / DI + EPSILON).reshape((rows, 1))
-        product = group_product(gg, lambda v: mm(v, w_out))
-        added = own(out_inv) * product
-        return entering + added, (entering, inv, normed, projected, mixer, starts, out_inv, added)
-
-    def backward(layer, kept, incoming, w_in, w_out):
-        entering, inv, normed, projected, mixer, starts, out_inv, added = kept
-        gain = small[layer]["norm"]
-        incoming32 = incoming.astype(jnp.float32)
-        dots = jnp.sum(incoming32 * added, axis=1).reshape((-1, LANES))
-        dots = group_rows(dots).reshape((rows, 1))
-        g = group_rows(incoming)
-        og = mm(g, w_out, 1, 1)
-        per_row = jnp.concatenate([out_inv, dots], axis=1)
+        return gg, squares.reshape((rows // LANES, LANES)), (normed, projected, mixer, starts)
+
+    def inverse(sums):
+        return lax.rsqrt(sums / DI + EPSILON)
+
+    def backward(layer, kept, g, og, per_row):
+        normed, projected, mixer, starts = kept
         pg, outgoing, wide, conv, head = mixer_backward(
             projected, marks, seg_row, small[layer], mixer, starts, og, per_row, DI
         )
         out_grad = low(mm(outgoing, g, 0, 0))
-        normed_grad = group_product(pg, lambda v: mm(v, w_in))
         in_grad = low(mm(pg, normed, 0, 0))
-        hat = entering * inv
-        hat_grad = normed_grad * gain
-        mean = jnp.mean(hat_grad * hat, axis=-1, keepdims=True)
-        source_grad = incoming32 + inv * (hat_grad - hat * mean)
-        norm_grad = jnp.sum(normed_grad * hat, axis=0)
         taps = jnp.concatenate([place_last(conv[:5, :width], quarter), conv[:5, width:]], axis=1)
         tiny = [
-            norm_grad[None],
+            jnp.zeros((1, D), jnp.float32),
             taps[:KW],
             taps[KW:],
             place_last(head[0:1, :heads], quarter),
@@ -1591,7 +1921,7 @@
         ]
         tiny = [jnp.moveaxis(t.reshape((t.shape[0], 4, -1)), 1, 0).reshape((4, -1)) for t in tiny]
         tiny = jnp.concatenate(tiny + [jnp.zeros((4, filler), jnp.float32)], axis=1)
-        return source_grad, in_grad, out_grad, tiny
+        return pg, in_grad, out_grad, tiny
 
     def scatter_in(grad):
         parts = grad.reshape((2, HALF, D))
@@ -1607,27 +1937,54 @@
         )
         return low(part.astype(jnp.float32) + swap_y(part).astype(jnp.float32))
 
-    middle, kept0 = forward(0, source.astype(jnp.float32), w_in0, w_out0)
-    in_rows_late = after(in_rows, kept0[4])
-    w_in1, w_out1 = gather_weights(1, in_rows_late, out_weight[0])
-    result, kept1 = forward(1, low(middle).astype(jnp.float32), w_in1, w_out1)
-    result_ways = go_back(low(result), 1)
-    middle_grad, in_grad1, out_grad1, tiny1 = backward(1, kept1, cotangent, w_in1, w_out1)
+    gg0, squares0, kept0 = forward(0, normed0, w_in0)
+    theirs, mine = group_parts(gg0, lambda v: mm(v, w_out0))
+    w_in1, w_out1, added0, middle, normed1, g1, out_inv0 = enter_second(
+        in_rows, out_weight[0], theirs, mine, squares0, source, small[1]["norm"][None], cotangent
+    )
+    out_inv0 = out_inv0.reshape((rows, 1))
+    og1 = mm(g1, w_out1, 1, 1)
+    middle32 = middle.astype(jnp.float32)
+    gg1, squares1, kept1 = forward(1, normed1, w_in1)
+    dots1 = jnp.sum(gg1.astype(jnp.float32) * og1, axis=1).reshape((rows // LANES, LANES))
+    sums1 = row_sums(jnp.stack([squares1, dots1]))
+    out_inv1 = inverse(sums1[0]).reshape((rows, 1))
+    per_row1 = jnp.concatenate([out_inv1, out_inv1 * sums1[1].reshape((rows, 1))], axis=1)
+    parts1 = group_parts(gg1, lambda v: mm(v, w_out1))
+    pg1, in_grad1, out_grad1, tiny1 = backward(1, kept1, g1, og1, per_row1)
+    result_ways = go_back(low(middle32 + own(out_inv1) * group_sum(parts1)), 1)
+
+    normed_grad = group_sum(group_parts(pg1, lambda v: mm(v, w_in1)))
+    inv = lax.rsqrt(jnp.mean(middle32 * middle32, axis=-1, keepdims=True) + EPSILON)
+    hat = middle32 * inv
+    hat_grad = normed_grad * small[1]["norm"]
+    mean = jnp.mean(hat_grad * hat, axis=-1, keepdims=True)
+    middle_grad = low(cotangent.astype(jnp.float32) + inv * (hat_grad - hat * mean))
+    norm_grad1 = jnp.sum(normed_grad * hat, axis=0).reshape((4, LANE_PART))
+    tiny1 = tiny1.at[:, :LANE_PART].add(norm_grad1)
     out_part1 = scatter_out(out_grad1)
     in_part1 = scatter_in(in_grad1)
-    entry_grad, in_grad0, out_grad0, tiny0 = backward(0, kept0, low(middle_grad), w_in0, w_out0)
-    grad_ways = go_back(low(entry_grad), 0)
-
-    boundary = jnp.stack(
-        [jnp.where(c == 0, grad_ways[m], result_ways[m]) for m in range(MICRO)]
-    ).astype(jnp.float32)[None, :, None]
-
+
+    dots0 = jnp.sum(middle_grad.astype(jnp.float32) * added0, axis=1).reshape((-1, LANES))
+    dots0 = group_rows(dots0).reshape((rows, 1))
+    g0 = group_rows(middle_grad)
+    og0 = mm(g0, w_out0, 1, 1)
+    per_row0 = jnp.concatenate([out_inv0, dots0], axis=1)
+    pg0, in_grad0, out_grad0, tiny0 = backward(0, kept0, g0, og0, per_row0)
+    theirs, mine = group_parts(pg0, lambda v: mm(v, w_in0))
     tiny = jnp.stack([tiny0, tiny1]).reshape((CORES, 4, -1, LANES))
-    in_grad0 = after(in_grad0, entry_grad)
-    in_all, out_all, tiny = finish_sums(in_grad0, out_grad0, in_part1, out_part1, tiny)
+    in_all, out_all, tiny, entry_grads = finish_sums(
+        in_grad0, out_grad0, in_part1, out_part1, tiny,
+        theirs, mine, source, middle_grad, small[0]["norm"][None],
+    )
     in_total = jnp.swapaxes(assemble_rows(in_all), 0, 1)[None]
     out_total = out_all.astype(jnp.float32)[None]
     tiny = tiny.reshape(-1)
+
+    boundary = jnp.stack(
+        [jnp.where(c == 0, entry_grads[m], result_ways[m]) for m in range(MICRO)]
+    ).astype(jnp.float32)[None, :, None]
+
     totals = []
     at = 0
     for p in params:

time: 930 us -> 810 us (0.87)
  waiting for transfers between devices: 150 us -> 46.8 us
  starting transfers between devices: 69.4 us -> 27.5 us
  Pallas kernels: 471 us -> 509 us
  matrix products: 115 us -> 102 us
    ppermute x13 -> x6, waiting for transfers between devices: 95.3 us -> 34.9 us  [swap_x(): return lax.ppermute(v, 'rep', [(i, i ^ 1) for i in range(4)])]
    pallas_call x2, Pallas kernels: 192 us -> 212 us  [the longest x1 117 us: enter_second(): pl.pallas_call(enter_second_kernel, in_specs=[anywhere] * 2 + [inside] *...]
    pallas_call x1, Pallas kernels: 168 us -> 186 us  [finish_sums(): pl.pallas_call(finish_kernel, in_specs=[pl.BlockSpec(memory_space=pltpu.V...]
    ppermute x4 -> x2, waiting for transfers between devices: 18.2 us -> 0.01 us  [go_back(): ways.append(lax.ppermute(value, axes, pairs))]
    ppermute x4 -> x2, starting transfers between devices: 22.4 us -> 8.99 us  [go_back(): ways.append(lax.ppermute(value, axes, pairs))]
    dot_general x20 -> x16, matrix products: 115 us -> 102 us  [mm(): lax.dot_general(a, b, (((da,), (db,)), ((), ())), preferred_element_type=...]
    dynamic_update_slice x22 -> x8, local copies, waits for them, and re-layouts: 17.1 us -> 5.01 us  [group_rows(): whole = lax.dynamic_update_slice_in_dim(whole, part, at * count, 0)]
    ppermute x2, waiting for transfers between devices: 20.9 us -> 10.2 us  [swap_y(): return lax.ppermute(v, 'rep', [(i, i ^ 2) for i in range(4)])]
  transfers between devices with their start and end apart: 44 -> 21, of which waited for: 17 -> 7; matrix products, arithmetic and copies ran while one was open for 16% -> 22% of each run, Pallas kernels for 28% -> 47%
where the time goes in v2:
time: 810 us; the launch traced here: 801 us
  Pallas kernels  509 us (63%)
  matrix products  102 us (13%)
  local copies, waits for them, and re-layouts  64 us (8%)
  waiting for transfers between devices  46.8 us (6%)
  other arithmetic  35.5 us (4%)
  starting transfers between devices  27.5 us (3%)
  between operations  15.3 us (2%)
    pallas_call x1, Pallas kernels, finish_sums(): pl.pallas_call(finish_kernel, in_specs=[pl.BlockSpec(memory_space=pltpu.V...  186 us
    pallas_call x1, Pallas kernels, enter_second(): pl.pallas_call(enter_second_kernel, in_specs=[anywhere] * 2 + [inside] *...  117 us
    dot_general x16, matrix products, mm(): lax.dot_general(a, b, (((da,), (db,)), ((), ())), preferred_element_type=...  102 us
    pallas_call x1, Pallas kernels, enter_first(): pl.pallas_call(enter_first_kernel, in_specs=[anywhere] * 3 + [inside], ou...  95.9 us
    pallas_call x2, Pallas kernels, mixer_backward(): pl.pallas_call(functools.partial(backward_kernel, width, whole_width), gr...  70 us
    ppermute x6, waiting for transfers between devices, swap_x(): return lax.ppermute(v, 'rep', [(i, i ^ 1) for i in range(4)])  34.9 us
    pallas_call x2, Pallas kernels, mixer_forward(): pl.pallas_call(functools.partial(forward_kernel, width), grid=(chunks,),...  31.7 us
  transfers between devices with their start and end apart: 21, of which 7 were waited for; matrix products, arithmetic and copies ran while one was open for 22% of the time, Pallas kernels for 47%

profile of v2, /device:TPU:16, one launch (start us, length us, event | category | flops | bytes accessed | tf_op | source)
XLA Modules:
  0.0 800.6 jit_solution(14631467003790402014)
XLA Ops:
  15.6 95.9 %enter_first.1 = (bf16[1856,1536]{1,0:T(8,128)(2,1)}, bf16[768,1536]{1,0:T(8,128)(2,1)}, bf16[256,1536]{1,0:T(8,128)(2,1)}, bf16[1024,1536]{1,0:T(8,128)(2,1)}, bf16[8,48,128]{2,1,0:T(8,128)(2,1)}) custom-call(bf16[6448,384]{1,0:T(8,128)(2,1)} %bitcast.184, bf16[768,1536]{1,0:T(8,128)(2,1)} %bitcast.187, bf16[1,2,1,256,1536]{4,3,2,1,0:T(8,128)(2,1)} %blocks_ref.1, ...), custom_call_target="tpu_custom_call" | custom-call | tf_op jit(solution)/shard_map/enter_first/pallas_call | solution.py:1078
  111.7 5.1 collective-permute-start.1
  116.8 4.7 collective-permute-start.2
  144.3 11.3 %convolution_convert_fusion.3.proj_ref.rim_ref = bf16[1024,1856]{1,0:T(8,128)(2,1)} fusion(bf16[1024,1536]{1,0:T(8,128)(2,1)} %get-tuple-element.57, bf16[1856,1536]{1,0:T(8,128)(2,1)} %get-tuple-element.58), kind=kOutput, calls=%fused_computation.5 | convolution fusion | flops 5840371712 | bytes 12648448 | tf_op jit(solution)/shard_map/dot_general | solution.py:424
  160.4 15.8 %mixer_forward.2 = (bf16[1024,768]{1,0:T(8,128)(2,1)}, f32[1024,1]{1,0:T(8,128)}, f32[1024,768]{1,0:T(8,128)}, f32[8,128,768]{2,1,0:T(8,128)}) custom-call(bf16[1024,1856]{1,0:T(8,128)(2,1)} %convolution_convert_fusion.3.proj_ref.rim_ref, f32[1024,8]{1,0:T(8,128)} %copy.116.marks_ref, f32[1,1024]{1,0:T(1,128)} %bitcast.216, ...), custom_call_target="tpu_custom_call" | custom-call | tf_op jit(solution)/shard_map/mixer_forward/pallas_call | solution.py:676
  180.7 4.6 convolution_convert_fusion.9.theirs_ref
  189.4 116.5 %enter_second.1 = (bf16[1856,1536]{1,0:T(8,128)(2,1)}, bf16[768,1536]{1,0:T(8,128)(2,1)}, f32[256,1536]{1,0:T(8,128)}, bf16[256,1536]{1,0:T(8,128)(2,1)}, bf16[1...) custom-call(bf16[6448,384]{1,0:T(8,128)(2,1)} %bitcast.185, bf16[768,1536]{1,0:T(8,128)(2,1)} %bitcast.188, ...), custom_call_target="tpu_custom_call" | custom-call | tf_op jit(solution)/shard_map/enter_second/pallas_call | solution.py:1190
  305.9 11.3 %convolution_convert_fusion.2.proj_ref.rim_ref = bf16[1024,1856]{1,0:T(8,128)(2,1)} fusion(bf16[1024,1536]{1,0:T(8,128)(2,1)} %get-tuple-element.68, bf16[1856,1536]{1,0:T(8,128)(2,1)} %get-tuple-element.69), kind=kOutput, calls=%fused_computation.4 | convolution fusion | flops 5840371712 | bytes 12648448 | tf_op jit(solution)/shard_map/dot_general | solution.py:424
  317.2 15.9 %mixer_forward.3 = (bf16[1024,768]{1,0:T(8,128)(2,1)}, f32[1024,1]{1,0:T(8,128)}, f32[1024,768]{1,0:T(8,128)}, f32[8,128,768]{2,1,0:T(8,128)}) custom-call(bf16[1024,1856]{1,0:T(8,128)(2,1)} %convolution_convert_fusion.2.proj_ref.rim_ref, f32[1024,8]{1,0:T(8,128)} %copy.116.marks_ref, f32[1,1024]{1,0:T(1,128)} %bitcast.217, ...), custom_call_target="tpu_custom_call" | custom-call | tf_op jit(solution)/shard_map/mixer_forward/pallas_call | solution.py:676
  338.1 4.4 multiply_reduce_fusion
  344.1 3.6 collective-permute-done.4
  348.8 35.0 %mixer_backward.2 = (bf16[1024,1856]{1,0:T(8,128)(2,1)}, bf16[1024,768]{1,0:T(8,128)(2,1)}, f32[8,768]{1,0:T(8,128)}, f32[8,1024]{1,0:T(8,128)}, f32[8,128]{1,0:T(8,128)}) custom-call(bf16[1024,1856]{1,0:T(8,128)(2,1)} %convolution_convert_fusion.2.proj_ref.rim_ref, bf16[1024,1856]{1,0:T(8,128)(2,1)} %convolution_convert_fusion.2.proj_ref.rim_ref, ...), custom_call_target="tpu_custom_call" | custom-call | tf_op jit(solution)/shard_map/mixer_backward/pallas_call | solution.py:715
  386.3 7.9 convolution_convert_fusion.8
  394.2 8.1 %convolution_convert_fusion = bf16[1856,1536]{1,0:T(8,128)(2,1)} fusion(bf16[1024,1856]{1,0:T(8,128)(2,1)S(1)} %copy-done.7, bf16[1024,1536]{1,0:T(8,128)(2,1)S(1)} %copy-done.31), kind=kOutput, calls=%fused_computation | convolution fusion | flops 5841321984 | bytes 12648448 | tf_op jit(solution)/shard_map/dot_general | solution.py:424
  402.6 6.5 convolution_convert_fusion.4
  409.6 3.6 dynamic-slice_bitcast_fusion
  415.6 7.0 convolution_add_fusion.1
  434.3 10.1 %collective-permute-done.6 = bf16[256,1536]{1,0:T(8,128)(2,1)S(1)} collective-permute-done((bf16[256,1536]{1,0:T(8,128)(2,1)}, bf16[256,1536]{1,0:T(8,128)(2,1)S(1)}, u32[]{:S(2)}, u32[]{:S(2)}) %collective-permute-start.6) | collective-permute-done | bytes 786464 | tf_op jit(solution)/shard_map/ppermute | solution.py:1224
  446.4 14.1 %collective-permute-done.16 = bf16[256,1536]{1,0:T(8,128)(2,1)S(1)} collective-permute-done((bf16[256,1536]{1,0:T(8,128)(2,1)}, bf16[256,1536]{1,0:T(8,128)(2,1)S(1)}, u32[]{:S(2)}, u32[]{:S(2)}) %collective-permute-start.16) | collective-permute-done | bytes 786464 | tf_op jit(solution)/shard_map/ppermute | solution.py:1224
  461.4 4.1 multiply_reduce_fusion.1
  474.2 7.4 collective-permute-start.18
  482.7 3.4 fusion
  486.1 7.1 collective-permute-done.8
  499.4 6.2 fusion.54.og_ref
  505.6 35.0 %mixer_backward.3 = (bf16[1024,1856]{1,0:T(8,128)(2,1)}, bf16[1024,768]{1,0:T(8,128)(2,1)}, f32[8,768]{1,0:T(8,128)}, f32[8,1024]{1,0:T(8,128)}, f32[8,128]{1,0:T(8,128)}) custom-call(bf16[1024,1856]{1,0:T(8,128)(2,1)} %convolution_convert_fusion.3.proj_ref.rim_ref, bf16[1024,1856]{1,0:T(8,128)(2,1)} %convolution_convert_fusion.3.proj_ref.rim_ref, ...), custom_call_target="tpu_custom_call" | custom-call | tf_op jit(solution)/shard_map/mixer_backward/pallas_call | solution.py:715
  549.2 7.9 fusion.55.mine_ref
  557.1 4.6 convolution_convert_fusion.7.theirs_ref
  561.7 8.1 %convolution_convert_fusion.1.grad_ref = bf16[1856,1536]{1,0:T(8,128)(2,1)} fusion(bf16[1024,1856]{1,0:T(8,128)(2,1)S(1)} %copy-done.6, bf16[1024,1536]{1,0:T(8,128)(2,1)S(1)} %copy-done.29), kind=kOutput, calls=%fused_computation.1 | convolution fusion | flops 5841321984 | bytes 12648448 | tf_op jit(solution)/shard_map/dot_general | solution.py:424
  569.8 5.8 convolution_convert_fusion.5.out_grad_ref
  575.6 10.2 %collective-permute-done.14 = bf16[192,1536]{1,0:T(8,128)(2,1)S(1)} collective-permute-done((bf16[192,1536]{1,0:T(8,128)(2,1)}, bf16[192,1536]{1,0:T(8,128)(2,1)S(1)}, u32[]{:S(2)}, u32[]{:S(2)}) %collective-permute-start.14) | collective-permute-done | bytes 589856 | tf_op jit(solution)/shard_map/ppermute | solution.py:1228
  586.8 186.4 %finish_sums.1 = (bf16[4,1856,384]{2,1,0:T(8,128)(2,1)}, bf16[768,1536]{1,0:T(8,128)(2,1)}, f32[42,128]{1,0:T(8,128)}, bf16[2,256,1536]{2,1,0:T(8,128)(2,1)}) custom-call(bf16[1856,1536]{1,0:T(8,128)(2,1)} %convolution_convert_fusion.1.grad_ref, bf16[768,1536]{1,0:T(8,128)(2,1)} %convolution_convert_fusion.5.out_grad_ref, bf16[928,384]{1,0:T(8,128)(2,1)} %bitcast.209, ...), custom_call_target="tpu_custom_call" | custom-call | tf_op jit(solution)/shard_map/finish_sums/pallas_call | solution.py:1676
  777.5 8.5 %assemble_rows.1 = f32[6448,384]{1,0:T(8,128)} custom-call(bf16[4,1856,384]{2,1,0:T(8,128)(2,1)} %get-tuple-element.90.part_ref.shared_ref, bf16[4,1856,384]{2,1,0:T(8,128)(2,1)} %get-tuple-element.90.part_ref.shared_ref), custom_call_target="tpu_custom_call" | custom-call | tf_op jit(solution)/shard_map/assemble_rows/pallas_call | solution.py:1735
  (334 shorter events, 109.1 us)
Async XLA Ops:
  7.2 562.6 %reduce-scatter.5.cloned.1.call-start = ((), (), s32[]{:S(2)}) async-start(), calls=%async_computation.3 | async-start | bytes 2949120 | tf_op jit(solution)/shard_map/reduce_scatter | solution.py:1935
  8.5 149.0 %collective-permute-start = (s32[2,2,4]{2,1,0:T(2,128)}, s32[2,2,4]{2,1,0:T(2,128)}, u32[]{:S(2)}, u32[]{:S(2)}) collective-permute-start(s32[2,2,4]{2,1,0:T(2,128)} %pad_add_fusion), channel_id=1, source_target_pairs={{0,1},{1,0},{2,3},{3,2},{4,5},{5,4},{6,7},{7,6},{8,9},{9,8},{10,11... | collective-permute-start | bytes 200 | tf_op jit(solution)/shard_map/ppermute | solution.py:1224
  15.6 96.0 %copy-start.3 = (bf16[1,2,1,256,1536]{4,3,2,1,0:T(8,128)(2,1)S(1)}, bf16[1,2,1,256,1536]{4,3,2,1,0:T(8,128)(2,1)}, u32[]{:S(2)}) copy-start(bf16[1,2,1,256,1536]{4,3,2,1,0:T(8,128)(2,1)} %blocks_ref.1) | copy-start | bytes 4718596
  111.7 76.7 %collective-permute-start.1 = (bf16[256,1536]{1,0:T(8,128)(2,1)S(1)}, bf16[256,1536]{1,0:T(8,128)(2,1)S(1)}, u32[]{:S(2)}, u32[]{:S(2)}) collective-permute-start(bf16[256,1536]{1,0:T(8,128)(2,1)S(1)} %get-tuple-element.123), channel_id=1, source_target_pairs={{0,8},{1,12},{2,10},{3,14},{4,24},{5,28},{6,26},{7,30},{8,9},{9,13... | collective-permute-start | bytes 2359304 | tf_op jit(solution)/shard_map/ppermute | solution.py:1804
  116.8 71.6 %collective-permute-start.2 = (bf16[256,1536]{1,0:T(8,128)(2,1)S(1)}, bf16[256,1536]{1,0:T(8,128)(2,1)S(1)}, u32[]{:S(2)}, u32[]{:S(2)}) collective-permute-start(bf16[256,1536]{1,0:T(8,128)(2,1)S(1)} %get-tuple-element.122), channel_id=1, source_target_pairs={{0,0},{1,4},{2,2},{3,6},{4,16},{5,20},{6,18},{7,22},{8,1},{9,5},{1... | collective-permute-start | bytes 2359304 | tf_op jit(solution)/shard_map/ppermute | solution.py:1803
  144.3 13.3 %copy-start.23 = (s32[2,1,4]{2,1,0:T(1,128)S(1)}, s32[2,1,4]{2,1,0:T(1,128)}, u32[]{:S(2)}) copy-start(s32[2,1,4]{2,1,0:T(1,128)} %param.16) | copy-start | bytes 100
  144.3 14.3 %copy-start.20 = (s32[1024]{0:T(1024)S(1)}, s32[1024]{0:T(1024)}, u32[]{:S(2)}) copy-start(s32[1024]{0:T(1024)} %get-tuple-element.158) | copy-start | bytes 12292
  144.3 14.3 %copy-start.21 = (s32[1024]{0:T(1024)S(1)}, s32[1024]{0:T(1024)}, u32[]{:S(2)}) copy-start(s32[1024]{0:T(1024)} %get-tuple-element.159) | copy-start | bytes 12292
  144.3 14.3 %copy-start.22 = (s32[1024]{0:T(1024)S(1)}, s32[1024]{0:T(1024)}, u32[]{:S(2)}) copy-start(s32[1024]{0:T(1024)} %iota_add_fusion.2) | copy-start | bytes 12292
  317.2 18.3 %copy-start.34 = (bf16[768,1536]{1,0:T(8,128)(2,1)S(1)}, bf16[768,1536]{1,0:T(8,128)(2,1)}, u32[]{:S(2)}) copy-start(bf16[768,1536]{1,0:T(8,128)(2,1)} %get-tuple-element.73) | copy-start | bytes 7077892
  338.0 85.7 %collective-permute-start.15 = (bf16[512,1536]{1,0:T(8,128)(2,1)}, bf16[512,1536]{1,0:T(8,128)(2,1)}, u32[]{:S(2)}, u32[]{:S(2)}) collective-permute-start(bf16[512,1536]{1,0:T(8,128)(2,1)} %convolution_convert_fusion.6), channel_id=1, source_target_pairs={{0,16},{16,0},{1,17},{17,1},{2,18},{18,2},{3,19},{19,3},{4,20},{20... | collective-permute-start | bytes 4718600 | tf_op jit(solution)/shard_map/ppermute | solution.py:1220
  342.7 1.4 collective-permute-start.3
  344.1 3.7 collective-permute-start.4
  394.2 21.5 %collective-permute-start.5 = (bf16[512,1536]{1,0:T(8,128)(2,1)}, bf16[512,1536]{1,0:T(8,128)(2,1)}, u32[]{:S(2)}, u32[]{:S(2)}) collective-permute-start(bf16[512,1536]{1,0:T(8,128)(2,1)} %convolution_convert_fusion.8), channel_id=1, source_target_pairs={{0,16},{16,0},{1,17},{17,1},{2,18},{18,2},{3,19},{19,3},{4,20},{20... | collective-permute-start | bytes 4718600 | tf_op jit(solution)/shard_map/ppermute | solution.py:1220
  409.5 177.3 %reduce-scatter.3.cloned.1.call-start = ((), (), s32[]{:S(2)}) async-start(), calls=%async_computation.2 | async-start | bytes 3563520 | tf_op jit(solution)/shard_map/reduce_scatter | solution.py:1932
  413.2 69.5 %collective-permute-start.13 = (bf16[928,1536]{1,0:T(8,128)(2,1)}, bf16[928,1536]{1,0:T(8,128)(2,1)}, u32[]{:S(2)}, u32[]{:S(2)}) collective-permute-start(bf16[928,1536]{1,0:T(8,128)(2,1)} %dynamic-slice_bitcast_fusion), channel_id=1, source_target_pairs={{0,2},{1,3},{2,0},{3,1},{4,6},{5,7},{6,4},{7,5},{8,10},{9,11},{10,... | collective-permute-start | bytes 8552456 | tf_op jit(solution)/shard_map/ppermute | solution.py:1228
  423.8 20.6 %collective-permute-start.6 = (bf16[256,1536]{1,0:T(8,128)(2,1)}, bf16[256,1536]{1,0:T(8,128)(2,1)S(1)}, u32[]{:S(2)}, u32[]{:S(2)}) collective-permute-start(bf16[256,1536]{1,0:T(8,128)(2,1)} %fusion.13), channel_id=1, source_target_pairs={{0,1},{1,0},{2,3},{3,2},{4,5},{5,4},{6,7},{7,6},{8,9},{9,8},{10,11... | collective-permute-start | bytes 2359304 | tf_op jit(solution)/shard_map/ppermute | solution.py:1224
  426.8 34.5 %copy-start.1 = (bf16[256,1536]{1,0:T(8,128)(2,1)S(1)}, bf16[256,1536]{1,0:T(8,128)(2,1)}, u32[]{:S(2)}) copy-start(bf16[256,1536]{1,0:T(8,128)(2,1)} %broadcast_select_fusion.g_ref) | copy-start | bytes 2359300
  429.5 31.0 %collective-permute-start.16 = (bf16[256,1536]{1,0:T(8,128)(2,1)}, bf16[256,1536]{1,0:T(8,128)(2,1)S(1)}, u32[]{:S(2)}, u32[]{:S(2)}) collective-permute-start(bf16[256,1536]{1,0:T(8,128)(2,1)} %fusion.14), channel_id=1, source_target_pairs={{0,1},{1,0},{2,3},{3,2},{4,5},{5,4},{6,7},{7,6},{8,9},{9,8},{10,11... | collective-permute-start | bytes 2359304 | tf_op jit(solution)/shard_map/ppermute | solution.py:1224
  434.3 27.1 %copy-start.5 = (f32[512,1536]{1,0:T(8,128)S(1)}, f32[512,1536]{1,0:T(8,128)}, u32[]{:S(2)}) copy-start(f32[512,1536]{1,0:T(8,128)} %copy-done.4) | copy-start | bytes 9437188
  465.5 20.7 %copy-start = (bf16[256,1536]{1,0:T(8,128)(2,1)}, bf16[256,1536]{1,0:T(8,128)(2,1)S(1)}, u32[]{:S(2)}) copy-start(bf16[256,1536]{1,0:T(8,128)(2,1)S(1)} %get-tuple-element.109.incoming_ref) | copy-start | bytes 2359300
  465.5 16.1 %copy-start.25 = (f32[8,128]{1,0:T(8,128)S(1)}, f32[8,128]{1,0:T(8,128)}, u32[]{:S(2)}) copy-start(f32[8,128]{1,0:T(8,128)} %get-tuple-element.77) | copy-start | bytes 12292
  465.5 6.0 collective-permute-start.10
  465.6 7.5 collective-permute-start.11
  465.9 29.5 %collective-permute-start.7 = (bf16[256,1536]{1,0:T(8,128)(2,1)S(1)}, bf16[256,1536]{1,0:T(8,128)(2,1)S(1)}, u32[]{:S(2)}, u32[]{:S(2)}) collective-permute-start(bf16[256,1536]{1,0:T(8,128)(2,1)S(1)} %get-tuple-element.109.incoming_ref), channel_id=1, source_target_pairs={{0,16},{16,0},{1,17},{17,1},{2,18},{18,2},{3,19},{19,3},{4,20},{20... | collective-permute-start | bytes 2359304 | tf_op jit(solution)/shard_map/ppermute | solution.py:1220
  466.1 27.2 %collective-permute-start.8 = (bf16[256,1536]{1,0:T(8,128)(2,1)S(1)}, bf16[256,1536]{1,0:T(8,128)(2,1)S(1)}, u32[]{:S(2)}, u32[]{:S(2)}) collective-permute-start(bf16[256,1536]{1,0:T(8,128)(2,1)S(1)} %get-tuple-element.109.incoming_ref), channel_id=1, source_target_pairs={{0,1},{1,0},{2,3},{3,2},{4,5},{5,4},{6,7},{7,6},{8,9},{9,8},{10,11... | collective-permute-start | bytes 2359304 | tf_op jit(solution)/shard_map/ppermute | solution.py:1224
  471.5 319.7 %collective-permute-start.17 = (bf16[256,1536]{1,0:T(8,128)(2,1)S(1)}, bf16[256,1536]{1,0:T(8,128)(2,1)}, u32[]{:S(2)}, u32[]{:S(2)}) collective-permute-start(bf16[256,1536]{1,0:T(8,128)(2,1)S(1)} %copy-done.12), channel_id=1, source_target_pairs={{0,16},{4,17},{2,18},{6,19},{16,20},{20,21},{18,22},{22,23},{1,24}... | collective-permute-start | bytes 2359304 | tf_op jit(solution)/shard_map/ppermute | solution.py:1789
  473.1 1.1 collective-permute-start.12
  474.2 317.0 %collective-permute-start.18 = (bf16[256,1536]{1,0:T(8,128)(2,1)S(1)}, bf16[256,1536]{1,0:T(8,128)(2,1)}, u32[]{:S(2)}, u32[]{:S(2)}) collective-permute-start(bf16[256,1536]{1,0:T(8,128)(2,1)S(1)} %copy-done.12), channel_id=1, source_target_pairs={{8,16},{12,17},{10,18},{14,19},{24,20},{28,21},{26,22},{30,23},{9,... | collective-permute-start | bytes 2359304 | tf_op jit(solution)/shard_map/ppermute | solution.py:1789
  493.2 4.1 collective-permute-start.9
  569.8 16.0 %collective-permute-start.14 = (bf16[192,1536]{1,0:T(8,128)(2,1)}, bf16[192,1536]{1,0:T(8,128)(2,1)S(1)}, u32[]{:S(2)}, u32[]{:S(2)}) collective-permute-start(bf16[192,1536]{1,0:T(8,128)(2,1)} %bitcast.210), channel_id=1, source_target_pairs={{0,2},{1,3},{2,0},{3,1},{4,6},{5,7},{6,4},{7,5},{8,10},{9,11},{10,... | collective-permute-start | bytes 1769480 | tf_op jit(solution)/shard_map/ppermute | solution.py:1228
  569.8 16.0 %copy-start.16 = (bf16[1,192,1536]{2,1,0:T(8,128)(2,1)S(1)}, bf16[1,192,1536]{2,1,0:T(8,128)(2,1)}, u32[]{:S(2)}) copy-start(bf16[1,192,1536]{2,1,0:T(8,128)(2,1)} %reduce-scatter.5.cloned.1.call-done) | copy-start | bytes 1769476
  (28 other events, 191.3 us)
Sparse Core Ops, SparseCore 0:
  409.7 49.8 reduce-scatter.4
  495.6 65.7 reduce-scatter.2

commit v3 on v2

--- a/solution.py
+++ b/solution.py
@@ -434,6 +434,22 @@
     return v.astype(jnp.bfloat16)
 
 
+def split(v, parts):
+    found = []
+    for _ in range(parts):
+        found.append(low(v))
+        v = v - found[-1].astype(jnp.float32)
+    return found
+
+
+def pick_sums(v, ones, parts=2):
+    return sum(mm(part, ones) for part in split(v, parts))
+
+
+def sums_of(ones, v, parts=3):
+    return sum(mm(ones, part) for part in split(v, parts))
+
+
 def iota(shape, dim):
     return lax.broadcasted_iota(jnp.int32, shape, dim)
 
@@ -466,7 +482,20 @@
     return 1.0 / (1.0 + jnp.exp(-v))
 
 
-def chunk_parts(width, proj, before8, marks, seg_row, conv_w, conv_b, dt_bias, rate, pick):
+def head_picks():
+    quarter = 2 * lax.rem(lax.axis_index("rep"), 2) + lax.axis_index("section")
+    given, local = iota((64, LANES), 0), iota((64, LANES), 1)
+    per = H // 16
+    taken = (lax.rem(lax.div(given, per), 4) == quarter) & (given < H)
+    taken = taken & (local == lax.div(given, 4 * per) * per + lax.rem(given, per))
+    return jnp.where(taken, 1.0, 0.0).astype(jnp.bfloat16)
+
+
+def chunk_parts(width, proj, before8, marks, seg_row, small_ref, pick):
+    conv_w = small_ref[0, 0:KW]
+    conv_b = small_ref[0, KW : KW + 1]
+    dt_bias = small_ref[0, 7:8, :LANES]
+    rate = small_ref[0, 8:9, :LANES]
     span = width + 2 * LANES
     gate = proj[:, :width].astype(jnp.float32)
     mixed = proj[:, width : width + span].astype(jnp.float32)
@@ -487,7 +516,7 @@
     step = softplus(stepped)
     decay = -step * rate
     lower = iota((Q, Q), 0) >= iota((Q, Q), 1)
-    total = exact(lower.astype(jnp.float32), decay)
+    total = sums_of(jnp.where(lower, 1.0, 0.0).astype(jnp.bfloat16), decay)
     linked = lower & (marks[:, 5:6] == seg_row)
     shut = jnp.where(linked, 0.0, -1e30)
     reach = jnp.exp(total) * marks[:, 3:4]
@@ -496,8 +525,7 @@
 
 
 def forward_kernel(
-    width, proj_ref, marks_ref, seg_ref, conv_w_ref, conv_b_ref, dt_bias_ref, rate_ref, pick_ref,
-    skip_ref, gain_ref, gg_ref, squares_ref, mixer_ref, starts_ref, state, before,
+    width, proj_ref, marks_ref, seg_ref, small_ref, gg_ref, squares_ref, mixer_ref, starts_ref, state, before,
 ):
     pairs = width // LANES
 
@@ -507,9 +535,9 @@
         before[...] = jnp.zeros_like(before)
 
     gate, mixed, _, _, _, active, _, step, _, total, shut, reach, tail = chunk_parts(
-        width, proj_ref[...], before[...], marks_ref[...], seg_ref[...], conv_w_ref[...],
-        conv_b_ref[...], dt_bias_ref[...], rate_ref[...], pick_ref[...],
-    )
+        width, proj_ref[...], before[...], marks_ref[...], seg_ref[...], small_ref, head_picks()
+    )
+    skip, gain = small_ref[0, 6:7, :width], small_ref[0, 5:6, :width]
     before[...] = mixed[Q - 8 :]
     heads = active[:, :width]
     b_low = low(active[:, width : width + LANES])
@@ -531,16 +559,55 @@
     state[...] = entry * widen(reach[Q - 1 : Q], pairs) + mm(
         b_turned, low(scaled * widen(tail, pairs))
     )
-    mixer_ref[...] = mixer
-    gated = (mixer + skip_ref[...] * heads) * (gate * sigmoid(gate))
+    out = mixer + skip * heads
+    mixer_ref[...] = out
+    gated = out * (gate * sigmoid(gate))
     squares_ref[...] = jnp.sum(gated * gated, axis=1, keepdims=True)
-    gg_ref[...] = low(gated * gain_ref[...])
+    gg_ref[...] = low(gated * gain)
+
+
+def gate_kernel(width, whole_width, proj_ref, small_ref, out_ref, og_ref, rows_ref, gate_grad_ref, out_grad_ref, sums_ref):
+    @pl.when(pl.program_id(0) == 0)
+    def _():
+        sums_ref[...] = jnp.zeros_like(sums_ref)
+
+    gate = proj_ref[...].astype(jnp.float32)
+    inv = rows_ref[:, 0:1]
+    dots = rows_ref[:, 1:2]
+    og = og_ref[...]
+    out = out_ref[...]
+    gate_sig = sigmoid(gate)
+    gate_on = gate * gate_sig
+    hat = out * gate_on * inv
+    gated_grad = inv * (small_ref[0, 5:6, :width] * og - hat * (dots * (1.0 / whole_width)))
+    out_grad_ref[...] = low(gated_grad * gate_on)
+    gate_grad_ref[...] = low(gated_grad * out * (gate_sig * (1.0 + gate * (1.0 - gate_sig))))
+    sums_ref[0:1] += jnp.sum(hat * og, axis=0, keepdims=True)
+
+
+def gate_backward(layer, projected, small, out, og, per_row, whole_width):
+    rows, width = out.shape
+    step = 2 * Q
+
+    def by_row(count):
+        return pl.BlockSpec((step, count), lambda i: (i, 0))
+
+    half = jax.ShapeDtypeStruct((rows, width), jnp.bfloat16)
+    return pl.pallas_call(
+        functools.partial(gate_kernel, width, whole_width),
+        grid=(rows // step,),
+        in_specs=[by_row(width), small_spec(layer), by_row(width), by_row(width), by_row(2)],
+        out_specs=[by_row(width), by_row(width), full_spec((8, width))],
+        out_shape=[half, half, jax.ShapeDtypeStruct((8, width), jnp.float32)],
+        compiler_params=pltpu.CompilerParams(vmem_limit_bytes=VMEM_BYTES),
+        cost_estimate=cost(6),
+        name="gate_backward",
+    )(projected, small, out, og, per_row)
 
 
 def backward_kernel(
-    width, whole_width, proj_ref, rim_ref, marks_ref, seg_ref, conv_w_ref, conv_b_ref, dt_bias_ref,
-    rate_ref, pick_ref, skip_ref, gain_ref, mixer_ref, starts_ref, og_ref, rows_ref,
-    pg_ref, outgoing_ref, wide_ref, conv_ref, head_ref, later, after,
+    width, proj_ref, rim_ref, marks_ref, seg_ref, small_ref, out_ref, starts_ref, out_grad_ref,
+    gate_grad_ref, pg_ref, conv_ref, head_ref, later, after, skips,
 ):
     pairs = width // LANES
     turn = pl.program_id(0)
@@ -550,7 +617,7 @@
     def _():
         later[...] = jnp.zeros_like(later)
         after[...] = jnp.zeros_like(after)
-        wide_ref[...] = jnp.zeros_like(wide_ref)
+        skips[...] = jnp.zeros_like(skips)
         conv_ref[...] = jnp.zeros_like(conv_ref)
         head_ref[...] = jnp.zeros_like(head_ref)
 
@@ -558,28 +625,20 @@
     marks = marks_ref[...]
     rim = rim_ref[...][8:, width : width + span].astype(jnp.float32)
     rim = jnp.where(chunk > 0, rim, 0.0)
-    gate, mixed, shifts, conv, sig, active, stepped, step, decay, total, shut, reach, tail = (
+    pick = head_picks()
+    skip, rate = small_ref[0, 6:7, :width], small_ref[0, 8:9, :LANES]
+    _, mixed, shifts, conv, sig, active, stepped, step, decay, total, shut, reach, tail = (
         chunk_parts(
-            width, proj_ref[...], rim, marks, seg_ref[...], conv_w_ref[...], conv_b_ref[...],
-            dt_bias_ref[...], rate_ref[...], pick_ref[...],
+            width, proj_ref[...], rim, marks, seg_ref[...], small_ref, pick
         )
     )
     heads = active[:, :width]
     b_low = low(active[:, width : width + LANES])
     c_low = low(active[:, width + LANES :])
 
-    inv = rows_ref[:, 0:1]
-    dots = rows_ref[:, 1:2]
-    og = og_ref[...]
-    mixer = mixer_ref[...]
-    out = mixer + skip_ref[...] * heads
-    gate_sig = sigmoid(gate)
-    gate_on = gate * gate_sig
-    hat = out * gate_on * inv
-    outgoing_ref[...] = low(hat * gain_ref[...])
-    gated_grad = inv * (gain_ref[...] * og - hat * (dots * (1.0 / whole_width)))
-    out_grad = gated_grad * gate_on
-    gate_grad = gated_grad * out * (gate_sig * (1.0 + gate * (1.0 - gate_sig)))
+    grad_low = out_grad_ref[...]
+    out_grad = grad_low.astype(jnp.float32)
+    mixer = out_ref[...] - skip * heads
 
     entry = starts_ref[0]
     entry_low = low(entry)
@@ -590,7 +649,6 @@
     step_wide = widen(step, pairs)
     scaled = heads * step_wide
     scaled_low = low(scaled)
-    grad_low = low(out_grad)
     from_late = widen(tail, pairs) * mm(b_low, late_low)
     inside = []
     score_grad = jnp.zeros((Q, Q), jnp.float32)
@@ -614,25 +672,26 @@
     later[...] = late * kept + mm(c_low, reached, 0, 0)
 
     scaled_seen = scaled_low.astype(jnp.float32)
-    balance = grad_low.astype(jnp.float32) * mixer - scaled_seen * scaled_grad
+    balance = out_grad * mixer - scaled_seen * scaled_grad
     closing = jnp.sum(scaled_seen * from_late, axis=0, keepdims=True) + kept * jnp.sum(
         late * entry, axis=0, keepdims=True
     )
-    picks = (iota((width, LANES), 0) // (LANES // 2) == iota((width, LANES), 1)).astype(jnp.float32)
-    sums = exact(
+    picks = iota((width, LANES), 0) // (LANES // 2) == iota((width, LANES), 1)
+    picks = jnp.where(picks, 1.0, 0.0).astype(jnp.bfloat16)
+    sums = pick_sums(
         jnp.concatenate([balance, heads * scaled_grad, jnp.broadcast_to(closing, (8, width))], 0),
         picks,
     )
-    upper = (iota((Q, Q), 0) <= iota((Q, Q), 1)).astype(jnp.float32)
-    decay_grad = exact(upper, sums[:Q]) + sums[2 * Q : 2 * Q + 1]
-    step_grad = sums[Q : 2 * Q] - decay_grad * rate_ref[...]
+    upper = jnp.where(iota((Q, Q), 0) <= iota((Q, Q), 1), 1.0, 0.0).astype(jnp.bfloat16)
+    decay_grad = sums_of(upper, sums[:Q]) + sums[2 * Q : 2 * Q + 1]
+    step_grad = sums[Q : 2 * Q] - decay_grad * rate
     raw_grad = step_grad * sigmoid(stepped)
 
-    head_grad = step_wide * scaled_grad + skip_ref[...] * out_grad
+    head_grad = step_wide * scaled_grad + skip * out_grad
     conv_grad = jnp.concatenate([head_grad, b_grad, c_grad], axis=1) * (
         sig * (1.0 + conv * (1.0 - sig))
     )
-    mixed_grad = conv_w_ref[KW - 1 : KW] * conv_grad
+    mixed_grad = small_ref[0, KW - 1 : KW] * conv_grad
     bottom = iota((8, span), 0)
     for lag in range(1, KW):
         sent = conv_grad * marks[:, lag - 1 : lag]
@@ -640,16 +699,16 @@
         ending = jnp.where(
             bottom >= 8 - lag, pltpu.roll(after[lag - 1], 8 - lag, 0), rolled[Q - 8 :]
         )
-        mixed_grad = mixed_grad + conv_w_ref[KW - 1 - lag : KW - lag] * jnp.concatenate(
+        mixed_grad = mixed_grad + small_ref[0, KW - 1 - lag : KW - lag] * jnp.concatenate(
             [rolled[: Q - 8], ending], axis=0
         )
         after[lag - 1] = sent[:8]
-    pg_ref[...] = low(
-        jnp.concatenate([gate_grad, mixed_grad, mm(low(raw_grad), pick_ref[...], 1, 1)], axis=1)
-    )
-
-    wide_ref[0:1] += jnp.sum(hat * og, axis=0, keepdims=True)
-    wide_ref[1:2] += jnp.sum(out_grad * heads, axis=0, keepdims=True)
+    pg_ref[:, :width] = gate_grad_ref[...]
+    pg_ref[:, width:] = low(
+        jnp.concatenate([mixed_grad, mm(low(raw_grad), pick, 1, 1)], axis=1)
+    )
+
+    skips[0:1] += jnp.sum(out_grad * heads, axis=0, keepdims=True)
     for lag in range(KW):
         conv_ref[KW - 1 - lag : KW - lag] += jnp.sum(
             conv_grad * shifts[lag], axis=0, keepdims=True
@@ -658,26 +717,104 @@
     head_ref[0:1] += jnp.sum(raw_grad, axis=0, keepdims=True)
     head_ref[1:2] += jnp.sum(decay_grad * decay, axis=0, keepdims=True)
 
+    @pl.when(chunk == 0)
+    def _():
+        head_ref[2:3] = pick_sums(skips[...], picks, 3)[0:1]
+
+
+def cost(micros):
+    return pl.CostEstimate(flops=micros * 1_100_000_000, bytes_accessed=0, transcendentals=0)
+
+
+def small_spec(layer):
+    return pl.BlockSpec((1, 16, 2 * D // 3), lambda i: (layer, 0, 0))
+
 
 def full_spec(shape):
     return pl.BlockSpec(shape, lambda i: (0,) * len(shape))
 
 
-def mixer_forward(projected, marks, seg_row, small):
+def product_kernel(place_ref, left_ref, weight_ref, theirs_ref, mine_ref):
+    turn = pl.program_id(0)
+    found = mm(left_ref[...], weight_ref[...])
+
+    @pl.when(turn < 2)
+    def _():
+        theirs_ref[...] = low(found)
+
+    @pl.when(turn >= 2)
+    def _():
+        mine_ref[...] = found
+
+
+def group_parts(c, left, weight):
+    rows, depth = left.shape
+    block, columns = rows // 4, weight.shape[1]
+
+    def left_at(i, at):
+        return (2 * lax.rem(i, 2) + jnp.where(i < 2, 1 - at[0], at[0]), 0)
+
+    return pl.pallas_call(
+        product_kernel,
+        grid_spec=pltpu.PrefetchScalarGridSpec(
+            num_scalar_prefetch=1,
+            grid=(4,),
+            in_specs=[
+                pl.BlockSpec((block, depth), left_at),
+                pl.BlockSpec((depth, columns), lambda i, at: (0, 0)),
+            ],
+            out_specs=[
+                pl.BlockSpec((block, columns), lambda i, at: (jnp.minimum(i, 1), 0)),
+                pl.BlockSpec((block, columns), lambda i, at: (jnp.maximum(i - 2, 0), 0)),
+            ],
+        ),
+        out_shape=[
+            jax.ShapeDtypeStruct((2 * block, columns), jnp.bfloat16),
+            jax.ShapeDtypeStruct((2 * block, columns), jnp.float32),
+        ],
+        compiler_params=pltpu.CompilerParams(vmem_limit_bytes=VMEM_BYTES),
+        cost_estimate=cost(6),
+        name="group_parts",
+    )(c.reshape((1,)), left, weight)
+
+
+def projection_kernel(left_ref, weight_ref, out_ref):
+    out_ref[...] = low(mm(left_ref[...], weight_ref[...], 1, 1))
+
+
+def projection(left, weight):
+    rows, depth = left.shape
+    block, columns = rows // 4, weight.shape[0]
+    return pl.pallas_call(
+        projection_kernel,
+        grid=(4,),
+        in_specs=[
+            pl.BlockSpec((block, depth), lambda i: (i, 0)),
+            pl.BlockSpec((columns, depth), lambda i: (0, 0)),
+        ],
+        out_specs=pl.BlockSpec((block, columns), lambda i: (i, 0)),
+        out_shape=jax.ShapeDtypeStruct((rows, columns), jnp.bfloat16),
+        compiler_params=pltpu.CompilerParams(vmem_limit_bytes=VMEM_BYTES),
+        cost_estimate=cost(6),
+        name="projection",
+    )(left, weight)
+
+
+def mixer_forward(layer, projected, marks, seg_row, small):
     rows, columns = projected.shape
-    width = small["gain"].shape[1]
+    width = DI // 4
     chunks = rows // Q
     span = width + 2 * LANES
 
     def by_row(count):
         return pl.BlockSpec((Q, count), lambda i: (i, 0))
 
-    weights = [small[k] for k in ("conv_w", "conv_b", "dt_bias", "rate", "pick", "skip", "gain")]
     return pl.pallas_call(
         functools.partial(forward_kernel, width),
         grid=(chunks,),
-        in_specs=[by_row(columns), by_row(8), pl.BlockSpec((1, Q), lambda i: (0, i))]
-        + [full_spec(w.shape) for w in weights],
+        in_specs=[
+            by_row(columns), by_row(8), pl.BlockSpec((1, Q), lambda i: (0, i)), small_spec(layer),
+        ],
         out_specs=[
             by_row(width),
             by_row(1),
@@ -695,55 +832,56 @@
             pltpu.VMEM((8, span), jnp.float32),
         ],
         compiler_params=pltpu.CompilerParams(vmem_limit_bytes=VMEM_BYTES),
+        cost_estimate=cost(16),
         name="mixer_forward",
-    )(projected, marks, seg_row, *weights)
-
-
-def mixer_backward(projected, marks, seg_row, small, mixer, starts, og, per_row, whole_width):
+    )(projected, marks, seg_row, small)
+
+
+def mixer_backward(layer, projected, marks, seg_row, small, out, starts, out_grad, gate_grad):
     rows, columns = projected.shape
-    width = small["gain"].shape[1]
+    width = out.shape[1]
     chunks = rows // Q
     span = width + 2 * LANES
 
     def by_row(count):
         return pl.BlockSpec((Q, count), lambda i: (chunks - 1 - i, 0))
 
-    weights = [small[k] for k in ("conv_w", "conv_b", "dt_bias", "rate", "pick", "skip", "gain")]
     rim = pl.BlockSpec(
         (16, columns), lambda i: (jnp.maximum((chunks - 1 - i) * (Q // 16) - 1, 0), 0)
     )
     return pl.pallas_call(
-        functools.partial(backward_kernel, width, whole_width),
+        functools.partial(backward_kernel, width),
         grid=(chunks,),
-        in_specs=[by_row(columns), rim, by_row(8), pl.BlockSpec((1, Q), lambda i: (0, chunks - 1 - i))]
-        + [full_spec(w.shape) for w in weights]
-        + [
+        in_specs=[
+            by_row(columns),
+            rim,
+            by_row(8),
+            pl.BlockSpec((1, Q), lambda i: (0, chunks - 1 - i)),
+            small_spec(layer),
             by_row(width),
             pl.BlockSpec((1, LANES, width), lambda i: (chunks - 1 - i, 0, 0)),
             by_row(width),
-            by_row(2),
+            by_row(width),
         ],
         out_specs=[
             by_row(columns),
-            by_row(width),
-            full_spec((8, width)),
             full_spec((8, span)),
             full_spec((8, LANES)),
         ],
         out_shape=[
             jax.ShapeDtypeStruct((rows, columns), jnp.bfloat16),
-            jax.ShapeDtypeStruct((rows, width), jnp.bfloat16),
-            jax.ShapeDtypeStruct((8, width), jnp.float32),
             jax.ShapeDtypeStruct((8, span), jnp.float32),
             jax.ShapeDtypeStruct((8, LANES), jnp.float32),
         ],
         scratch_shapes=[
             pltpu.VMEM((LANES, width), jnp.float32),
             pltpu.VMEM((KW - 1, 8, span), jnp.float32),
+            pltpu.VMEM((8, width), jnp.float32),
         ],
         compiler_params=pltpu.CompilerParams(vmem_limit_bytes=VMEM_BYTES),
+        cost_estimate=cost(33),
         name="mixer_backward",
-    )(projected, projected, marks, seg_row, *weights, mixer, starts, og, per_row)
+    )(projected, projected, marks, seg_row, small, out, starts, out_grad, gate_grad)
 
 
 CORES = 2
@@ -755,6 +893,10 @@
 LANE_PART = D // 4
 OUT_PART = DI // 16
 UNITS = CHUNKS + 1
+GATE = DI // GROUP
+GATE_HALF = GATE // 2
+REST_HALF = HALF - GATE_HALF
+STEPS = ((0, 192), (192, 192), (0, 272), (272, 272))
 
 
 def place():
@@ -926,7 +1068,10 @@
         self.c, self.z, self.y, self.x = place()
 
     def copy(self, i, xx, cc, device):
-        piece = self.whole.at[rows_at((2 * xx + cc) * self.count, self.count)]
+        if self.count is None:
+            piece = self.whole.at[2 * xx + cc]
+        else:
+            piece = self.whole.at[rows_at((2 * xx + cc) * self.count, self.count)]
         return mesh_copy(piece, piece, self.send.at[i], self.recv.at[i], device)
 
     def near(self):
@@ -939,7 +1084,10 @@
         return self.copy(2, 1 - self.x, self.c, {"section": 1 - self.c})
 
     def begin(self, value):
-        self.whole[rows_at((2 * self.x + self.c) * self.count, self.count)] = value
+        if self.count is None:
+            self.whole[2 * self.x + self.c] = value
+        else:
+            self.whole[rows_at((2 * self.x + self.c) * self.count, self.count)] = value
         self.near().start()
         self.other().start()
 
@@ -958,9 +1106,53 @@
     return low(rows * inv * gain)
 
 
+def turn_by(value, step, counts, which):
+    found = pltpu.roll(value, step * counts[0], 1) if counts[0] else value
+    for k in range(1, len(counts)):
+        other = pltpu.roll(value, step * counts[k], 1) if counts[k] else value
+        found = jnp.where(which == k, other, found)
+    return found
+
+
+def small_parts(layer, quarter, params_ref, small_ref):
+    width, group = DI // GROUP, DI // 16
+    piece = CONV // 4
+    lane = iota((16, width), 1)
+    pieces = [params_ref[4 * layer + zz].astype(jnp.float32) for zz in range(4)]
+    gap = jnp.zeros((16, CONV - pieces[0].shape[1]), jnp.float32)
+    conv = jnp.zeros((16, CONV), jnp.float32)
+    for zz in range(4):
+        own = jnp.where(iota(pieces[zz].shape, 1) < piece, pieces[zz], 0.0)
+        conv = conv + pltpu.roll(jnp.concatenate([own, gap], axis=1), zz * piece, 1)
+
+    def turned(part, zz):
+        moved = turn_by(part, group, [(zz - k) % GROUP for k in range(GROUP)], quarter)
+        return jnp.where(lax.div(lane, group) == zz, moved, 0.0)
+
+    taps = sum(turned(conv[:, zz * width : (zz + 1) * width], zz) for zz in range(4))
+    gain = sum(turned(pieces[zz][:, :width], zz) for zz in range(4))
+    per = H // 16
+    head, given = iota((LANES, LANES), 1), iota((LANES, LANES), 0)
+    heads = jnp.zeros((16, LANES), jnp.float32)
+    for zz in range(4):
+        taken = (lax.div(head, per) == zz) & (given == per * quarter + lax.rem(head, per))
+        heads = heads + mm(low(pieces[zz][:, :LANES]), jnp.where(taken, 1.0, 0.0).astype(jnp.bfloat16))
+    wide_head = iota((LANES, width), 1)
+    wide = jnp.where(lax.div(wide_head, P_SIZE) == iota((LANES, width), 0), 1.0, 0.0)
+    skip = mm(low(heads), wide.astype(jnp.bfloat16))
+    small_ref[layer] = jnp.zeros(small_ref.shape[1:], jnp.float32)
+    small_ref[layer, 0:5, :width] = taps[0:5]
+    small_ref[layer, 0:5, width:] = conv[0:5, DI:]
+    small_ref[layer, 5:6, :width] = gain[5:6]
+    small_ref[layer, 6:7, :width] = skip[9:10]
+    small_ref[layer, 7:8, :LANES] = heads[7:8]
+    rate = jnp.exp(heads[8:9])
+    small_ref[layer, 8:9, :LANES] = jnp.where(iota((1, LANES), 1) < H // GROUP, rate, 0.0)
+
+
 def enter_first_kernel(
-    in_ref, out_ref, blocks_ref, flat_ref, w_ref, wo_ref, rows_ref, normed_ref, params_ref,
-    row_send, row_recv, home_send, home_recv, p_send, p_recv, *sems,
+    in_ref, out_ref, blocks_ref, flat_ref, w_ref, wo_ref, rows_ref, normed_ref, small_ref, norms_ref,
+    params_ref, row_send, row_recv, home_send, home_recv, p_send, p_recv, *sems,
 ):
     c, z, y, x = place()
     weights = WeightGather(0, in_ref, out_ref, w_ref, wo_ref, sems)
@@ -1024,11 +1216,6 @@
         param_copy(i).start()
     params_ref[4 * c + z] = flat_ref[...]
     weights.begin()
-    for unit in range(CHUNKS):
-        weights.first(unit)
-    for unit in range(CHUNKS):
-        weights.arrive(unit, 1)
-
     for i in range(7):
         param_from(i).wait_recv()
 
@@ -1042,13 +1229,23 @@
         def _():
             own_copy(m).wait()
 
-    gains = [params_ref[zz].astype(jnp.float32) for zz in range(4)]
-    gain = jnp.concatenate([g[i : i + 1] for g in gains for i in range(3)], axis=1)
+    for layer in range(2):
+        for zz in range(4):
+            part = params_ref[4 * layer + zz].astype(jnp.float32)[6:7, :LANE_PART]
+            norms_ref[layer, :, zz * LANE_PART : (zz + 1) * LANE_PART] = jnp.broadcast_to(
+                part, (8, LANE_PART)
+            )
+    gain = norms_ref[0, 0:1]
+    for unit in range(CHUNKS):
+        weights.first(unit)
     gather.begin(normal_rows(rows_ref[...].astype(jnp.float32), gain))
-    for unit in range(CHUNKS):
-        weights.arrive(unit, 2)
+    for k in (1, 2):
+        for unit in range(CHUNKS):
+            weights.arrive(unit, k)
     weights.first(CHUNKS)
     gather.middle()
+    for layer in range(2):
+        small_parts(layer, 2 * x + c, params_ref, small_ref)
     for unit in range(CHUNKS):
         weights.arrive(unit, 3)
     for k in (1, 2, 3):
@@ -1078,14 +1275,15 @@
     return pl.pallas_call(
         enter_first_kernel,
         in_specs=[anywhere] * 3 + [inside],
-        out_specs=[inside] * 5,
+        out_specs=[inside] * 6,
         out_shape=weight_shapes()
         + [
             jax.ShapeDtypeStruct((block, D), jnp.bfloat16),
             jax.ShapeDtypeStruct((GROUP * block, D), jnp.bfloat16),
-            jax.ShapeDtypeStruct((2 * 4,) + flat.shape, jnp.bfloat16),
+            jax.ShapeDtypeStruct((CORES, 16, DI // GROUP + 2 * N), jnp.float32),
+            jax.ShapeDtypeStruct((CORES, 8, D), jnp.float32),
         ],
-        scratch_shapes=[dma((3,)), dma((3,)), dma((MICRO,)), dma((1,)), dma((7,)), dma((7,))]
+        scratch_shapes=[pltpu.VMEM((2 * 4,) + flat.shape, jnp.bfloat16), dma((3,)), dma((3,)), dma((MICRO,)), dma((1,)), dma((7,)), dma((7,))]
         + weight_scratch(),
         compiler_params=pltpu.CompilerParams(
             collective_id=0, has_side_effects=True, vmem_limit_bytes=VMEM_BYTES
@@ -1246,54 +1444,58 @@
     return lax.optimization_barrier((value,) + earlier)[0]
 
 
-def pick_last(v, quarter):
-    parts = v.reshape(v.shape[:-1] + (4, GROUP, v.shape[-1] // (4 * GROUP)))
-    return lax.dynamic_index_in_dim(parts, quarter, v.ndim, False).reshape(v.shape[:-1] + (-1,))
-
-
-def place_last(v, quarter):
-    parts = v.reshape(v.shape[:-1] + (4, 1, v.shape[-1] // 4))
-    empty = jnp.zeros(v.shape[:-1] + (4, GROUP, v.shape[-1] // 4), v.dtype)
-    return lax.dynamic_update_slice_in_dim(empty, parts, quarter, v.ndim).reshape(
-        v.shape[:-1] + (-1,)
-    )
-
-
-def finish_kernel(
-    grad_ref, out_grad_ref, late_ref, late_out_ref, tiny_ref,
-    theirs_ref, mine_ref, entering_ref, incoming_ref, gain_ref,
-    all_ref, out_all_ref, tiny_out_ref, bound_ref,
-    n_core, n_send, n_across, n_done, tiny_mine, y_buf, z_buf, s_buf, zo_buf, so_buf, yo_buf, yo_mine, t1_buf, t1_sum, t2_buf, t2_sum, t3_buf,
-    y_send, y_recv, z_send, z_recv, zo_send, zo_recv, yo_sem,
-    core_send, core_recv, x_send, x_recv, ya_send, ya_recv, relay_send, relay_recv,
-    xo_send, xo_recv, t_send, t_recv, n_sem, home_send, home_recv,
-):
+def sum_kernel(layer, *refs):
+    last = layer == 0
+    (
+        gate_ref, grad_ref, out_grad_ref, theirs_ref, mine_ref, entering_ref, incoming_ref, gain_ref,
+        extra_ref,
+    ) = refs[:9]
+    if last:
+        small_refs = (refs[9:12], refs[12:15])
+        late_refs, late_out_refs = refs[15:19], refs[19:21]
+        refs = refs[:9] + refs[21:]
+    else:
+        r_theirs_ref, r_mine_ref, r_inv_ref = refs[9:12]
+        refs = refs[:9] + refs[12:]
+    all_ref, out_all_ref, bound_ref = refs[9:12]
+    (
+        n_core, n_send, n_across, n_done, y_buf, z_buf, s_buf, yo_buf, yo_mine,
+        y_send, y_recv, z_send, z_recv, yo_sem, core_send, core_recv,
+        x_send, x_recv, ya_send, ya_recv, relay_send, relay_recv, xo_send, xo_recv, n_sem,
+    ) = refs[19:44]
+    if last:
+        total_refs = refs[12:19]
+        tiny_mine, t1_buf, t1_sum, t2_buf, t2_sum, t3_buf = refs[44:50]
+        t_send, t_recv, home_send, home_recv = refs[50:]
+    else:
+        g_ref, g_all_ref, dots_ref, norm_ref = refs[12:16]
+        r_core, r_send, r_across = refs[44:47]
+        row_send, row_recv, dot_send, dot_recv, r_sem, home_send, home_recv = refs[47:]
     c, z, y, x = place()
     quarter = 2 * x + c
     core, x_other, y_other = {"section": 1 - c}, {"rep": 2 * y + 1 - x}, {"rep": 2 * (1 - y) + x}
-    diagonal = {"rep": 2 * (1 - y) + 1 - x}
-    part = HALF // CHUNKS
-
+    chunks = range(len(STEPS))
+    block = n_done.shape[0]
     copy = mesh_copy
 
-    block = n_done.shape[0]
-    home = {"section": 0, "shard": quarter, "rep": 2 * y + lax.rem(z, 2)}
-    at_home = (c == 0) & (z == quarter) & (x == lax.rem(z, 2))
+    home = {"section": layer, "shard": quarter, "rep": 2 * y + lax.rem(z, 2)}
+    at_home = (c == layer) & (z == quarter) & (x == lax.rem(z, 2))
     guests = tuple(
         {"section": lax.rem(z, 2), "shard": 2 * m + x, "rep": 2 * y + lax.div(z, 2)}
         for m in range(MICRO)
     )
-
+    guest_self = tuple(
+        (c == layer) & (lax.rem(z, 2) == layer) & (z == 2 * m + x) & (x == lax.div(z, 2))
+        for m in range(MICRO)
+    )
+    reps = (x_other, y_other, {"rep": 2 * (1 - y) + 1 - x})
+    shards = tuple({"shard": lax.rem(z + away, 4)} for away in (1, 2, 3))
     barrier = pltpu.get_barrier_semaphore()
-    reps = (x_other, y_other, diagonal)
-    shards = tuple({"shard": lax.rem(z + away, 4)} for away in (1, 2, 3))
-
     for device in (core,) + reps + shards:
         greet(barrier, device)
     for m in range(MICRO):
-        own = (lax.rem(z, 2) == 0) & (z == 2 * m + x) & (x == lax.div(z, 2))
-
-        @pl.when((c == 0) & jnp.logical_not(own))
+
+        @pl.when((c == layer) & jnp.logical_not(guest_self[m]))
         def _():
             greet(barrier, guests[m])
 
@@ -1308,14 +1510,17 @@
         return found
 
     def grad_part(shard, side, ch):
-        return grad_ref.at[
-            rows_at(side * HALF + ch * part, part),
-            pl.ds(pl.multiple_of(shard * LANE_PART, LANES), LANE_PART),
-        ]
+        lanes = pl.ds(pl.multiple_of(shard * LANE_PART, LANES), LANE_PART)
+        if ch < 2:
+            return gate_ref.at[pl.ds(*STEPS[ch]), lanes]
+        return grad_ref.at[rows_at(side * REST_HALF + STEPS[ch][0], STEPS[ch][1]), lanes]
+
+    def span_of(ch):
+        return pl.ds(STEPS[ch][0] + (0 if ch < 2 else GATE_HALF), STEPS[ch][1])
 
     def y_copy(shard, ch):
         return copy(
-            grad_part(shard, 1 - y, ch), y_buf.at[shard, pl.ds(ch * part, part)],
+            grad_part(shard, 1 - y, ch), y_buf.at[shard, span_of(ch)],
             y_send.at[shard, ch], y_recv.at[shard, ch], y_other,
         )
 
@@ -1328,29 +1533,20 @@
     def z_copy(shard, ch):
         there, slot = z_target(shard)
         return copy(
-            s_buf.at[shard, pl.ds(ch * part, part)], z_buf.at[slot, pl.ds(ch * part, part)],
+            s_buf.at[shard, span_of(ch)], z_buf.at[slot, span_of(ch)],
             z_send.at[shard, ch], z_recv.at[slot, ch], there,
         )
 
     def z_wait(slot, ch):
         there, _ = z_target(shard_at(0))
         copy(
-            s_buf.at[0, pl.ds(ch * part, part)], z_buf.at[slot, pl.ds(ch * part, part)],
+            s_buf.at[0, span_of(ch)], z_buf.at[slot, span_of(ch)],
             z_send.at[0, ch], z_recv.at[slot, ch], there,
         ).wait_recv()
 
-    def zo_copy(shard):
-        there, slot = z_target(shard)
-        return copy(
-            so_buf.at[shard], zo_buf.at[slot], zo_send.at[shard], zo_recv.at[slot], there
-        )
-
-    def zo_wait(slot):
-        there, _ = z_target(shard_at(0))
-        copy(so_buf.at[0], zo_buf.at[slot], zo_send.at[0], zo_recv.at[slot], there).wait_recv()
-
     def all_part(which, side, ch):
-        return all_ref.at[which, rows_at(side * HALF + ch * part, part)]
+        start = side * GATE_HALF if ch < 2 else GATE + side * REST_HALF
+        return all_ref.at[which, rows_at(start + STEPS[ch][0], STEPS[ch][1])]
 
     def out_part(which):
         return out_all_ref.at[rows_at(which * OUT_PART, OUT_PART)]
@@ -1375,40 +1571,18 @@
         x_copy(who, ch).start()
         ya_copy(who, ch).start()
 
-    def late_copy(ch):
+    def owner_copy(ch):
+        span = span_of(ch)
+        piece = all_part(quarter, y, ch)
+        return copy(s_buf.at[z, span], piece, core_send.at[ch], core_recv.at[ch], core)
+
+    def owner_out_copy():
         return copy(
-            late_ref.at[pl.ds(ch * part, part)], all_part(quarter, y, ch),
-            core_send.at[ch], core_recv.at[ch], core,
+            yo_mine, out_part(quarter), core_send.at[len(STEPS)], core_recv.at[len(STEPS)], core
         )
 
-    def late_out_copy():
-        return copy(
-            late_out_ref, out_part(quarter), core_send.at[CHUNKS], core_recv.at[CHUNKS], core
-        )
-
-    def first_copy(ch):
-        piece = all_part(quarter, y, ch)
-        return copy(z_buf.at[4, pl.ds(ch * part, part)], piece, core_send.at[ch], core_recv.at[ch], core)
-
-    def first_out_copy():
-        return copy(
-            yo_mine, out_part(quarter), core_send.at[CHUNKS], core_recv.at[CHUNKS], core
-        )
-
-    def t1_copy():
-        return copy(tiny_mine.at[1 - c], t1_buf, t_send.at[0], t_recv.at[0], core)
-
-    def t2_copy(away):
-        return copy(
-            t1_sum.at[lax.rem(z + away, 4)], t2_buf.at[away - 1],
-            t_send.at[away], t_recv.at[away], shards[away - 1],
-        )
-
-    def t3_copy(i):
-        return copy(t2_sum, t3_buf.at[i], t_send.at[4 + i], t_recv.at[4 + i], reps[i])
-
     def yo_copy():
-        return copy(yo_mine, yo_buf, yo_sem.at[0], yo_sem.at[1], y_other)
+        return copy(out_grad_ref, yo_buf, yo_sem.at[0], yo_sem.at[1], y_other)
 
     def n_core_copy():
         return copy(theirs_ref, n_core, n_sem.at[0], n_sem.at[1], core)
@@ -1419,51 +1593,68 @@
     def home_copy(m):
         return copy(n_done, bound_ref.at[m], home_send.at[0], home_recv.at[m], home)
 
+    def go_home():
+        for m in range(MICRO):
+            there = lax.div(z, 2) == m
+
+            @pl.when(there & jnp.logical_not(at_home))
+            def _():
+                home_copy(m).start()
+
+            @pl.when(there & at_home)
+            def _():
+                bound_ref[m] = n_done[...]
+
+    if last:
+
+        def t1_copy():
+            return copy(tiny_mine.at[1 - c], t1_buf, t_send.at[0], t_recv.at[0], core)
+
+        def t2_copy(away):
+            return copy(
+                t1_sum, t2_buf.at[away - 1], t_send.at[away], t_recv.at[away], shards[away - 1]
+            )
+
+        def t3_copy(i):
+            return copy(t2_sum, t3_buf.at[i], t_send.at[4 + i], t_recv.at[4 + i], reps[i])
+
+    else:
+
+        def r_core_copy():
+            return copy(r_theirs_ref, r_core, r_sem.at[0], r_sem.at[1], core)
+
+        def r_x_copy():
+            return copy(r_send, r_across, r_sem.at[2], r_sem.at[3], x_other)
+
+        def r_summed(which):
+            rows = rows_at(which * block, block)
+            return r_mine_ref[rows] + r_core[rows].astype(jnp.float32)
+
+        g_gather = RowGather(g_all_ref, block, (row_send, row_recv))
+        dot_gather = RowGather(dots_ref, None, (dot_send, dot_recv))
+
     n_core_copy().start()
-    for i in range(4):
-        shard = shard_at(i)
-        for ch in range(CHUNKS):
-            y_copy(shard, ch).start()
-
-    @pl.when(c == 0)
-    def _():
-        for ch in range(CHUNKS):
-            late_copy(ch).start()
-        late_out_copy().start()
-
-    @pl.when(c == 1)
-    def _():
-        for ch in range(CHUNKS):
-            all_part(quarter, y, ch)[...] = late_ref[pl.ds(ch * part, part)]
-        out_part(quarter)[...] = late_out_ref[...]
-
-    def own_out(shard):
-        return out_grad_ref[rows_at(shard * OUT_PART, OUT_PART)].astype(jnp.float32)
+    if not last:
+        r_core_copy().start()
+    yo_copy().start()
+    for ch in chunks[2:]:
+        for i in range(4):
+            y_copy(shard_at(i), ch).start()
 
     def more(shard):
         return ((shard > z) & (z > 0)) | ((shard < z) & (z < 3))
 
-    def send_out(i):
-        shard = shard_at(i)
-
-        @pl.when(more(shard))
-        def _():
-            zo_wait(shard)
-            so_buf[shard] = low(own_out(shard) + zo_buf[shard].astype(jnp.float32))
-
-        @pl.when(jnp.logical_not(more(shard)))
-        def _():
-            so_buf[shard] = out_grad_ref[rows_at(shard * OUT_PART, OUT_PART)]
-
-        zo_copy(shard).start()
+    def y_sum(shard, ch):
+        own = grad_part(shard, y, ch)[...].astype(jnp.float32)
+        if ch < 2:
+            return own
+        y_copy(shard, ch).wait_recv()
+        return own + y_buf[shard, span_of(ch)].astype(jnp.float32)
 
     def send_in(i, ch):
         shard = shard_at(i)
-        span = pl.ds(ch * part, part)
-        y_copy(shard, ch).wait_recv()
-        both = grad_part(shard, y, ch)[...].astype(jnp.float32) + y_buf[shard, span].astype(
-            jnp.float32
-        )
+        span = span_of(ch)
+        both = y_sum(shard, ch)
 
         @pl.when(more(shard))
         def _():
@@ -1476,7 +1667,55 @@
 
         z_copy(shard, ch).start()
 
-    send_out(0)
+    def finish(ch):
+        span = span_of(ch)
+        s_buf[z, span] = low(y_sum(z, ch))
+
+        @pl.when(z > 0)
+        def _():
+            z_wait(z, ch)
+            s_buf[z, span] = low(
+                s_buf[z, span].astype(jnp.float32) + z_buf[z, span].astype(jnp.float32)
+            )
+
+        @pl.when(z < 3)
+        def _():
+            z_wait(4, ch)
+            s_buf[z, span] = low(
+                s_buf[z, span].astype(jnp.float32) + z_buf[4, span].astype(jnp.float32)
+            )
+
+        if not last:
+            all_ref[span] = s_buf[z, span]
+            return
+
+        @pl.when(c != layer)
+        def _():
+            owner_copy(ch).start()
+
+        @pl.when(c == layer)
+        def _():
+            all_part(quarter, y, ch)[...] = s_buf[z, span]
+            spread(layer, ch)
+
+    def pass_on(ch):
+        if not last:
+            return
+
+        @pl.when(c == layer)
+        def _():
+            owner_copy(ch).wait_recv()
+            spread(1 - layer, ch)
+
+    def relay(ch):
+        if not last:
+            return
+
+        @pl.when(c == layer)
+        def _():
+            for who in (layer, 1 - layer):
+                ya_copy(who, ch).wait_recv()
+                relay_copy(who, ch).start()
 
     def summed(which):
         rows = rows_at(which * block, block)
@@ -1485,9 +1724,25 @@
     n_core_copy().wait_recv()
     n_send[...] = low(summed(1 - x))
     n_x_copy().start()
-    for ch in range(CHUNKS):
-        send_in(0, ch)
-    send_out(1)
+    send_in(0, 0)
+    send_in(0, 1)
+    send_in(1, 0)
+    send_in(1, 1)
+    yo_copy().wait()
+    yo_mine[...] = low(out_grad_ref[...].astype(jnp.float32) + yo_buf[...].astype(jnp.float32))
+
+    if last:
+
+        @pl.when(c != layer)
+        def _():
+            owner_out_copy().start()
+
+        @pl.when(c == layer)
+        def _():
+            out_part(quarter)[...] = yo_mine[...]
+
+    else:
+        out_all_ref[...] = yo_mine[...]
 
     n_x_copy().wait_recv()
     normed_grad = summed(x) + n_across[...].astype(jnp.float32)
@@ -1496,222 +1751,249 @@
     hat = entering * inv
     hat_grad = normed_grad * gain_ref[...]
     mean = jnp.mean(hat_grad * hat, axis=-1, keepdims=True)
-    n_done[...] = low(incoming_ref[...].astype(jnp.float32) + inv * (hat_grad - hat * mean))
-    for m in range(MICRO):
-        there = lax.div(z, 2) == m
-
-        @pl.when(there & jnp.logical_not(at_home))
+    source_grad = low(incoming_ref[...].astype(jnp.float32) + inv * (hat_grad - hat * mean))
+    norm_grad = jnp.sum(normed_grad * hat, axis=0, keepdims=True)
+    if last:
+        n_done[...] = source_grad
+        go_home()
+        small_totals(0, quarter, small_refs[0], norm_grad, tiny_mine)
+        small_totals(1, quarter, small_refs[1], extra_ref[...], tiny_mine)
+        t1_copy().start()
+    else:
+        g_ref[...] = source_grad
+        g_gather.begin(source_grad)
+        norm_ref[...] = norm_grad
+        dots = jnp.sum(source_grad.astype(jnp.float32) * extra_ref[...], axis=1, keepdims=True)
+        flat = [
+            jnp.broadcast_to(dots[i * LANES : (i + 1) * LANES], (LANES, LANES)).T[:1]
+            for i in range(block // LANES)
+        ]
+        flat.append(jnp.zeros((8 - len(flat), LANES), jnp.float32))
+        dot_gather.begin(jnp.concatenate(flat, axis=0))
+        r_core_copy().wait_recv()
+        r_send[...] = low(r_summed(1 - x))
+        r_x_copy().start()
+
+    send_in(2, 0)
+    send_in(2, 1)
+    send_in(0, 2)
+    finish(0)
+    if last:
+
+        @pl.when(c == layer)
         def _():
-            home_copy(m).start()
-
-        @pl.when(there & at_home)
+            owner_out_copy().wait_recv()
+            for who in range(CORES):
+                xo_copy(who).start()
+
+        t1_copy().wait_recv()
+        t1_sum[...] = tiny_mine[c] + t1_buf[...]
+        for away in (1, 2, 3):
+            t2_copy(away).start()
+    else:
+        g_gather.middle()
+        dot_gather.middle()
+    send_in(1, 2)
+    finish(1)
+    pass_on(0)
+    send_in(2, 2)
+    send_in(0, 3)
+    pass_on(1)
+    if last:
+        for away in (1, 2, 3):
+            t2_copy(away).wait_recv()
+        t2_sum[...] = (t1_sum[...] + t2_buf[0]) + (t2_buf[1] + t2_buf[2])
+        for i in range(3):
+            t3_copy(i).start()
+    else:
+        r_x_copy().wait_recv()
+        product = r_summed(x) + r_across[...].astype(jnp.float32)
+        n_done[...] = low(entering + r_inv_ref[...] * product)
+        go_home()
+    send_in(1, 3)
+    finish(2)
+    relay(0)
+    send_in(2, 3)
+    pass_on(2)
+    relay(1)
+    finish(3)
+    pass_on(3)
+    relay(2)
+    relay(3)
+
+    if last:
+
+        @pl.when(c == layer)
         def _():
-            bound_ref[m] = n_done[...]
-
-    norm_grad = jnp.sum(normed_grad * hat, axis=0, keepdims=True)
-    tiny_mine[...] = tiny_ref[...]
-    for zz in range(4):
-        for row in range(3):
-            at = (3 * zz + row) * LANES
-            tiny_mine[0, zz, row : row + 1] += norm_grad[:, at : at + LANES]
-    t1_copy().start()
-
-    @pl.when(c == 1)
-    def _():
-        for ch in range(CHUNKS):
-            late_copy(ch).wait_recv()
+            for ch in chunks:
+                for who in range(CORES):
+                    x_copy(who, ch).wait()
+                    ya_copy(who, ch).wait_send()
+                    relay_copy(who, ch).wait()
             for who in range(CORES):
-                x_copy(who, ch).start()
-        late_out_copy().wait_recv()
-        for who in range(CORES):
-            xo_copy(who).start()
-
-    for ch in range(CHUNKS):
-        send_in(1, ch)
-    send_out(2)
-
-    t1_copy().wait_recv()
-    t1_sum[...] = tiny_mine[c] + t1_buf[...]
-    for away in (1, 2, 3):
-        t2_copy(away).start()
-    for ch in range(CHUNKS):
-        send_in(2, ch)
-
-    @pl.when(c == 1)
-    def _():
-        for ch in range(CHUNKS):
-            for who in range(CORES):
-                ya_copy(who, ch).start()
-
-    yo_mine[...] = low(own_out(z))
-
-    @pl.when(z > 0)
-    def _():
-        zo_wait(z)
-        yo_mine[...] = low(own_out(z) + zo_buf[z].astype(jnp.float32))
-
-    @pl.when(z < 3)
-    def _():
-        zo_wait(4)
-        yo_mine[...] = low(yo_mine[...].astype(jnp.float32) + zo_buf[4].astype(jnp.float32))
-
-    yo_copy().start()
-    for away in (1, 2, 3):
-        t2_copy(away).wait_recv()
-    t2_sum[...] = (t1_sum[z] + t2_buf[0]) + (t2_buf[1] + t2_buf[2])
-    for i in range(3):
-        t3_copy(i).start()
-
-    for ch in range(CHUNKS):
-        span = pl.ds(ch * part, part)
-        y_copy(z, ch).wait_recv()
-        s_buf[z, span] = low(
-            grad_part(z, y, ch)[...].astype(jnp.float32) + y_buf[z, span].astype(jnp.float32)
-        )
-
-        @pl.when(z > 0)
+                xo_copy(who).wait()
+
+        @pl.when(c != layer)
         def _():
-            z_wait(z, ch)
-            s_buf[z, span] = low(
-                s_buf[z, span].astype(jnp.float32) + z_buf[z, span].astype(jnp.float32)
-            )
-
-        @pl.when(z < 3)
-        def _():
-            z_wait(4, ch)
-            s_buf[z, span] = low(
-                s_buf[z, span].astype(jnp.float32) + z_buf[4, span].astype(jnp.float32)
-            )
-
-        @pl.when(c == 1)
-        def _():
-            z_buf[4, span] = s_buf[z, span]
-            first_copy(ch).start()
-
-        @pl.when(c == 0)
-        def _():
-            all_part(quarter, y, ch)[...] = s_buf[z, span]
-            spread(0, ch)
-            first_copy(ch).wait_recv()
-            spread(1, ch)
-
-    yo_copy().wait()
-    total = low(yo_mine[...].astype(jnp.float32) + yo_buf[...].astype(jnp.float32))
-
-    @pl.when(c == 0)
-    def _():
-        out_part(quarter)[...] = total
-
-    @pl.when(c == 1)
-    def _():
-        yo_mine[...] = total
-        first_out_copy().start()
-
-    @pl.when(c == 0)
-    def _():
-        first_out_copy().wait_recv()
-        for who in range(CORES):
-            xo_copy(who).start()
-
-    for i in range(3):
-        t3_copy(i).wait_recv()
-    tiny_out_ref[...] = (t2_sum[...] + t3_buf[0]) + (t3_buf[1] + t3_buf[2])
-
-    for ch in range(CHUNKS):
-        for who in range(CORES):
-            ya_copy(who, ch).wait_recv()
-            relay_copy(who, ch).start()
-    for ch in range(CHUNKS):
-        for who in range(CORES):
-            x_copy(who, ch).wait()
-            ya_copy(who, ch).wait_send()
-            relay_copy(who, ch).wait()
-    for who in range(CORES):
-        xo_copy(who).wait()
-    n_core_copy().wait_send()
-    n_x_copy().wait_send()
+            for i, (xx, yy) in enumerate(((x, y), (1 - x, y), (x, 1 - y), (1 - x, 1 - y))):
+                for who in range(CORES):
+                    for ch in chunks:
+                        all_part(2 * xx + who, yy, ch)[...] = late_refs[i][who, span_of(ch)]
+            for i, xx in enumerate((x, 1 - x)):
+                for who in range(CORES):
+                    out_part(2 * xx + who)[...] = late_out_refs[i][who]
+
+    if last:
+        for i in range(3):
+            t3_copy(i).wait_recv()
+        t1_buf[...] = (t2_sum[...] + t3_buf[0]) + (t3_buf[1] + t3_buf[2])
+        own_totals(z, t1_buf, total_refs)
+
+        t1_copy().wait_send()
+        for away in (1, 2, 3):
+            t2_copy(away).wait_send()
+        for i in range(3):
+            t3_copy(i).wait_send()
+    else:
+        g_gather.end()
+        dot_gather.end()
+        r_core_copy().wait_send()
+        r_x_copy().wait_send()
 
     @pl.when(jnp.logical_not(at_home))
     def _():
         home_copy(0).wait_send()
 
     for m in range(MICRO):
-        own = (lax.rem(z, 2) == 0) & (z == 2 * m + x) & (x == lax.div(z, 2))
-
-        @pl.when((c == 0) & jnp.logical_not(own))
+
+        @pl.when((c == layer) & jnp.logical_not(guest_self[m]))
         def _():
             home_copy(m).wait_recv()
 
-    t1_copy().wait_send()
-    for away in (1, 2, 3):
-        t2_copy(away).wait_send()
+    n_core_copy().wait_send()
+    n_x_copy().wait_send()
     for i in range(3):
-        t3_copy(i).wait_send()
-        zo_copy(shard_at(i)).wait_send()
-        for ch in range(CHUNKS):
+        for ch in chunks:
             z_copy(shard_at(i), ch).wait_send()
     for i in range(4):
-        for ch in range(CHUNKS):
+        for ch in chunks[2:]:
             y_copy(shard_at(i), ch).wait_send()
 
-    @pl.when(c == 0)
-    def _():
-        for ch in range(CHUNKS):
-            late_copy(ch).wait_send()
-        late_out_copy().wait_send()
-
-    @pl.when(c == 1)
-    def _():
-        for ch in range(CHUNKS):
-            first_copy(ch).wait_send()
-        first_out_copy().wait_send()
-
-
-def finish_sums(grad, out_grad, late, late_out, tiny, theirs, mine, entering, incoming, gain):
+    if last:
+
+        @pl.when(c != layer)
+        def _():
+            for ch in chunks:
+                owner_copy(ch).wait_send()
+            owner_out_copy().wait_send()
+
+
+def small_totals(layer, quarter, refs, norm_grad, tiny):
+    conv_ref, gain_ref, head_ref = refs
+    width, group = DI // GROUP, DI // 16
+    lane = iota((8, width), 1)
+    wide = jnp.where(iota((8, width), 0) == 5, jnp.broadcast_to(gain_ref[0:1], (8, width)), conv_ref[:, :width])
+    for zz in range(4):
+        moved = turn_by(wide, group, [(k - zz) % GROUP for k in range(GROUP)], quarter)
+        tiny[layer, :, zz * width : (zz + 1) * width] = jnp.where(
+            lax.div(lane, group) == quarter, moved, 0.0
+        )
+    tiny[layer, :, DI:] = conv_ref[:, width:]
+    tiny[layer, 6:7, :D] = norm_grad
+    per = H // 16
+    given, head = iota((LANES, LANES), 0), iota((LANES, LANES), 1)
+    taken = (lax.rem(lax.div(head, per), 4) == quarter) & (head < H)
+    taken = taken & (given == lax.div(head, 4 * per) * per + lax.rem(head, per))
+    heads = exact(head_ref[...], jnp.where(taken, 1.0, 0.0))
+    for row in range(3):
+        tiny[layer, 6:7, D + row * LANES : D + (row + 1) * LANES] = heads[row : row + 1]
+
+
+def own_totals(z, whole, refs):
+    norm_ref, taps_ref, bias_ref, *head_refs, gain_ref = refs
+    piece = CONV // 4
+    taps = turn_by(whole[...], piece, [(4 - k) % 4 for k in range(4)], z)
+    taps_ref[...] = taps[0:KW, :piece]
+    bias_ref[...] = taps[KW : KW + 1, :piece]
+    width = DI // 4
+    gain_ref[...] = whole[:, pl.ds(pl.multiple_of(z * width, LANES), width)][5:6]
+    norm_ref[...] = whole[:, pl.ds(pl.multiple_of(z * LANE_PART, LANES), LANE_PART)][6:7]
+    per = H // 4
+    for row, ref in enumerate(head_refs):
+        heads = whole[:, D + row * LANES : D + (row + 1) * LANES]
+        heads = turn_by(heads, 1, [(LANES - k * per) % LANES for k in range(4)], z)
+        ref[...] = heads[6:7, :per]
+
+
+def layer_sums(layer, gate, grad, out_grad, theirs, mine, entering, incoming, gain, extra, *more):
     dma = pltpu.SemaphoreType.DMA
+    inside = pl.BlockSpec(memory_space=pltpu.VMEM)
     span = (HALF, LANE_PART)
     out = (OUT_PART, D)
-    small = tiny.shape[2:]
-    two = (CORES, CHUNKS)
+    steps = len(STEPS)
+    two = (CORES, steps)
+    rows = entering.shape
+    half, whole = jnp.bfloat16, jnp.float32
+    last = layer == 0
+    out_shape = [
+        jax.ShapeDtypeStruct((GROUP, LOCAL, LANE_PART) if last else span, half),
+        jax.ShapeDtypeStruct((DI // GROUP, D) if last else out, half),
+        jax.ShapeDtypeStruct((MICRO,) + rows, half),
+    ]
+    scratch = [
+        pltpu.VMEM(theirs.shape, half),
+        pltpu.VMEM(rows, half),
+        pltpu.VMEM(rows, half),
+        pltpu.VMEM(rows, half),
+        pltpu.VMEM((4,) + span, half),
+        pltpu.VMEM((5,) + span, half),
+        pltpu.VMEM((4,) + span, half),
+        pltpu.VMEM(out, half),
+        pltpu.VMEM(out, half),
+        dma((4, steps)), dma((4, steps)), dma((4, steps)), dma((5, steps)), dma((2,)),
+        dma((steps + 1,)), dma((steps + 1,)),
+        dma(two), dma(two), dma(two), dma(two), dma(two), dma(two),
+        dma((CORES,)), dma((CORES,)), dma((4,)),
+    ]
+    if layer == 0:
+        small = (8, CONV)
+        piece = CONV // 4
+        shapes = ((1, LANE_PART), (KW, piece), (1, piece)) + ((1, H // 4),) * 3 + ((1, DI // 4),)
+        out_shape += [jax.ShapeDtypeStruct(shape, whole) for shape in shapes]
+        scratch += [
+            pltpu.VMEM((CORES,) + small, whole),
+            pltpu.VMEM(small, whole),
+            pltpu.VMEM(small, whole),
+            pltpu.VMEM((3,) + small, whole),
+            pltpu.VMEM(small, whole),
+            pltpu.VMEM((3,) + small, whole),
+            dma((7,)), dma((7,)), dma((1,)), dma((MICRO,)),
+        ]
+    else:
+        out_shape += [
+            jax.ShapeDtypeStruct(rows, half),
+            jax.ShapeDtypeStruct((GROUP * rows[0], D), half),
+            jax.ShapeDtypeStruct((GROUP, 8, LANES), whole),
+            jax.ShapeDtypeStruct((1, D), whole),
+        ]
+        out_shape += [jax.ShapeDtypeStruct((8, LANES), whole)] * 3
+        scratch += [
+            pltpu.VMEM(theirs.shape, half),
+            pltpu.VMEM(rows, half),
+            pltpu.VMEM(rows, half),
+            dma((3,)), dma((3,)), dma((3,)), dma((3,)), dma((4,)), dma((1,)), dma((MICRO,)),
+        ]
     return pl.pallas_call(
-        finish_kernel,
-        in_specs=[pl.BlockSpec(memory_space=pltpu.VMEM)] * 10,
-        out_specs=[pl.BlockSpec(memory_space=pltpu.VMEM)] * 4,
-        out_shape=[
-            jax.ShapeDtypeStruct((GROUP, LOCAL, LANE_PART), jnp.bfloat16),
-            jax.ShapeDtypeStruct((DI // GROUP, D), jnp.bfloat16),
-            jax.ShapeDtypeStruct(small, jnp.float32),
-            jax.ShapeDtypeStruct((MICRO,) + entering.shape, jnp.bfloat16),
-        ],
-        scratch_shapes=[
-            pltpu.VMEM(theirs.shape, jnp.bfloat16),
-            pltpu.VMEM(entering.shape, jnp.bfloat16),
-            pltpu.VMEM(entering.shape, jnp.bfloat16),
-            pltpu.VMEM(entering.shape, jnp.bfloat16),
-            pltpu.VMEM(tiny.shape, jnp.float32),
-            pltpu.VMEM((4,) + span, jnp.bfloat16),
-            pltpu.VMEM((5,) + span, jnp.bfloat16),
-            pltpu.VMEM((4,) + span, jnp.bfloat16),
-            pltpu.VMEM((5,) + out, jnp.bfloat16),
-            pltpu.VMEM((4,) + out, jnp.bfloat16),
-            pltpu.VMEM(out, jnp.bfloat16),
-            pltpu.VMEM(out, jnp.bfloat16),
-            pltpu.VMEM((4,) + small, jnp.float32),
-            pltpu.VMEM((4,) + small, jnp.float32),
-            pltpu.VMEM((3,) + small, jnp.float32),
-            pltpu.VMEM(small, jnp.float32),
-            pltpu.VMEM((3,) + small, jnp.float32),
-            dma((4, CHUNKS)), dma((4, CHUNKS)), dma((4, CHUNKS)), dma((5, CHUNKS)),
-            dma((4,)), dma((5,)), dma((2,)),
-            dma((CHUNKS + 1,)), dma((CHUNKS + 1,)),
-            dma(two), dma(two), dma(two), dma(two), dma(two), dma(two),
-            dma((CORES,)), dma((CORES,)), dma((7,)), dma((7,)), dma((4,)), dma((1,)), dma((MICRO,)),
-        ],
+        functools.partial(sum_kernel, layer),
+        in_specs=[inside] * (9 + len(more)),
+        out_specs=[inside] * 10,
+        out_shape=out_shape,
+        scratch_shapes=scratch,
         compiler_params=pltpu.CompilerParams(
-            collective_id=2, has_side_effects=True, vmem_limit_bytes=VMEM_BYTES
+            collective_id=2 + layer, has_side_effects=True, vmem_limit_bytes=VMEM_BYTES
         ),
-        name="finish_sums",
-    )(grad, out_grad, late, late_out, tiny, theirs, mine, entering, incoming, gain)
+        name="layer_sums",
+    )(gate, grad, out_grad, theirs, mine, entering, incoming, gain, extra, *more)
 
 
 def assemble_kernel(part_ref, shared_ref, total_ref):
@@ -1782,22 +2064,14 @@
     straight = [(spot(*p), home(p[0], p[1], p[2])) for p in places]
     crossed = [(spot(*p), home(1 - p[0], p[1], p[2])) for p in places]
 
-    def go_back(value, cc):
-        ways = []
-        for m in range(MICRO):
-            pairs = [(home(m, zz, rr), spot(cc, zz, rr)) for zz in range(4) for rr in range(4)]
-            ways.append(lax.ppermute(value, axes, pairs))
-        return ways
-
     params = (norm_gain, conv_weight, conv_bias, dt_bias, a_log, d_skip, out_gain)
-    count = sum(p.size for p in params)
-    filler = -count % LANES
-    flat = jnp.concatenate(
-        [p.reshape(-1) for p in params] + [jnp.zeros((-count % (16 * LANES),), jnp.bfloat16)]
-    )
+    lanes = -(-conv_bias.shape[1] // LANES) * LANES
+    given = (conv_weight[0], conv_bias, out_gain, norm_gain, dt_bias, a_log, d_skip)
+    flat = [jnp.pad(p, ((0, 0), (0, lanes - p.shape[1]))) for p in given]
+    flat = jnp.concatenate(flat + [jnp.zeros((6, lanes), jnp.bfloat16)], axis=0)
     in_rows = jnp.swapaxes(in_weight[0], 0, 1)
-    w_in0, w_out0, source, normed0, flat = enter_first(
-        in_rows, out_weight[0], boundary_in, flat.reshape((-1, LANES))
+    w_in0, w_out0, source, normed0, small, norms = enter_first(
+        in_rows, out_weight[0], boundary_in, flat
     )
     late_in = after(boundary_in, source)[0, :, 0]
     arrive_a = lax.ppermute(lax.dynamic_index_in_dim(late_in, c, 0, False), axes, straight)
@@ -1824,69 +2098,6 @@
     marks = jnp.stack(columns + [jnp.zeros((rows,), jnp.float32)] * 2, axis=1)
     seg_row = segment.astype(jnp.float32)[None]
 
-    flat = flat.reshape((CORES, 4, -1)).astype(jnp.float32)
-
-    given = jnp.arange(SHARED - 2 * N + 16)[:, None]
-    local = jnp.arange(LANES)[None, :]
-    picked = (given % 12 // 3 == quarter) & (local == given // 12 * 3 + given % 3) & (given < H)
-    picked = low(picked.astype(jnp.float32))
-
-    def layer_params(layer):
-        found = []
-        at = 0
-        for p in params:
-            part = flat[layer, :, at : at + p.size].reshape((4,) + p.shape[1:])
-            at += p.size
-            found.append(jnp.moveaxis(part, 0, -2).reshape(p.shape[1:-1] + (-1,)))
-        gain, conv_w, conv_b, dt_b, log_a, skip, gain_out = found
-
-        def spread(v):
-            return jnp.pad(pick_last(v, quarter), (0, LANES - heads))[None]
-
-        def taps(v):
-            return jnp.concatenate([pick_last(v[:, :DI], quarter), v[:, DI:]], axis=1)
-
-        return {
-            "norm": gain,
-            "conv_w": taps(conv_w),
-            "conv_b": taps(conv_b[None]),
-            "dt_bias": spread(dt_b),
-            "rate": spread(jnp.exp(log_a)),
-            "pick": picked,
-            "skip": jnp.repeat(pick_last(skip, quarter), P_SIZE)[None],
-            "gain": pick_last(gain_out, quarter)[None],
-        }
-
-    small = [layer_params(0), layer_params(1)]
-
-    def group_rows(v):
-        count = v.shape[0]
-        near = swap_x(v)
-        other = swap_core(v)
-        far = swap_core(near)
-        whole = jnp.zeros((GROUP * count,) + v.shape[1:], v.dtype)
-        for part, at in (
-            (v, 2 * x + c),
-            (other, 2 * x + 1 - c),
-            (near, 2 * (1 - x) + c),
-            (far, 2 * (1 - x) + 1 - c),
-        ):
-            whole = lax.dynamic_update_slice_in_dim(whole, part, at * count, 0)
-        return whole
-
-    def group_parts(left, product):
-        blocks = left.reshape((2, 2, block) + left.shape[1:])
-        theirs = lax.dynamic_index_in_dim(blocks, 1 - c, 1, False)
-        theirs = low(product(theirs.reshape((2 * block,) + left.shape[1:])))
-        mine = lax.dynamic_index_in_dim(blocks, c, 1, False)
-        return theirs, product(mine.reshape((2 * block,) + left.shape[1:]))
-
-    def group_sum(parts):
-        theirs, mine = parts
-        both = (mine + swap_core(theirs).astype(jnp.float32)).reshape((2, block, -1))
-        across = swap_x(low(lax.dynamic_index_in_dim(both, 1 - x, 0, False)))
-        return lax.dynamic_index_in_dim(both, x, 0, False) + across.astype(jnp.float32)
-
     def own(v):
         return lax.dynamic_slice_in_dim(v, (2 * x + c) * block, block, 0)
 
@@ -1895,107 +2106,92 @@
         return v + swap_x(v)
 
     def forward(layer, normed, w_in):
-        projected = low(mm(normed, w_in, 1, 1))
-        gg, squares, mixer, starts = mixer_forward(projected, marks, seg_row, small[layer])
+        projected = projection(normed, w_in)
+        gg, squares, mixer, starts = mixer_forward(layer, projected, marks, seg_row, small)
         return gg, squares.reshape((rows // LANES, LANES)), (normed, projected, mixer, starts)
 
     def inverse(sums):
         return lax.rsqrt(sums / DI + EPSILON)
 
-    def backward(layer, kept, g, og, per_row):
-        normed, projected, mixer, starts = kept
-        pg, outgoing, wide, conv, head = mixer_backward(
-            projected, marks, seg_row, small[layer], mixer, starts, og, per_row, DI
+    def out_sum(gg, out_inv, g):
+        outgoing = low(gg.astype(jnp.float32) * out_inv)
+        grad = low(mm(outgoing, g, 0, 0)).reshape((4, OUT_PART, D))
+        return lax.psum_scatter(grad, "shard", scatter_dimension=0, tiled=False)
+
+    def backward(layer, kept, og, per_row, ready=(), sent_on=()):
+        normed, projected, out, starts = kept
+        gate_grad, out_grad, gains = gate_backward(
+            layer, projected, small, out, og, per_row, DI
         )
-        out_grad = low(mm(outgoing, g, 0, 0))
-        in_grad = low(mm(pg, normed, 0, 0))
-        taps = jnp.concatenate([place_last(conv[:5, :width], quarter), conv[:5, width:]], axis=1)
-        tiny = [
-            jnp.zeros((1, D), jnp.float32),
-            taps[:KW],
-            taps[KW:],
-            place_last(head[0:1, :heads], quarter),
-            place_last(head[1:2, :heads], quarter),
-            place_last(wide[1].reshape((1, heads, P_SIZE)).sum(axis=2), quarter),
-            place_last(wide[0:1], quarter),
-        ]
-        tiny = [jnp.moveaxis(t.reshape((t.shape[0], 4, -1)), 1, 0).reshape((4, -1)) for t in tiny]
-        tiny = jnp.concatenate(tiny + [jnp.zeros((4, filler), jnp.float32)], axis=1)
-        return pg, in_grad, out_grad, tiny
-
-    def scatter_in(grad):
-        parts = grad.reshape((2, HALF, D))
-        sent = swap_y(lax.dynamic_index_in_dim(parts, 1 - y, 0, False))
-        kept = lax.dynamic_index_in_dim(parts, y, 0, False)
-        both = low(kept.astype(jnp.float32) + sent.astype(jnp.float32))
-        both = jnp.stack([both[:, zz * LANE_PART : (zz + 1) * LANE_PART] for zz in range(4)])
-        return lax.psum_scatter(both, "shard", scatter_dimension=0, tiled=False)
-
-    def scatter_out(grad):
-        part = lax.psum_scatter(
-            grad.reshape((4, OUT_PART, D)), "shard", scatter_dimension=0, tiled=False
+        gate = low(mm(gate_grad, normed, 0, 0)).reshape((2, GATE_HALF, D))
+        sent = lax.dynamic_index_in_dim(gate, 1 - y, 0, False)
+        received = swap_y(sent)
+        gate = lax.dynamic_index_in_dim(gate, y, 0, False)
+        pg, conv, head = mixer_backward(
+            layer, projected, marks, seg_row, small, out, starts, out_grad, after(gate_grad, sent, *ready)
         )
-        return low(part.astype(jnp.float32) + swap_y(part).astype(jnp.float32))
+        pg = after(pg, *sent_on)
+        gate = low(gate.astype(jnp.float32) + received.astype(jnp.float32))
+        rest = low(mm(pg[:, GATE:], normed, 0, 0))
+        return pg, gate, rest, (conv, gains, head)
 
     gg0, squares0, kept0 = forward(0, normed0, w_in0)
-    theirs, mine = group_parts(gg0, lambda v: mm(v, w_out0))
+    theirs, mine = group_parts(c, gg0, w_out0)
     w_in1, w_out1, added0, middle, normed1, g1, out_inv0 = enter_second(
-        in_rows, out_weight[0], theirs, mine, squares0, source, small[1]["norm"][None], cotangent
+        in_rows, out_weight[0], theirs, mine, squares0, source, norms[1, 0:1], cotangent
     )
     out_inv0 = out_inv0.reshape((rows, 1))
     og1 = mm(g1, w_out1, 1, 1)
-    middle32 = middle.astype(jnp.float32)
     gg1, squares1, kept1 = forward(1, normed1, w_in1)
     dots1 = jnp.sum(gg1.astype(jnp.float32) * og1, axis=1).reshape((rows // LANES, LANES))
     sums1 = row_sums(jnp.stack([squares1, dots1]))
     out_inv1 = inverse(sums1[0]).reshape((rows, 1))
     per_row1 = jnp.concatenate([out_inv1, out_inv1 * sums1[1].reshape((rows, 1))], axis=1)
-    parts1 = group_parts(gg1, lambda v: mm(v, w_out1))
-    pg1, in_grad1, out_grad1, tiny1 = backward(1, kept1, g1, og1, per_row1)
-    result_ways = go_back(low(middle32 + own(out_inv1) * group_sum(parts1)), 1)
-
-    normed_grad = group_sum(group_parts(pg1, lambda v: mm(v, w_in1)))
-    inv = lax.rsqrt(jnp.mean(middle32 * middle32, axis=-1, keepdims=True) + EPSILON)
-    hat = middle32 * inv
-    hat_grad = normed_grad * small[1]["norm"]
-    mean = jnp.mean(hat_grad * hat, axis=-1, keepdims=True)
-    middle_grad = low(cotangent.astype(jnp.float32) + inv * (hat_grad - hat * mean))
-    norm_grad1 = jnp.sum(normed_grad * hat, axis=0).reshape((4, LANE_PART))
-    tiny1 = tiny1.at[:, :LANE_PART].add(norm_grad1)
-    out_part1 = scatter_out(out_grad1)
-    in_part1 = scatter_in(in_grad1)
-
-    dots0 = jnp.sum(middle_grad.astype(jnp.float32) * added0, axis=1).reshape((-1, LANES))
-    dots0 = group_rows(dots0).reshape((rows, 1))
-    g0 = group_rows(middle_grad)
+    out_theirs, out_mine = group_parts(c, gg1, w_out1)
+    out_part1 = out_sum(gg1, out_inv1, g1)
+    pg1, gate1, rest1, small_grads1 = backward(1, kept1, og1, per_row1)
+    theirs, mine = group_parts(c, pg1, w_in1)
+    in_sum1, out_sum1, results, middle_grad, g0, dots0, norm_grad1, *_ = layer_sums(
+        1, gate1, rest1, out_part1, theirs, mine, middle, cotangent, norms[1, 0:1], added0,
+        out_theirs, out_mine, own(out_inv1),
+    )
+    dots0 = dots0[:, : block // LANES].reshape((rows, 1))
+
+    def on_second(v, flip):
+        return lax.ppermute(v, ("section", "rep"), [(4 + i, 4 + (i ^ flip)) for i in range(4)])
+
+    def to_second(v):
+        return jnp.stack([lax.ppermute(v, "section", [(0, 1)]), v])
+
+    in_own, out_own = to_second(in_sum1), to_second(out_sum1)
+    in_near, in_across = on_second(in_own, 1), on_second(in_own, 2)
+    out_near = on_second(out_own, 1)
+    in_far = on_second(in_across, 1)
+
     og0 = mm(g0, w_out0, 1, 1)
+    out_part0 = out_sum(gg0, out_inv0, g0)
     per_row0 = jnp.concatenate([out_inv0, dots0], axis=1)
-    pg0, in_grad0, out_grad0, tiny0 = backward(0, kept0, g0, og0, per_row0)
-    theirs, mine = group_parts(pg0, lambda v: mm(v, w_in0))
-    tiny = jnp.stack([tiny0, tiny1]).reshape((CORES, 4, -1, LANES))
-    in_all, out_all, tiny, entry_grads = finish_sums(
-        in_grad0, out_grad0, in_part1, out_part1, tiny,
-        theirs, mine, source, middle_grad, small[0]["norm"][None],
+    pg0, gate0, rest0, small_grads0 = backward(
+        0, kept0, og0, per_row0, (in_own, out_own), (in_near, in_across, out_near)
+    )
+    theirs, mine = group_parts(c, pg0, w_in0)
+    in_all, out_all, entry_grads, *totals = layer_sums(
+        0, gate0, rest0, out_part0, theirs, mine, source, middle_grad, norms[0, 0:1], norm_grad1,
+        *small_grads0, *small_grads1, in_own, in_near, in_across, in_far, out_own, out_near,
     )
     in_total = jnp.swapaxes(assemble_rows(in_all), 0, 1)[None]
     out_total = out_all.astype(jnp.float32)[None]
-    tiny = tiny.reshape(-1)
 
     boundary = jnp.stack(
-        [jnp.where(c == 0, entry_grads[m], result_ways[m]) for m in range(MICRO)]
+        [jnp.where(c == 0, entry_grads[m], results[m]) for m in range(MICRO)]
     ).astype(jnp.float32)[None, :, None]
 
-    totals = []
-    at = 0
-    for p in params:
-        totals.append(tiny[at : at + p.size].reshape(p.shape))
-        at += p.size
     norm_total, conv_total, bias_total, dt_total, log_total, skip_total, gain_total = totals
     return (
         boundary,
         norm_total,
         in_total,
-        conv_total,
+        conv_total[None],
         bias_total,
         dt_total,
         log_total,

time: 810 us -> 748 us (0.923)
  Pallas kernels: 509 us -> 618 us
  matrix products: 102 us -> 45.7 us
  local copies, waits for them, and re-layouts: 64 us -> 18.6 us
  waiting for transfers between devices: 46.8 us -> 2.45 us
  other arithmetic: 35.5 us -> 17.9 us
    pallas_call x3 -> x12, Pallas kernels: 256 us -> 377 us  [the longest x2 248 us: layer_sums(): pl.pallas_call(functools.partial(sum_kernel, layer), in_specs=[inside] *...]
    dot_general x16 -> x8, matrix products: 102 us -> 45.7 us  [mm(): lax.dot_general(a, b, (((da,), (db,)), ((), ())), preferred_element_type=...]
    ppermute x6 -> x2, waiting for transfers between devices: 34.9 us -> 0.01 us  [swap_x(): return lax.ppermute(v, 'rep', [(i, i ^ 1) for i in range(4)])]
    pallas_call x1, Pallas kernels: 117 us -> 94.5 us  [enter_second(): pl.pallas_call(enter_second_kernel, in_specs=[anywhere] * 2 + [inside] *...]
    pallas_call x1, Pallas kernels: 95.9 us -> 108 us  [enter_first(): pl.pallas_call(enter_first_kernel, in_specs=[anywhere] * 3 + [inside], ou...]
    dynamic_slice x10 -> x0, local copies, waits for them, and re-layouts: 10.4 us -> none  [the longest x2 5.28 us: group_parts(): mine = lax.dynamic_index_in_dim(blocks, c, 1, False)]
    ppermute x2, waiting for transfers between devices: 10.2 us -> 0.01 us  [swap_y(): return lax.ppermute(v, 'rep', [(i, i ^ 2) for i in range(4)])]
    slice x23 -> x1, local copies, waits for them, and re-layouts: 9.49 us -> 0.72 us  [per_device_split(): dots0 = dots0[:, :block // LANES].reshape((rows, 1))]
  transfers between devices with their start and end apart: 21 -> 15, of which waited for: 7 -> 2; matrix products, arithmetic and copies ran while one was open for 22% -> 7% of each run, Pallas kernels for 47% -> 32%
where the time goes in v3:
time: 748 us; the launch traced here: 740 us
  Pallas kernels  618 us (83%)
  matrix products  45.7 us (6%)
  starting transfers between devices  21.9 us (3%)
  local copies, waits for them, and re-layouts  18.6 us (2%)
  other arithmetic  17.9 us (2%)
  between operations  14.9 us (2%)
    pallas_call x2, Pallas kernels, layer_sums(): pl.pallas_call(functools.partial(sum_kernel, layer), in_specs=[inside] *...  248 us
    pallas_call x1, Pallas kernels, enter_first(): pl.pallas_call(enter_first_kernel, in_specs=[anywhere] * 3 + [inside], ou...  108 us
    pallas_call x1, Pallas kernels, enter_second(): pl.pallas_call(enter_second_kernel, in_specs=[anywhere] * 2 + [inside] *...  94.5 us
    pallas_call x2, Pallas kernels, mixer_backward(): pl.pallas_call(functools.partial(backward_kernel, width), grid=(chunks,),...  54.3 us
    dot_general x8, matrix products, mm(): lax.dot_general(a, b, (((da,), (db,)), ((), ())), preferred_element_type=...  45.7 us
    pallas_call x4, Pallas kernels, group_parts(): pl.pallas_call(product_kernel, grid_spec=pltpu.PrefetchScalarGridSpec(num...  38.7 us
    pallas_call x2, Pallas kernels, mixer_forward(): pl.pallas_call(functools.partial(forward_kernel, width), grid=(chunks,),...  30.5 us
    pallas_call x2, Pallas kernels, projection(): pl.pallas_call(projection_kernel, grid=(4,), in_specs=[pl.BlockSpec((bloc...  22.3 us
  transfers between devices with their start and end apart: 15, of which 2 were waited for; matrix products, arithmetic and copies ran while one was open for 7% of the time, Pallas kernels for 32%

profile of v3, /device:TPU:16, one launch (start us, length us, event | category | flops | bytes accessed | tf_op | source)
XLA Modules:
  0.0 739.5 jit_solution(3569836166913971374)
XLA Ops:
  15.5 107.7 %enter_first.1 = (bf16[1856,1536]{1,0:T(8,128)(2,1)}, bf16[768,1536]{1,0:T(8,128)(2,1)}, bf16[256,1536]{1,0:T(8,128)(2,1)}, bf16[1024,1536]{1,0:T(8,128)(2,1)}, ...) custom-call(bf16[6448,384]{1,0:T(8,128)(2,1)} %bitcast.82, bf16[768,1536]{1,0:T(8,128)(2,1)} %bitcast.85, ...), custom_call_target="tpu_custom_call" | custom-call | tf_op jit(solution)/shard_map/enter_first/pallas_call | solution.py:1275
  123.3 4.7 collective-permute-start.2
  128.0 4.3 collective-permute-start.1
  133.8 11.2 %projection.2.proj_ref.rim_ref = bf16[1024,1856]{1,0:T(8,128)(2,1)} custom-call(bf16[1024,1536]{1,0:T(8,128)(2,1)} %get-tuple-element.72.left_ref, bf16[1856,1536]{1,0:T(8,128)(2,1)} %get-tuple-element.73.weight_ref), custom_call_target="tpu_custom_call" | custom-call | flops 6600000000 | tf_op jit(solution)/shard_map/projection/pallas_call | solution.py:788
  147.2 15.1 %mixer_forward.2 = (bf16[1024,768]{1,0:T(8,128)(2,1)}, f32[1024,1]{1,0:T(8,128)}, f32[1024,768]{1,0:T(8,128)}, f32[8,128,768]{2,1,0:T(8,128)}) custom-call(bf16[1024,1856]{1,0:T(8,128)(2,1)} %projection.2.proj_ref.rim_ref, f32[1024,8]{1,0:T(8,128)} %copy.52.marks_ref, f32[1,1024]{1,0:T(1,128)} %bitcast.120, f32[2,16,1024]{2,1,0:T(8,128)} %get-tuple-element.74.small_ref), custom_call_target="tpu_custom_call" | custom-call | flops 17600000000 | tf_op jit(solution)/shard_map/mixer_forward/pallas_call | solution.py:812
  162.4 1.8 reduce
  164.2 7.2 group_parts.4
  172.4 94.5 %enter_second.1 = (bf16[1856,1536]{1,0:T(8,128)(2,1)}, bf16[768,1536]{1,0:T(8,128)(2,1)}, f32[256,1536]{1,0:T(8,128)}, bf16[256,1536]{1,0:T(8,128)(2,1)}, bf16[1...) custom-call(bf16[6448,384]{1,0:T(8,128)(2,1)} %bitcast.83, bf16[768,1536]{1,0:T(8,128)(2,1)} %bitcast.86, ...), custom_call_target="tpu_custom_call" | custom-call | tf_op jit(solution)/shard_map/enter_second/pallas_call | solution.py:1388
  266.9 11.2 %projection.3.proj_ref.rim_ref = bf16[1024,1856]{1,0:T(8,128)(2,1)} custom-call(bf16[1024,1536]{1,0:T(8,128)(2,1)} %get-tuple-element.84.left_ref, bf16[1856,1536]{1,0:T(8,128)(2,1)} %get-tuple-element.85.weight_ref), custom_call_target="tpu_custom_call" | custom-call | flops 6600000000 | tf_op jit(solution)/shard_map/projection/pallas_call | solution.py:788
  278.0 15.4 %mixer_forward.3 = (bf16[1024,768]{1,0:T(8,128)(2,1)}, f32[1024,1]{1,0:T(8,128)}, f32[1024,768]{1,0:T(8,128)}, f32[8,128,768]{2,1,0:T(8,128)}) custom-call(bf16[1024,1856]{1,0:T(8,128)(2,1)} %projection.3.proj_ref.rim_ref, f32[1024,8]{1,0:T(8,128)} %copy.52.marks_ref, f32[1,1024]{1,0:T(1,128)} %bitcast.121, f32[2,16,1024]{2,1,0:T(8,128)} %get-tuple-element.74.small_ref), custom_call_target="tpu_custom_call" | custom-call | flops 17600000000 | tf_op jit(solution)/shard_map/mixer_forward/pallas_call | solution.py:812
  294.7 6.0 fusion
  301.9 7.2 group_parts.6
  310.2 6.9 gate_backward.2
  317.1 4.5 convolution_convert_fusion.5
  323.2 4.1 convolution_convert_fusion.4
  328.3 27.1 %mixer_backward.2 = (bf16[1024,1856]{1,0:T(8,128)(2,1)}, f32[8,1024]{1,0:T(8,128)}, f32[8,128]{1,0:T(8,128)}) custom-call(bf16[1024,1856]{1,0:T(8,128)(2,1)} %projection.3.proj_ref.rim_ref, bf16[1024,1856]{1,0:T(8,128)(2,1)} %projection.3.proj_ref.rim_ref, f32[1024,8]{1,0:T(8,128)} %copy.52.marks_ref, f32[1,1024]{1,0:T(1,128)} %bitcast.122, ...), custom_call_target="tpu_custom_call" | custom-call | flops 36300001280 | tf_op jit(solution)/shard_map/mixer_backward/pallas_call | solution.py:852
  355.5 12.2 %group_parts.5 = (bf16[512,1536]{1,0:T(8,128)(2,1)}, f32[512,1536]{1,0:T(8,128)}) custom-call(s32[1]{0:T(128)} %bitcast.18.place_ref, bf16[1024,1856]{1,0:T(8,128)(2,1)} %get-tuple-element.95.left_ref, bf16[1856,1536]{1,0:T(8,128)(2,1)} %get-tuple-element.85.weight_ref), custom_call_target="tpu_custom_call" | custom-call | flops 6600000000 | tf_op jit(solution)/shard_map/group_parts/pallas_call | solution.py:757
  367.7 6.8 convolution_convert_fusion.1.refs_1_
  374.5 2.6 fusion.4.refs_0_
  378.3 114.2 %layer_sums.2 = (bf16[928,384]{1,0:T(8,128)(2,1)}, bf16[192,1536]{1,0:T(8,128)(2,1)}, bf16[2,256,1536]{2,1,0:T(8,128)(2,1)}, bf16[256,1536]{1,0:T(8,128)(2,1)}, ...) custom-call(bf16[384,1536]{1,0:T(8,128)(2,1)} %fusion.4.refs_0_, ...), custom_call_target="tpu_custom_call" | custom-call | tf_op jit(solution)/shard_map/layer_sums/pallas_call | solution.py:1986
  497.3 7.1 fusion.21.og_ref
  504.3 4.1 convolution_convert_fusion.2
  508.5 6.7 gate_backward.3
  515.2 5.1 convolution_convert_fusion.3
  527.7 27.2 %mixer_backward.3 = (bf16[1024,1856]{1,0:T(8,128)(2,1)}, f32[8,1024]{1,0:T(8,128)}, f32[8,128]{1,0:T(8,128)}) custom-call(bf16[1024,1856]{1,0:T(8,128)(2,1)} %projection.2.proj_ref.rim_ref, bf16[1024,1856]{1,0:T(8,128)(2,1)} %projection.2.proj_ref.rim_ref, f32[1024,8]{1,0:T(8,128)} %copy.52.marks_ref, f32[1,1024]{1,0:T(1,128)} %bitcast.123, ...), custom_call_target="tpu_custom_call" | custom-call | flops 36300001280 | tf_op jit(solution)/shard_map/mixer_backward/pallas_call | solution.py:852
  554.9 2.6 fusion.3.refs_0_
  558.5 12.0 %group_parts.7 = (bf16[512,1536]{1,0:T(8,128)(2,1)}, f32[512,1536]{1,0:T(8,128)}) custom-call(s32[1]{0:T(128)} %bitcast.18.place_ref, bf16[1024,1856]{1,0:T(8,128)(2,1)} %get-tuple-element.112.left_ref, bf16[1856,1536]{1,0:T(8,128)(2,1)} %get-tuple-element.73.weight_ref), custom_call_target="tpu_custom_call" | custom-call | flops 6600000000 | tf_op jit(solution)/shard_map/group_parts/pallas_call | solution.py:757
  570.5 8.0 %convolution_convert_fusion.refs_1_ = bf16[1088,1536]{1,0:T(8,128)(2,1)} fusion(bf16[1024,1536]{1,0:T(8,128)(2,1)} %get-tuple-element.72.left_ref, bf16[1024,1856]{1,0:T(8,128)(2,1)} %get-tuple-element.112.left_ref), kind=kOutput, calls=%fused_computation | convolution fusion | flops 3424223232 | bytes 8847360 | tf_op jit(solution)/shard_map/dot_general | solution.py:424
  579.6 133.7 %layer_sums.3 = (bf16[4,1856,384]{2,1,0:T(8,128)(2,1)}, bf16[768,1536]{1,0:T(8,128)(2,1)}, bf16[2,256,1536]{2,1,0:T(8,128)(2,1)}, f32[1,384]{1,0:T(1,128)}, f32[...) custom-call(bf16[384,1536]{1,0:T(8,128)(2,1)} %fusion.3.refs_0_, ...), custom_call_target="tpu_custom_call" | custom-call | tf_op jit(solution)/shard_map/layer_sums/pallas_call | solution.py:1986
  713.3 4.5 bitcast_convert_fusion
  717.8 8.5 %assemble_rows.1 = f32[6448,384]{1,0:T(8,128)} custom-call(bf16[4,1856,384]{2,1,0:T(8,128)(2,1)} %get-tuple-element.126.part_ref.shared_ref, bf16[4,1856,384]{2,1,0:T(8,128)(2,1)} %get-tuple-element.126.part_ref.shared_ref), custom_call_target="tpu_custom_call" | custom-call | tf_op jit(solution)/shard_map/assemble_rows/pallas_call | solution.py:2017
  726.5 1.9 maximum_convert_fusion
  (134 shorter events, 38.5 us)
Async XLA Ops:
  7.2 371.2 %reduce-scatter.3.cloned.1.call-start = ((), (), s32[]{:S(2)}) async-start(), calls=%async_computation.2 | async-start | bytes 2949120 | tf_op jit(solution)/shard_map/reduce_scatter | solution.py:2119
  7.9 137.1 %collective-permute-start = (s32[2,2,4]{2,1,0:T(2,128)S(1)}, s32[2,2,4]{2,1,0:T(2,128)S(1)}, u32[]{:S(2)}, u32[]{:S(2)}) collective-permute-start(s32[2,2,4]{2,1,0:T(2,128)S(1)} %pad_add_fusion), channel_id=1, source_target_pairs={{0,1},{1,0},{2,3},{3,2},{4,5},{5,4},{6,7},{7,6},{8,9},{9,8},{10,11... | collective-permute-start | bytes 200 | tf_op jit(solution)/shard_map/ppermute | solution.py:1422
  15.4 107.7 %copy-start = (bf16[1,2,1,256,1536]{4,3,2,1,0:T(8,128)(2,1)S(1)}, bf16[1,2,1,256,1536]{4,3,2,1,0:T(8,128)(2,1)}, u32[]{:S(2)}) copy-start(bf16[1,2,1,256,1536]{4,3,2,1,0:T(8,128)(2,1)} %blocks_ref.1) | copy-start | bytes 4718596
  123.3 48.0 %collective-permute-start.2 = (bf16[256,1536]{1,0:T(8,128)(2,1)S(1)}, bf16[256,1536]{1,0:T(8,128)(2,1)S(1)}, u32[]{:S(2)}, u32[]{:S(2)}) collective-permute-start(bf16[256,1536]{1,0:T(8,128)(2,1)S(1)} %get-tuple-element.142), channel_id=1, source_target_pairs={{0,0},{1,4},{2,2},{3,6},{4,16},{5,20},{6,18},{7,22},{8,1},{9,5},{1... | collective-permute-start | bytes 2359304 | tf_op jit(solution)/shard_map/ppermute | solution.py:2077
  128.0 43.3 %collective-permute-start.1 = (bf16[256,1536]{1,0:T(8,128)(2,1)S(1)}, bf16[256,1536]{1,0:T(8,128)(2,1)S(1)}, u32[]{:S(2)}, u32[]{:S(2)}) collective-permute-start(bf16[256,1536]{1,0:T(8,128)(2,1)S(1)} %get-tuple-element.143), channel_id=1, source_target_pairs={{0,8},{1,12},{2,10},{3,14},{4,24},{5,28},{6,26},{7,30},{8,9},{9,13... | collective-permute-start | bytes 2359304 | tf_op jit(solution)/shard_map/ppermute | solution.py:2078
  133.8 11.2 %copy-start.10 = (s32[2,1,4]{2,1,0:T(1,128)S(1)}, s32[2,1,4]{2,1,0:T(1,128)}, u32[]{:S(2)}) copy-start(s32[2,1,4]{2,1,0:T(1,128)} %param.14) | copy-start | bytes 100
  133.8 11.2 %copy-start.11 = (s32[2,1,4]{2,1,0:T(1,128)S(1)}, s32[2,1,4]{2,1,0:T(1,128)}, u32[]{:S(2)}) copy-start(s32[2,1,4]{2,1,0:T(1,128)} %param.13) | copy-start | bytes 100
  278.0 16.7 %copy-start.18 = (bf16[1024,1536]{1,0:T(8,128)(2,1)S(1)}, bf16[1024,1536]{1,0:T(8,128)(2,1)}, u32[]{:S(2)}) copy-start(bf16[1024,1536]{1,0:T(8,128)(2,1)} %get-tuple-element.87) | copy-start | bytes 9437188
  300.7 1.2 collective-permute-start.3
  301.9 7.2 collective-permute-start.4
  310.2 6.9 copy-start.16
  317.1 6.1 copy-start.19
  321.7 52.8 %collective-permute-start.5 = (bf16[384,1536]{1,0:T(8,128)(2,1)S(1)}, bf16[384,1536]{1,0:T(8,128)(2,1)}, u32[]{:S(2)}, u32[]{:S(2)}) collective-permute-start(bf16[384,1536]{1,0:T(8,128)(2,1)S(1)} %dynamic-slice_bitcast_fusion.1), channel_id=1, source_target_pairs={{0,2},{1,3},{2,0},{3,1},{4,6},{5,7},{6,4},{7,5},{8,10},{9,11},{10,... | collective-permute-start | bytes 3538952 | tf_op jit(solution)/shard_map/ppermute | solution.py:1426
  327.3 251.2 %reduce-scatter.5.cloned.1.call-start = ((), (), s32[]{:S(2)}) async-start(), calls=%async_computation.3 | async-start | bytes 2949120 | tf_op jit(solution)/shard_map/reduce_scatter | solution.py:2119
  355.5 12.3 %copy-start.17 = (bf16[1024,1536]{1,0:T(8,128)(2,1)S(1)}, bf16[1024,1536]{1,0:T(8,128)(2,1)}, u32[]{:S(2)}) copy-start(bf16[1024,1536]{1,0:T(8,128)(2,1)} %get-tuple-element.84.left_ref) | copy-start | bytes 9437188
  378.3 115.0 %copy-start.12 = (f32[8,128]{1,0:T(8,128)S(1)}, f32[8,128]{1,0:T(8,128)}, u32[]{:S(2)}) copy-start(f32[8,128]{1,0:T(8,128)} %get-tuple-element.103) | copy-start | bytes 12292
  494.4 28.7 %collective-permute-start.8 = (bf16[192,1536]{1,0:T(8,128)(2,1)}, bf16[192,1536]{1,0:T(8,128)(2,1)S(1)}, u32[]{:S(2)}, u32[]{:S(2)}) collective-permute-start(bf16[192,1536]{1,0:T(8,128)(2,1)} %get-tuple-element.109), channel_id=1, source_target_pairs={{0,16},{1,17},{2,18},{3,19},{4,20},{5,21},{6,22},{7,23},{8,24},{9,... | collective-permute-start | bytes 1769480 | tf_op jit(solution)/shard_map/ppermute | solution.py:2164
  495.7 29.3 %collective-permute-start.7 = (bf16[928,384]{1,0:T(8,128)(2,1)}, bf16[928,384]{1,0:T(8,128)(2,1)S(1)}, u32[]{:S(2)}, u32[]{:S(2)}) collective-permute-start(bf16[928,384]{1,0:T(8,128)(2,1)} %get-tuple-element.108), channel_id=1, source_target_pairs={{0,16},{1,17},{2,18},{3,19},{4,20},{5,21},{6,22},{7,23},{8,24},{9,... | collective-permute-start | bytes 2138120 | tf_op jit(solution)/shard_map/ppermute | solution.py:2164
  497.3 7.1 copy-start.20
  497.3 7.1 copy-start.25
  521.6 33.3 %collective-permute-start.6 = (bf16[384,1536]{1,0:T(8,128)(2,1)}, bf16[384,1536]{1,0:T(8,128)(2,1)}, u32[]{:S(2)}, u32[]{:S(2)}) collective-permute-start(bf16[384,1536]{1,0:T(8,128)(2,1)} %dynamic-slice_bitcast_fusion), channel_id=1, source_target_pairs={{0,2},{1,3},{2,0},{3,1},{4,6},{5,7},{6,4},{7,5},{8,10},{9,11},{10,... | collective-permute-start | bytes 3538952 | tf_op jit(solution)/shard_map/ppermute | solution.py:1426
  523.2 31.6 %copy-start.2 = (bf16[2,192,1536]{2,1,0:T(8,128)(2,1)}, bf16[2,192,1536]{2,1,0:T(8,128)(2,1)S(1)}, u32[]{:S(2)}) copy-start(bf16[2,192,1536]{2,1,0:T(8,128)(2,1)S(1)} %pad_maximum_fusion.1.refs_19_) | copy-start | bytes 3538948
  523.2 34.2 %collective-permute-start.11 = (bf16[2,192,1536]{2,1,0:T(8,128)(2,1)S(1)}, bf16[2,192,1536]{2,1,0:T(8,128)(2,1)}, u32[]{:S(2)}, u32[]{:S(2)}) collective-permute-start(bf16[2,192,1536]{2,1,0:T(8,128)(2,1)S(1)} %pad_maximum_fusion.1.refs_19_), channel_id=1, source_target_pairs={{16,17},{17,16},{18,19},{19,18},{20,21},{21,20},{22,23},{23,22},{2... | collective-permute-start | bytes 3538952 | tf_op jit(solution)/shard_map/ppermute | solution.py:2161
  525.1 29.7 %copy-start.1 = (bf16[2,928,384]{2,1,0:T(8,128)(2,1)}, bf16[2,928,384]{2,1,0:T(8,128)(2,1)S(1)}, u32[]{:S(2)}) copy-start(bf16[2,928,384]{2,1,0:T(8,128)(2,1)S(1)} %pad_maximum_fusion.refs_15_) | copy-start | bytes 4276228
  525.1 32.3 %collective-permute-start.10 = (bf16[2,928,384]{2,1,0:T(8,128)(2,1)S(1)}, bf16[2,928,384]{2,1,0:T(8,128)(2,1)S(1)}, u32[]{:S(2)}, u32[]{:S(2)}) collective-permute-start(bf16[2,928,384]{2,1,0:T(8,128)(2,1)S(1)} %pad_maximum_fusion.refs_15_), channel_id=1, source_target_pairs={{16,18},{17,19},{18,16},{19,17},{20,22},{21,23},{22,20},{23,21},{2... | collective-permute-start | bytes 4276232 | tf_op jit(solution)/shard_map/ppermute | solution.py:2161
  525.9 31.5 %collective-permute-start.9 = (bf16[2,928,384]{2,1,0:T(8,128)(2,1)S(1)}, bf16[2,928,384]{2,1,0:T(8,128)(2,1)}, u32[]{:S(2)}, u32[]{:S(2)}) collective-permute-start(bf16[2,928,384]{2,1,0:T(8,128)(2,1)S(1)} %pad_maximum_fusion.refs_15_), channel_id=1, source_target_pairs={{16,17},{17,16},{18,19},{19,18},{20,21},{21,20},{22,23},{23,22},{2... | collective-permute-start | bytes 4276232 | tf_op jit(solution)/shard_map/ppermute | solution.py:2161
  557.4 13.1 %copy-start.5 = (bf16[2,928,384]{2,1,0:T(8,128)(2,1)}, bf16[2,928,384]{2,1,0:T(8,128)(2,1)S(1)}, u32[]{:S(2)}) copy-start(bf16[2,928,384]{2,1,0:T(8,128)(2,1)S(1)} %collective-permute-done.10.refs_17_) | copy-start | bytes 4276228
  557.5 21.1 %collective-permute-start.12 = (bf16[2,928,384]{2,1,0:T(8,128)(2,1)S(1)}, bf16[2,928,384]{2,1,0:T(8,128)(2,1)S(1)}, u32[]{:S(2)}, u32[]{:S(2)}) collective-permute-start(bf16[2,928,384]{2,1,0:T(8,128)(2,1)S(1)} %collective-permute-done.10.refs_17_), channel_id=1, source_target_pairs={{16,17},{17,16},{18,19},{19,18},{20,21},{21,20},{22,23},{23,22},{2... | collective-permute-start | bytes 4276232 | tf_op jit(solution)/shard_map/ppermute | solution.py:2161
  717.8 8.5 %copy-start.3 = (bf16[2,256,1536]{2,1,0:T(8,128)(2,1)S(1)}, bf16[2,256,1536]{2,1,0:T(8,128)(2,1)}, u32[]{:S(2)}) copy-start(bf16[2,256,1536]{2,1,0:T(8,128)(2,1)} %get-tuple-element.124) | copy-start | bytes 4718596
  717.8 8.5 %copy-start.4 = (bf16[2,256,1536]{2,1,0:T(8,128)(2,1)S(1)}, bf16[2,256,1536]{2,1,0:T(8,128)(2,1)}, u32[]{:S(2)}) copy-start(bf16[2,256,1536]{2,1,0:T(8,128)(2,1)} %get-tuple-element.123) | copy-start | bytes 4718596
  726.5 4.7 copy-start.21
  726.5 5.2 copy-start.14
  (9 other events, 25.5 us)
Sparse Core Ops, SparseCore 0:
  327.4 50.8 reduce-scatter.2
  508.6 48.0 reduce-scatter.4

commit v4 on v3

--- a/solution.py
+++ b/solution.py
@@ -482,6 +482,10 @@
     return 1.0 / (1.0 + jnp.exp(-v))
 
 
+def gate_of(v):
+    return 0.5 * jnp.tanh(0.5 * v) + 0.5
+
+
 def head_picks():
     quarter = 2 * lax.rem(lax.axis_index("rep"), 2) + lax.axis_index("section")
     given, local = iota((64, LANES), 0), iota((64, LANES), 1)
@@ -510,7 +514,7 @@
     conv = conv_b
     for lag in range(KW):
         conv = conv + conv_w[KW - 1 - lag : KW - lag] * shifts[lag]
-    sig = sigmoid(conv)
+    sig = gate_of(conv)
     active = conv * sig
     stepped = raw + dt_bias
     step = softplus(stepped)
@@ -561,7 +565,7 @@
     )
     out = mixer + skip * heads
     mixer_ref[...] = out
-    gated = out * (gate * sigmoid(gate))
+    gated = out * (gate * gate_of(gate))
     squares_ref[...] = jnp.sum(gated * gated, axis=1, keepdims=True)
     gg_ref[...] = low(gated * gain)
 
@@ -576,7 +580,7 @@
     dots = rows_ref[:, 1:2]
     og = og_ref[...]
     out = out_ref[...]
-    gate_sig = sigmoid(gate)
+    gate_sig = gate_of(gate)
     gate_on = gate * gate_sig
     hat = out * gate_on * inv
     gated_grad = inv * (small_ref[0, 5:6, :width] * og - hat * (dots * (1.0 / whole_width)))
@@ -734,48 +738,44 @@
     return pl.BlockSpec(shape, lambda i: (0,) * len(shape))
 
 
-def product_kernel(place_ref, left_ref, weight_ref, theirs_ref, mine_ref):
-    turn = pl.program_id(0)
-    found = mm(left_ref[...], weight_ref[...])
-
-    @pl.when(turn < 2)
+def product_kernel(left_ref, weight_ref, theirs_ref, mine_ref, ordered_ref):
+    c = lax.axis_index("section")
+    block = left_ref.shape[0] // 4
+
+    @pl.when(pl.program_id(0) == 0)
     def _():
-        theirs_ref[...] = low(found)
-
-    @pl.when(turn >= 2)
-    def _():
-        mine_ref[...] = found
-
-
-def group_parts(c, left, weight):
+        for i in range(4):
+            at = 2 * (i % 2) + (1 - c if i < 2 else c)
+            rows = pl.ds(pl.multiple_of(at * block, block), block)
+            ordered_ref[i * block : (i + 1) * block] = left_ref[rows]
+
+    found = mm(ordered_ref[...], weight_ref[...])
+    theirs_ref[...] = low(found[: 2 * block])
+    mine_ref[...] = found[2 * block :]
+
+
+def group_parts(left, weight):
     rows, depth = left.shape
-    block, columns = rows // 4, weight.shape[1]
-
-    def left_at(i, at):
-        return (2 * lax.rem(i, 2) + jnp.where(i < 2, 1 - at[0], at[0]), 0)
-
+    columns = weight.shape[1]
+    step = columns // 3
+    half = rows // 2
     return pl.pallas_call(
         product_kernel,
-        grid_spec=pltpu.PrefetchScalarGridSpec(
-            num_scalar_prefetch=1,
-            grid=(4,),
-            in_specs=[
-                pl.BlockSpec((block, depth), left_at),
-                pl.BlockSpec((depth, columns), lambda i, at: (0, 0)),
-            ],
-            out_specs=[
-                pl.BlockSpec((block, columns), lambda i, at: (jnp.minimum(i, 1), 0)),
-                pl.BlockSpec((block, columns), lambda i, at: (jnp.maximum(i - 2, 0), 0)),
-            ],
-        ),
+        grid=(3,),
+        in_specs=[
+            pl.BlockSpec((rows, depth), lambda i: (0, 0)),
+            pl.BlockSpec((depth, step), lambda i: (0, i)),
+        ],
+        out_specs=[pl.BlockSpec((half, step), lambda i: (0, i))] * 2,
         out_shape=[
-            jax.ShapeDtypeStruct((2 * block, columns), jnp.bfloat16),
-            jax.ShapeDtypeStruct((2 * block, columns), jnp.float32),
+            jax.ShapeDtypeStruct((half, columns), jnp.bfloat16),
+            jax.ShapeDtypeStruct((half, columns), jnp.float32),
         ],
+        scratch_shapes=[pltpu.VMEM((rows, depth), jnp.bfloat16)],
         compiler_params=pltpu.CompilerParams(vmem_limit_bytes=VMEM_BYTES),
         cost_estimate=cost(6),
         name="group_parts",
-    )(c.reshape((1,)), left, weight)
+    )(left, weight)
 
 
 def projection_kernel(left_ref, weight_ref, out_ref):
@@ -784,15 +784,16 @@
 
 def projection(left, weight):
     rows, depth = left.shape
-    block, columns = rows // 4, weight.shape[0]
+    columns = weight.shape[0]
+    step = 640
     return pl.pallas_call(
         projection_kernel,
-        grid=(4,),
+        grid=(pl.cdiv(columns, step),),
         in_specs=[
-            pl.BlockSpec((block, depth), lambda i: (i, 0)),
-            pl.BlockSpec((columns, depth), lambda i: (0, 0)),
+            pl.BlockSpec((rows, depth), lambda i: (0, 0)),
+            pl.BlockSpec((step, depth), lambda i: (i, 0)),
         ],
-        out_specs=pl.BlockSpec((block, columns), lambda i: (i, 0)),
+        out_specs=pl.BlockSpec((rows, step), lambda i: (0, i)),
         out_shape=jax.ShapeDtypeStruct((rows, columns), jnp.bfloat16),
         compiler_params=pltpu.CompilerParams(vmem_limit_bytes=VMEM_BYTES),
         cost_estimate=cost(6),
@@ -1459,47 +1460,31 @@
         refs = refs[:9] + refs[12:]
     all_ref, out_all_ref, bound_ref = refs[9:12]
     (
-        n_core, n_send, n_across, n_done, y_buf, z_buf, s_buf, yo_buf, yo_mine,
+        n_core, n_send, n_across, y_buf, z_buf, s_buf, yo_buf, yo_mine,
         y_send, y_recv, z_send, z_recv, yo_sem, core_send, core_recv,
         x_send, x_recv, ya_send, ya_recv, relay_send, relay_recv, xo_send, xo_recv, n_sem,
-    ) = refs[19:44]
+    ) = refs[19:43]
     if last:
         total_refs = refs[12:19]
-        tiny_mine, t1_buf, t1_sum, t2_buf, t2_sum, t3_buf = refs[44:50]
-        t_send, t_recv, home_send, home_recv = refs[50:]
+        tiny_mine, t1_buf, t1_sum, t2_buf, t2_sum, t3_buf, g_mine, g_buf, g_sum, g_all = refs[43:53]
+        t_send, t_recv, g_send, g_recv = refs[53:]
     else:
         g_ref, g_all_ref, dots_ref, norm_ref = refs[12:16]
-        r_core, r_send, r_across = refs[44:47]
-        row_send, row_recv, dot_send, dot_recv, r_sem, home_send, home_recv = refs[47:]
+        r_core, r_send, r_across = refs[43:46]
+        row_send, row_recv, dot_send, dot_recv, r_sem = refs[46:]
     c, z, y, x = place()
     quarter = 2 * x + c
     core, x_other, y_other = {"section": 1 - c}, {"rep": 2 * y + 1 - x}, {"rep": 2 * (1 - y) + x}
     chunks = range(len(STEPS))
-    block = n_done.shape[0]
+    block = n_send.shape[0]
     copy = mesh_copy
 
-    home = {"section": layer, "shard": quarter, "rep": 2 * y + lax.rem(z, 2)}
-    at_home = (c == layer) & (z == quarter) & (x == lax.rem(z, 2))
-    guests = tuple(
-        {"section": lax.rem(z, 2), "shard": 2 * m + x, "rep": 2 * y + lax.div(z, 2)}
-        for m in range(MICRO)
-    )
-    guest_self = tuple(
-        (c == layer) & (lax.rem(z, 2) == layer) & (z == 2 * m + x) & (x == lax.div(z, 2))
-        for m in range(MICRO)
-    )
     reps = (x_other, y_other, {"rep": 2 * (1 - y) + 1 - x})
     shards = tuple({"shard": lax.rem(z + away, 4)} for away in (1, 2, 3))
     barrier = pltpu.get_barrier_semaphore()
     for device in (core,) + reps + shards:
         greet(barrier, device)
-    for m in range(MICRO):
-
-        @pl.when((c == layer) & jnp.logical_not(guest_self[m]))
-        def _():
-            greet(barrier, guests[m])
-
-    pl.semaphore_wait(barrier, 8 - at_home.astype(jnp.int32))
+    pl.semaphore_wait(barrier, 7)
 
     orders = ((3, 2, 1, 0), (3, 0, 2, 1), (0, 3, 1, 2), (0, 1, 2, 3))
 
@@ -1560,8 +1545,11 @@
         return copy(piece, piece, ya_send.at[who, ch], ya_recv.at[who, ch], y_other)
 
     def relay_copy(who, ch):
-        piece = all_part(2 * x + who, 1 - y, ch)
-        return copy(piece, piece, relay_send.at[who, ch], relay_recv.at[who, ch], x_other)
+        if who == 0:
+            piece = all_part(2 * x, 1 - y, ch)
+            return copy(piece, piece, relay_send.at[0, ch], relay_recv.at[0, ch], x_other)
+        piece = all_part(2 * (1 - x) + 1, y, ch)
+        return copy(piece, piece, relay_send.at[1, ch], relay_recv.at[1, ch], y_other)
 
     def xo_copy(who):
         piece = out_part(2 * x + who)
@@ -1590,21 +1578,6 @@
     def n_x_copy():
         return copy(n_send, n_across, n_sem.at[2], n_sem.at[3], x_other)
 
-    def home_copy(m):
-        return copy(n_done, bound_ref.at[m], home_send.at[0], home_recv.at[m], home)
-
-    def go_home():
-        for m in range(MICRO):
-            there = lax.div(z, 2) == m
-
-            @pl.when(there & jnp.logical_not(at_home))
-            def _():
-                home_copy(m).start()
-
-            @pl.when(there & at_home)
-            def _():
-                bound_ref[m] = n_done[...]
-
     if last:
 
         def t1_copy():
@@ -1618,6 +1591,15 @@
         def t3_copy(i):
             return copy(t2_sum, t3_buf.at[i], t_send.at[4 + i], t_recv.at[4 + i], reps[i])
 
+        def g1_copy():
+            return copy(g_mine, g_buf.at[0], g_send.at[0], g_recv.at[0], core)
+
+        def g2_copy(away):
+            return copy(g_sum, g_buf.at[away], g_send.at[away], g_recv.at[away], shards[away - 1])
+
+        def g3_copy(i):
+            return copy(g_all, g_buf.at[4 + i], g_send.at[4 + i], g_recv.at[4 + i], reps[i])
+
     else:
 
         def r_core_copy():
@@ -1636,10 +1618,11 @@
     n_core_copy().start()
     if not last:
         r_core_copy().start()
-    yo_copy().start()
     for ch in chunks[2:]:
         for i in range(4):
             y_copy(shard_at(i), ch).start()
+        if ch == 2:
+            yo_copy().start()
 
     def more(shard):
         return ((shard > z) & (z > 0)) | ((shard < z) & (z < 3))
@@ -1713,53 +1696,43 @@
 
         @pl.when(c == layer)
         def _():
-            for who in (layer, 1 - layer):
-                ya_copy(who, ch).wait_recv()
-                relay_copy(who, ch).start()
+            ya_copy(0, ch).wait_recv()
+            relay_copy(0, ch).start()
+            x_copy(1, ch).wait_recv()
+            relay_copy(1, ch).start()
 
     def summed(which):
         rows = rows_at(which * block, block)
         return mine_ref[rows] + n_core[rows].astype(jnp.float32)
 
-    n_core_copy().wait_recv()
-    n_send[...] = low(summed(1 - x))
-    n_x_copy().start()
-    send_in(0, 0)
-    send_in(0, 1)
-    send_in(1, 0)
-    send_in(1, 1)
-    yo_copy().wait()
-    yo_mine[...] = low(out_grad_ref[...].astype(jnp.float32) + yo_buf[...].astype(jnp.float32))
-
-    if last:
-
-        @pl.when(c != layer)
-        def _():
-            owner_out_copy().start()
-
-        @pl.when(c == layer)
-        def _():
-            out_part(quarter)[...] = yo_mine[...]
-
-    else:
-        out_all_ref[...] = yo_mine[...]
-
-    n_x_copy().wait_recv()
-    normed_grad = summed(x) + n_across[...].astype(jnp.float32)
-    entering = entering_ref[...].astype(jnp.float32)
-    inv = lax.rsqrt(jnp.mean(entering * entering, axis=-1, keepdims=True) + EPSILON)
-    hat = entering * inv
-    hat_grad = normed_grad * gain_ref[...]
-    mean = jnp.mean(hat_grad * hat, axis=-1, keepdims=True)
-    source_grad = low(incoming_ref[...].astype(jnp.float32) + inv * (hat_grad - hat * mean))
-    norm_grad = jnp.sum(normed_grad * hat, axis=0, keepdims=True)
-    if last:
-        n_done[...] = source_grad
-        go_home()
-        small_totals(0, quarter, small_refs[0], norm_grad, tiny_mine)
-        small_totals(1, quarter, small_refs[1], extra_ref[...], tiny_mine)
-        t1_copy().start()
-    else:
+    def start_across():
+        n_core_copy().wait_recv()
+        n_send[...] = low(summed(1 - x))
+        n_x_copy().start()
+
+    def norm_step():
+        n_x_copy().wait_recv()
+        if not last:
+            r_core_copy().wait_recv()
+            r_send[...] = low(r_summed(1 - x))
+            r_x_copy().start()
+        normed_grad = summed(x) + n_across[...].astype(jnp.float32)
+        entering = entering_ref[...].astype(jnp.float32)
+        inv = lax.rsqrt(jnp.mean(entering * entering, axis=-1, keepdims=True) + EPSILON)
+        hat = entering * inv
+        hat_grad = normed_grad * gain_ref[...]
+        mean = jnp.mean(hat_grad * hat, axis=-1, keepdims=True)
+        source_grad = low(incoming_ref[...].astype(jnp.float32) + inv * (hat_grad - hat * mean))
+        norm_grad = jnp.sum(normed_grad * hat, axis=0, keepdims=True)
+        if last:
+            bound_ref[...] = source_grad
+            g_mine[...] = jnp.broadcast_to(norm_grad, g_mine.shape)
+
+            @pl.when(c != layer)
+            def _():
+                g1_copy().start()
+
+            return
         g_ref[...] = source_grad
         g_gather.begin(source_grad)
         norm_ref[...] = norm_grad
@@ -1770,64 +1743,125 @@
         ]
         flat.append(jnp.zeros((8 - len(flat), LANES), jnp.float32))
         dot_gather.begin(jnp.concatenate(flat, axis=0))
-        r_core_copy().wait_recv()
-        r_send[...] = low(r_summed(1 - x))
-        r_x_copy().start()
-
-    send_in(2, 0)
-    send_in(2, 1)
-    send_in(0, 2)
-    finish(0)
-    if last:
-
+
+    def result_step():
+        r_x_copy().wait_recv()
+        product = r_summed(x) + r_across[...].astype(jnp.float32)
+        bound_ref[...] = low(entering_ref[...].astype(jnp.float32) + r_inv_ref[...] * product)
+
+    def out_step():
+        yo_copy().wait()
+        total = low(out_grad_ref[...].astype(jnp.float32) + yo_buf[...].astype(jnp.float32))
+        if not last:
+            out_all_ref[...] = total
+            return
+        yo_mine[...] = total
+
+        @pl.when(c != layer)
+        def _():
+            owner_out_copy().start()
+
+        @pl.when(c == layer)
+        def _():
+            out_part(quarter)[...] = yo_mine[...]
+
+    def out_across():
         @pl.when(c == layer)
         def _():
             owner_out_copy().wait_recv()
             for who in range(CORES):
                 xo_copy(who).start()
 
-        t1_copy().wait_recv()
-        t1_sum[...] = tiny_mine[c] + t1_buf[...]
-        for away in (1, 2, 3):
-            t2_copy(away).start()
+    def early_small():
+        if last:
+            small_totals(0, quarter, small_refs[0], None, tiny_mine)
+            small_totals(1, quarter, small_refs[1], extra_ref[...], tiny_mine)
+            t1_copy().start()
+
+    def small_along_z():
+        if last:
+            t1_copy().wait_recv()
+            t1_sum[...] = tiny_mine[c] + t1_buf[...]
+            for away in (1, 2, 3):
+                t2_copy(away).start()
+
+    def small_across():
+        if last:
+            for away in (1, 2, 3):
+                t2_copy(away).wait_recv()
+            t2_sum[...] = (t1_sum[...] + t2_buf[0]) + (t2_buf[1] + t2_buf[2])
+            for i in range(3):
+                t3_copy(i).start()
+
+    def gain_along_z():
+        @pl.when(c == layer)
+        def _():
+            g1_copy().wait_recv()
+            g_sum[...] = g_mine[...] + g_buf[0]
+            for away in (1, 2, 3):
+                g2_copy(away).start()
+
+    def gain_across():
+        @pl.when(c == layer)
+        def _():
+            for away in (1, 2, 3):
+                g2_copy(away).wait_recv()
+            g_all[...] = (g_sum[...] + g_buf[1]) + (g_buf[2] + g_buf[3])
+            for i in range(3):
+                g3_copy(i).start()
+
+    send_in(0, 0)
+    send_in(0, 1)
+    start_across()
+    early_small()
+    send_in(1, 0)
+    send_in(0, 2)
+    send_in(1, 1)
+    small_along_z()
+    send_in(2, 0)
+    send_in(1, 2)
+    send_in(2, 1)
+    finish(0)
+    small_across()
+    norm_step()
+    out_step()
+    send_in(2, 2)
+    finish(1)
+    if last:
+        out_across()
+    pass_on(0)
+    send_in(0, 3)
+    pass_on(1)
+    finish(2)
+    if last:
+        gain_along_z()
+        send_in(1, 3)
+        pass_on(2)
+        relay(0)
+        send_in(2, 3)
+        relay(1)
+        gain_across()
+        finish(3)
+        pass_on(3)
+        relay(2)
+        relay(3)
     else:
+        send_in(1, 3)
+        result_step()
+        send_in(2, 3)
         g_gather.middle()
         dot_gather.middle()
-    send_in(1, 2)
-    finish(1)
-    pass_on(0)
-    send_in(2, 2)
-    send_in(0, 3)
-    pass_on(1)
+        finish(3)
+
     if last:
-        for away in (1, 2, 3):
-            t2_copy(away).wait_recv()
-        t2_sum[...] = (t1_sum[...] + t2_buf[0]) + (t2_buf[1] + t2_buf[2])
-        for i in range(3):
-            t3_copy(i).start()
-    else:
-        r_x_copy().wait_recv()
-        product = r_summed(x) + r_across[...].astype(jnp.float32)
-        n_done[...] = low(entering + r_inv_ref[...] * product)
-        go_home()
-    send_in(1, 3)
-    finish(2)
-    relay(0)
-    send_in(2, 3)
-    pass_on(2)
-    relay(1)
-    finish(3)
-    pass_on(3)
-    relay(2)
-    relay(3)
-
-    if last:
 
         @pl.when(c == layer)
         def _():
             for ch in chunks:
+                x_copy(0, ch).wait_recv()
+                ya_copy(1, ch).wait_recv()
                 for who in range(CORES):
-                    x_copy(who, ch).wait()
+                    x_copy(who, ch).wait_send()
                     ya_copy(who, ch).wait_send()
                     relay_copy(who, ch).wait()
             for who in range(CORES):
@@ -1847,6 +1881,22 @@
         for i in range(3):
             t3_copy(i).wait_recv()
         t1_buf[...] = (t2_sum[...] + t3_buf[0]) + (t3_buf[1] + t3_buf[2])
+
+        @pl.when(c == layer)
+        def _():
+            for i in range(3):
+                g3_copy(i).wait_recv()
+            total = (g_all[...] + g_buf[4]) + (g_buf[5] + g_buf[6])
+            t1_buf[6:7, :D] = total[0:1]
+            for away in (1, 2, 3):
+                g2_copy(away).wait_send()
+            for i in range(3):
+                g3_copy(i).wait_send()
+
+        @pl.when(c != layer)
+        def _():
+            g1_copy().wait_send()
+
         own_totals(z, t1_buf, total_refs)
 
         t1_copy().wait_send()
@@ -1859,16 +1909,6 @@
         dot_gather.end()
         r_core_copy().wait_send()
         r_x_copy().wait_send()
-
-    @pl.when(jnp.logical_not(at_home))
-    def _():
-        home_copy(0).wait_send()
-
-    for m in range(MICRO):
-
-        @pl.when((c == layer) & jnp.logical_not(guest_self[m]))
-        def _():
-            home_copy(m).wait_recv()
 
     n_core_copy().wait_send()
     n_x_copy().wait_send()
@@ -1899,7 +1939,7 @@
             lax.div(lane, group) == quarter, moved, 0.0
         )
     tiny[layer, :, DI:] = conv_ref[:, width:]
-    tiny[layer, 6:7, :D] = norm_grad
+    tiny[layer, 6:7, :D] = jnp.zeros((1, D), jnp.float32) if norm_grad is None else norm_grad
     per = H // 16
     given, head = iota((LANES, LANES), 0), iota((LANES, LANES), 1)
     taken = (lax.rem(lax.div(head, per), 4) == quarter) & (head < H)
@@ -1938,11 +1978,10 @@
     out_shape = [
         jax.ShapeDtypeStruct((GROUP, LOCAL, LANE_PART) if last else span, half),
         jax.ShapeDtypeStruct((DI // GROUP, D) if last else out, half),
-        jax.ShapeDtypeStruct((MICRO,) + rows, half),
+        jax.ShapeDtypeStruct(rows, half),
     ]
     scratch = [
         pltpu.VMEM(theirs.shape, half),
-        pltpu.VMEM(rows, half),
         pltpu.VMEM(rows, half),
         pltpu.VMEM(rows, half),
         pltpu.VMEM((4,) + span, half),
@@ -1967,7 +2006,11 @@
             pltpu.VMEM((3,) + small, whole),
             pltpu.VMEM(small, whole),
             pltpu.VMEM((3,) + small, whole),
-            dma((7,)), dma((7,)), dma((1,)), dma((MICRO,)),
+            pltpu.VMEM((8, D), whole),
+            pltpu.VMEM((7, 8, D), whole),
+            pltpu.VMEM((8, D), whole),
+            pltpu.VMEM((8, D), whole),
+            dma((7,)), dma((7,)), dma((7,)), dma((7,)),
         ]
     else:
         out_shape += [
@@ -1981,7 +2024,7 @@
             pltpu.VMEM(theirs.shape, half),
             pltpu.VMEM(rows, half),
             pltpu.VMEM(rows, half),
-            dma((3,)), dma((3,)), dma((3,)), dma((3,)), dma((4,)), dma((1,)), dma((MICRO,)),
+            dma((3,)), dma((3,)), dma((3,)), dma((3,)), dma((4,)),
         ]
     return pl.pallas_call(
         functools.partial(sum_kernel, layer),
@@ -1996,36 +2039,49 @@
     )(gate, grad, out_grad, theirs, mine, entering, incoming, gain, extra, *more)
 
 
-def assemble_kernel(part_ref, shared_ref, total_ref):
-    last = pl.program_id(0) == 8
+def assemble_kernel(part_ref, shared_ref, out_ref, total_ref, out_total_ref):
+    turn = pl.program_id(0)
     step = DI // 16
 
-    @pl.when(last)
+    @pl.when(turn == 8)
     def _():
         shared = [shared_ref[i, :SHARED].astype(jnp.float32) for i in range(GROUP)]
         total_ref[:SHARED] = (shared[0] + shared[1]) + (shared[2] + shared[3])
 
-    @pl.when(jnp.logical_not(last))
+    @pl.when(turn < 8)
     def _():
         for i in range(GROUP):
             total_ref[i * step : (i + 1) * step] = part_ref[i].astype(jnp.float32)
-
-
-def assemble_rows(parts):
+        out_total_ref[0] = out_ref[...].astype(jnp.float32)
+
+
+def assemble_rows(parts, out):
     lanes = parts.shape[-1]
     step = DI // 16
+    some = out.shape[0] // 8
+
+    def near(i):
+        return jnp.minimum(i, 7)
+
     return pl.pallas_call(
         assemble_kernel,
         grid=(9,),
         in_specs=[
-            pl.BlockSpec((GROUP, step, lanes), lambda i: (0, jnp.minimum(i, 7), 0)),
+            pl.BlockSpec((GROUP, step, lanes), lambda i: (0, near(i), 0)),
             pl.BlockSpec((GROUP, 2 * step, lanes), lambda i: (0, 4, 0)),
+            pl.BlockSpec((some, out.shape[1]), lambda i: (near(i), 0)),
         ],
-        out_specs=pl.BlockSpec((GROUP * step, lanes), lambda i: (i, 0)),
-        out_shape=jax.ShapeDtypeStruct((DI + CONV + H, lanes), jnp.float32),
+        out_specs=[
+            pl.BlockSpec((GROUP * step, lanes), lambda i: (i, 0)),
+            pl.BlockSpec((1, some, out.shape[1]), lambda i: (0, near(i), 0)),
+        ],
+        out_shape=[
+            jax.ShapeDtypeStruct((DI + CONV + H, lanes), jnp.float32),
+            jax.ShapeDtypeStruct((1,) + out.shape, jnp.float32),
+        ],
         compiler_params=pltpu.CompilerParams(vmem_limit_bytes=VMEM_BYTES),
         name="assemble_rows",
-    )(parts, parts)
+    )(parts, parts, out)
 
 
 def per_device_split(
@@ -2059,10 +2115,7 @@
     def home(m, zz, rr):
         return spot(zz % 2, 2 * m + rr % 2, (rr // 2) * 2 + zz // 2)
 
-    places = [(cc, zz, rr) for cc in range(2) for zz in range(4) for rr in range(4)]
     axes = ("section", "shard", "rep")
-    straight = [(spot(*p), home(p[0], p[1], p[2])) for p in places]
-    crossed = [(spot(*p), home(1 - p[0], p[1], p[2])) for p in places]
 
     params = (norm_gain, conv_weight, conv_bias, dt_bias, a_log, d_skip, out_gain)
     lanes = -(-conv_bias.shape[1] // LANES) * LANES
@@ -2074,9 +2127,13 @@
         in_rows, out_weight[0], boundary_in, flat
     )
     late_in = after(boundary_in, source)[0, :, 0]
-    arrive_a = lax.ppermute(lax.dynamic_index_in_dim(late_in, c, 0, False), axes, straight)
-    arrive_b = lax.ppermute(lax.dynamic_index_in_dim(late_in, 1 - c, 0, False), axes, crossed)
-    cotangent = jnp.where(z < 2, arrive_b, arrive_a)
+    arrivals = [
+        lax.ppermute(
+            late_in[m], axes, [(spot(1, zz, rr), home(m, zz, rr)) for zz in range(4) for rr in range(4)]
+        )
+        for m in range(MICRO)
+    ]
+    cotangent = jnp.where(z < 2, *arrivals)
 
     order = jnp.stack([lengths[:, 0], seq_order[:, 0]])
     order = jnp.where(x == z % 2, order, swap_x(order))
@@ -2136,7 +2193,7 @@
         return pg, gate, rest, (conv, gains, head)
 
     gg0, squares0, kept0 = forward(0, normed0, w_in0)
-    theirs, mine = group_parts(c, gg0, w_out0)
+    theirs, mine = group_parts(gg0, w_out0)
     w_in1, w_out1, added0, middle, normed1, g1, out_inv0 = enter_second(
         in_rows, out_weight[0], theirs, mine, squares0, source, norms[1, 0:1], cotangent
     )
@@ -2147,11 +2204,11 @@
     sums1 = row_sums(jnp.stack([squares1, dots1]))
     out_inv1 = inverse(sums1[0]).reshape((rows, 1))
     per_row1 = jnp.concatenate([out_inv1, out_inv1 * sums1[1].reshape((rows, 1))], axis=1)
-    out_theirs, out_mine = group_parts(c, gg1, w_out1)
+    out_theirs, out_mine = group_parts(gg1, w_out1)
     out_part1 = out_sum(gg1, out_inv1, g1)
     pg1, gate1, rest1, small_grads1 = backward(1, kept1, og1, per_row1)
-    theirs, mine = group_parts(c, pg1, w_in1)
-    in_sum1, out_sum1, results, middle_grad, g0, dots0, norm_grad1, *_ = layer_sums(
+    theirs, mine = group_parts(pg1, w_in1)
+    in_sum1, out_sum1, result, middle_grad, g0, dots0, norm_grad1, *_ = layer_sums(
         1, gate1, rest1, out_part1, theirs, mine, middle, cotangent, norms[1, 0:1], added0,
         out_theirs, out_mine, own(out_inv1),
     )
@@ -2168,19 +2225,30 @@
     out_near = on_second(out_own, 1)
     in_far = on_second(in_across, 1)
 
+    def go_home(value, cc):
+        return [
+            lax.ppermute(
+                value, axes, [(home(m, zz, rr), spot(cc, zz, rr)) for zz in range(4) for rr in range(4)]
+            )
+            for m in range(MICRO)
+        ]
+
+    results = go_home(result, 1)
+
     og0 = mm(g0, w_out0, 1, 1)
-    out_part0 = out_sum(gg0, out_inv0, g0)
+    out_part0 = out_sum(gg0, out_inv0, after(g0, *results))
     per_row0 = jnp.concatenate([out_inv0, dots0], axis=1)
     pg0, gate0, rest0, small_grads0 = backward(
         0, kept0, og0, per_row0, (in_own, out_own), (in_near, in_across, out_near)
     )
-    theirs, mine = group_parts(c, pg0, w_in0)
-    in_all, out_all, entry_grads, *totals = layer_sums(
+    theirs, mine = group_parts(pg0, w_in0)
+    in_all, out_all, entry_grad, *totals = layer_sums(
         0, gate0, rest0, out_part0, theirs, mine, source, middle_grad, norms[0, 0:1], norm_grad1,
         *small_grads0, *small_grads1, in_own, in_near, in_across, in_far, out_own, out_near,
     )
-    in_total = jnp.swapaxes(assemble_rows(in_all), 0, 1)[None]
-    out_total = out_all.astype(jnp.float32)[None]
+    entry_grads = go_home(entry_grad, 0)
+    in_total, out_total = assemble_rows(in_all, out_all)
+    in_total = jnp.swapaxes(in_total, 0, 1)[None]
 
     boundary = jnp.stack(
         [jnp.where(c == 0, entry_grads[m], results[m]) for m in range(MICRO)]

time: 748 us -> 703 us (0.940)
  Pallas kernels: 618 us -> 544 us
  waiting for transfers between devices: 2.45 us -> 30.2 us
    pallas_call x2, Pallas kernels: 248 us -> 170 us  [layer_sums(): pl.pallas_call(functools.partial(sum_kernel, layer), in_specs=[inside] *...]
    ppermute x2 -> x6, waiting for transfers between devices: 0.01 us -> 26.7 us  [the longest x4 26.7 us: go_home(): lax.ppermute(value, axes, [(home(m, zz, rr), spot(cc, zz, rr)) for zz in...]
  transfers between devices with their start and end apart: 15 -> 19, of which waited for: 2 -> 5; matrix products, arithmetic and copies ran while one was open for 7% -> 8% of each run, Pallas kernels for 32% -> 35%
where the time goes in v4:
time: 703 us; the launch traced here: 691 us
  Pallas kernels  544 us (77%)
  matrix products  43.5 us (6%)
  waiting for transfers between devices  30.2 us (4%)
  starting transfers between devices  27.9 us (4%)
  local copies, waits for them, and re-layouts  17.3 us (2%)
  between operations  15 us (2%)
  other arithmetic  13.5 us (2%)
    pallas_call x2, Pallas kernels, layer_sums(): pl.pallas_call(functools.partial(sum_kernel, layer), in_specs=[inside] *...  170 us
    pallas_call x1, Pallas kernels, enter_first(): pl.pallas_call(enter_first_kernel, in_specs=[anywhere] * 3 + [inside], ou...  108 us
    pallas_call x1, Pallas kernels, enter_second(): pl.pallas_call(enter_second_kernel, in_specs=[anywhere] * 2 + [inside] *...  100 us
    pallas_call x2, Pallas kernels, mixer_backward(): pl.pallas_call(functools.partial(backward_kernel, width), grid=(chunks,),...  54.3 us
    dot_general x8, matrix products, mm(): lax.dot_general(a, b, (((da,), (db,)), ((), ())), preferred_element_type=...  43.5 us
    pallas_call x4, Pallas kernels, group_parts(): pl.pallas_call(product_kernel, grid=(3,), in_specs=[pl.BlockSpec((rows, d...  35 us
    pallas_call x2, Pallas kernels, mixer_forward(): pl.pallas_call(functools.partial(forward_kernel, width), grid=(chunks,),...  30.2 us
    ppermute x4, waiting for transfers between devices, go_home(): lax.ppermute(value, axes, [(home(m, zz, rr), spot(cc, zz, rr)) for zz in...  26.7 us
  transfers between devices with their start and end apart: 19, of which 5 were waited for; matrix products, arithmetic and copies ran while one was open for 8% of the time, Pallas kernels for 35%

profile of v4, /device:TPU:16, one launch (start us, length us, event | category | flops | bytes accessed | tf_op | source)
XLA Modules:
  0.0 691.4 jit_solution(11795283665443971075)
XLA Ops:
  15.5 107.7 %enter_first.1 = (bf16[1856,1536]{1,0:T(8,128)(2,1)}, bf16[768,1536]{1,0:T(8,128)(2,1)}, bf16[256,1536]{1,0:T(8,128)(2,1)}, bf16[1024,1536]{1,0:T(8,128)(2,1)}, ...) custom-call(bf16[6448,384]{1,0:T(8,128)(2,1)} %bitcast.78, bf16[768,1536]{1,0:T(8,128)(2,1)} %bitcast.80, ...), custom_call_target="tpu_custom_call" | custom-call | tf_op jit(solution)/shard_map/enter_first/pallas_call | solution.py:1276
  126.8 11.5 %projection.2.proj_ref.rim_ref = bf16[1024,1856]{1,0:T(8,128)(2,1)} custom-call(bf16[1024,1536]{1,0:T(8,128)(2,1)} %get-tuple-element.75.left_ref, bf16[1856,1536]{1,0:T(8,128)(2,1)} %get-tuple-element.76.weight_ref), custom_call_target="tpu_custom_call" | custom-call | flops 6600000000 | tf_op jit(solution)/shard_map/projection/pallas_call | solution.py:789
  140.6 15.0 %mixer_forward.2 = (bf16[1024,768]{1,0:T(8,128)(2,1)}, f32[1024,1]{1,0:T(8,128)}, f32[1024,768]{1,0:T(8,128)}, f32[8,128,768]{2,1,0:T(8,128)}) custom-call(bf16[1024,1856]{1,0:T(8,128)(2,1)} %projection.2.proj_ref.rim_ref, f32[1024,8]{1,0:T(8,128)} %copy.52.marks_ref, f32[1,1024]{1,0:T(1,128)} %bitcast.115, f32[2,16,1024]{2,1,0:T(8,128)} %get-tuple-element.77.small_ref), custom_call_target="tpu_custom_call" | custom-call | flops 17600000000 | tf_op jit(solution)/shard_map/mixer_forward/pallas_call | solution.py:813
  157.4 6.3 group_parts.4
  164.7 100.0 %enter_second.1 = (bf16[1856,1536]{1,0:T(8,128)(2,1)}, bf16[768,1536]{1,0:T(8,128)(2,1)}, f32[256,1536]{1,0:T(8,128)}, bf16[256,1536]{1,0:T(8,128)(2,1)}, bf16[1...) custom-call(bf16[6448,384]{1,0:T(8,128)(2,1)} %bitcast.79, bf16[768,1536]{1,0:T(8,128)(2,1)} %bitcast.81, ...), custom_call_target="tpu_custom_call" | custom-call | tf_op jit(solution)/shard_map/enter_second/pallas_call | solution.py:1389
  264.7 11.5 %projection.3.proj_ref.rim_ref = bf16[1024,1856]{1,0:T(8,128)(2,1)} custom-call(bf16[1024,1536]{1,0:T(8,128)(2,1)} %get-tuple-element.87.left_ref, bf16[1856,1536]{1,0:T(8,128)(2,1)} %get-tuple-element.88.weight_ref), custom_call_target="tpu_custom_call" | custom-call | flops 6600000000 | tf_op jit(solution)/shard_map/projection/pallas_call | solution.py:789
  276.2 15.3 %mixer_forward.3 = (bf16[1024,768]{1,0:T(8,128)(2,1)}, f32[1024,1]{1,0:T(8,128)}, f32[1024,768]{1,0:T(8,128)}, f32[8,128,768]{2,1,0:T(8,128)}) custom-call(bf16[1024,1856]{1,0:T(8,128)(2,1)} %projection.3.proj_ref.rim_ref, f32[1024,8]{1,0:T(8,128)} %copy.52.marks_ref, f32[1,1024]{1,0:T(1,128)} %bitcast.116, f32[2,16,1024]{2,1,0:T(8,128)} %get-tuple-element.77.small_ref), custom_call_target="tpu_custom_call" | custom-call | flops 17600000000 | tf_op jit(solution)/shard_map/mixer_forward/pallas_call | solution.py:813
  292.7 6.0 fusion
  301.5 6.4 group_parts.6
  309.0 6.8 gate_backward.2
  315.8 4.5 convolution_convert_fusion.5
  321.9 4.1 convolution_convert_fusion.4
  327.1 27.1 %mixer_backward.2 = (bf16[1024,1856]{1,0:T(8,128)(2,1)}, f32[8,1024]{1,0:T(8,128)}, f32[8,128]{1,0:T(8,128)}) custom-call(bf16[1024,1856]{1,0:T(8,128)(2,1)} %projection.3.proj_ref.rim_ref, bf16[1024,1856]{1,0:T(8,128)(2,1)} %projection.3.proj_ref.rim_ref, f32[1024,8]{1,0:T(8,128)} %copy.52.marks_ref, f32[1,1024]{1,0:T(1,128)} %bitcast.117, ...), custom_call_target="tpu_custom_call" | custom-call | flops 36300001280 | tf_op jit(solution)/shard_map/mixer_backward/pallas_call | solution.py:853
  354.2 11.3 %group_parts.5 = (bf16[512,1536]{1,0:T(8,128)(2,1)}, f32[512,1536]{1,0:T(8,128)}) custom-call(bf16[1024,1856]{1,0:T(8,128)(2,1)} %get-tuple-element.98.left_ref, bf16[1856,1536]{1,0:T(8,128)(2,1)} %get-tuple-element.88.weight_ref), custom_call_target="tpu_custom_call" | custom-call | flops 6600000000 | tf_op jit(solution)/shard_map/group_parts/pallas_call | solution.py:762
  365.4 6.8 convolution_convert_fusion.1.refs_1_
  372.2 2.7 fusion.4.refs_0_
  375.1 75.1 %layer_sums.2 = (bf16[928,384]{1,0:T(8,128)(2,1)}, bf16[192,1536]{1,0:T(8,128)(2,1)}, bf16[256,1536]{1,0:T(8,128)(2,1)}, bf16[256,1536]{1,0:T(8,128)(2,1)}, bf16...) custom-call(bf16[384,1536]{1,0:T(8,128)(2,1)} %fusion.4.refs_0_, ...), custom_call_target="tpu_custom_call" | custom-call | tf_op jit(solution)/shard_map/layer_sums/pallas_call | solution.py:2029
  450.2 3.1 collective-permute-start.13
  455.8 3.0 collective-permute-start.8
  460.1 6.2 fusion.21.og_ref
  466.3 6.7 gate_backward.3
  473.0 5.0 convolution_convert_fusion.3
  483.9 2.9 collective-permute-done.13
  488.6 4.1 convolution_convert_fusion.2
  492.7 27.2 %mixer_backward.3 = (bf16[1024,1856]{1,0:T(8,128)(2,1)}, f32[8,1024]{1,0:T(8,128)}, f32[8,128]{1,0:T(8,128)}) custom-call(bf16[1024,1856]{1,0:T(8,128)(2,1)} %projection.2.proj_ref.rim_ref, bf16[1024,1856]{1,0:T(8,128)(2,1)} %projection.2.proj_ref.rim_ref, f32[1024,8]{1,0:T(8,128)} %copy.52.marks_ref, f32[1,1024]{1,0:T(1,128)} %bitcast.118, ...), custom_call_target="tpu_custom_call" | custom-call | flops 36300001280 | tf_op jit(solution)/shard_map/mixer_backward/pallas_call | solution.py:853
  520.0 2.6 fusion.3.refs_0_
  523.7 11.1 %group_parts.7 = (bf16[512,1536]{1,0:T(8,128)(2,1)}, f32[512,1536]{1,0:T(8,128)}) custom-call(bf16[1024,1856]{1,0:T(8,128)(2,1)} %get-tuple-element.115.left_ref, bf16[1856,1536]{1,0:T(8,128)(2,1)} %get-tuple-element.76.weight_ref), custom_call_target="tpu_custom_call" | custom-call | flops 6600000000 | tf_op jit(solution)/shard_map/group_parts/pallas_call | solution.py:762
  534.8 6.8 convolution_convert_fusion.refs_1_
  543.7 95.0 %layer_sums.3 = (bf16[4,1856,384]{2,1,0:T(8,128)(2,1)}, bf16[768,1536]{1,0:T(8,128)(2,1)}, bf16[256,1536]{1,0:T(8,128)(2,1)}, f32[1,384]{1,0:T(1,128)}, f32[4,83...) custom-call(bf16[384,1536]{1,0:T(8,128)(2,1)} %fusion.3.refs_0_, ...), custom_call_target="tpu_custom_call" | custom-call | tf_op jit(solution)/shard_map/layer_sums/pallas_call | solution.py:2029
  638.7 4.3 collective-permute-start.16
  644.3 10.0 %assemble_rows.1 = (f32[6448,384]{1,0:T(8,128)}, f32[1,768,1536]{2,1,0:T(8,128)}) custom-call(bf16[4,1856,384]{2,1,0:T(8,128)(2,1)} %get-tuple-element.130.part_ref.shared_ref, bf16[4,1856,384]{2,1,0:T(8,128)(2,1)} %get-tuple-element.130.part_ref.shared_ref, bf16[768,1536]{1,0:T(8,128)(2,1)} %get-tuple-element.131.out_ref), custom_call_target="tpu_custom_call" | custom-call | tf_op jit(solution)/shard_map/assemble_rows/pallas_call | solution.py:2066
  654.3 23.8 %collective-permute-done.16 = bf16[256,1536]{1,0:T(8,128)(2,1)S(1)} collective-permute-done((bf16[256,1536]{1,0:T(8,128)(2,1)}, bf16[256,1536]{1,0:T(8,128)(2,1)S(1)}, u32[]{:S(2)}, u32[]{:S(2)}) %collective-permute-start.16) | collective-permute-done | bytes 786464 | tf_op jit(solution)/shard_map/ppermute | solution.py:2230
  (144 shorter events, 46.7 us)
Async XLA Ops:
  7.2 367.9 %reduce-scatter.3.cloned.1.call-start = ((), (), s32[]{:S(2)}) async-start(), calls=%async_computation.2 | async-start | bytes 2949120 | tf_op jit(solution)/shard_map/reduce_scatter | solution.py:2176
  7.9 130.4 %collective-permute-start = (s32[2,2,4]{2,1,0:T(2,128)S(1)}, s32[2,2,4]{2,1,0:T(2,128)S(1)}, u32[]{:S(2)}, u32[]{:S(2)}) collective-permute-start(s32[2,2,4]{2,1,0:T(2,128)S(1)} %pad_add_fusion), channel_id=1, source_target_pairs={{0,1},{1,0},{2,3},{3,2},{4,5},{5,4},{6,7},{7,6},{8,9},{9,8},{10,11... | collective-permute-start | bytes 200 | tf_op jit(solution)/shard_map/ppermute | solution.py:1423
  15.4 107.8 %copy-start = (bf16[1,2,1,256,1536]{4,3,2,1,0:T(8,128)(2,1)S(1)}, bf16[1,2,1,256,1536]{4,3,2,1,0:T(8,128)(2,1)}, u32[]{:S(2)}) copy-start(bf16[1,2,1,256,1536]{4,3,2,1,0:T(8,128)(2,1)} %blocks_ref.1) | copy-start | bytes 4718596
  123.3 40.4 %collective-permute-start.2 = (bf16[256,1536]{1,0:T(8,128)(2,1)S(1)}, bf16[256,1536]{1,0:T(8,128)(2,1)S(1)}, u32[]{:S(2)}, u32[]{:S(2)}) collective-permute-start(bf16[256,1536]{1,0:T(8,128)(2,1)S(1)} %get-tuple-element.146), channel_id=1, source_target_pairs={{16,8},{17,12},{18,10},{19,14},{20,24},{21,28},{22,26},{23,30},{24... | collective-permute-start | bytes 2359304 | tf_op jit(solution)/shard_map/ppermute | solution.py:2131
  124.6 39.1 %collective-permute-start.1 = (bf16[256,1536]{1,0:T(8,128)(2,1)S(1)}, bf16[256,1536]{1,0:T(8,128)(2,1)S(1)}, u32[]{:S(2)}, u32[]{:S(2)}) collective-permute-start(bf16[256,1536]{1,0:T(8,128)(2,1)S(1)} %get-tuple-element.147), channel_id=1, source_target_pairs={{16,0},{17,4},{18,2},{19,6},{20,16},{21,20},{22,18},{23,22},{24,1}... | collective-permute-start | bytes 2359304 | tf_op jit(solution)/shard_map/ppermute | solution.py:2131
  126.8 11.5 %copy-start.9 = (s32[2,1,4]{2,1,0:T(1,128)S(1)}, s32[2,1,4]{2,1,0:T(1,128)}, u32[]{:S(2)}) copy-start(s32[2,1,4]{2,1,0:T(1,128)} %param.14) | copy-start | bytes 100
  126.8 11.5 %copy-start.10 = (s32[2,1,4]{2,1,0:T(1,128)S(1)}, s32[2,1,4]{2,1,0:T(1,128)}, u32[]{:S(2)}) copy-start(s32[2,1,4]{2,1,0:T(1,128)} %param.13) | copy-start | bytes 100
  276.2 16.5 %copy-start.18 = (bf16[1024,1536]{1,0:T(8,128)(2,1)S(1)}, bf16[1024,1536]{1,0:T(8,128)(2,1)}, u32[]{:S(2)}) copy-start(bf16[1024,1536]{1,0:T(8,128)(2,1)} %get-tuple-element.90) | copy-start | bytes 9437188
  298.8 1.2 collective-permute-start.3
  299.9 7.9 %collective-permute-start.4 = (f32[2,8,128]{2,1,0:T(8,128)S(1)}, f32[2,8,128]{2,1,0:T(8,128)S(1)}, u32[]{:S(2)}, u32[]{:S(2)}) collective-permute-start(f32[2,8,128]{2,1,0:T(8,128)S(1)} %fusion.20), channel_id=1, source_target_pairs={{0,1},{1,0},{2,3},{3,2},{4,5},{5,4},{6,7},{7,6},{8,9},{9,8},{10,11... | collective-permute-start | bytes 24584 | tf_op jit(solution)/shard_map/ppermute | solution.py:1423
  320.4 51.8 %collective-permute-start.5 = (bf16[384,1536]{1,0:T(8,128)(2,1)S(1)}, bf16[384,1536]{1,0:T(8,128)(2,1)}, u32[]{:S(2)}, u32[]{:S(2)}) collective-permute-start(bf16[384,1536]{1,0:T(8,128)(2,1)S(1)} %dynamic-slice_bitcast_fusion.1), channel_id=1, source_target_pairs={{0,2},{1,3},{2,0},{3,1},{4,6},{5,7},{6,4},{7,5},{8,10},{9,11},{10,... | collective-permute-start | bytes 3538952 | tf_op jit(solution)/shard_map/ppermute | solution.py:1427
  326.0 217.7 %reduce-scatter.5.cloned.1.call-start = ((), (), s32[]{:S(2)}) async-start(), calls=%async_computation.3 | async-start | bytes 2949120 | tf_op jit(solution)/shard_map/reduce_scatter | solution.py:2176
  354.1 11.3 %copy-start.17 = (bf16[1024,1536]{1,0:T(8,128)(2,1)S(1)}, bf16[1024,1536]{1,0:T(8,128)(2,1)}, u32[]{:S(2)}) copy-start(bf16[1024,1536]{1,0:T(8,128)(2,1)} %get-tuple-element.87.left_ref) | copy-start | bytes 9437188
  375.1 79.7 %copy-start.11 = (f32[8,128]{1,0:T(8,128)S(1)}, f32[8,128]{1,0:T(8,128)}, u32[]{:S(2)}) copy-start(f32[8,128]{1,0:T(8,128)} %get-tuple-element.106) | copy-start | bytes 12292
  375.1 85.1 %copy-start.21 = (bf16[768,1536]{1,0:T(8,128)(2,1)S(1)}, bf16[768,1536]{1,0:T(8,128)(2,1)}, u32[]{:S(2)}) copy-start(bf16[768,1536]{1,0:T(8,128)(2,1)} %get-tuple-element.80.weight_ref) | copy-start | bytes 7077892
  450.2 36.6 %collective-permute-start.13 = (bf16[256,1536]{1,0:T(8,128)(2,1)}, bf16[256,1536]{1,0:T(8,128)(2,1)}, u32[]{:S(2)}, u32[]{:S(2)}) collective-permute-start(bf16[256,1536]{1,0:T(8,128)(2,1)} %get-tuple-element.116), channel_id=1, source_target_pairs={{8,16},{12,17},{10,18},{14,19},{24,20},{28,21},{26,22},{30,23},{9,... | collective-permute-start | bytes 2359304 | tf_op jit(solution)/shard_map/ppermute | solution.py:2230
  453.3 35.3 %collective-permute-start.12 = (bf16[256,1536]{1,0:T(8,128)(2,1)}, bf16[256,1536]{1,0:T(8,128)(2,1)S(1)}, u32[]{:S(2)}, u32[]{:S(2)}) collective-permute-start(bf16[256,1536]{1,0:T(8,128)(2,1)} %get-tuple-element.116), channel_id=1, source_target_pairs={{0,16},{4,17},{2,18},{6,19},{16,20},{20,21},{18,22},{22,23},{1,24}... | collective-permute-start | bytes 2359304 | tf_op jit(solution)/shard_map/ppermute | solution.py:2230
  455.8 24.0 %collective-permute-start.8 = (bf16[192,1536]{1,0:T(8,128)(2,1)}, bf16[192,1536]{1,0:T(8,128)(2,1)S(1)}, u32[]{:S(2)}, u32[]{:S(2)}) collective-permute-start(bf16[192,1536]{1,0:T(8,128)(2,1)} %get-tuple-element.112), channel_id=1, source_target_pairs={{0,16},{1,17},{2,18},{3,19},{4,20},{5,21},{6,22},{7,23},{8,24},{9,... | collective-permute-start | bytes 1769480 | tf_op jit(solution)/shard_map/ppermute | solution.py:2221
  458.8 22.9 %collective-permute-start.7 = (bf16[928,384]{1,0:T(8,128)(2,1)}, bf16[928,384]{1,0:T(8,128)(2,1)S(1)}, u32[]{:S(2)}, u32[]{:S(2)}) collective-permute-start(bf16[928,384]{1,0:T(8,128)(2,1)} %get-tuple-element.111), channel_id=1, source_target_pairs={{0,16},{1,17},{2,18},{3,19},{4,20},{5,21},{6,22},{7,23},{8,24},{9,... | collective-permute-start | bytes 2138120 | tf_op jit(solution)/shard_map/ppermute | solution.py:2221
  479.1 40.8 %collective-permute-start.6 = (bf16[384,1536]{1,0:T(8,128)(2,1)}, bf16[384,1536]{1,0:T(8,128)(2,1)}, u32[]{:S(2)}, u32[]{:S(2)}) collective-permute-start(bf16[384,1536]{1,0:T(8,128)(2,1)} %dynamic-slice_bitcast_fusion), channel_id=1, source_target_pairs={{0,2},{1,3},{2,0},{3,1},{4,6},{5,7},{6,4},{7,5},{8,10},{9,11},{10,... | collective-permute-start | bytes 3538952 | tf_op jit(solution)/shard_map/ppermute | solution.py:1427
  479.8 8.8 %copy-start.20 = (bf16[1024,1536]{1,0:T(8,128)(2,1)S(1)}, bf16[1024,1536]{1,0:T(8,128)(2,1)}, u32[]{:S(2)}) copy-start(bf16[1024,1536]{1,0:T(8,128)(2,1)} %get-tuple-element.117) | copy-start | bytes 9437188
  479.8 8.8 %copy-start.26 = (bf16[1024,768]{1,0:T(8,128)(2,1)S(1)}, bf16[1024,768]{1,0:T(8,128)(2,1)}, u32[]{:S(2)}) copy-start(bf16[1024,768]{1,0:T(8,128)(2,1)} %get-tuple-element.79.left_ref) | copy-start | bytes 4718596
  479.9 12.8 %copy-start.2 = (bf16[2,192,1536]{2,1,0:T(8,128)(2,1)}, bf16[2,192,1536]{2,1,0:T(8,128)(2,1)S(1)}, u32[]{:S(2)}) copy-start(bf16[2,192,1536]{2,1,0:T(8,128)(2,1)S(1)} %pad_maximum_fusion.1.refs_19_) | copy-start | bytes 3538948
  479.9 42.6 %collective-permute-start.11 = (bf16[2,192,1536]{2,1,0:T(8,128)(2,1)S(1)}, bf16[2,192,1536]{2,1,0:T(8,128)(2,1)}, u32[]{:S(2)}, u32[]{:S(2)}) collective-permute-start(bf16[2,192,1536]{2,1,0:T(8,128)(2,1)S(1)} %pad_maximum_fusion.1.refs_19_), channel_id=1, source_target_pairs={{16,17},{17,16},{18,19},{19,18},{20,21},{21,20},{22,23},{23,22},{2... | collective-permute-start | bytes 3538952 | tf_op jit(solution)/shard_map/ppermute | solution.py:2218
  481.9 10.8 %copy-start.1 = (bf16[2,928,384]{2,1,0:T(8,128)(2,1)}, bf16[2,928,384]{2,1,0:T(8,128)(2,1)S(1)}, u32[]{:S(2)}) copy-start(bf16[2,928,384]{2,1,0:T(8,128)(2,1)S(1)} %pad_maximum_fusion.refs_15_) | copy-start | bytes 4276228
  481.9 40.6 %collective-permute-start.10 = (bf16[2,928,384]{2,1,0:T(8,128)(2,1)S(1)}, bf16[2,928,384]{2,1,0:T(8,128)(2,1)}, u32[]{:S(2)}, u32[]{:S(2)}) collective-permute-start(bf16[2,928,384]{2,1,0:T(8,128)(2,1)S(1)} %pad_maximum_fusion.refs_15_), channel_id=1, source_target_pairs={{16,18},{17,19},{18,16},{19,17},{20,22},{21,23},{22,20},{23,21},{2... | collective-permute-start | bytes 4276232 | tf_op jit(solution)/shard_map/ppermute | solution.py:2218
  486.8 35.7 %collective-permute-start.9 = (bf16[2,928,384]{2,1,0:T(8,128)(2,1)S(1)}, bf16[2,928,384]{2,1,0:T(8,128)(2,1)}, u32[]{:S(2)}, u32[]{:S(2)}) collective-permute-start(bf16[2,928,384]{2,1,0:T(8,128)(2,1)S(1)} %pad_maximum_fusion.refs_15_), channel_id=1, source_target_pairs={{16,17},{17,16},{18,19},{19,18},{20,21},{21,20},{22,23},{23,22},{2... | collective-permute-start | bytes 4276232 | tf_op jit(solution)/shard_map/ppermute | solution.py:2218
  492.7 27.3 %copy-start.4 = (bf16[768,1536]{1,0:T(8,128)(2,1)S(1)}, bf16[768,1536]{1,0:T(8,128)(2,1)}, u32[]{:S(2)}) copy-start(bf16[768,1536]{1,0:T(8,128)(2,1)} %copy-done.3) | copy-start | bytes 7077892
  522.5 12.2 %copy-start.15 = (bf16[1024,1536]{1,0:T(8,128)(2,1)S(1)}, bf16[1024,1536]{1,0:T(8,128)(2,1)}, u32[]{:S(2)}) copy-start(bf16[1024,1536]{1,0:T(8,128)(2,1)} %get-tuple-element.75.left_ref) | copy-start | bytes 9437188
  522.5 19.0 %collective-permute-start.14 = (bf16[2,928,384]{2,1,0:T(8,128)(2,1)}, bf16[2,928,384]{2,1,0:T(8,128)(2,1)S(1)}, u32[]{:S(2)}, u32[]{:S(2)}) collective-permute-start(bf16[2,928,384]{2,1,0:T(8,128)(2,1)} %collective-permute-done.10.refs_17_), channel_id=1, source_target_pairs={{16,17},{17,16},{18,19},{19,18},{20,21},{21,20},{22,23},{23,22},{2... | collective-permute-start | bytes 4276232 | tf_op jit(solution)/shard_map/ppermute | solution.py:2218
  638.7 39.4 %collective-permute-start.16 = (bf16[256,1536]{1,0:T(8,128)(2,1)}, bf16[256,1536]{1,0:T(8,128)(2,1)S(1)}, u32[]{:S(2)}, u32[]{:S(2)}) collective-permute-start(bf16[256,1536]{1,0:T(8,128)(2,1)} %get-tuple-element.128), channel_id=1, source_target_pairs={{8,0},{12,1},{10,2},{14,3},{24,4},{28,5},{26,6},{30,7},{9,8},{13,9... | collective-permute-start | bytes 2359304 | tf_op jit(solution)/shard_map/ppermute | solution.py:2230
  643.0 35.2 %collective-permute-start.15 = (bf16[256,1536]{1,0:T(8,128)(2,1)}, bf16[256,1536]{1,0:T(8,128)(2,1)S(1)}, u32[]{:S(2)}, u32[]{:S(2)}) collective-permute-start(bf16[256,1536]{1,0:T(8,128)(2,1)} %get-tuple-element.128), channel_id=1, source_target_pairs={{0,0},{4,1},{2,2},{6,3},{16,4},{20,5},{18,6},{22,7},{1,8},{5,9},{3... | collective-permute-start | bytes 2359304 | tf_op jit(solution)/shard_map/ppermute | solution.py:2230
  (14 other events, 49.3 us)
Sparse Core Ops, SparseCore 0:
  326.2 48.8 reduce-scatter.2
  492.8 50.8 reduce-scatter.4

commit v5 on v4

--- a/solution.py
+++ b/solution.py
@@ -566,7 +566,8 @@
     out = mixer + skip * heads
     mixer_ref[...] = out
     gated = out * (gate * gate_of(gate))
-    squares_ref[...] = jnp.sum(gated * gated, axis=1, keepdims=True)
+    squares = jnp.sum(gated * gated, axis=1, keepdims=True)
+    squares_ref[0] = jnp.broadcast_to(squares, (Q, LANES)).T[:1]
     gg_ref[...] = low(gated * gain)
 
 
@@ -818,13 +819,13 @@
         ],
         out_specs=[
             by_row(width),
-            by_row(1),
+            pl.BlockSpec((1, 1, Q), lambda i: (i, 0, 0)),
             by_row(width),
             pl.BlockSpec((1, LANES, width), lambda i: (i, 0, 0)),
         ],
         out_shape=[
             jax.ShapeDtypeStruct((rows, width), jnp.bfloat16),
-            jax.ShapeDtypeStruct((rows, 1), jnp.float32),
+            jax.ShapeDtypeStruct((chunks, 1, Q), jnp.float32),
             jax.ShapeDtypeStruct((rows, width), jnp.float32),
             jax.ShapeDtypeStruct((chunks, LANES, width), jnp.float32),
         ],
@@ -1460,31 +1461,50 @@
         refs = refs[:9] + refs[12:]
     all_ref, out_all_ref, bound_ref = refs[9:12]
     (
-        n_core, n_send, n_across, y_buf, z_buf, s_buf, yo_buf, yo_mine,
+        n_core, n_send, n_across, n_done, y_buf, z_buf, s_buf, yo_buf, yo_mine,
         y_send, y_recv, z_send, z_recv, yo_sem, core_send, core_recv,
         x_send, x_recv, ya_send, ya_recv, relay_send, relay_recv, xo_send, xo_recv, n_sem,
-    ) = refs[19:43]
+    ) = refs[19:44]
     if last:
         total_refs = refs[12:19]
-        tiny_mine, t1_buf, t1_sum, t2_buf, t2_sum, t3_buf, g_mine, g_buf, g_sum, g_all = refs[43:53]
-        t_send, t_recv, g_send, g_recv = refs[53:]
+        tiny_mine, t1_buf, t1_sum, t2_buf, t2_sum, t3_buf, g_mine, g_buf, g_sum, g_all = refs[44:54]
+        t_send, t_recv, home_send, home_recv, g_send, g_recv = refs[54:]
     else:
         g_ref, g_all_ref, dots_ref, norm_ref = refs[12:16]
-        r_core, r_send, r_across = refs[43:46]
-        row_send, row_recv, dot_send, dot_recv, r_sem = refs[46:]
+        r_core, r_send, r_across = refs[44:47]
+        row_send, row_recv, dot_send, dot_recv, r_sem = refs[47:]
     c, z, y, x = place()
     quarter = 2 * x + c
     core, x_other, y_other = {"section": 1 - c}, {"rep": 2 * y + 1 - x}, {"rep": 2 * (1 - y) + x}
     chunks = range(len(STEPS))
-    block = n_send.shape[0]
+    block = n_done.shape[0]
     copy = mesh_copy
 
+    home = {"section": layer, "shard": quarter, "rep": 2 * y + lax.rem(z, 2)}
+    at_home = (c == layer) & (z == quarter) & (x == lax.rem(z, 2))
+    guests = tuple(
+        {"section": lax.rem(z, 2), "shard": 2 * m + x, "rep": 2 * y + lax.div(z, 2)}
+        for m in range(MICRO)
+    )
+    guest_self = tuple(
+        (c == layer) & (lax.rem(z, 2) == layer) & (z == 2 * m + x) & (x == lax.div(z, 2))
+        for m in range(MICRO)
+    )
     reps = (x_other, y_other, {"rep": 2 * (1 - y) + 1 - x})
     shards = tuple({"shard": lax.rem(z + away, 4)} for away in (1, 2, 3))
     barrier = pltpu.get_barrier_semaphore()
     for device in (core,) + reps + shards:
         greet(barrier, device)
-    pl.semaphore_wait(barrier, 7)
+    if last:
+        for m in range(MICRO):
+
+            @pl.when((c == layer) & jnp.logical_not(guest_self[m]))
+            def _():
+                greet(barrier, guests[m])
+
+        pl.semaphore_wait(barrier, 8 - at_home.astype(jnp.int32))
+    else:
+        pl.semaphore_wait(barrier, 7)
 
     orders = ((3, 2, 1, 0), (3, 0, 2, 1), (0, 3, 1, 2), (0, 1, 2, 3))
 
@@ -1561,12 +1581,13 @@
 
     def owner_copy(ch):
         span = span_of(ch)
-        piece = all_part(quarter, y, ch)
+        piece = all_part(quarter, y, ch) if last else all_ref.at[1 - layer, span]
         return copy(s_buf.at[z, span], piece, core_send.at[ch], core_recv.at[ch], core)
 
     def owner_out_copy():
+        piece = out_part(quarter) if last else out_all_ref.at[1 - layer]
         return copy(
-            yo_mine, out_part(quarter), core_send.at[len(STEPS)], core_recv.at[len(STEPS)], core
+            yo_mine, piece, core_send.at[len(STEPS)], core_recv.at[len(STEPS)], core
         )
 
     def yo_copy():
@@ -1577,6 +1598,21 @@
 
     def n_x_copy():
         return copy(n_send, n_across, n_sem.at[2], n_sem.at[3], x_other)
+
+    def home_copy(m):
+        return copy(n_done, bound_ref.at[m], home_send.at[0], home_recv.at[m], home)
+
+    def go_home():
+        for m in range(MICRO):
+            there = lax.div(z, 2) == m
+
+            @pl.when(there & jnp.logical_not(at_home))
+            def _():
+                home_copy(m).start()
+
+            @pl.when(there & at_home)
+            def _():
+                bound_ref[m] = n_done[...]
 
     if last:
 
@@ -1668,18 +1704,17 @@
                 s_buf[z, span].astype(jnp.float32) + z_buf[4, span].astype(jnp.float32)
             )
 
-        if not last:
-            all_ref[span] = s_buf[z, span]
-            return
-
         @pl.when(c != layer)
         def _():
             owner_copy(ch).start()
 
         @pl.when(c == layer)
         def _():
-            all_part(quarter, y, ch)[...] = s_buf[z, span]
-            spread(layer, ch)
+            if last:
+                all_part(quarter, y, ch)[...] = s_buf[z, span]
+                spread(layer, ch)
+            else:
+                all_ref[layer, span] = s_buf[z, span]
 
     def pass_on(ch):
         if not last:
@@ -1725,7 +1760,7 @@
         source_grad = low(incoming_ref[...].astype(jnp.float32) + inv * (hat_grad - hat * mean))
         norm_grad = jnp.sum(normed_grad * hat, axis=0, keepdims=True)
         if last:
-            bound_ref[...] = source_grad
+            n_done[...] = source_grad
             g_mine[...] = jnp.broadcast_to(norm_grad, g_mine.shape)
 
             @pl.when(c != layer)
@@ -1752,9 +1787,6 @@
     def out_step():
         yo_copy().wait()
         total = low(out_grad_ref[...].astype(jnp.float32) + yo_buf[...].astype(jnp.float32))
-        if not last:
-            out_all_ref[...] = total
-            return
         yo_mine[...] = total
 
         @pl.when(c != layer)
@@ -1763,7 +1795,10 @@
 
         @pl.when(c == layer)
         def _():
-            out_part(quarter)[...] = yo_mine[...]
+            if last:
+                out_part(quarter)[...] = yo_mine[...]
+            else:
+                out_all_ref[layer] = yo_mine[...]
 
     def out_across():
         @pl.when(c == layer)
@@ -1839,6 +1874,7 @@
         pass_on(2)
         relay(0)
         send_in(2, 3)
+        go_home()
         relay(1)
         gain_across()
         finish(3)
@@ -1910,6 +1946,18 @@
         r_core_copy().wait_send()
         r_x_copy().wait_send()
 
+    if last:
+
+        @pl.when(jnp.logical_not(at_home))
+        def _():
+            home_copy(0).wait_send()
+
+        for m in range(MICRO):
+
+            @pl.when((c == layer) & jnp.logical_not(guest_self[m]))
+            def _():
+                home_copy(m).wait_recv()
+
     n_core_copy().wait_send()
     n_x_copy().wait_send()
     for i in range(3):
@@ -1919,13 +1967,20 @@
         for ch in chunks[2:]:
             y_copy(shard_at(i), ch).wait_send()
 
-    if last:
-
-        @pl.when(c != layer)
+
+    @pl.when(c != layer)
+    def _():
+        for ch in chunks:
+            owner_copy(ch).wait_send()
+        owner_out_copy().wait_send()
+
+    if not last:
+
+        @pl.when(c == layer)
         def _():
             for ch in chunks:
-                owner_copy(ch).wait_send()
-            owner_out_copy().wait_send()
+                owner_copy(ch).wait_recv()
+            owner_out_copy().wait_recv()
 
 
 def small_totals(layer, quarter, refs, norm_grad, tiny):
@@ -1976,12 +2031,13 @@
     half, whole = jnp.bfloat16, jnp.float32
     last = layer == 0
     out_shape = [
-        jax.ShapeDtypeStruct((GROUP, LOCAL, LANE_PART) if last else span, half),
-        jax.ShapeDtypeStruct((DI // GROUP, D) if last else out, half),
-        jax.ShapeDtypeStruct(rows, half),
+        jax.ShapeDtypeStruct((GROUP, LOCAL, LANE_PART) if last else (CORES,) + span, half),
+        jax.ShapeDtypeStruct((DI // GROUP, D) if last else (CORES,) + out, half),
+        jax.ShapeDtypeStruct((MICRO,) + rows if last else rows, half),
     ]
     scratch = [
         pltpu.VMEM(theirs.shape, half),
+        pltpu.VMEM(rows, half),
         pltpu.VMEM(rows, half),
         pltpu.VMEM(rows, half),
         pltpu.VMEM((4,) + span, half),
@@ -2010,7 +2066,7 @@
             pltpu.VMEM((7, 8, D), whole),
             pltpu.VMEM((8, D), whole),
             pltpu.VMEM((8, D), whole),
-            dma((7,)), dma((7,)), dma((7,)), dma((7,)),
+            dma((7,)), dma((7,)), dma((1,)), dma((MICRO,)), dma((7,)), dma((7,)),
         ]
     else:
         out_shape += [
@@ -2208,7 +2264,7 @@
     out_part1 = out_sum(gg1, out_inv1, g1)
     pg1, gate1, rest1, small_grads1 = backward(1, kept1, og1, per_row1)
     theirs, mine = group_parts(pg1, w_in1)
-    in_sum1, out_sum1, result, middle_grad, g0, dots0, norm_grad1, *_ = layer_sums(
+    in_own, out_own, result, middle_grad, g0, dots0, norm_grad1, *_ = layer_sums(
         1, gate1, rest1, out_part1, theirs, mine, middle, cotangent, norms[1, 0:1], added0,
         out_theirs, out_mine, own(out_inv1),
     )
@@ -2217,23 +2273,15 @@
     def on_second(v, flip):
         return lax.ppermute(v, ("section", "rep"), [(4 + i, 4 + (i ^ flip)) for i in range(4)])
 
-    def to_second(v):
-        return jnp.stack([lax.ppermute(v, "section", [(0, 1)]), v])
-
-    in_own, out_own = to_second(in_sum1), to_second(out_sum1)
     in_near, in_across = on_second(in_own, 1), on_second(in_own, 2)
     out_near = on_second(out_own, 1)
     in_far = on_second(in_across, 1)
-
-    def go_home(value, cc):
-        return [
-            lax.ppermute(
-                value, axes, [(home(m, zz, rr), spot(cc, zz, rr)) for zz in range(4) for rr in range(4)]
-            )
-            for m in range(MICRO)
-        ]
-
-    results = go_home(result, 1)
+    results = [
+        lax.ppermute(
+            result, axes, [(home(m, zz, rr), spot(1, zz, rr)) for zz in range(4) for rr in range(4)]
+        )
+        for m in range(MICRO)
+    ]
 
     og0 = mm(g0, w_out0, 1, 1)
     out_part0 = out_sum(gg0, out_inv0, after(g0, *results))
@@ -2242,11 +2290,10 @@
         0, kept0, og0, per_row0, (in_own, out_own), (in_near, in_across, out_near)
     )
     theirs, mine = group_parts(pg0, w_in0)
-    in_all, out_all, entry_grad, *totals = layer_sums(
+    in_all, out_all, entry_grads, *totals = layer_sums(
         0, gate0, rest0, out_part0, theirs, mine, source, middle_grad, norms[0, 0:1], norm_grad1,
         *small_grads0, *small_grads1, in_own, in_near, in_across, in_far, out_own, out_near,
     )
-    entry_grads = go_home(entry_grad, 0)
     in_total, out_total = assemble_rows(in_all, out_all)
     in_total = jnp.swapaxes(in_total, 0, 1)[None]
 

time: 703 us -> 684 us (0.973)
  waiting for transfers between devices: 30.2 us -> 10.8 us
  Pallas kernels: 544 us -> 559 us
  starting transfers between devices: 27.9 us -> 19.9 us
    ppermute x6 -> x2, waiting for transfers between devices: 26.7 us -> 7.16 us  [per_device_split(): lax.ppermute(result, axes, [(home(m, zz, rr), spot(1, zz, rr)) for zz in...]
    pallas_call x2, Pallas kernels: 170 us -> 185 us  [layer_sums(): pl.pallas_call(functools.partial(sum_kernel, layer), in_specs=[inside] *...]
    ppermute x6 -> x2, starting transfers between devices: 13.7 us -> 4.67 us  [per_device_split(): lax.ppermute(result, axes, [(home(m, zz, rr), spot(1, zz, rr)) for zz in...]
  transfers between devices with their start and end apart: 19 -> 15, of which waited for: 5 -> 4; matrix products, arithmetic and copies ran while one was open for 8% -> 7% of each run, Pallas kernels for 35% -> 34%
where the time goes in v5:
time: 684 us; the launch traced here: 675 us
  Pallas kernels  559 us (82%)
  matrix products  42.2 us (6%)
  starting transfers between devices  19.9 us (3%)
  local copies, waits for them, and re-layouts  16.4 us (2%)
  between operations  14.9 us (2%)
  other arithmetic  11.4 us (2%)
  waiting for transfers between devices  10.8 us (2%)
    pallas_call x2, Pallas kernels, layer_sums(): pl.pallas_call(functools.partial(sum_kernel, layer), in_specs=[inside] *...  185 us
    pallas_call x1, Pallas kernels, enter_first(): pl.pallas_call(enter_first_kernel, in_specs=[anywhere] * 3 + [inside], ou...  108 us
    pallas_call x1, Pallas kernels, enter_second(): pl.pallas_call(enter_second_kernel, in_specs=[anywhere] * 2 + [inside] *...  100 us
    pallas_call x2, Pallas kernels, mixer_backward(): pl.pallas_call(functools.partial(backward_kernel, width), grid=(chunks,),...  54.2 us
    dot_general x8, matrix products, mm(): lax.dot_general(a, b, (((da,), (db,)), ((), ())), preferred_element_type=...  42.2 us
    pallas_call x4, Pallas kernels, group_parts(): pl.pallas_call(product_kernel, grid=(3,), in_specs=[pl.BlockSpec((rows, d...  35 us
    pallas_call x2, Pallas kernels, mixer_forward(): pl.pallas_call(functools.partial(forward_kernel, width), grid=(chunks,),...  29.9 us
    pallas_call x2, Pallas kernels, projection(): pl.pallas_call(projection_kernel, grid=(pl.cdiv(columns, step),), in_spec...  23 us
  transfers between devices with their start and end apart: 15, of which 4 were waited for; matrix products, arithmetic and copies ran while one was open for 7% of the time, Pallas kernels for 34%

profile of v5, /device:TPU:16, one launch (start us, length us, event | category | flops | bytes accessed | tf_op | source)
XLA Modules:
  0.0 674.6 jit_solution(2821518514766657469)
XLA Ops:
  15.5 107.7 %enter_first.1 = (bf16[1856,1536]{1,0:T(8,128)(2,1)}, bf16[768,1536]{1,0:T(8,128)(2,1)}, bf16[256,1536]{1,0:T(8,128)(2,1)}, bf16[1024,1536]{1,0:T(8,128)(2,1)}, ...) custom-call(bf16[6448,384]{1,0:T(8,128)(2,1)} %bitcast.82, bf16[768,1536]{1,0:T(8,128)(2,1)} %bitcast.84, ...), custom_call_target="tpu_custom_call" | custom-call | tf_op jit(solution)/shard_map/enter_first/pallas_call | solution.py:1277
  126.8 11.5 %projection.2.proj_ref.rim_ref = bf16[1024,1856]{1,0:T(8,128)(2,1)} custom-call(bf16[1024,1536]{1,0:T(8,128)(2,1)} %get-tuple-element.75.left_ref, bf16[1856,1536]{1,0:T(8,128)(2,1)} %get-tuple-element.76.weight_ref), custom_call_target="tpu_custom_call" | custom-call | flops 6600000000 | tf_op jit(solution)/shard_map/projection/pallas_call | solution.py:790
  140.6 14.9 %mixer_forward.2 = (bf16[1024,768]{1,0:T(8,128)(2,1)}, f32[8,1,128]{2,1,0:T(1,128)}, f32[1024,768]{1,0:T(8,128)}, f32[8,128,768]{2,1,0:T(8,128)}) custom-call(bf16[1024,1856]{1,0:T(8,128)(2,1)} %projection.2.proj_ref.rim_ref, f32[1024,8]{1,0:T(8,128)} %copy.52.marks_ref, f32[1,1024]{1,0:T(1,128)} %bitcast.115, f32[2,16,1024]{2,1,0:T(8,128)} %get-tuple-element.77.small_ref), custom_call_target="tpu_custom_call" | custom-call | flops 17600000000 | tf_op jit(solution)/shard_map/mixer_forward/pallas_call | solution.py:814
  155.5 6.3 group_parts.4
  162.8 100.0 %enter_second.1 = (bf16[1856,1536]{1,0:T(8,128)(2,1)}, bf16[768,1536]{1,0:T(8,128)(2,1)}, f32[256,1536]{1,0:T(8,128)}, bf16[256,1536]{1,0:T(8,128)(2,1)}, bf16[1...) custom-call(bf16[6448,384]{1,0:T(8,128)(2,1)} %bitcast.83, bf16[768,1536]{1,0:T(8,128)(2,1)} %bitcast.85, ...), custom_call_target="tpu_custom_call" | custom-call | tf_op jit(solution)/shard_map/enter_second/pallas_call | solution.py:1390
  262.8 11.5 %projection.3.proj_ref.rim_ref = bf16[1024,1856]{1,0:T(8,128)(2,1)} custom-call(bf16[1024,1536]{1,0:T(8,128)(2,1)} %get-tuple-element.87.left_ref, bf16[1856,1536]{1,0:T(8,128)(2,1)} %get-tuple-element.88.weight_ref), custom_call_target="tpu_custom_call" | custom-call | flops 6600000000 | tf_op jit(solution)/shard_map/projection/pallas_call | solution.py:790
  274.3 15.1 %mixer_forward.3 = (bf16[1024,768]{1,0:T(8,128)(2,1)}, f32[8,1,128]{2,1,0:T(1,128)}, f32[1024,768]{1,0:T(8,128)}, f32[8,128,768]{2,1,0:T(8,128)}) custom-call(bf16[1024,1856]{1,0:T(8,128)(2,1)} %projection.3.proj_ref.rim_ref, f32[1024,8]{1,0:T(8,128)} %copy.52.marks_ref, f32[1,1024]{1,0:T(1,128)} %bitcast.116, f32[2,16,1024]{2,1,0:T(8,128)} %get-tuple-element.77.small_ref), custom_call_target="tpu_custom_call" | custom-call | flops 17600000000 | tf_op jit(solution)/shard_map/mixer_forward/pallas_call | solution.py:814
  289.4 5.3 fusion
  297.4 6.4 group_parts.6
  304.8 6.8 %gate_backward.2 = (bf16[1024,768]{1,0:T(8,128)(2,1)}, bf16[1024,768]{1,0:T(8,128)(2,1)}, f32[8,768]{1,0:T(8,128)}) custom-call(bf16[1024,1856]{1,0:T(8,128)(2,1)} %projection.3.proj_ref.rim_ref, f32[2,16,1024]{2,1,0:T(8,128)} %get-tuple-element.77.small_ref, f32[1024,768]{1,0:T(8,128)} %get-tuple-element.89.out_ref, f32[1024,768]{1,0:T(8,128)} %get-tuple-element.163.og_ref, ...), custom_call_target="tpu_custom_call" | custom-call | flops 6600000000 | tf_op jit(solution)/shard_map/gate_backward/pallas_call | solution.py:601
  311.6 4.5 convolution_convert_fusion.5
  317.8 4.1 convolution_convert_fusion.4
  322.9 27.1 %mixer_backward.2 = (bf16[1024,1856]{1,0:T(8,128)(2,1)}, f32[8,1024]{1,0:T(8,128)}, f32[8,128]{1,0:T(8,128)}) custom-call(bf16[1024,1856]{1,0:T(8,128)(2,1)} %projection.3.proj_ref.rim_ref, bf16[1024,1856]{1,0:T(8,128)(2,1)} %projection.3.proj_ref.rim_ref, f32[1024,8]{1,0:T(8,128)} %copy.52.marks_ref, f32[1,1024]{1,0:T(1,128)} %bitcast.117, ...), custom_call_target="tpu_custom_call" | custom-call | flops 36300001280 | tf_op jit(solution)/shard_map/mixer_backward/pallas_call | solution.py:854
  350.0 11.3 %group_parts.5 = (bf16[512,1536]{1,0:T(8,128)(2,1)}, f32[512,1536]{1,0:T(8,128)}) custom-call(bf16[1024,1856]{1,0:T(8,128)(2,1)} %get-tuple-element.98.left_ref, bf16[1856,1536]{1,0:T(8,128)(2,1)} %get-tuple-element.88.weight_ref), custom_call_target="tpu_custom_call" | custom-call | flops 6600000000 | tf_op jit(solution)/shard_map/group_parts/pallas_call | solution.py:763
  361.3 6.8 %convolution_convert_fusion.1.refs_1_ = bf16[1088,1536]{1,0:T(8,128)(2,1)} fusion(bf16[1024,1536]{1,0:T(8,128)(2,1)S(1)} %copy-done.13, bf16[1024,1856]{1,0:T(8,128)(2,1)} %get-tuple-element.98.left_ref), kind=kOutput, calls=%fused_computation.1 | convolution fusion | flops 3424223232 | bytes 8847360 | tf_op jit(solution)/shard_map/dot_general | solution.py:424
  368.1 2.6 fusion.4.refs_0_
  370.9 75.8 %layer_sums.2 = (bf16[2,928,384]{2,1,0:T(8,128)(2,1)}, bf16[2,192,1536]{2,1,0:T(8,128)(2,1)}, bf16[256,1536]{1,0:T(8,128)(2,1)}, bf16[256,1536]{1,0:T(8,128)(2,1...) custom-call(bf16[384,1536]{1,0:T(8,128)(2,1)} %fusion.4.refs_0_, ...), custom_call_target="tpu_custom_call" | custom-call | tf_op jit(solution)/shard_map/layer_sums/pallas_call | solution.py:2085
  446.7 3.1 collective-permute-start.11
  456.7 6.2 fusion.23.og_ref
  464.6 6.9 %gate_backward.3 = (bf16[1024,768]{1,0:T(8,128)(2,1)}, bf16[1024,768]{1,0:T(8,128)(2,1)}, f32[8,768]{1,0:T(8,128)}) custom-call(bf16[1024,1856]{1,0:T(8,128)(2,1)} %projection.2.proj_ref.rim_ref, f32[2,16,1024]{2,1,0:T(8,128)} %get-tuple-element.77.small_ref, f32[1024,768]{1,0:T(8,128)} %get-tuple-element.78.out_ref, f32[1024,768]{1,0:T(8,128)} %fusion.23.og_ref, ...), custom_call_target="tpu_custom_call" | custom-call | flops 6600000000 | tf_op jit(solution)/shard_map/gate_backward/pallas_call | solution.py:601
  471.5 4.5 convolution_convert_fusion.3
  476.1 7.2 %collective-permute-done.11 = bf16[256,1536]{1,0:T(8,128)(2,1)} collective-permute-done((bf16[256,1536]{1,0:T(8,128)(2,1)}, bf16[256,1536]{1,0:T(8,128)(2,1)}, u32[]{:S(2)}, u32[]{:S(2)}) %collective-permute-start.11) | collective-permute-done | bytes 786464 | tf_op jit(solution)/shard_map/ppermute | solution.py:2280
  483.3 2.1 collective-permute-start.6
  485.4 4.1 convolution_convert_fusion.2
  489.5 27.1 %mixer_backward.3 = (bf16[1024,1856]{1,0:T(8,128)(2,1)}, f32[8,1024]{1,0:T(8,128)}, f32[8,128]{1,0:T(8,128)}) custom-call(bf16[1024,1856]{1,0:T(8,128)(2,1)} %projection.2.proj_ref.rim_ref, bf16[1024,1856]{1,0:T(8,128)(2,1)} %projection.2.proj_ref.rim_ref, f32[1024,8]{1,0:T(8,128)} %copy.52.marks_ref, f32[1,1024]{1,0:T(1,128)} %bitcast.118, ...), custom_call_target="tpu_custom_call" | custom-call | flops 36300001280 | tf_op jit(solution)/shard_map/mixer_backward/pallas_call | solution.py:854
  516.6 2.6 fusion.3.refs_0_
  520.4 11.1 %group_parts.7 = (bf16[512,1536]{1,0:T(8,128)(2,1)}, f32[512,1536]{1,0:T(8,128)}) custom-call(bf16[1024,1856]{1,0:T(8,128)(2,1)} %get-tuple-element.115.left_ref, bf16[1856,1536]{1,0:T(8,128)(2,1)} %get-tuple-element.76.weight_ref), custom_call_target="tpu_custom_call" | custom-call | flops 6600000000 | tf_op jit(solution)/shard_map/group_parts/pallas_call | solution.py:763
  531.4 6.8 %convolution_convert_fusion.refs_1_ = bf16[1088,1536]{1,0:T(8,128)(2,1)} fusion(bf16[1024,1536]{1,0:T(8,128)(2,1)S(1)} %copy-done.11, bf16[1024,1856]{1,0:T(8,128)(2,1)} %get-tuple-element.115.left_ref), kind=kOutput, calls=%fused_computation | convolution fusion | flops 3424223232 | bytes 8847360 | tf_op jit(solution)/shard_map/dot_general | solution.py:424
  538.2 2.2 reduce-scatter.5.cloned.1.call-done
  540.5 109.5 %layer_sums.3 = (bf16[4,1856,384]{2,1,0:T(8,128)(2,1)}, bf16[768,1536]{1,0:T(8,128)(2,1)}, bf16[2,256,1536]{2,1,0:T(8,128)(2,1)}, f32[1,384]{1,0:T(1,128)}, f32[...) custom-call(bf16[384,1536]{1,0:T(8,128)(2,1)} %fusion.3.refs_0_, ...), custom_call_target="tpu_custom_call" | custom-call | tf_op jit(solution)/shard_map/layer_sums/pallas_call | solution.py:2085
  651.5 1.9 maximum_convert_fusion
  653.4 10.0 %assemble_rows.1 = (f32[6448,384]{1,0:T(8,128)}, f32[1,768,1536]{2,1,0:T(8,128)}) custom-call(bf16[4,1856,384]{2,1,0:T(8,128)(2,1)} %get-tuple-element.130.part_ref.shared_ref, bf16[4,1856,384]{2,1,0:T(8,128)(2,1)} %get-tuple-element.130.part_ref.shared_ref, bf16[768,1536]{1,0:T(8,128)(2,1)} %get-tuple-element.131.out_ref), custom_call_target="tpu_custom_call" | custom-call | tf_op jit(solution)/shard_map/assemble_rows/pallas_call | solution.py:2122
  (125 shorter events, 37.0 us)
Async XLA Ops:
  7.2 363.7 %reduce-scatter.3.cloned.1.call-start = ((), (), s32[]{:S(2)}) async-start(), calls=%async_computation.2 | async-start | bytes 2949120 | tf_op jit(solution)/shard_map/reduce_scatter | solution.py:2232
  7.9 130.4 %collective-permute-start = (s32[2,2,4]{2,1,0:T(2,128)S(1)}, s32[2,2,4]{2,1,0:T(2,128)S(1)}, u32[]{:S(2)}, u32[]{:S(2)}) collective-permute-start(s32[2,2,4]{2,1,0:T(2,128)S(1)} %pad_add_fusion), channel_id=1, source_target_pairs={{0,1},{1,0},{2,3},{3,2},{4,5},{5,4},{6,7},{7,6},{8,9},{9,8},{10,11... | collective-permute-start | bytes 200 | tf_op jit(solution)/shard_map/ppermute | solution.py:1424
  15.4 107.8 %copy-start = (bf16[1,2,1,256,1536]{4,3,2,1,0:T(8,128)(2,1)S(1)}, bf16[1,2,1,256,1536]{4,3,2,1,0:T(8,128)(2,1)}, u32[]{:S(2)}) copy-start(bf16[1,2,1,256,1536]{4,3,2,1,0:T(8,128)(2,1)} %blocks_ref.1) | copy-start | bytes 4718596
  123.3 38.4 %collective-permute-start.2 = (bf16[256,1536]{1,0:T(8,128)(2,1)S(1)}, bf16[256,1536]{1,0:T(8,128)(2,1)S(1)}, u32[]{:S(2)}, u32[]{:S(2)}) collective-permute-start(bf16[256,1536]{1,0:T(8,128)(2,1)S(1)} %get-tuple-element.148), channel_id=1, source_target_pairs={{16,8},{17,12},{18,10},{19,14},{20,24},{21,28},{22,26},{23,30},{24... | collective-permute-start | bytes 2359304 | tf_op jit(solution)/shard_map/ppermute | solution.py:2187
  124.6 37.1 %collective-permute-start.1 = (bf16[256,1536]{1,0:T(8,128)(2,1)S(1)}, bf16[256,1536]{1,0:T(8,128)(2,1)S(1)}, u32[]{:S(2)}, u32[]{:S(2)}) collective-permute-start(bf16[256,1536]{1,0:T(8,128)(2,1)S(1)} %get-tuple-element.149), channel_id=1, source_target_pairs={{16,0},{17,4},{18,2},{19,6},{20,16},{21,20},{22,18},{23,22},{24,1}... | collective-permute-start | bytes 2359304 | tf_op jit(solution)/shard_map/ppermute | solution.py:2187
  126.8 11.5 %copy-start.4 = (s32[2,1,4]{2,1,0:T(1,128)S(1)}, s32[2,1,4]{2,1,0:T(1,128)}, u32[]{:S(2)}) copy-start(s32[2,1,4]{2,1,0:T(1,128)} %param.14) | copy-start | bytes 100
  126.8 11.5 %copy-start.5 = (s32[2,1,4]{2,1,0:T(1,128)S(1)}, s32[2,1,4]{2,1,0:T(1,128)}, u32[]{:S(2)}) copy-start(s32[2,1,4]{2,1,0:T(1,128)} %param.13) | copy-start | bytes 100
  274.3 15.1 %copy-start.14 = (bf16[1024,1536]{1,0:T(8,128)(2,1)S(1)}, bf16[1024,1536]{1,0:T(8,128)(2,1)}, u32[]{:S(2)}) copy-start(bf16[1024,1536]{1,0:T(8,128)(2,1)} %get-tuple-element.90) | copy-start | bytes 9437188
  274.3 15.1 %copy-start.18 = (bf16[768,1536]{1,0:T(8,128)(2,1)S(1)}, bf16[768,1536]{1,0:T(8,128)(2,1)}, u32[]{:S(2)}) copy-start(bf16[768,1536]{1,0:T(8,128)(2,1)} %get-tuple-element.91.weight_ref) | copy-start | bytes 7077892
  294.7 1.2 collective-permute-start.3
  295.8 7.9 %collective-permute-start.4 = (f32[2,8,128]{2,1,0:T(8,128)S(1)}, f32[2,8,128]{2,1,0:T(8,128)S(1)}, u32[]{:S(2)}, u32[]{:S(2)}) collective-permute-start(f32[2,8,128]{2,1,0:T(8,128)S(1)} %fusion.22), channel_id=1, source_target_pairs={{0,1},{1,0},{2,3},{3,2},{4,5},{5,4},{6,7},{7,6},{8,9},{9,8},{10,11... | collective-permute-start | bytes 24584 | tf_op jit(solution)/shard_map/ppermute | solution.py:1424
  316.2 51.8 %collective-permute-start.5 = (bf16[384,1536]{1,0:T(8,128)(2,1)S(1)}, bf16[384,1536]{1,0:T(8,128)(2,1)}, u32[]{:S(2)}, u32[]{:S(2)}) collective-permute-start(bf16[384,1536]{1,0:T(8,128)(2,1)S(1)} %dynamic-slice_bitcast_fusion.1), channel_id=1, source_target_pairs={{0,2},{1,3},{2,0},{3,1},{4,6},{5,7},{6,4},{7,5},{8,10},{9,11},{10,... | collective-permute-start | bytes 3538952 | tf_op jit(solution)/shard_map/ppermute | solution.py:1428
  321.9 218.6 %reduce-scatter.5.cloned.1.call-start = ((), (), s32[]{:S(2)}) async-start(), calls=%async_computation.3 | async-start | bytes 2949120 | tf_op jit(solution)/shard_map/reduce_scatter | solution.py:2232
  350.0 11.3 %copy-start.13 = (bf16[1024,1536]{1,0:T(8,128)(2,1)S(1)}, bf16[1024,1536]{1,0:T(8,128)(2,1)}, u32[]{:S(2)}) copy-start(bf16[1024,1536]{1,0:T(8,128)(2,1)} %get-tuple-element.87.left_ref) | copy-start | bytes 9437188
  370.9 84.7 %copy-start.6 = (f32[8,128]{1,0:T(8,128)S(1)}, f32[8,128]{1,0:T(8,128)}, u32[]{:S(2)}) copy-start(f32[8,128]{1,0:T(8,128)} %get-tuple-element.106) | copy-start | bytes 12292
  370.9 85.8 %copy-start.17 = (bf16[768,1536]{1,0:T(8,128)(2,1)S(1)}, bf16[768,1536]{1,0:T(8,128)(2,1)}, u32[]{:S(2)}) copy-start(bf16[768,1536]{1,0:T(8,128)(2,1)} %get-tuple-element.80.weight_ref) | copy-start | bytes 7077892
  446.7 36.6 %collective-permute-start.11 = (bf16[256,1536]{1,0:T(8,128)(2,1)}, bf16[256,1536]{1,0:T(8,128)(2,1)}, u32[]{:S(2)}, u32[]{:S(2)}) collective-permute-start(bf16[256,1536]{1,0:T(8,128)(2,1)} %get-tuple-element.116), channel_id=1, source_target_pairs={{8,16},{12,17},{10,18},{14,19},{24,20},{28,21},{26,22},{30,23},{9,... | collective-permute-start | bytes 2359304 | tf_op jit(solution)/shard_map/ppermute | solution.py:2280
  449.8 35.6 %collective-permute-start.10 = (bf16[256,1536]{1,0:T(8,128)(2,1)}, bf16[256,1536]{1,0:T(8,128)(2,1)}, u32[]{:S(2)}, u32[]{:S(2)}) collective-permute-start(bf16[256,1536]{1,0:T(8,128)(2,1)} %get-tuple-element.116), channel_id=1, source_target_pairs={{0,16},{4,17},{2,18},{6,19},{16,20},{20,21},{18,22},{22,23},{1,24}... | collective-permute-start | bytes 2359304 | tf_op jit(solution)/shard_map/ppermute | solution.py:2280
  451.4 67.8 %collective-permute-start.8 = (bf16[2,928,384]{2,1,0:T(8,128)(2,1)}, bf16[2,928,384]{2,1,0:T(8,128)(2,1)}, u32[]{:S(2)}, u32[]{:S(2)}) collective-permute-start(bf16[2,928,384]{2,1,0:T(8,128)(2,1)} %get-tuple-element.111.refs_15_), channel_id=1, source_target_pairs={{16,18},{17,19},{18,16},{19,17},{20,22},{21,23},{22,20},{23,21},{2... | collective-permute-start | bytes 4276232 | tf_op jit(solution)/shard_map/ppermute | solution.py:2274
  453.2 66.0 %collective-permute-start.7 = (bf16[2,928,384]{2,1,0:T(8,128)(2,1)}, bf16[2,928,384]{2,1,0:T(8,128)(2,1)}, u32[]{:S(2)}, u32[]{:S(2)}) collective-permute-start(bf16[2,928,384]{2,1,0:T(8,128)(2,1)} %get-tuple-element.111.refs_15_), channel_id=1, source_target_pairs={{16,17},{17,16},{18,19},{19,18},{20,21},{21,20},{22,23},{23,22},{2... | collective-permute-start | bytes 4276232 | tf_op jit(solution)/shard_map/ppermute | solution.py:2274
  462.9 56.3 %collective-permute-start.9 = (bf16[2,192,1536]{2,1,0:T(8,128)(2,1)}, bf16[2,192,1536]{2,1,0:T(8,128)(2,1)}, u32[]{:S(2)}, u32[]{:S(2)}) collective-permute-start(bf16[2,192,1536]{2,1,0:T(8,128)(2,1)} %get-tuple-element.112.refs_19_), channel_id=1, source_target_pairs={{16,17},{17,16},{18,19},{19,18},{20,21},{21,20},{22,23},{23,22},{2... | collective-permute-start | bytes 3538952 | tf_op jit(solution)/shard_map/ppermute | solution.py:2274
  471.5 13.9 %copy-start.16 = (bf16[1024,1536]{1,0:T(8,128)(2,1)S(1)}, bf16[1024,1536]{1,0:T(8,128)(2,1)}, u32[]{:S(2)}) copy-start(bf16[1024,1536]{1,0:T(8,128)(2,1)} %get-tuple-element.117) | copy-start | bytes 9437188
  483.3 33.4 %collective-permute-start.6 = (bf16[384,1536]{1,0:T(8,128)(2,1)S(1)}, bf16[384,1536]{1,0:T(8,128)(2,1)}, u32[]{:S(2)}, u32[]{:S(2)}) collective-permute-start(bf16[384,1536]{1,0:T(8,128)(2,1)S(1)} %dynamic-slice_bitcast_fusion), channel_id=1, source_target_pairs={{0,2},{1,3},{2,0},{3,1},{4,6},{5,7},{6,4},{7,5},{8,10},{9,11},{10,... | collective-permute-start | bytes 3538952 | tf_op jit(solution)/shard_map/ppermute | solution.py:1428
  519.2 12.2 %copy-start.11 = (bf16[1024,1536]{1,0:T(8,128)(2,1)S(1)}, bf16[1024,1536]{1,0:T(8,128)(2,1)}, u32[]{:S(2)}) copy-start(bf16[1024,1536]{1,0:T(8,128)(2,1)} %get-tuple-element.75.left_ref) | copy-start | bytes 9437188
  519.2 19.0 %collective-permute-start.12 = (bf16[2,928,384]{2,1,0:T(8,128)(2,1)}, bf16[2,928,384]{2,1,0:T(8,128)(2,1)S(1)}, u32[]{:S(2)}, u32[]{:S(2)}) collective-permute-start(bf16[2,928,384]{2,1,0:T(8,128)(2,1)} %collective-permute-done.8.refs_17_), channel_id=1, source_target_pairs={{16,17},{17,16},{18,19},{19,18},{20,21},{21,20},{22,23},{23,22},{2... | collective-permute-start | bytes 4276232 | tf_op jit(solution)/shard_map/ppermute | solution.py:2274
  653.4 10.1 %copy-start.9 = (f32[1,384]{1,0:T(1,128)S(1)}, f32[1,384]{1,0:T(1,128)}, u32[]{:S(2)}) copy-start(f32[1,384]{1,0:T(1,128)} %get-tuple-element.179) | copy-start | bytes 4612
  653.4 10.6 %copy-start.3 = (f32[4,832]{1,0:T(4,128)S(1)}, f32[4,832]{1,0:T(4,128)}, u32[]{:S(2)}) copy-start(f32[4,832]{1,0:T(4,128)} %get-tuple-element.133) | copy-start | bytes 39940
  653.4 11.2 %copy-start.7 = (f32[1,832]{1,0:T(1,128)S(1)}, f32[1,832]{1,0:T(1,128)}, u32[]{:S(2)}) copy-start(f32[1,832]{1,0:T(1,128)} %get-tuple-element.182) | copy-start | bytes 9988
  653.4 11.8 %copy-start.21 = (f32[1,12]{1,0:T(1,128)S(1)}, f32[1,12]{1,0:T(1,128)}, u32[]{:S(2)}) copy-start(f32[1,12]{1,0:T(1,128)} %get-tuple-element.183) | copy-start | bytes 148
  653.4 12.3 %copy-start.20 = (f32[1,12]{1,0:T(1,128)S(1)}, f32[1,12]{1,0:T(1,128)}, u32[]{:S(2)}) copy-start(f32[1,12]{1,0:T(1,128)} %get-tuple-element.184) | copy-start | bytes 148
  653.4 12.8 %copy-start.19 = (f32[1,12]{1,0:T(1,128)S(1)}, f32[1,12]{1,0:T(1,128)}, u32[]{:S(2)}) copy-start(f32[1,12]{1,0:T(1,128)} %get-tuple-element.185) | copy-start | bytes 148
  653.4 13.3 %copy-start.8 = (f32[1,768]{1,0:T(1,128)S(1)}, f32[1,768]{1,0:T(1,128)}, u32[]{:S(2)}) copy-start(f32[1,768]{1,0:T(1,128)} %get-tuple-element.186) | copy-start | bytes 9220
  (7 other events, 38.3 us)
Sparse Core Ops, SparseCore 0:
  322.0 48.8 reduce-scatter.2
  489.6 50.7 reduce-scatter.4

commit v6 on v5

--- a/solution.py
+++ b/solution.py
@@ -1449,7 +1449,7 @@
 def sum_kernel(layer, *refs):
     last = layer == 0
     (
-        gate_ref, grad_ref, out_grad_ref, theirs_ref, mine_ref, entering_ref, incoming_ref, gain_ref,
+        gate_ref, grad_ref, out_grad_ref, left_ref, weight_ref, entering_ref, incoming_ref, gain_ref,
         extra_ref,
     ) = refs[:9]
     if last:
@@ -1461,18 +1461,18 @@
         refs = refs[:9] + refs[12:]
     all_ref, out_all_ref, bound_ref = refs[9:12]
     (
-        n_core, n_send, n_across, n_done, y_buf, z_buf, s_buf, yo_buf, yo_mine,
+        theirs_ref, mine_ref, n_core, n_send, n_across, n_done, y_buf, z_buf, s_buf, yo_buf, yo_mine,
         y_send, y_recv, z_send, z_recv, yo_sem, core_send, core_recv,
         x_send, x_recv, ya_send, ya_recv, relay_send, relay_recv, xo_send, xo_recv, n_sem,
-    ) = refs[19:44]
+    ) = refs[19:46]
     if last:
         total_refs = refs[12:19]
-        tiny_mine, t1_buf, t1_sum, t2_buf, t2_sum, t3_buf, g_mine, g_buf, g_sum, g_all = refs[44:54]
-        t_send, t_recv, home_send, home_recv, g_send, g_recv = refs[54:]
+        tiny_mine, t1_buf, t1_sum, t2_buf, t2_sum, t3_buf, g_mine, g_buf, g_sum, g_all = refs[46:56]
+        t_send, t_recv, home_send, home_recv, g_send, g_recv, late_sem = refs[56:]
     else:
         g_ref, g_all_ref, dots_ref, norm_ref = refs[12:16]
-        r_core, r_send, r_across = refs[44:47]
-        row_send, row_recv, dot_send, dot_recv, r_sem = refs[47:]
+        r_core, r_send, r_across = refs[46:49]
+        row_send, row_recv, dot_send, dot_recv, r_sem = refs[49:]
     c, z, y, x = place()
     quarter = 2 * x + c
     core, x_other, y_other = {"section": 1 - c}, {"rep": 2 * y + 1 - x}, {"rep": 2 * (1 - y) + x}
@@ -1651,7 +1651,6 @@
         g_gather = RowGather(g_all_ref, block, (row_send, row_recv))
         dot_gather = RowGather(dots_ref, None, (dot_send, dot_recv))
 
-    n_core_copy().start()
     if not last:
         r_core_copy().start()
     for ch in chunks[2:]:
@@ -1739,6 +1738,28 @@
     def summed(which):
         rows = rows_at(which * block, block)
         return mine_ref[rows] + n_core[rows].astype(jnp.float32)
+
+    def late_copies():
+        pairs = []
+        for i, (xx, yy) in enumerate(((x, y), (1 - x, y), (x, 1 - y), (1 - x, 1 - y))):
+            for who in range(CORES):
+                found, whole = late_refs[i].at[who], all_ref.at[2 * xx + who]
+                pairs.append(
+                    (found.at[pl.ds(0, GATE_HALF)], whole.at[rows_at(yy * GATE_HALF, GATE_HALF)])
+                )
+                pairs.append(
+                    (
+                        found.at[pl.ds(GATE_HALF, REST_HALF)],
+                        whole.at[rows_at(GATE + yy * REST_HALF, REST_HALF)],
+                    )
+                )
+        for i, xx in enumerate((x, 1 - x)):
+            for who in range(CORES):
+                pairs.append((late_out_refs[i].at[who], out_part(2 * xx + who)))
+        return [
+            pltpu.make_async_copy(source, target, late_sem.at[n])
+            for n, (source, target) in enumerate(pairs)
+        ]
 
     def start_across():
         n_core_copy().wait_recv()
@@ -1845,8 +1866,28 @@
             for i in range(3):
                 g3_copy(i).start()
 
+    def product(core_of, target):
+        rows = [
+            left_ref[rows_at((2 * i + core_of) * block, block)] for i in range(2)
+        ]
+        rows = jnp.concatenate(rows, axis=0)
+        step = D // 3
+        for i in range(3):
+            lanes = slice(i * step, (i + 1) * step)
+            target[:, lanes] = mm(rows, weight_ref[:, lanes]).astype(target.dtype)
+
     send_in(0, 0)
     send_in(0, 1)
+    if last:
+
+        @pl.when(c != layer)
+        def _():
+            for late in late_copies():
+                late.start()
+
+    product(1 - c, theirs_ref)
+    n_core_copy().start()
+    product(c, mine_ref)
     start_across()
     early_small()
     send_in(1, 0)
@@ -1905,13 +1946,8 @@
 
         @pl.when(c != layer)
         def _():
-            for i, (xx, yy) in enumerate(((x, y), (1 - x, y), (x, 1 - y), (1 - x, 1 - y))):
-                for who in range(CORES):
-                    for ch in chunks:
-                        all_part(2 * xx + who, yy, ch)[...] = late_refs[i][who, span_of(ch)]
-            for i, xx in enumerate((x, 1 - x)):
-                for who in range(CORES):
-                    out_part(2 * xx + who)[...] = late_out_refs[i][who]
+            for late in late_copies():
+                late.wait()
 
     if last:
         for i in range(3):
@@ -2020,7 +2056,7 @@
         ref[...] = heads[6:7, :per]
 
 
-def layer_sums(layer, gate, grad, out_grad, theirs, mine, entering, incoming, gain, extra, *more):
+def layer_sums(layer, gate, grad, out_grad, left, weight, entering, incoming, gain, extra, *more):
     dma = pltpu.SemaphoreType.DMA
     inside = pl.BlockSpec(memory_space=pltpu.VMEM)
     span = (HALF, LANE_PART)
@@ -2028,6 +2064,7 @@
     steps = len(STEPS)
     two = (CORES, steps)
     rows = entering.shape
+    two_blocks = (2 * rows[0], rows[1])
     half, whole = jnp.bfloat16, jnp.float32
     last = layer == 0
     out_shape = [
@@ -2036,7 +2073,9 @@
         jax.ShapeDtypeStruct((MICRO,) + rows if last else rows, half),
     ]
     scratch = [
-        pltpu.VMEM(theirs.shape, half),
+        pltpu.VMEM(two_blocks, half),
+        pltpu.VMEM(two_blocks, whole),
+        pltpu.VMEM(two_blocks, half),
         pltpu.VMEM(rows, half),
         pltpu.VMEM(rows, half),
         pltpu.VMEM(rows, half),
@@ -2067,6 +2106,7 @@
             pltpu.VMEM((8, D), whole),
             pltpu.VMEM((8, D), whole),
             dma((7,)), dma((7,)), dma((1,)), dma((MICRO,)), dma((7,)), dma((7,)),
+            dma((20,)),
         ]
     else:
         out_shape += [
@@ -2077,22 +2117,23 @@
         ]
         out_shape += [jax.ShapeDtypeStruct((8, LANES), whole)] * 3
         scratch += [
-            pltpu.VMEM(theirs.shape, half),
+            pltpu.VMEM(two_blocks, half),
             pltpu.VMEM(rows, half),
             pltpu.VMEM(rows, half),
             dma((3,)), dma((3,)), dma((3,)), dma((3,)), dma((4,)),
         ]
+    beside = 6 if last else 0
     return pl.pallas_call(
         functools.partial(sum_kernel, layer),
-        in_specs=[inside] * (9 + len(more)),
+        in_specs=[inside] * (9 + len(more) - beside) + [pl.BlockSpec(memory_space=pl.ANY)] * beside,
         out_specs=[inside] * 10,
         out_shape=out_shape,
         scratch_shapes=scratch,
         compiler_params=pltpu.CompilerParams(
-            collective_id=2 + layer, has_side_effects=True, vmem_limit_bytes=VMEM_BYTES
+            collective_id=2 + layer, has_side_effects=True, vmem_limit_bytes=62 * 1024 * 1024
         ),
         name="layer_sums",
-    )(gate, grad, out_grad, theirs, mine, entering, incoming, gain, extra, *more)
+    )(gate, grad, out_grad, left, weight, entering, incoming, gain, extra, *more)
 
 
 def assemble_kernel(part_ref, shared_ref, out_ref, total_ref, out_total_ref):
@@ -2263,9 +2304,8 @@
     out_theirs, out_mine = group_parts(gg1, w_out1)
     out_part1 = out_sum(gg1, out_inv1, g1)
     pg1, gate1, rest1, small_grads1 = backward(1, kept1, og1, per_row1)
-    theirs, mine = group_parts(pg1, w_in1)
     in_own, out_own, result, middle_grad, g0, dots0, norm_grad1, *_ = layer_sums(
-        1, gate1, rest1, out_part1, theirs, mine, middle, cotangent, norms[1, 0:1], added0,
+        1, gate1, rest1, out_part1, pg1, w_in1, middle, cotangent, norms[1, 0:1], added0,
         out_theirs, out_mine, own(out_inv1),
     )
     dots0 = dots0[:, : block // LANES].reshape((rows, 1))
@@ -2276,22 +2316,21 @@
     in_near, in_across = on_second(in_own, 1), on_second(in_own, 2)
     out_near = on_second(out_own, 1)
     in_far = on_second(in_across, 1)
+    og0 = mm(g0, w_out0, 1, 1)
+    out_part0 = out_sum(gg0, out_inv0, g0)
+    result = after(result, out_part0)
     results = [
         lax.ppermute(
             result, axes, [(home(m, zz, rr), spot(1, zz, rr)) for zz in range(4) for rr in range(4)]
         )
         for m in range(MICRO)
     ]
-
-    og0 = mm(g0, w_out0, 1, 1)
-    out_part0 = out_sum(gg0, out_inv0, after(g0, *results))
     per_row0 = jnp.concatenate([out_inv0, dots0], axis=1)
     pg0, gate0, rest0, small_grads0 = backward(
-        0, kept0, og0, per_row0, (in_own, out_own), (in_near, in_across, out_near)
-    )
-    theirs, mine = group_parts(pg0, w_in0)
+        0, kept0, og0, per_row0, (in_own, out_own), (in_near, in_across, out_near, result)
+    )
     in_all, out_all, entry_grads, *totals = layer_sums(
-        0, gate0, rest0, out_part0, theirs, mine, source, middle_grad, norms[0, 0:1], norm_grad1,
+        0, gate0, rest0, out_part0, pg0, w_in0, source, middle_grad, norms[0, 0:1], norm_grad1,
         *small_grads0, *small_grads1, in_own, in_near, in_across, in_far, out_own, out_near,
     )
     in_total, out_total = assemble_rows(in_all, out_all)

time: 684 us -> 682 us (level)
  Pallas kernels: 559 us -> 548 us
    pallas_call x4 -> x2, Pallas kernels: 35 us -> 12.6 us  [group_parts(): pl.pallas_call(product_kernel, grid=(3,), in_specs=[pl.BlockSpec((rows, d...]
    reduce_scatter x2, waiting for transfers between devices: 2.48 us -> 14.6 us  [out_sum(): return lax.psum_scatter(grad, 'shard', scatter_dimension=0, tiled=False)]
    pallas_call x2, Pallas kernels: 185 us -> 197 us  [layer_sums(): pl.pallas_call(functools.partial(sum_kernel, layer), in_specs=[inside] *...]
    ppermute x2, waiting for transfers between devices: 7.16 us -> 0.01 us  [per_device_split(): lax.ppermute(result, axes, [(home(m, zz, rr), spot(1, zz, rr)) for zz in...]
  transfers between devices with their start and end apart: 15 -> 15, of which waited for: 4 -> 3; matrix products, arithmetic and copies ran while one was open for 7% -> 8% of each run, Pallas kernels for 34% -> 49%
where the time goes in v6:
time: 682 us; the launch traced here: 672 us
  Pallas kernels  548 us (80%)
  matrix products  47 us (7%)
  starting transfers between devices  20.9 us (3%)
  local copies, waits for them, and re-layouts  16.4 us (2%)
  waiting for transfers between devices  15.8 us (2%)
  between operations  14.7 us (2%)
  other arithmetic  8.84 us (1%)
    pallas_call x2, Pallas kernels, layer_sums(): pl.pallas_call(functools.partial(sum_kernel, layer), in_specs=[inside] *...  197 us
    pallas_call x1, Pallas kernels, enter_first(): pl.pallas_call(enter_first_kernel, in_specs=[anywhere] * 3 + [inside], ou...  108 us
    pallas_call x1, Pallas kernels, enter_second(): pl.pallas_call(enter_second_kernel, in_specs=[anywhere] * 2 + [inside] *...  100 us
    pallas_call x2, Pallas kernels, mixer_backward(): pl.pallas_call(functools.partial(backward_kernel, width), grid=(chunks,),...  54.2 us
    dot_general x8, matrix products, mm(): lax.dot_general(a, b, (((da,), (db,)), ((), ())), preferred_element_type=...  47 us
    pallas_call x2, Pallas kernels, mixer_forward(): pl.pallas_call(functools.partial(forward_kernel, width), grid=(chunks,),...  29.9 us
    pallas_call x2, Pallas kernels, projection(): pl.pallas_call(projection_kernel, grid=(pl.cdiv(columns, step),), in_spec...  23 us
    reduce_scatter x2, waiting for transfers between devices, out_sum(): return lax.psum_scatter(grad, 'shard', scatter_dimension=0, tiled=False)  14.6 us
  transfers between devices with their start and end apart: 15, of which 3 were waited for; matrix products, arithmetic and copies ran while one was open for 8% of the time, Pallas kernels for 49%

profile of v6, /device:TPU:16, one launch (start us, length us, event | category | flops | bytes accessed | tf_op | source)
XLA Modules:
  0.0 671.7 jit_solution(8359139134198773754)
XLA Ops:
  15.4 107.7 %enter_first.1 = (bf16[1856,1536]{1,0:T(8,128)(2,1)}, bf16[768,1536]{1,0:T(8,128)(2,1)}, bf16[256,1536]{1,0:T(8,128)(2,1)}, bf16[1024,1536]{1,0:T(8,128)(2,1)}, ...) custom-call(bf16[6448,384]{1,0:T(8,128)(2,1)} %bitcast.82, bf16[768,1536]{1,0:T(8,128)(2,1)} %bitcast.84, ...), custom_call_target="tpu_custom_call" | custom-call | tf_op jit(solution)/shard_map/enter_first/pallas_call | solution.py:1277
  126.8 11.5 %projection.2.proj_ref.rim_ref = bf16[1024,1856]{1,0:T(8,128)(2,1)} custom-call(bf16[1024,1536]{1,0:T(8,128)(2,1)} %get-tuple-element.71.left_ref, bf16[1856,1536]{1,0:T(8,128)(2,1)} %get-tuple-element.72.weight_ref.refs_4_), custom_call_target="tpu_custom_call" | custom-call | flops 6600000000 | tf_op jit(solution)/shard_map/projection/pallas_call | solution.py:790
  140.6 14.9 %mixer_forward.2 = (bf16[1024,768]{1,0:T(8,128)(2,1)}, f32[8,1,128]{2,1,0:T(1,128)}, f32[1024,768]{1,0:T(8,128)}, f32[8,128,768]{2,1,0:T(8,128)}) custom-call(bf16[1024,1856]{1,0:T(8,128)(2,1)} %projection.2.proj_ref.rim_ref, f32[1024,8]{1,0:T(8,128)} %copy.52.marks_ref, f32[1,1024]{1,0:T(1,128)} %bitcast.115, f32[2,16,1024]{2,1,0:T(8,128)} %get-tuple-element.73.small_ref), custom_call_target="tpu_custom_call" | custom-call | flops 17600000000 | tf_op jit(solution)/shard_map/mixer_forward/pallas_call | solution.py:814
  155.5 6.3 group_parts.2
  162.8 100.0 %enter_second.1 = (bf16[1856,1536]{1,0:T(8,128)(2,1)}, bf16[768,1536]{1,0:T(8,128)(2,1)}, f32[256,1536]{1,0:T(8,128)}, bf16[256,1536]{1,0:T(8,128)(2,1)}, bf16[1...) custom-call(bf16[6448,384]{1,0:T(8,128)(2,1)} %bitcast.83, bf16[768,1536]{1,0:T(8,128)(2,1)} %bitcast.85, ...), custom_call_target="tpu_custom_call" | custom-call | tf_op jit(solution)/shard_map/enter_second/pallas_call | solution.py:1390
  262.8 11.5 %projection.3.proj_ref.rim_ref = bf16[1024,1856]{1,0:T(8,128)(2,1)} custom-call(bf16[1024,1536]{1,0:T(8,128)(2,1)} %get-tuple-element.83.left_ref, bf16[1856,1536]{1,0:T(8,128)(2,1)} %get-tuple-element.84.weight_ref.refs_4_), custom_call_target="tpu_custom_call" | custom-call | flops 6600000000 | tf_op jit(solution)/shard_map/projection/pallas_call | solution.py:790
  274.3 15.1 %mixer_forward.3 = (bf16[1024,768]{1,0:T(8,128)(2,1)}, f32[8,1,128]{2,1,0:T(1,128)}, f32[1024,768]{1,0:T(8,128)}, f32[8,128,768]{2,1,0:T(8,128)}) custom-call(bf16[1024,1856]{1,0:T(8,128)(2,1)} %projection.3.proj_ref.rim_ref, f32[1024,8]{1,0:T(8,128)} %copy.52.marks_ref, f32[1,1024]{1,0:T(1,128)} %bitcast.116, f32[2,16,1024]{2,1,0:T(8,128)} %get-tuple-element.73.small_ref), custom_call_target="tpu_custom_call" | custom-call | flops 17600000000 | tf_op jit(solution)/shard_map/mixer_forward/pallas_call | solution.py:814
  289.4 5.3 fusion
  295.8 2.2 collective-permute-start.4
  298.0 6.3 group_parts.3
  305.4 6.8 %gate_backward.2 = (bf16[1024,768]{1,0:T(8,128)(2,1)}, bf16[1024,768]{1,0:T(8,128)(2,1)}, f32[8,768]{1,0:T(8,128)}) custom-call(bf16[1024,1856]{1,0:T(8,128)(2,1)} %projection.3.proj_ref.rim_ref, f32[2,16,1024]{2,1,0:T(8,128)} %get-tuple-element.73.small_ref, f32[1024,768]{1,0:T(8,128)} %get-tuple-element.85.out_ref, f32[1024,768]{1,0:T(8,128)} %get-tuple-element.155.og_ref, ...), custom_call_target="tpu_custom_call" | custom-call | flops 6600000000 | tf_op jit(solution)/shard_map/gate_backward/pallas_call | solution.py:601
  312.3 4.5 convolution_convert_fusion.5
  318.4 4.1 convolution_convert_fusion.4
  322.7 27.1 %mixer_backward.2 = (bf16[1024,1856]{1,0:T(8,128)(2,1)}, f32[8,1024]{1,0:T(8,128)}, f32[8,128]{1,0:T(8,128)}) custom-call(bf16[1024,1856]{1,0:T(8,128)(2,1)} %projection.3.proj_ref.rim_ref, bf16[1024,1856]{1,0:T(8,128)(2,1)} %projection.3.proj_ref.rim_ref, f32[1024,8]{1,0:T(8,128)} %copy.52.marks_ref, f32[1,1024]{1,0:T(1,128)} %bitcast.117, ...), custom_call_target="tpu_custom_call" | custom-call | flops 36300001280 | tf_op jit(solution)/shard_map/mixer_backward/pallas_call | solution.py:854
  350.6 8.1 %convolution_convert_fusion.1.refs_1_ = bf16[1088,1536]{1,0:T(8,128)(2,1)} fusion(bf16[1024,1536]{1,0:T(8,128)(2,1)} %get-tuple-element.83.left_ref, bf16[1024,1856]{1,0:T(8,128)(2,1)} %get-tuple-element.94.refs_3_), kind=kOutput, calls=%fused_computation.1 | convolution fusion | flops 3424223232 | bytes 8847360 | tf_op jit(solution)/shard_map/dot_general | solution.py:424
  358.7 2.6 fusion.4.refs_0_
  361.3 9.5 %reduce-scatter.3.cloned.1.call-done = bf16[1,192,1536]{2,1,0:T(8,128)(2,1)} async-done(((bf16[4,192,1536]{2,1,0:T(8,128)(2,1)}), bf16[1,192,1536]{2,1,0:T(8,128)(2,1)}) %reduce-scatter.3.cloned.1.call-update) | async-done | bytes 589840 | tf_op jit(solution)/shard_map/reduce_scatter | solution.py:2273
  370.8 84.9 %layer_sums.2 = (bf16[2,928,384]{2,1,0:T(8,128)(2,1)}, bf16[2,192,1536]{2,1,0:T(8,128)(2,1)}, bf16[256,1536]{1,0:T(8,128)(2,1)}, bf16[256,1536]{1,0:T(8,128)(2,1...) custom-call(bf16[384,1536]{1,0:T(8,128)(2,1)} %fusion.4.refs_0_, ...), custom_call_target="tpu_custom_call" | custom-call | tf_op jit(solution)/shard_map/layer_sums/pallas_call | solution.py:2126
  459.1 7.1 %fusion.23.og_ref = f32[1024,768]{1,0:T(8,128)} fusion(bf16[1024,1536]{1,0:T(8,128)(2,1)} %get-tuple-element.99, bf16[768,1536]{1,0:T(8,128)(2,1)} %get-tuple-element.76.weight_ref), kind=kOutput, calls=%fused_computation.85 | convolution fusion | flops 2415919104 | bytes 8650752 | tf_op jit(solution)/shard_map/dot_general | solution.py:424
  466.2 4.1 convolution_convert_fusion.2
  470.3 1.8 collective-permute-start.9
  472.1 6.7 gate_backward.3
  478.7 5.4 convolution_convert_fusion.3
  485.2 2.1 collective-permute-start.10
  487.4 27.1 %mixer_backward.3 = (bf16[1024,1856]{1,0:T(8,128)(2,1)}, f32[8,1024]{1,0:T(8,128)}, f32[8,128]{1,0:T(8,128)}) custom-call(bf16[1024,1856]{1,0:T(8,128)(2,1)} %projection.2.proj_ref.rim_ref, bf16[1024,1856]{1,0:T(8,128)(2,1)} %projection.2.proj_ref.rim_ref, f32[1024,8]{1,0:T(8,128)} %copy.52.marks_ref, f32[1,1024]{1,0:T(1,128)} %bitcast.118, ...), custom_call_target="tpu_custom_call" | custom-call | flops 36300001280 | tf_op jit(solution)/shard_map/mixer_backward/pallas_call | solution.py:854
  515.8 5.1 reduce-scatter.5.cloned.1.call-done
  520.9 1.5 collective-permute-start.11
  522.4 5.5 collective-permute-start.12
  527.9 8.5 %convolution_convert_fusion.refs_1_ = bf16[1088,1536]{1,0:T(8,128)(2,1)} fusion(bf16[1024,1536]{1,0:T(8,128)(2,1)} %get-tuple-element.71.left_ref, bf16[1024,1856]{1,0:T(8,128)(2,1)} %get-tuple-element.111.refs_3_), kind=kOutput, calls=%fused_computation | convolution fusion | flops 3424223232 | bytes 8847360 | tf_op jit(solution)/shard_map/dot_general | solution.py:424
  536.4 112.2 %layer_sums.3 = (bf16[4,1856,384]{2,1,0:T(8,128)(2,1)}, bf16[768,1536]{1,0:T(8,128)(2,1)}, bf16[2,256,1536]{2,1,0:T(8,128)(2,1)}, f32[1,384]{1,0:T(1,128)}, f32[...) custom-call(bf16[384,1536]{1,0:T(8,128)(2,1)} %fusion.3.refs_0_, ...), custom_call_target="tpu_custom_call" | custom-call | tf_op jit(solution)/shard_map/layer_sums/pallas_call | solution.py:2126
  648.6 10.1 %assemble_rows.1 = (f32[6448,384]{1,0:T(8,128)}, f32[1,768,1536]{2,1,0:T(8,128)}) custom-call(bf16[4,1856,384]{2,1,0:T(8,128)(2,1)} %get-tuple-element.122.part_ref.shared_ref, bf16[4,1856,384]{2,1,0:T(8,128)(2,1)} %get-tuple-element.122.part_ref.shared_ref, bf16[768,1536]{1,0:T(8,128)(2,1)} %get-tuple-element.123.out_ref), custom_call_target="tpu_custom_call" | custom-call | tf_op jit(solution)/shard_map/assemble_rows/pallas_call | solution.py:2163
  658.9 1.9 maximum_convert_fusion
  (119 shorter events, 29.7 us)
Async XLA Ops:
  7.2 363.7 %reduce-scatter.3.cloned.1.call-start = ((), (), s32[]{:S(2)}) async-start(), calls=%async_computation.2 | async-start | bytes 2949120 | tf_op jit(solution)/shard_map/reduce_scatter | solution.py:2273
  7.9 130.4 %collective-permute-start = (s32[2,2,4]{2,1,0:T(2,128)S(1)}, s32[2,2,4]{2,1,0:T(2,128)S(1)}, u32[]{:S(2)}, u32[]{:S(2)}) collective-permute-start(s32[2,2,4]{2,1,0:T(2,128)S(1)} %pad_add_fusion), channel_id=1, source_target_pairs={{0,1},{1,0},{2,3},{3,2},{4,5},{5,4},{6,7},{7,6},{8,9},{9,8},{10,11... | collective-permute-start | bytes 200 | tf_op jit(solution)/shard_map/ppermute | solution.py:1424
  15.4 107.7 %copy-start = (bf16[1,2,1,256,1536]{4,3,2,1,0:T(8,128)(2,1)S(1)}, bf16[1,2,1,256,1536]{4,3,2,1,0:T(8,128)(2,1)}, u32[]{:S(2)}) copy-start(bf16[1,2,1,256,1536]{4,3,2,1,0:T(8,128)(2,1)} %blocks_ref.1) | copy-start | bytes 4718596
  123.3 38.5 %collective-permute-start.1 = (bf16[256,1536]{1,0:T(8,128)(2,1)S(1)}, bf16[256,1536]{1,0:T(8,128)(2,1)S(1)}, u32[]{:S(2)}, u32[]{:S(2)}) collective-permute-start(bf16[256,1536]{1,0:T(8,128)(2,1)S(1)} %get-tuple-element.141), channel_id=1, source_target_pairs={{16,0},{17,4},{18,2},{19,6},{20,16},{21,20},{22,18},{23,22},{24,1}... | collective-permute-start | bytes 2359304 | tf_op jit(solution)/shard_map/ppermute | solution.py:2228
  124.0 37.7 %collective-permute-start.2 = (bf16[256,1536]{1,0:T(8,128)(2,1)S(1)}, bf16[256,1536]{1,0:T(8,128)(2,1)S(1)}, u32[]{:S(2)}, u32[]{:S(2)}) collective-permute-start(bf16[256,1536]{1,0:T(8,128)(2,1)S(1)} %get-tuple-element.140), channel_id=1, source_target_pairs={{16,8},{17,12},{18,10},{19,14},{20,24},{21,28},{22,26},{23,30},{24... | collective-permute-start | bytes 2359304 | tf_op jit(solution)/shard_map/ppermute | solution.py:2228
  126.8 11.5 %copy-start.6 = (s32[2,1,4]{2,1,0:T(1,128)S(1)}, s32[2,1,4]{2,1,0:T(1,128)}, u32[]{:S(2)}) copy-start(s32[2,1,4]{2,1,0:T(1,128)} %param.14) | copy-start | bytes 100
  126.8 11.5 %copy-start.7 = (s32[2,1,4]{2,1,0:T(1,128)S(1)}, s32[2,1,4]{2,1,0:T(1,128)}, u32[]{:S(2)}) copy-start(s32[2,1,4]{2,1,0:T(1,128)} %param.13) | copy-start | bytes 100
  274.3 15.1 %copy-start.13 = (bf16[1024,1536]{1,0:T(8,128)(2,1)S(1)}, bf16[1024,1536]{1,0:T(8,128)(2,1)}, u32[]{:S(2)}) copy-start(bf16[1024,1536]{1,0:T(8,128)(2,1)} %get-tuple-element.86) | copy-start | bytes 9437188
  274.3 15.1 %copy-start.16 = (bf16[768,1536]{1,0:T(8,128)(2,1)S(1)}, bf16[768,1536]{1,0:T(8,128)(2,1)}, u32[]{:S(2)}) copy-start(bf16[768,1536]{1,0:T(8,128)(2,1)} %get-tuple-element.87.weight_ref) | copy-start | bytes 7077892
  289.3 5.3 copy-start.4
  294.6 1.2 collective-permute-start.3
  295.8 8.6 %collective-permute-start.4 = (f32[2,8,128]{2,1,0:T(8,128)S(1)}, f32[2,8,128]{2,1,0:T(8,128)S(1)}, u32[]{:S(2)}, u32[]{:S(2)}) collective-permute-start(f32[2,8,128]{2,1,0:T(8,128)S(1)} %fusion.22), channel_id=1, source_target_pairs={{0,1},{1,0},{2,3},{3,2},{4,5},{5,4},{6,7},{7,6},{8,9},{9,8},{10,11... | collective-permute-start | bytes 24584 | tf_op jit(solution)/shard_map/ppermute | solution.py:1424
  305.4 6.8 %copy-start.12 = (bf16[1024,1536]{1,0:T(8,128)(2,1)S(1)}, bf16[1024,1536]{1,0:T(8,128)(2,1)}, u32[]{:S(2)}) copy-start(bf16[1024,1536]{1,0:T(8,128)(2,1)} %get-tuple-element.83.left_ref) | copy-start | bytes 9437188
  312.3 6.1 copy-start.14
  316.9 41.8 %collective-permute-start.5 = (bf16[384,1536]{1,0:T(8,128)(2,1)S(1)}, bf16[384,1536]{1,0:T(8,128)(2,1)}, u32[]{:S(2)}, u32[]{:S(2)}) collective-permute-start(bf16[384,1536]{1,0:T(8,128)(2,1)S(1)} %dynamic-slice_bitcast_fusion.1), channel_id=1, source_target_pairs={{0,2},{1,3},{2,0},{3,1},{4,6},{5,7},{6,4},{7,5},{8,10},{9,11},{10,... | collective-permute-start | bytes 3538952 | tf_op jit(solution)/shard_map/ppermute | solution.py:1428
  322.5 198.4 %reduce-scatter.5.cloned.1.call-start = ((), (), s32[]{:S(2)}) async-start(), calls=%async_computation.3 | async-start | bytes 2949120 | tf_op jit(solution)/shard_map/reduce_scatter | solution.py:2273
  370.8 87.2 %copy-start.8 = (f32[8,128]{1,0:T(8,128)S(1)}, f32[8,128]{1,0:T(8,128)}, u32[]{:S(2)}) copy-start(f32[8,128]{1,0:T(8,128)} %get-tuple-element.100) | copy-start | bytes 12292
  455.8 72.1 %collective-permute-start.7 = (bf16[2,928,384]{2,1,0:T(8,128)(2,1)}, bf16[2,928,384]{2,1,0:T(8,128)(2,1)S(1)}, u32[]{:S(2)}, u32[]{:S(2)}) collective-permute-start(bf16[2,928,384]{2,1,0:T(8,128)(2,1)} %get-tuple-element.105.refs_15_), channel_id=1, source_target_pairs={{16,17},{17,16},{18,19},{19,18},{20,21},{21,20},{22,23},{23,22},{2... | collective-permute-start | bytes 4276232 | tf_op jit(solution)/shard_map/ppermute | solution.py:2314
  456.5 28.7 %collective-permute-start.8 = (bf16[2,928,384]{2,1,0:T(8,128)(2,1)}, bf16[2,928,384]{2,1,0:T(8,128)(2,1)S(1)}, u32[]{:S(2)}, u32[]{:S(2)}) collective-permute-start(bf16[2,928,384]{2,1,0:T(8,128)(2,1)} %get-tuple-element.105.refs_15_), channel_id=1, source_target_pairs={{16,18},{17,19},{18,16},{19,17},{20,22},{21,23},{22,20},{23,21},{2... | collective-permute-start | bytes 4276232 | tf_op jit(solution)/shard_map/ppermute | solution.py:2314
  459.1 7.1 %copy-start.15 = (bf16[1024,1536]{1,0:T(8,128)(2,1)S(1)}, bf16[1024,1536]{1,0:T(8,128)(2,1)}, u32[]{:S(2)}) copy-start(bf16[1024,1536]{1,0:T(8,128)(2,1)} %get-tuple-element.99) | copy-start | bytes 9437188
  459.1 7.1 %copy-start.21 = (bf16[1024,768]{1,0:T(8,128)(2,1)S(1)}, bf16[1024,768]{1,0:T(8,128)(2,1)}, u32[]{:S(2)}) copy-start(bf16[1024,768]{1,0:T(8,128)(2,1)} %get-tuple-element.75.left_ref) | copy-start | bytes 4718596
  470.3 57.6 %collective-permute-start.9 = (bf16[2,192,1536]{2,1,0:T(8,128)(2,1)}, bf16[2,192,1536]{2,1,0:T(8,128)(2,1)}, u32[]{:S(2)}, u32[]{:S(2)}) collective-permute-start(bf16[2,192,1536]{2,1,0:T(8,128)(2,1)} %get-tuple-element.106.refs_19_), channel_id=1, source_target_pairs={{16,17},{17,16},{18,19},{19,18},{20,21},{21,20},{22,23},{23,22},{2... | collective-permute-start | bytes 3538952 | tf_op jit(solution)/shard_map/ppermute | solution.py:2314
  484.2 30.3 %collective-permute-start.6 = (bf16[384,1536]{1,0:T(8,128)(2,1)S(1)}, bf16[384,1536]{1,0:T(8,128)(2,1)S(1)}, u32[]{:S(2)}, u32[]{:S(2)}) collective-permute-start(bf16[384,1536]{1,0:T(8,128)(2,1)S(1)} %dynamic-slice_bitcast_fusion), channel_id=1, source_target_pairs={{0,2},{1,3},{2,0},{3,1},{4,6},{5,7},{6,4},{7,5},{8,10},{9,11},{10,... | collective-permute-start | bytes 3538952 | tf_op jit(solution)/shard_map/ppermute | solution.py:1428
  485.2 29.2 %copy-start.3 = (bf16[2,928,384]{2,1,0:T(8,128)(2,1)}, bf16[2,928,384]{2,1,0:T(8,128)(2,1)S(1)}, u32[]{:S(2)}) copy-start(bf16[2,928,384]{2,1,0:T(8,128)(2,1)S(1)} %collective-permute-done.8.refs_17_) | copy-start | bytes 4276228
  485.2 51.1 %collective-permute-start.10 = (bf16[2,928,384]{2,1,0:T(8,128)(2,1)S(1)}, bf16[2,928,384]{2,1,0:T(8,128)(2,1)}, u32[]{:S(2)}, u32[]{:S(2)}) collective-permute-start(bf16[2,928,384]{2,1,0:T(8,128)(2,1)S(1)} %collective-permute-done.8.refs_17_), channel_id=1, source_target_pairs={{16,17},{17,16},{18,19},{19,18},{20,21},{21,20},{22,23},{23,22},{2... | collective-permute-start | bytes 4276232 | tf_op jit(solution)/shard_map/ppermute | solution.py:2314
  520.9 137.8 %collective-permute-start.11 = (bf16[256,1536]{1,0:T(8,128)(2,1)}, bf16[256,1536]{1,0:T(8,128)(2,1)}, u32[]{:S(2)}, u32[]{:S(2)}) collective-permute-start(bf16[256,1536]{1,0:T(8,128)(2,1)} %get-tuple-element.110), channel_id=1, source_target_pairs={{0,16},{4,17},{2,18},{6,19},{16,20},{20,21},{18,22},{22,23},{1,24}... | collective-permute-start | bytes 2359304 | tf_op jit(solution)/shard_map/ppermute | solution.py:2323
  522.4 136.3 %collective-permute-start.12 = (bf16[256,1536]{1,0:T(8,128)(2,1)}, bf16[256,1536]{1,0:T(8,128)(2,1)}, u32[]{:S(2)}, u32[]{:S(2)}) collective-permute-start(bf16[256,1536]{1,0:T(8,128)(2,1)} %get-tuple-element.110), channel_id=1, source_target_pairs={{8,16},{12,17},{10,18},{14,19},{24,20},{28,21},{26,22},{30,23},{9,... | collective-permute-start | bytes 2359304 | tf_op jit(solution)/shard_map/ppermute | solution.py:2323
  527.9 8.5 %copy-start.2 = (bf16[2,928,384]{2,1,0:T(8,128)(2,1)}, bf16[2,928,384]{2,1,0:T(8,128)(2,1)S(1)}, u32[]{:S(2)}) copy-start(bf16[2,928,384]{2,1,0:T(8,128)(2,1)S(1)} %collective-permute-done.7.refs_16_) | copy-start | bytes 4276228
  648.5 10.1 %copy-start.1 = (bf16[2,256,1536]{2,1,0:T(8,128)(2,1)S(1)}, bf16[2,256,1536]{2,1,0:T(8,128)(2,1)}, u32[]{:S(2)}) copy-start(bf16[2,256,1536]{2,1,0:T(8,128)(2,1)} %get-tuple-element.120) | copy-start | bytes 4718596
  658.9 4.2 copy-start.18
  658.9 4.7 copy-start.17
  658.9 5.2 copy-start.10
  (5 other events, 12.8 us)
Sparse Core Ops, SparseCore 0:
  322.6 48.1 reduce-scatter.2
  470.4 50.4 reduce-scatter.4
